TPU v7x, 32 devices: a whole 2x2x4 slice. The times are simulated.
32 devices in a mesh: dp: 4 (over y, x), expert: 8 (over z, core).
Axes of the slice: x: 2, y: 2, z: 4, core: 2. Of those that a mesh axis runs over, the one named last changes fastest.
Arguments:
- query_rows: bfloat16 [8, 512, 2048], P('dp', 'expert'), may hold values from -4 to 4
- key_rows: bfloat16 [8, 512, 256], P('dp', 'expert'), may hold values from -4 to 4
- value_rows: bfloat16 [8, 512, 256], P('dp', 'expert'), may hold values from -6 to 6
- gate_logits: bfloat16 [8, 512, 2048], P('dp', 'expert'), may hold values from -6 to 6
- gated_grad: bfloat16 [8, 512, 2048], P('dp', 'expert'), may hold values from -6 to 6
- moe_input: bfloat16 [4096, 2048], P(('dp', 'expert')), may hold values from -6 to 6
- out_grad: bfloat16 [4096, 2048], P(('dp', 'expert')), may hold values from -24 to 24
- routes: int32 [4096, 10], P(('dp', 'expert')), may hold values from 0 to 511, as said below
- route_weights: bfloat16 [4096, 10], P(('dp', 'expert')), may hold values from 0.019897461 to 0.29882812
- gate_proj: bfloat16 [8, 2048, 256], P('expert', 'dp'), may hold values from -0.125 to 0.125
- up_proj: bfloat16 [8, 2048, 256], P('expert', 'dp'), may hold values from -0.125 to 0.125
- down_proj: bfloat16 [8, 256, 2048], P('expert', None, 'dp'), may hold values from -0.375 to 0.375
Outputs:
- query_grad: bfloat16 [8, 512, 2048], P('dp', 'expert')
- key_grad: bfloat16 [8, 512, 256], P('dp', 'expert')
- value_grad: bfloat16 [8, 512, 256], P('dp', 'expert')
- gate_grad: bfloat16 [8, 512, 2048], P('dp', 'expert')
- input_grad: bfloat16 [4096, 2048], P(('dp', 'expert'))
- route_grad: bfloat16 [4096, 10], P(('dp', 'expert'))
- gate_proj_grad: float32 [8, 2048, 256], P('expert', 'dp')
- up_proj_grad: float32 [8, 2048, 256], P('expert', 'dp')
- down_proj_grad: float32 [8, 256, 2048], P('expert', None, 'dp')
Inputs may be any that keep to these rules, and one draw needn't show every extreme that they name: `routes`: each token names 10 different experts. A token names at most one expert below 8; the 128 tokens of one block name each such expert at most 2 times, and in every data group one expert below 8 is named exactly 2 times by every block of the group.
All inputs are finite; a program needn't handle non-finite values.
Results may differ from a plain program's by a relative error of at most 0.035.
Values may be sent and summed in bfloat16 or wider, within the bound.
No kernel may reach another device: no remote copies, remote signals or barrier semaphores. Data moves between devices by JAX's collectives and lax.ppermute only.
A program may use at most 64 MiB of HBM per device.

v0:
```python
import jax
import jax.numpy as jnp
from jax import lax
from jax.sharding import PartitionSpec as P

HEADS = 8
HEAD = 256
CAP = 2


def keep_state(run_state):
    return run_state


def block_scores(queries, keys_block, block_start, first_position, score_scale):
    scores = (
        jnp.einsum("sphd,srd->shpr", queries, keys_block, preferred_element_type=jnp.float32)
        * score_scale
    )
    query_pos = first_position + jnp.arange(queries.shape[1])
    key_pos = block_start + jnp.arange(keys_block.shape[1])
    allowed = key_pos[None, :] <= query_pos[:, None]
    return (scores, allowed[None, None])


def shards(
    query_rows,
    key_rows,
    value_rows,
    gate_logits,
    gated_grad,
    moe_input,
    out_grad,
    routes,
    route_weights,
    gate_proj,
    up_proj,
    down_proj,
):
    seq_count, shard_len, row_width = query_rows.shape
    devices = lax.axis_size("expert")
    position = lax.axis_index("expert")
    first_position = position * shard_len
    last_position = first_position + shard_len - 1
    total_len = shard_len * devices
    block_len = min(total_len, max(shard_len, 128))
    block_count = total_len // block_len
    shards_per_block = block_len // shard_len
    score_scale = HEAD ** (-0.5)
    queries = query_rows.reshape(seq_count, shard_len, HEADS, HEAD)
    packed = jnp.concatenate([key_rows, value_rows], axis=2)
    gathered = lax.all_gather(packed, "expert", axis=1, tiled=True)

    def take_block(block_index):
        block_start = block_index * block_len
        key_piece = lax.dynamic_slice_in_dim(gathered, block_start, block_len, 1)
        return (block_start, key_piece[:, :, :HEAD], key_piece[:, :, HEAD:])

    def max_step(block_index, loop_carry):
        block_start, keys_block, values_block = take_block(block_index)

        def max_update(run_state):
            prior_max, prior_sum = run_state
            scores, allowed = block_scores(
                queries, keys_block, block_start, first_position, score_scale
            )
            masked = jnp.where(allowed, scores, -jnp.inf)
            new_max = jnp.maximum(prior_max, jnp.max(masked, axis=3))
            new_sum = prior_sum * jnp.exp(prior_max - new_max) + jnp.sum(
                jnp.exp(masked - new_max[..., None]), axis=3
            )
            return (new_max, new_sum)

        return lax.cond(block_start <= last_position, max_update, keep_state, loop_carry)

    stat_shape = (seq_count, HEADS, shard_len)
    run_max, run_sum = lax.fori_loop(
        0,
        block_count,
        max_step,
        (jnp.full(stat_shape, -jnp.inf, jnp.float32), jnp.zeros(stat_shape, jnp.float32)),
    )
    log_total = run_max + jnp.log(run_sum)

    def context_step(block_index, loop_carry):
        block_start, keys_block, values_block = take_block(block_index)

        def context_update(running_total):
            scores, allowed = block_scores(
                queries, keys_block, block_start, first_position, score_scale
            )
            exact_probs = jnp.where(allowed, jnp.exp(scores - log_total[..., None]), 0.0)
            return running_total + jnp.einsum(
                "shpr,srd->sphd",
                exact_probs.astype(jnp.bfloat16),
                values_block,
                preferred_element_type=jnp.float32,
            )

        return lax.cond(block_start <= last_position, context_update, keep_state, loop_carry)

    context = lax.fori_loop(
        0, block_count, context_step, jnp.zeros((seq_count, shard_len, HEADS, HEAD), jnp.float32)
    )
    sigmoid_gate = jax.nn.sigmoid(gate_logits.astype(jnp.float32)).reshape(
        seq_count, shard_len, HEADS, HEAD
    )
    upstream = gated_grad.astype(jnp.float32).reshape(seq_count, shard_len, HEADS, HEAD)
    context_grad = (upstream * sigmoid_gate).astype(jnp.bfloat16)
    gate_grad = (
        (upstream * context * sigmoid_gate * (1.0 - sigmoid_gate))
        .astype(jnp.bfloat16)
        .reshape(seq_count, shard_len, row_width)
    )
    grad_dot = jnp.transpose(jnp.sum(context_grad.astype(jnp.float32) * context, axis=3), (0, 2, 1))

    def grad_step(block_index, loop_carry):
        block_start, keys_block, values_block = take_block(block_index)

        def grad_update(run_state):
            query_total, pair_buffer = run_state
            scores, allowed = block_scores(
                queries, keys_block, block_start, first_position, score_scale
            )
            exact_probs = jnp.where(allowed, jnp.exp(scores - log_total[..., None]), 0.0)
            probs_low = exact_probs.astype(jnp.bfloat16)
            prob_grad = jnp.einsum(
                "sphd,srd->shpr", context_grad, values_block, preferred_element_type=jnp.float32
            )
            score_grad = (exact_probs * (prob_grad - grad_dot[..., None]) * score_scale).astype(
                jnp.bfloat16
            )
            query_total = query_total + jnp.einsum(
                "shpr,srd->sphd", score_grad, keys_block, preferred_element_type=jnp.float32
            )
            key_part = jnp.einsum(
                "shpr,sphd->srd", score_grad, queries, preferred_element_type=jnp.float32
            ).astype(jnp.bfloat16)
            value_part = jnp.einsum(
                "shpr,sphd->srd", probs_low, context_grad, preferred_element_type=jnp.float32
            ).astype(jnp.bfloat16)
            pair_block = jnp.concatenate([key_part, value_part], axis=2)
            pair_block = jnp.moveaxis(
                pair_block.reshape(seq_count, shards_per_block, shard_len, 2 * HEAD), 1, 0
            )
            pair_buffer = lax.dynamic_update_slice_in_dim(
                pair_buffer, pair_block, block_start // shard_len, 0
            )
            return (query_total, pair_buffer)

        return lax.cond(block_start <= last_position, grad_update, keep_state, loop_carry)

    query_total, pair_buffer = lax.fori_loop(
        0,
        block_count,
        grad_step,
        (
            jnp.zeros((seq_count, shard_len, HEADS, HEAD), jnp.float32),
            jnp.zeros((devices, seq_count, shard_len, 2 * HEAD), jnp.bfloat16),
        ),
    )
    query_grad = query_total.astype(jnp.bfloat16).reshape(seq_count, shard_len, row_width)
    token_count, model_width = moe_input.shape
    live_slot = routes < devices
    has_live = jnp.any(live_slot, axis=1)
    live_expert = jnp.sum(jnp.where(live_slot, routes, 0), axis=1)
    token_weight = jnp.sum(jnp.where(live_slot, route_weights.astype(jnp.float32), 0.0), axis=1)
    member = (live_expert[:, None] == jnp.arange(devices)[None, :]) & has_live[:, None]
    earlier = (jnp.arange(token_count)[None, :] < jnp.arange(token_count)[:, None]).astype(
        jnp.bfloat16
    )
    before = jnp.dot(earlier, member.astype(jnp.bfloat16), preferred_element_type=jnp.float32)
    slot_rank = jnp.sum(jnp.where(member, before, 0.0), axis=1)
    placed = member.T[:, None, :] & (
        slot_rank[None, None, :] == jnp.arange(CAP)[None, :, None].astype(jnp.float32)
    )
    dispatch_mat = placed.reshape(devices * CAP, token_count).astype(jnp.bfloat16)
    rows_send = (
        jnp.dot(dispatch_mat, moe_input, preferred_element_type=jnp.float32)
        .astype(jnp.bfloat16)
        .reshape(devices, CAP, model_width)
    )
    grads_send = (
        jnp.dot(dispatch_mat, out_grad, preferred_element_type=jnp.float32)
        .astype(jnp.bfloat16)
        .reshape(devices, CAP, model_width)
    )
    weights_send = jnp.sum(jnp.where(placed, token_weight[None, None, :], 0.0), axis=2).astype(
        jnp.bfloat16
    )
    gate_full, up_full, down_full = (
        lax.all_gather(gate_proj, "dp", axis=1, tiled=True),
        lax.all_gather(up_proj, "dp", axis=1, tiled=True),
        lax.all_gather(down_proj, "dp", axis=2, tiled=True),
    )
    gate_mat = gate_full[0]
    up_mat = up_full[0]
    down_mat = down_full[0]
    rows_in, grads_in, weights_in = (
        lax.all_to_all(rows_send, "expert", split_axis=0, concat_axis=0, tiled=True),
        lax.all_to_all(grads_send, "expert", split_axis=0, concat_axis=0, tiled=True),
        lax.all_to_all(weights_send, "expert", split_axis=0, concat_axis=0, tiled=True),
    )
    flat_rows = rows_in.reshape(devices * CAP, model_width)
    flat_grads = grads_in.reshape(devices * CAP, model_width)
    gate_pre = jnp.dot(flat_rows, gate_mat, preferred_element_type=jnp.float32)
    up_pre = jnp.dot(flat_rows, up_mat, preferred_element_type=jnp.float32)
    sigmoid_pre = jax.nn.sigmoid(gate_pre)
    silu_value = gate_pre * sigmoid_pre
    hidden = (silu_value * up_pre).astype(jnp.bfloat16)
    expert_out = jnp.dot(hidden, down_mat, preferred_element_type=jnp.float32)
    weight_back = jnp.sum(expert_out * flat_grads.astype(jnp.float32), axis=1).astype(jnp.bfloat16)
    scaled_grad = (
        weights_in.reshape(-1)[:, None].astype(jnp.float32) * flat_grads.astype(jnp.float32)
    ).astype(jnp.bfloat16)
    contract_last = (((1,), (1,)), ((), ()))
    hidden_grad = lax.dot_general(
        scaled_grad, down_mat, contract_last, preferred_element_type=jnp.float32
    )
    slope = sigmoid_pre * (1.0 + gate_pre * (1.0 - sigmoid_pre))
    gate_rows = (hidden_grad * up_pre * slope).astype(jnp.bfloat16)
    up_rows = (hidden_grad * silu_value).astype(jnp.bfloat16)
    input_rows = (
        lax.dot_general(gate_rows, gate_mat, contract_last, preferred_element_type=jnp.float32)
        + lax.dot_general(up_rows, up_mat, contract_last, preferred_element_type=jnp.float32)
    ).astype(jnp.bfloat16)
    hidden_width = hidden.shape[1]
    contract_first = (((0,), (0,)), ((), ()))
    summed = lax.psum_scatter(
        jnp.concatenate(
            [
                lax.dot_general(
                    flat_rows, gate_rows, contract_first, preferred_element_type=jnp.float32
                ),
                lax.dot_general(
                    flat_rows, up_rows, contract_first, preferred_element_type=jnp.float32
                ),
                lax.dot_general(
                    scaled_grad, hidden, contract_first, preferred_element_type=jnp.float32
                ),
            ],
            axis=1,
        ).astype(jnp.bfloat16),
        "dp",
        scatter_dimension=0,
        tiled=True,
    ).astype(jnp.float32)
    gate_proj_grad = summed[:, :hidden_width][None]
    up_proj_grad = summed[:, hidden_width : 2 * hidden_width][None]
    down_proj_grad = jnp.transpose(summed[:, 2 * hidden_width :])[None]
    pairs_back, input_back, weights_back = (
        lax.all_to_all(pair_buffer, "expert", split_axis=0, concat_axis=0, tiled=True),
        lax.all_to_all(
            input_rows.reshape(devices, CAP, model_width),
            "expert",
            split_axis=0,
            concat_axis=0,
            tiled=True,
        ),
        lax.all_to_all(
            weight_back.reshape(devices, CAP), "expert", split_axis=0, concat_axis=0, tiled=True
        ),
    )
    pair_total = jnp.sum(pairs_back.astype(jnp.float32), axis=0).astype(jnp.bfloat16)
    key_grad = pair_total[:, :, :HEAD]
    value_grad = pair_total[:, :, HEAD:]
    input_grad = lax.dot_general(
        dispatch_mat,
        input_back.reshape(devices * CAP, model_width),
        contract_first,
        preferred_element_type=jnp.float32,
    ).astype(jnp.bfloat16)
    token_back = jnp.sum(
        dispatch_mat.astype(jnp.float32) * weights_back.reshape(-1).astype(jnp.float32)[:, None],
        axis=0,
    )
    route_grad = jnp.where(live_slot, token_back[:, None], 0.0).astype(jnp.bfloat16)
    return (
        query_grad,
        key_grad,
        value_grad,
        gate_grad,
        input_grad,
        route_grad,
        gate_proj_grad,
        up_proj_grad,
        down_proj_grad,
    )


def solution(mesh):
    return jax.shard_map(
        shards,
        mesh=mesh,
        in_specs=(
            P("dp", "expert", None),
            P("dp", "expert", None),
            P("dp", "expert", None),
            P("dp", "expert", None),
            P("dp", "expert", None),
            P(("dp", "expert"), None),
            P(("dp", "expert"), None),
            P(("dp", "expert"), None),
            P(("dp", "expert"), None),
            P("expert", "dp", None),
            P("expert", "dp", None),
            P("expert", None, "dp"),
        ),
        out_specs=(
            P("dp", "expert", None),
            P("dp", "expert", None),
            P("dp", "expert", None),
            P("dp", "expert", None),
            P(("dp", "expert"), None),
            P(("dp", "expert"), None),
            P("expert", "dp", None),
            P("expert", "dp", None),
            P("expert", None, "dp"),
        ),
        check_vma=False,
    )
```

profile of v0, /device:TPU:0, one launch (start us, length us, event | category | flops | bytes accessed | tf_op | source)
XLA Modules:
  0.0 222.3 jit_solution(12494536839138368519)
XLA Ops:
  10.3 0.7 select_reduce_fusion.1
  12.9 6.3 %all-to-all-start.3 = ((bf16[8,2,2048]{2,1,0:T(2,128)(2,1)}), bf16[8,2,2048]{2,1,0:T(2,128)(2,1)S(1)}, u32[]{:S(2)}, u32[]{:S(2)}) async-start(bf16[8,2,2048]{2,1,0:T(2,128)(2,1)} %reshape.306), calls=%async_computation.3 | async-start | bytes 131072 | tf_op jit(solution)/shard_map/all_to_all | solution.py:200
  19.2 1.2 convolution_convert_fusion.4
  21.2 4.0 %all-to-all-done.3 = bf16[8,2,2048]{2,1,0:T(2,128)(2,1)S(1)} async-done(((bf16[8,2,2048]{2,1,0:T(2,128)(2,1)}), bf16[8,2,2048]{2,1,0:T(2,128)(2,1)S(1)}, u32[]{:S(2)}, u32[]{:S(2)}) %all-to-all-start.3) | async-done | bytes 65568 | tf_op jit(solution)/shard_map/all_to_all | solution.py:200
  25.2 3.4 %all-to-all-start.2 = ((bf16[8,2,2048]{2,1,0:T(2,128)(2,1)}), bf16[8,2,2048]{2,1,0:T(2,128)(2,1)S(1)}, u32[]{:S(2)}, u32[]{:S(2)}) async-start(bf16[8,2,2048]{2,1,0:T(2,128)(2,1)} %reshape.305), calls=%async_computation.2 | async-start | bytes 131072 | tf_op jit(solution)/shard_map/all_to_all | solution.py:201
  28.6 5.8 %all-to-all-done.2 = bf16[8,2,2048]{2,1,0:T(2,128)(2,1)S(1)} async-done(((bf16[8,2,2048]{2,1,0:T(2,128)(2,1)}), bf16[8,2,2048]{2,1,0:T(2,128)(2,1)S(1)}, u32[]{:S(2)}, u32[]{:S(2)}) %all-to-all-start.2) | async-done | bytes 65568 | tf_op jit(solution)/shard_map/all_to_all | solution.py:201
  34.4 5.7 %all-gather.11.cloned.1.call-done = bf16[1,2048,256]{2,1,0:T(8,128)(2,1)} async-done(((bf16[1,512,256]{2,1,0:T(8,128)(2,1)}), bf16[1,2048,256]{2,1,0:T(8,128)(2,1)}) %all-gather.11.cloned.1.call-update) | async-done | bytes 1048592 | tf_op jit(solution)/shard_map/all_gather | solution.py:192
  40.1 1.5 fusion.41
  41.6 27.0 %all-gather.9.cloned.1.call-done = bf16[1,2048,256]{2,1,0:T(8,128)(2,1)} async-done(((bf16[1,512,256]{2,1,0:T(8,128)(2,1)}), bf16[1,2048,256]{2,1,0:T(8,128)(2,1)}) %all-gather.9.cloned.1.call-update) | async-done | bytes 1048592 | tf_op jit(solution)/shard_map/all_gather | solution.py:193
  68.6 1.5 multiply_convert_fusion.3
  70.1 26.9 %all-gather.7.cloned.1.call-done = bf16[1,256,2048]{2,1,0:T(8,128)(2,1)} async-done(((bf16[1,256,512]{2,1,0:T(8,128)(2,1)}), bf16[1,256,2048]{2,1,0:T(8,128)(2,1)}) %all-gather.7.cloned.1.call-update) | async-done | bytes 1048592 | tf_op jit(solution)/shard_map/all_gather | solution.py:194
  96.9 1.6 fusion.34
  99.2 4.6 %all-to-all-start.5 = ((bf16[8,1,2]{2,1,0:T(2,128)(2,1)}), bf16[8,1,2]{2,1,0:T(2,128)(2,1)S(1)}, u32[]{:S(2)}, u32[]{:S(2)}) async-start(bf16[8,1,2]{2,1,0:T(2,128)(2,1)} %convert_element_type.223), calls=%async_computation.5 | async-start | bytes 8192 | tf_op jit(solution)/shard_map/all_to_all | solution.py:260
  104.5 4.8 %all-to-all-done.5 = bf16[8,1,2]{2,1,0:T(2,128)(2,1)S(1)} async-done(((bf16[8,1,2]{2,1,0:T(2,128)(2,1)}), bf16[8,1,2]{2,1,0:T(2,128)(2,1)S(1)}, u32[]{:S(2)}, u32[]{:S(2)}) %all-to-all-start.5) | async-done | bytes 64 | tf_op jit(solution)/shard_map/all_to_all | solution.py:260
  110.4 3.3 %all-to-all-start.1 = ((bf16[8,1,2]{2,1,0:T(2,128)(2,1)}), bf16[8,1,2]{2,1,0:T(2,128)(2,1)S(1)}, u32[]{:S(2)}, u32[]{:S(2)}) async-start(bf16[8,1,2]{2,1,0:T(2,128)(2,1)} %copy.74), calls=%async_computation.1 | async-start | bytes 8192 | tf_op jit(solution)/shard_map/all_to_all | solution.py:202
  114.3 4.8 %all-to-all-done.1 = bf16[8,1,2]{2,1,0:T(2,128)(2,1)S(1)} async-done(((bf16[8,1,2]{2,1,0:T(2,128)(2,1)}), bf16[8,1,2]{2,1,0:T(2,128)(2,1)S(1)}, u32[]{:S(2)}, u32[]{:S(2)}) %all-to-all-start.1) | async-done | bytes 64 | tf_op jit(solution)/shard_map/all_to_all | solution.py:202
  119.4 1.6 multiply_convert_fusion.4
  122.5 1.9 pad_maximum_fusion.1
  124.3 1.0 copy-done.4
  125.4 1.5 add_divide_fusion
  126.9 1.3 copy.95
  128.2 2.2 copy.94
  131.9 3.4 %all-to-all-start.4 = ((bf16[8,2,2048]{2,1,0:T(2,128)(2,1)}), bf16[8,2,2048]{2,1,0:T(2,128)(2,1)S(1)}, u32[]{:S(2)}, u32[]{:S(2)}) async-start(bf16[8,2,2048]{2,1,0:T(2,128)(2,1)} %reshape.308), calls=%async_computation.4 | async-start | bytes 131072 | tf_op jit(solution)/shard_map/all_to_all | solution.py:253
  135.2 3.6 %all-gather.5.cloned.1.call-done = bf16[2,512,512]{2,1,0:T(8,128)(2,1)} async-done(((bf16[2,64,512]{2,1,0:T(8,128)(2,1)}), bf16[2,512,512]{2,1,0:T(8,128)(2,1)}) %all-gather.5.cloned.1.call-update) | async-done | bytes 1048592 | tf_op jit(solution)/shard_map/all_gather | solution.py:52
  138.9 1.9 while.46
  138.9 1.8 conditional.6
  138.9 1.3 fusion.59
  140.9 1.8 while.47
  141.0 1.6 conditional.7
  141.1 1.5 fusion.3
  142.7 2.7 %multiply_reduce_fusion = (f32[2,64,8]{2,1,0:T(8,128)S(1)}, bf16[2,64,8,256]{3,2,1,0:T(8,128)(2,1)S(1)}, bf16[2,64,8,256]{3,2,1,0:T(8,128)(2,1)}) fusion(f32[2,64,8,256]{3,1,2,0:T(8,128)S(1)} %get-tuple-element.678, f32[2,64,8,256]{3,2,1,0:T(8,128)S(1)} %bitcast.182, f32[2,64,8,256]{3,2,1,0:T(8,128)} %bitcast.183), kind=kLoop, calls=%fused_computation.88 | loop fusion | flops 2620416 | bytes 4198400 | tf_op jit(solution)/shard_map/reduce_sum | solution.py:115
  145.7 1.1 broadcast_in_dim.117
  146.8 5.1 %while.48 = (s32[]{:T(128)}, f32[2,64,8,256]{3,1,2,0:T(8,128)S(1)}, bf16[8,2,64,512]{3,2,0,1:T(8,128)(2,1)}, s32[]{:T(128)}, s32[]{:T(128)}, /*index=5*/bf16[2,5...) while((s32[]{:T(128)}, f32[2,64,8,256]{3,1,2,0:T(8,128)S(1)}, ...), condition=%wide.region_14.15_spmd, body=%wide.region_11.14_spmd.sunk | while | flops 337518784 | bytes 8284160 | solution.py:153
  146.8 5.1 %conditional.8 = ((f32[2,64,8,256]{3,1,2,0:T(8,128)S(1)}, bf16[8,2,64,512]{3,2,0,1:T(8,128)(2,1)})) conditional(s32[]{:T(128)} %convert_element_type.261, (f32[2,64,8,256]{3,1,2,0:T(8,128)S(1)}, bf16[8,2,64,512]{3,2,0,1:T(8,128)(2,1)}) %tuple.151, (s32[]{:T(128)}, s32[]{:T(128)}, bf16[2,512,512]{2,1,0:T(8,128)(2,1)}, ...), branch_computations={%region_12.12_spmd, %region_13.13_spmd} | conditional | flops 337518784 | bytes 8283921 | solution.py:151
  146.9 1.2 fusion.24
  148.1 1.2 fusion.25
  149.4 1.2 fusion.17
  151.2 0.7 constant_dynamic-update-slice_fusion
  152.0 2.3 %copy.71 = bf16[8,2,64,512]{3,2,1,0:T(8,128)(2,1)} copy(bf16[8,2,64,512]{3,2,0,1:T(8,128)(2,1)} %get-tuple-element.680) | data formatting | bytes 2097152 | tf_op jit(solution)/shard_map/while | solution.py:153
  154.3 29.2 %all-to-all-start = ((bf16[8,2,64,512]{3,2,1,0:T(8,128)(2,1)}), bf16[8,2,64,512]{3,2,1,0:T(8,128)(2,1)S(1)}, u32[]{:S(2)}, u32[]{:S(2)}) async-start(bf16[8,2,64,512]{3,2,1,0:T(8,128)(2,1)} %copy.71), calls=%async_computation | async-start | bytes 2097152 | tf_op jit(solution)/shard_map/all_to_all | solution.py:252
  184.1 1.1 fusion.32
  185.3 0.8 copy.93
  186.1 2.1 reshape.304
  188.2 21.9 %all-to-all-done = bf16[8,2,64,512]{3,2,1,0:T(8,128)(2,1)S(1)} async-done(((bf16[8,2,64,512]{3,2,1,0:T(8,128)(2,1)}), bf16[8,2,64,512]{3,2,1,0:T(8,128)(2,1)S(1)}, u32[]{:S(2)}, u32[]{:S(2)}) %all-to-all-start) | async-done | bytes 1048608 | tf_op jit(solution)/shard_map/all_to_all | solution.py:252
  210.9 1.3 convert_element_type.218
  212.2 0.9 slice_bitcast_fusion
  213.2 1.0 copy.82
  214.2 1.0 copy.83
  (94 shorter events, 14.2 us)
Async XLA Ops:
  8.0 4.0 %copy-start = (bf16[128,2048]{1,0:T(8,128)(2,1)S(1)}, bf16[128,2048]{1,0:T(8,128)(2,1)}, u32[]{:S(2)}) copy-start(bf16[128,2048]{1,0:T(8,128)(2,1)} %param.29) | copy-start | bytes 1572868
  8.0 95.8 %copy-start.5 = (bf16[2,64,256]{2,1,0:T(8,128)(2,1)S(1)}, bf16[2,64,256]{2,1,0:T(8,128)(2,1)}, u32[]{:S(2)}) copy-start(bf16[2,64,256]{2,1,0:T(8,128)(2,1)} %param.26) | copy-start | bytes 196612
  8.0 95.8 %copy-start.6 = (bf16[2,64,256]{2,1,0:T(8,128)(2,1)S(1)}, bf16[2,64,256]{2,1,0:T(8,128)(2,1)}, u32[]{:S(2)}) copy-start(bf16[2,64,256]{2,1,0:T(8,128)(2,1)} %param.25) | copy-start | bytes 196612
  8.0 32.0 %all-gather.11.cloned.1.call-start = ((), (), s32[]{:S(2)}) async-start(), calls=%async_computation.10 | async-start | bytes 1310720 | tf_op jit(solution)/shard_map/all_gather | solution.py:192
  8.8 59.8 %all-gather.9.cloned.1.call-start = ((), (), s32[]{:S(2)}) async-start(), calls=%async_computation.9 | async-start | bytes 1310720 | tf_op jit(solution)/shard_map/all_gather | solution.py:193
  9.5 87.4 %all-gather.7.cloned.1.call-start = ((), (), s32[]{:S(2)}) async-start(), calls=%async_computation.8 | async-start | bytes 1310720 | tf_op jit(solution)/shard_map/all_gather | solution.py:194
  12.9 12.2 %all-to-all-start.3 = ((bf16[8,2,2048]{2,1,0:T(2,128)(2,1)}), bf16[8,2,2048]{2,1,0:T(2,128)(2,1)S(1)}, u32[]{:S(2)}, u32[]{:S(2)}) async-start(bf16[8,2,2048]{2,1,0:T(2,128)(2,1)} %reshape.306), calls=%async_computation.3 | async-start | bytes 131072 | tf_op jit(solution)/shard_map/all_to_all | solution.py:200
  25.2 9.2 %all-to-all-start.2 = ((bf16[8,2,2048]{2,1,0:T(2,128)(2,1)}), bf16[8,2,2048]{2,1,0:T(2,128)(2,1)S(1)}, u32[]{:S(2)}, u32[]{:S(2)}) async-start(bf16[8,2,2048]{2,1,0:T(2,128)(2,1)} %reshape.305), calls=%async_computation.2 | async-start | bytes 131072 | tf_op jit(solution)/shard_map/all_to_all | solution.py:201
  99.2 10.1 %all-to-all-start.5 = ((bf16[8,1,2]{2,1,0:T(2,128)(2,1)}), bf16[8,1,2]{2,1,0:T(2,128)(2,1)S(1)}, u32[]{:S(2)}, u32[]{:S(2)}) async-start(bf16[8,1,2]{2,1,0:T(2,128)(2,1)} %convert_element_type.223), calls=%async_computation.5 | async-start | bytes 8192 | tf_op jit(solution)/shard_map/all_to_all | solution.py:260
  110.4 8.7 %all-to-all-start.1 = ((bf16[8,1,2]{2,1,0:T(2,128)(2,1)}), bf16[8,1,2]{2,1,0:T(2,128)(2,1)S(1)}, u32[]{:S(2)}, u32[]{:S(2)}) async-start(bf16[8,1,2]{2,1,0:T(2,128)(2,1)} %copy.74), calls=%async_computation.1 | async-start | bytes 8192 | tf_op jit(solution)/shard_map/all_to_all | solution.py:202
  113.7 25.1 %all-gather.5.cloned.1.call-start = ((), (), s32[]{:S(2)}) async-start(), calls=%async_computation.7 | async-start | bytes 1179648 | tf_op jit(solution)/shard_map/all_gather | solution.py:52
  114.3 96.6 %reduce-scatter.2.cloned.1.call-start = ((), (), s32[]{:S(2)}) async-start(), calls=%async_computation.11 | async-start | bytes 3932160 | tf_op jit(solution)/shard_map/reduce_scatter | solution.py:229
  124.3 1.0 copy-start.4
  125.4 5.1 %copy-start.1 = (bf16[1,2048,256]{2,1,0:T(8,128)(2,1)S(1)}, bf16[1,2048,256]{2,1,0:T(8,128)(2,1)}, u32[]{:S(2)}) copy-start(bf16[1,2048,256]{2,1,0:T(8,128)(2,1)} %all-gather.11.cloned.1.call-done) | copy-start | bytes 3145732
  125.4 5.4 %copy-start.2 = (bf16[1,2048,256]{2,1,0:T(8,128)(2,1)S(1)}, bf16[1,2048,256]{2,1,0:T(8,128)(2,1)}, u32[]{:S(2)}) copy-start(bf16[1,2048,256]{2,1,0:T(8,128)(2,1)} %all-gather.9.cloned.1.call-done) | copy-start | bytes 3145732
  131.9 22.4 %all-to-all-start.4 = ((bf16[8,2,2048]{2,1,0:T(2,128)(2,1)}), bf16[8,2,2048]{2,1,0:T(2,128)(2,1)S(1)}, u32[]{:S(2)}, u32[]{:S(2)}) async-start(bf16[8,2,2048]{2,1,0:T(2,128)(2,1)} %reshape.308), calls=%async_computation.4 | async-start | bytes 131072 | tf_op jit(solution)/shard_map/all_to_all | solution.py:253
  140.9 1.8 copy-start.3
  154.3 55.8 %all-to-all-start = ((bf16[8,2,64,512]{3,2,1,0:T(8,128)(2,1)}), bf16[8,2,64,512]{3,2,1,0:T(8,128)(2,1)S(1)}, u32[]{:S(2)}, u32[]{:S(2)}) async-start(bf16[8,2,64,512]{3,2,1,0:T(8,128)(2,1)} %copy.71), calls=%async_computation | async-start | bytes 2097152 | tf_op jit(solution)/shard_map/all_to_all | solution.py:252
Sparse Core Ops, SparseCore 0:
  10.7 29.3 all-gather.10
  41.9 26.6 all-gather.8
  70.4 26.4 all-gather.6
  124.5 41.1 reduce-scatter.1
Sparse Core Ops, SparseCore 1:
  116.4 22.4 all-gather.4
where the time goes:
time: 224 us; the launch traced here: 222 us
  waiting for transfers between devices  107 us (48%)
  starting transfers between devices  50.3 us (22%)
  local copies, waits for them, and re-layouts  19.6 us (9%)
  matrix products  18.1 us (8%)
  between operations  15.5 us (7%)
  other arithmetic  11.3 us (5%)
    all_to_all x1, starting transfers between devices, shards(): lax.all_to_all(pair_buffer, 'expert', split_axis=0, concat_axis=0, tiled=...  29.2 us
    all_gather x1, waiting for transfers between devices, shards(): lax.all_gather(up_proj, 'dp', axis=1, tiled=True)  27 us
    all_gather x1, waiting for transfers between devices, shards(): lax.all_gather(down_proj, 'dp', axis=2, tiled=True)  26.9 us
    all_to_all x1, waiting for transfers between devices, shards(): lax.all_to_all(pair_buffer, 'expert', split_axis=0, concat_axis=0, tiled=...  21.9 us
    unnamed x19, local copies, waits for them, and re-layouts  6.66 us
    all_to_all x1, starting transfers between devices, shards(): lax.all_to_all(rows_send, 'expert', split_axis=0, concat_axis=0, tiled=True)  6.33 us
    all_to_all x1, waiting for transfers between devices, shards(): lax.all_to_all(grads_send, 'expert', split_axis=0, concat_axis=0, tiled=T...  5.81 us
    all_gather x1, waiting for transfers between devices, shards(): lax.all_gather(gate_proj, 'dp', axis=1, tiled=True)  5.7 us
  transfers between devices with their start and end apart: 11, of which 9 were waited for; matrix products, arithmetic and copies ran while one was open for 18% of the time, Pallas kernels for 0%

commit v1 on v0

v1 whole, which is shorter than its diff:
```python
import functools

import jax
import jax.numpy as jnp
from jax import lax
from jax.experimental import pallas as pl
from jax.experimental.pallas import tpu as pltpu
from jax.sharding import PartitionSpec as P

HEADS = 8
HEAD = 256
CAP = 2
LANES = 128
BF16 = jnp.bfloat16
F32 = jnp.float32
MIB = 1 << 20


def dot(a, b, ca=1, cb=0):
    return lax.dot_general(a, b, (((ca,), (cb,)), ((), ())), preferred_element_type=F32)


def iota(shape, dim):
    return lax.broadcasted_iota(jnp.int32, shape, dim)


def params(mib):
    return pltpu.CompilerParams(vmem_limit_bytes=mib * MIB)


def cost(flops, bytes_accessed):
    return pl.CostEstimate(flops=int(flops), bytes_accessed=int(bytes_accessed), transcendentals=0)


def attention_kernel(chips, *refs):
    q_ref, logit_ref, grad_ref = refs[:3]
    kv_refs = refs[3 : 3 + 2 * chips]
    query_grad_ref, gate_grad_ref, other_ref = refs[3 + 2 * chips : 6 + 2 * chips]
    mine_refs = refs[6 + 2 * chips :]
    length = q_ref.shape[1]
    keys_total = 2 * chips * length
    scale = HEAD ** (-0.5)
    position = lax.axis_index("expert")
    chip, core = position // 2, position % 2

    def stacked(ref):
        return jnp.concatenate(
            [ref[0, :, h * HEAD : (h + 1) * HEAD] for h in range(HEADS)], axis=0
        )

    queries = stacked(q_ref)
    keys = jnp.concatenate([r[0, :, :HEAD] for r in kv_refs], axis=0)
    values = jnp.concatenate([r[0, :, HEAD:] for r in kv_refs], axis=0)
    rows = HEADS * length
    shape = (rows, keys_total)
    row_pos = iota(shape, 0) % length
    col = iota(shape, 1)
    col_pos = col % length
    half = (col // length) % 2
    back = col // (2 * length)
    core_full = jnp.full(shape, core, jnp.int32)
    allowed = ((back > 0) & (back <= chip)) | (
        (back == 0) & (((half == 0) & (col_pos <= row_pos)) | ((half == 1) & (core_full == 1)))
    )
    scores = jnp.where(allowed, dot(queries, keys, 1, 1) * scale, -jnp.inf)
    row_max = jnp.max(scores, axis=1, keepdims=True)
    unnormed = jnp.exp(scores - row_max)
    probs = unnormed / jnp.sum(unnormed, axis=1, keepdims=True)
    probs_low = probs.astype(BF16)
    context = dot(probs_low, values)
    gate = jax.nn.sigmoid(stacked(logit_ref).astype(F32))
    upstream = stacked(grad_ref).astype(F32)
    context_grad = (upstream * gate).astype(BF16)
    gate_grad = (upstream * context * gate * (1.0 - gate)).astype(BF16)
    grad_dot = jnp.sum(context_grad.astype(F32) * context, axis=1, keepdims=True)
    prob_grad = dot(context_grad, values, 1, 1)
    score_grad = (probs * (prob_grad - grad_dot) * scale).astype(BF16)
    key_part = dot(score_grad, queries, 0, 0).astype(BF16)
    value_part = dot(probs_low, context_grad, 0, 0).astype(BF16)
    query_grad = dot(score_grad, keys).astype(BF16)
    for h in range(HEADS):
        rows_h = slice(h * length, (h + 1) * length)
        query_grad_ref[0, :, h * HEAD : (h + 1) * HEAD] = query_grad[rows_h]
        gate_grad_ref[0, :, h * HEAD : (h + 1) * HEAD] = gate_grad[rows_h]
    for d in range(chips):
        start = 2 * d * length
        mine_refs[d][0, :, :HEAD] = key_part[start : start + length]
        mine_refs[d][0, :, HEAD:] = value_part[start : start + length]
        other_ref[d, 0, :, :HEAD] = key_part[start + length : start + 2 * length]
        other_ref[d, 0, :, HEAD:] = value_part[start + length : start + 2 * length]


def attention(query_rows, gate_logits, gated_grad, pieces):
    seqs, length, width = query_rows.shape
    chips = len(pieces) // 2
    wide = pl.BlockSpec((1, length, width), lambda s: (s, 0, 0))
    narrow = pl.BlockSpec((1, length, 2 * HEAD), lambda s: (s, 0, 0))
    piece = jax.ShapeDtypeStruct((seqs, length, 2 * HEAD), BF16)
    full = jax.ShapeDtypeStruct((seqs, length, width), BF16)
    flops = 12 * seqs * HEADS * length * 2 * chips * length * HEAD
    out = pl.pallas_call(
        functools.partial(attention_kernel, chips),
        grid=(seqs,),
        in_specs=[wide] * 3 + [narrow] * (2 * chips),
        out_specs=[
            wide,
            wide,
            pl.BlockSpec((chips, 1, length, 2 * HEAD), lambda s: (0, s, 0, 0)),
        ]
        + [narrow] * chips,
        out_shape=[full, full, jax.ShapeDtypeStruct((chips,) + piece.shape, BF16)] + [piece] * chips,
        compiler_params=params(56),
        cost_estimate=cost(flops * 4, 8 * MIB),
        name="attention",
    )(query_rows, gate_logits, gated_grad, *pieces)
    return out[0], out[1], out[2], out[3:]


def merge_kernel(chips, *refs):
    mine, arrived, outs = refs[:chips], refs[chips], refs[chips + 1 :]
    for d in range(chips):
        outs[d][...] = (mine[d][...].astype(F32) + arrived[d].astype(F32)).astype(BF16)


def merge(mine, arrived):
    chips = len(mine)
    return pl.pallas_call(
        functools.partial(merge_kernel, chips),
        out_shape=[jax.ShapeDtypeStruct(mine[0].shape, BF16)] * chips,
        compiler_params=params(32),
        cost_estimate=cost(MIB, 2 * MIB),
        name="merge",
    )(*mine, arrived)


def close_kernel(*refs):
    parts, (key_ref, value_ref) = refs[:-2], refs[-2:]
    total = parts[0][...].astype(F32)
    for part in parts[1:]:
        total = total + part[...].astype(F32)
    key_ref[...] = total[:, :, :HEAD].astype(BF16)
    value_ref[...] = total[:, :, HEAD:].astype(BF16)


def close(parts):
    seqs, length, _ = parts[0].shape
    half = jax.ShapeDtypeStruct((seqs, length, HEAD), BF16)
    return pl.pallas_call(
        close_kernel,
        out_shape=[half, half],
        compiler_params=params(32),
        cost_estimate=cost(MIB, MIB),
        name="close",
    )(*parts)


def slots(routes_ref, weights_ref, experts):
    routes = routes_ref[...]
    tokens = routes.shape[0]
    live = routes < experts
    expert = jnp.sum(jnp.where(live, routes, 0), axis=1, keepdims=True)
    has_live = jnp.sum(live.astype(jnp.int32), axis=1, keepdims=True) > 0
    weight = jnp.sum(
        jnp.where(live, weights_ref[...].astype(F32), 0.0), axis=1, keepdims=True
    )
    wide = max(experts, LANES)
    member = (iota((tokens, wide), 1) == expert) & has_live
    earlier = (iota((tokens, tokens), 1) < iota((tokens, tokens), 0)).astype(BF16)
    before = dot(earlier, member.astype(BF16))
    rank = jnp.sum(jnp.where(member, before, 0.0), axis=1, keepdims=True).astype(jnp.int32)
    return jnp.where(has_live, expert * CAP + rank, -1), weight, live


def dispatch_kernel(experts, groups, rows, input_ref, grad_ref, routes_ref, weights_ref, out_ref):
    slot, weight, _ = slots(routes_ref, weights_ref, experts)
    tokens, width = input_ref.shape
    share = width // groups
    pieces = share // LANES
    total = experts * rows
    slot_row = jnp.transpose(jnp.broadcast_to(slot.astype(F32), (tokens, LANES)))[:1].astype(
        jnp.int32
    )
    sent = (input_ref[...], (weight * grad_ref[...].astype(F32)).astype(BF16))
    shape = (total, tokens)
    row = iota(shape, 0)
    inner = row % rows
    hit = slot_row == (row // rows) * CAP + (inner // pieces) % CAP
    acc = None
    for a in range(2):
        for l in range(pieces):
            pick = hit & (inner // (CAP * pieces) == a) & (inner % pieces == l)
            source = jnp.concatenate(
                [
                    sent[a][:, g * share + l * LANES : g * share + (l + 1) * LANES]
                    for g in range(groups)
                ],
                axis=1,
            )
            term = dot(pick.astype(BF16), source)
            acc = term if acc is None else acc + term
    acc = acc.astype(BF16)
    for g in range(groups):
        out_ref[g * total : (g + 1) * total, :] = acc[:, g * LANES : (g + 1) * LANES]


def enter_kernel(
    sources, rows, recv_ref, gate_ref, up_ref, down_ref, input_ref, grad_ref, own_ref, send_ref
):
    pieces = input_ref.shape[1] // LANES
    block = min(sources, 32)
    shape = (block * CAP, block * rows)
    out_row, in_row = iota(shape, 0), iota(shape, 1)
    base = (out_row // CAP) * rows + (out_row % CAP) * pieces
    picks = [
        [(in_row == base + a * CAP * pieces + l).astype(BF16) for l in range(pieces)]
        for a in range(2)
    ]
    for b in range(sources // block):
        arrived = recv_ref[b * block * rows : (b + 1) * block * rows, :]
        here = slice(b * block * CAP, (b + 1) * block * CAP)
        inputs, grads = (
            jnp.concatenate([dot(pick, arrived) for pick in picks[a]], axis=1).astype(BF16)
            for a in range(2)
        )
        input_ref[here, :] = inputs
        grad_ref[here, :] = grads
        partial = jnp.concatenate(
            [dot(inputs, gate_ref[0]), dot(inputs, up_ref[0]), dot(grads, down_ref[0], 1, 1)],
            axis=1,
        )
        own_ref[here, :] = partial
        send_ref[here, :] = partial.astype(BF16)


def middle_kernel(sources, rows, peers, *refs):
    own_ref = refs[0]
    parts = refs[1 : 1 + peers]
    gate_ref, up_ref, back_ref, hidden_ref, gate_rows_ref, up_rows_ref = refs[1 + peers :]
    share = gate_ref.shape[1]
    pieces = share // LANES
    hid = gate_ref.shape[2]
    block = min(sources, 32)
    shape = (block * rows, block * CAP)
    out_row, in_row = iota(shape, 0), iota(shape, 1)
    same = out_row // rows == in_row // CAP
    inner, which = out_row % rows, in_row % CAP
    picks = [(same & (inner == which * pieces + l)).astype(BF16) for l in range(pieces)]
    pick_dot = (same & (inner == CAP * pieces + which)).astype(BF16)
    for b in range(sources // block):
        here = slice(b * block * CAP, (b + 1) * block * CAP)
        total = own_ref[here, :]
        for part in parts:
            total = total + part[here, :].astype(F32)
        gate_pre, up_pre, hidden_grad = total[:, :hid], total[:, hid : 2 * hid], total[:, 2 * hid :]
        sig = jax.nn.sigmoid(gate_pre)
        silu = gate_pre * sig
        hidden = (silu * up_pre).astype(BF16)
        slope = sig * (1.0 + gate_pre * (1.0 - sig))
        gate_rows = (hidden_grad * up_pre * slope).astype(BF16)
        up_rows = (hidden_grad * silu).astype(BF16)
        hidden_ref[here, :] = hidden
        gate_rows_ref[here, :] = gate_rows
        up_rows_ref[here, :] = up_rows
        routed = jnp.sum(hidden.astype(F32) * hidden_grad, axis=1, keepdims=True)
        high = routed.astype(BF16)
        low = (routed - high.astype(F32)).astype(BF16)
        lane = iota((block * CAP, LANES), 1)
        routed_wide = jnp.where(lane < LANES // 2, high.astype(F32), low.astype(F32)).astype(BF16)
        input_rows = (
            dot(gate_rows, gate_ref[0], 1, 1) + dot(up_rows, up_ref[0], 1, 1)
        ).astype(BF16)
        back = dot(pick_dot, routed_wide)
        for l in range(pieces):
            back = back + dot(picks[l], input_rows[:, l * LANES : (l + 1) * LANES])
        back_ref[b * block * rows : (b + 1) * block * rows, :] = back.astype(BF16)


def weight_kernel(
    input_ref, grad_ref, hidden_ref, gate_rows_ref, up_rows_ref, gate_out, up_out, down_out
):
    gate_out[0] = dot(input_ref[...], gate_rows_ref[...], 0, 0)
    up_out[0] = dot(input_ref[...], up_rows_ref[...], 0, 0)
    down_out[0] = dot(hidden_ref[...], grad_ref[...], 0, 0)


def combine_kernel(
    experts, groups, rows, back_ref, routes_ref, weights_ref, input_grad_ref, route_grad_ref
):
    slot, weight, live = slots(routes_ref, weights_ref, experts)
    tokens, width = input_grad_ref.shape
    share = width // groups
    pieces = share // LANES
    total = experts * rows
    shape = (tokens, total)
    col = iota(shape, 1)
    inner = col % rows
    expert = col // rows
    hit = (slot == expert * CAP + inner // pieces) & (inner < CAP * pieces)
    wide = jnp.concatenate([back_ref[g * total : (g + 1) * total, :] for g in range(groups)], axis=1)
    for l in range(pieces):
        grad = dot((hit & (inner % pieces == l)).astype(BF16), wide).astype(BF16)
        for g in range(groups):
            input_grad_ref[:, g * share + l * LANES : g * share + (l + 1) * LANES] = grad[
                :, g * LANES : (g + 1) * LANES
            ]
    hit_dot = slot == expert * CAP + inner - CAP * pieces
    hit_dot = hit_dot & (inner >= CAP * pieces) & (inner < CAP * (pieces + 1))
    routed = dot(hit_dot.astype(BF16), back_ref[:total, :])
    routed = routed[:, :1] + routed[:, LANES // 2 : LANES // 2 + 1]
    routed = routed / jnp.where(weight > 0.0, weight, 1.0)
    route_grad_ref[...] = jnp.where(live, routed, 0.0).astype(BF16)


def shards(
    query_rows,
    key_rows,
    value_rows,
    gate_logits,
    gated_grad,
    moe_input,
    out_grad,
    routes,
    route_weights,
    gate_proj,
    up_proj,
    down_proj,
):
    devices = lax.axis_size("expert")
    groups = lax.axis_size("dp")
    sources = devices * groups
    chips = devices // 2
    tokens, width = moe_input.shape
    share = width // groups
    pieces = share // LANES
    hid = gate_proj.shape[2]
    rows = -(-2 * CAP * pieces // 16) * 16
    axes = ("dp", "expert")
    swap = [(i, i ^ 1) for i in range(devices)]

    packed = jnp.concatenate([key_rows, value_rows], axis=2)
    mine = [packed]
    for d in range(1, chips):
        up = [(i, i + 2 * d) for i in range(devices - 2 * d)]
        mine.append(lax.ppermute(packed, "expert", up))
    pieces_kv = []
    for block in mine:
        pieces_kv += [block, lax.ppermute(block, "expert", swap)]

    send = pl.pallas_call(
        functools.partial(dispatch_kernel, devices, groups, rows),
        out_shape=jax.ShapeDtypeStruct((sources * rows, LANES), BF16),
        compiler_params=params(48),
        cost_estimate=cost(2e9, 2 * MIB),
        name="dispatch",
    )(moe_input, out_grad, routes, route_weights)
    recv = lax.all_to_all(
        send.reshape(sources, rows, LANES), axes, split_axis=0, concat_axis=0, tiled=True
    ).reshape(sources * rows, LANES)

    slot_rows = jax.ShapeDtypeStruct((sources * CAP, share), BF16)
    hid_rows = jax.ShapeDtypeStruct((sources * CAP, hid), BF16)
    inputs, grads, own, sent = pl.pallas_call(
        functools.partial(enter_kernel, sources, rows),
        out_shape=[
            slot_rows,
            slot_rows,
            jax.ShapeDtypeStruct((sources * CAP, 3 * hid), F32),
            jax.ShapeDtypeStruct((sources * CAP, 3 * hid), BF16),
        ],
        compiler_params=params(48),
        cost_estimate=cost(2e9, 2 * MIB),
        name="enter",
    )(recv, gate_proj, up_proj, down_proj)
    parts = []
    for k in range(1, groups):
        parts.append(lax.ppermute(sent, "dp", [(g, g ^ k) for g in range(groups)]))
    back, hidden, gate_rows, up_rows = pl.pallas_call(
        functools.partial(middle_kernel, sources, rows, groups - 1),
        out_shape=[jax.ShapeDtypeStruct((sources * rows, LANES), BF16)] + [hid_rows] * 3,
        compiler_params=params(48),
        cost_estimate=cost(2e9, 2 * MIB),
        name="middle",
    )(own, *parts, gate_proj, up_proj)
    returned = lax.all_to_all(
        back.reshape(sources, rows, LANES), axes, split_axis=0, concat_axis=0, tiled=True
    ).reshape(sources * rows, LANES)
    gate_proj_grad, up_proj_grad, down_proj_grad = pl.pallas_call(
        weight_kernel,
        out_shape=[
            jax.ShapeDtypeStruct(gate_proj.shape, F32),
            jax.ShapeDtypeStruct(up_proj.shape, F32),
            jax.ShapeDtypeStruct(down_proj.shape, F32),
        ],
        compiler_params=params(48),
        cost_estimate=cost(2e9, 2 * MIB),
        name="weight_grads",
    )(inputs, grads, hidden, gate_rows, up_rows)
    input_grad, route_grad = pl.pallas_call(
        functools.partial(combine_kernel, devices, groups, rows),
        out_shape=[
            jax.ShapeDtypeStruct(moe_input.shape, BF16),
            jax.ShapeDtypeStruct(routes.shape, BF16),
        ],
        compiler_params=params(48),
        cost_estimate=cost(2e9, 2 * MIB),
        name="combine",
    )(returned, routes, route_weights)

    query_grad, gate_grad, other_parts, mine_parts = attention(
        query_rows, gate_logits, gated_grad, pieces_kv
    )
    arrived = lax.ppermute(other_parts, "expert", swap)
    merged = merge(mine_parts, arrived)
    terms = [merged[0]]
    for d in range(1, chips):
        down = [(i, i - 2 * d) for i in range(2 * d, devices)]
        terms.append(lax.ppermute(merged[d], "expert", down))
    key_grad, value_grad = close(terms)
    return (
        query_grad,
        key_grad,
        value_grad,
        gate_grad,
        input_grad,
        route_grad,
        gate_proj_grad,
        up_proj_grad,
        down_proj_grad,
    )


def solution(mesh):
    rows3 = P("dp", "expert", None)
    tokens2 = P(("dp", "expert"), None)
    weights = P("expert", "dp", None)
    weights_down = P("expert", None, "dp")
    return jax.shard_map(
        shards,
        mesh=mesh,
        in_specs=(rows3,) * 5 + (tokens2,) * 4 + (weights, weights, weights_down),
        out_specs=(rows3,) * 4 + (tokens2,) * 2 + (weights, weights, weights_down),
        check_vma=False,
    )
```

time: 224 us -> 67.6 us (0.30)
  waiting for transfers between devices: 107 us -> 14.8 us
  matrix products: 18.1 us -> 0 us
  starting transfers between devices: 50.3 us -> 33.2 us
  between operations: 15.5 us -> 0.95 us
  local copies, waits for them, and re-layouts: 19.6 us -> 5.16 us
  Pallas kernels: 0 us -> 13 us
  other arithmetic: 11.3 us -> 0 us
    all_gather x4 -> x0, waiting for transfers between devices: 63.2 us -> none  [the longest x1 27 us: shards(): lax.all_gather(up_proj, 'dp', axis=1, tiled=True)]
    all_to_all x6 -> x2, waiting for transfers between devices: 41.3 us -> 2.6 us  [the longest x1 2.6 us: shards(): lax.all_to_all(back.reshape(sources, rows, LANES), axes, split_axis=0, co...]
    all_to_all x6 -> x2, starting transfers between devices: 50.1 us -> 15.9 us  [the longest x1 8.55 us: shards(): lax.all_to_all(back.reshape(sources, rows, LANES), axes, split_axis=0, co...]
    dot_general x20 -> x0, matrix products: 18.1 us -> none  [the longest x2 2.52 us: block_scores(): jnp.einsum('sphd,srd->shpr', queries, keys_block, preferred_element_type=...]
    ppermute x0 -> x14, starting transfers between devices: none -> 17.3 us  [the longest x3 9.3 us: shards(): mine.append(lax.ppermute(packed, 'expert', up))]
    pallas_call x0 -> x8, Pallas kernels: none -> 13 us  [the longest x1 5.92 us: attention(): pl.pallas_call(functools.partial(attention_kernel, chips), grid=(seqs,),...]
    ppermute x0 -> x14, waiting for transfers between devices: none -> 12.2 us  [the longest x3 8.47 us: shards(): terms.append(lax.ppermute(merged[d], 'expert', down))]
    reshape x7 -> x0, local copies, waits for them, and re-layouts: 5.09 us -> none  [the longest x1 2.07 us: shards(): gate_grad = (upstream * context * sigmoid_gate * (1.0 - sigmoid_gate)).as...]
  transfers between devices with their start and end apart: 11 -> 16, of which waited for: 9 -> 4; matrix products, arithmetic and copies ran while one was open for 18% -> 1% of each run, Pallas kernels for 0% -> 16%
where the time goes in v1:
time: 67.6 us; the launch traced here: 67.1 us
  starting transfers between devices  33.2 us (49%)
  waiting for transfers between devices  14.8 us (22%)
  Pallas kernels  13 us (19%)
  local copies, waits for them, and re-layouts  5.16 us (8%)
  between operations  0.95 us (1%)
    ppermute x3, starting transfers between devices, shards(): mine.append(lax.ppermute(packed, 'expert', up))  9.3 us
    all_to_all x1, starting transfers between devices, shards(): lax.all_to_all(back.reshape(sources, rows, LANES), axes, split_axis=0, co...  8.55 us
    ppermute x3, waiting for transfers between devices, shards(): terms.append(lax.ppermute(merged[d], 'expert', down))  8.47 us
    all_to_all x1, starting transfers between devices, shards(): lax.all_to_all(send.reshape(sources, rows, LANES), axes, split_axis=0, co...  7.32 us
    pallas_call x1, Pallas kernels, attention(): pl.pallas_call(functools.partial(attention_kernel, chips), grid=(seqs,),...  5.92 us
    unnamed x44, local copies, waits for them, and re-layouts  5.15 us
    ppermute x3, starting transfers between devices, shards(): terms.append(lax.ppermute(merged[d], 'expert', down))  3.88 us
    ppermute x3, waiting for transfers between devices, shards(): mine.append(lax.ppermute(packed, 'expert', up))  3.73 us
  transfers between devices with their start and end apart: 16, of which 4 were waited for; matrix products, arithmetic and copies ran while one was open for 1% of the time, Pallas kernels for 16%

profile of v1, /device:TPU:0, one launch (start us, length us, event | category | flops | bytes accessed | tf_op | source)
XLA Modules:
  0.0 67.1 jit_solution(4842167031719700330)
XLA Ops:
  0.7 0.8 %copy.21.routes_ref = s32[128,10]{1,0:T(8,128)S(1)} copy(s32[128,10]{0,1:T(8,128)} %param.19) | data formatting | bytes 10240 | tf_op args[7]
  1.5 0.1 copy.22.weights_ref
  1.6 1.0 %copy-done.4 = bf16[128,2048]{1,0:T(8,128)(2,1)S(1)} copy-done((bf16[128,2048]{1,0:T(8,128)(2,1)S(1)}, bf16[128,2048]{1,0:T(8,128)(2,1)}, u32[]{:S(2)}) %copy-start.4) | copy-done | bytes 524312
  2.6 1.0 %copy-done.5 = bf16[128,2048]{1,0:T(8,128)(2,1)S(1)} copy-done((bf16[128,2048]{1,0:T(8,128)(2,1)S(1)}, bf16[128,2048]{1,0:T(8,128)(2,1)}, u32[]{:S(2)}) %copy-start.5) | copy-done | bytes 524312
  3.7 1.5 %dispatch.1 = bf16[512,128]{1,0:T(8,128)(2,1)} custom-call(bf16[128,2048]{1,0:T(8,128)(2,1)S(1)} %copy-done.4, bf16[128,2048]{1,0:T(8,128)(2,1)S(1)} %copy-done.5, s32[128,10]{1,0:T(8,128)S(1)} %copy.21.routes_ref, bf16[128,10]{1,0:T(8,128)(2,1)S(1)} %copy.22.weights_ref), custom_call_target="tpu_custom_call" | custom-call | flops 2000000000 | bytes 2097152 | tf_op jit(solution)/shard_map/dispatch/pallas_call | solution.py:349
  5.2 7.3 %all-to-all-start = ((bf16[32,16,128]{2,1,0:T(8,128)(2,1)}), bf16[32,16,128]{2,1,0:T(8,128)(2,1)S(1)}, u32[]{:S(2)}, u32[]{:S(2)}) async-start(bf16[32,16,128]{2,1,0:T(8,128)(2,1)} %bitcast), calls=%async_computation | async-start | bytes 262144 | tf_op jit(solution)/shard_map/all_to_all | solution.py:356
  12.6 0.0 copy-start.11
  12.6 3.7 %collective-permute-start.1 = (bf16[2,64,512]{2,1,0:T(8,128)(2,1)S(1)}, bf16[2,64,512]{2,1,0:T(8,128)(2,1)S(1)}, u32[]{:S(2)}, u32[]{:S(2)}) collective-permute-start(bf16[2,64,512]{2,1,0:T(8,128)(2,1)S(1)} %constant_dynamic-update-slice_fusion.refs_3_), channel_id=1, source_target_pairs={{0,2},{1,3},{2,4},{3,5},{4,6},{5,7},{8,10},{9,11},{10,12},{11,13},... | collective-permute-start | bytes 393224 | tf_op jit(solution)/shard_map/ppermute | solution.py:344
  16.3 4.3 %collective-permute-start.3 = (bf16[2,64,512]{2,1,0:T(8,128)(2,1)S(1)}, bf16[2,64,512]{2,1,0:T(8,128)(2,1)S(1)}, u32[]{:S(2)}, u32[]{:S(2)}) collective-permute-start(bf16[2,64,512]{2,1,0:T(8,128)(2,1)S(1)} %constant_dynamic-update-slice_fusion.refs_3_), channel_id=1, source_target_pairs={{0,4},{1,5},{2,6},{3,7},{8,12},{9,13},{10,14},{11,15},{16,20},{17,... | collective-permute-start | bytes 393224 | tf_op jit(solution)/shard_map/ppermute | solution.py:344
  20.6 1.3 %collective-permute-start.5 = (bf16[2,64,512]{2,1,0:T(8,128)(2,1)S(1)}, bf16[2,64,512]{2,1,0:T(8,128)(2,1)S(1)}, u32[]{:S(2)}, u32[]{:S(2)}) collective-permute-start(bf16[2,64,512]{2,1,0:T(8,128)(2,1)S(1)} %constant_dynamic-update-slice_fusion.refs_3_), channel_id=1, source_target_pairs={{0,6},{1,7},{8,14},{9,15},{16,22},{17,23},{24,30},{25,31}} | collective-permute-start | bytes 393224 | tf_op jit(solution)/shard_map/ppermute | solution.py:344
  21.9 0.1 collective-permute-start
  22.0 0.0 collective-permute-done.1.refs_5_
  22.0 0.0 copy-start.13
  22.0 0.5 collective-permute-start.2
  22.5 2.0 %collective-permute-done.3.refs_7_ = bf16[2,64,512]{2,1,0:T(8,128)(2,1)S(1)} collective-permute-done((bf16[2,64,512]{2,1,0:T(8,128)(2,1)S(1)}, bf16[2,64,512]{2,1,0:T(8,128)(2,1)S(1)}, u32[]{:S(2)}, u32[]{:S(2)}) %collective-permute-start.3) | collective-permute-done | bytes 131104 | tf_op jit(solution)/shard_map/ppermute | solution.py:344
  24.5 0.0 collective-permute-start.4
  24.5 1.7 %collective-permute-done.5.refs_9_ = bf16[2,64,512]{2,1,0:T(8,128)(2,1)S(1)} collective-permute-done((bf16[2,64,512]{2,1,0:T(8,128)(2,1)S(1)}, bf16[2,64,512]{2,1,0:T(8,128)(2,1)S(1)}, u32[]{:S(2)}, u32[]{:S(2)}) %collective-permute-start.5) | collective-permute-done | bytes 131104 | tf_op jit(solution)/shard_map/ppermute | solution.py:344
  26.2 0.0 collective-permute-start.6
  26.2 0.0 all-to-all-done
  26.2 0.5 enter.1
  26.8 0.1 copy-done.15
  26.9 1.5 %collective-permute-start.11 = (bf16[64,768]{1,0:T(8,128)(2,1)S(1)}, bf16[64,768]{1,0:T(8,128)(2,1)S(1)}, u32[]{:S(2)}, u32[]{:S(2)}) collective-permute-start(bf16[64,768]{1,0:T(8,128)(2,1)S(1)} %get-tuple-element.49), channel_id=1, source_target_pairs={{0,8},{8,0},{16,24},{24,16},{1,9},{9,1},{17,25},{25,17},{2,10},{10... | collective-permute-start | bytes 294920 | tf_op jit(solution)/shard_map/ppermute | solution.py:376
  28.3 0.0 collective-permute-done.refs_4_
  28.4 1.5 %collective-permute-start.12 = (bf16[64,768]{1,0:T(8,128)(2,1)S(1)}, bf16[64,768]{1,0:T(8,128)(2,1)S(1)}, u32[]{:S(2)}, u32[]{:S(2)}) collective-permute-start(bf16[64,768]{1,0:T(8,128)(2,1)S(1)} %get-tuple-element.49), channel_id=1, source_target_pairs={{0,16},{8,24},{16,0},{24,8},{1,17},{9,25},{17,1},{25,9},{2,18},{10... | collective-permute-start | bytes 294920 | tf_op jit(solution)/shard_map/ppermute | solution.py:376
  29.9 0.0 collective-permute-done.2.refs_6_
  29.9 0.5 collective-permute-start.13
  30.4 0.0 collective-permute-done.4.refs_8_
  30.4 0.0 collective-permute-done.6.refs_10_
  30.4 0.1 copy-done.17
  30.5 0.5 copy-done.18
  31.0 0.6 copy-done.19
  31.7 5.9 %attention.1 = (bf16[2,64,2048]{2,1,0:T(8,128)(2,1)}, bf16[2,64,2048]{2,1,0:T(8,128)(2,1)}, bf16[4,2,64,512]{3,2,1,0:T(8,128)(2,1)}, bf16[2,64,512]{2,1,0:T(8,12...) custom-call(bf16[2,64,2048]{2,1,0:T(8,128)(2,1)} %refs_0_.1, ...), custom_call_target="tpu_custom_call" | custom-call | flops 6442450944 | bytes 8388608 | tf_op jit(solution)/shard_map/attention/pallas_call | solution.py:101
  37.6 0.1 collective-permute-start.7
  37.7 0.0 collective-permute-done.11.refs_1_
  37.7 0.0 collective-permute-done.12.refs_2_
  37.7 1.4 %middle.1 = (bf16[512,128]{1,0:T(8,128)(2,1)}, bf16[64,256]{1,0:T(8,128)(2,1)S(1)}, bf16[64,256]{1,0:T(8,128)(2,1)S(1)}, bf16[64,256]{1,0:T(8,128)(2,1)S(1)}) custom-call(f32[64,768]{1,0:T(8,128)S(1)} %get-tuple-element.48.refs_0_, bf16[64,768]{1,0:T(8,128)(2,1)S(1)} %collective-permute-done.11.refs_1_, bf16[64,768]{1,0:T(8,128)(2,1)S(1)} %collective-permute-done.12.refs_2_, ...), custom_call_target="tpu_custom_call" | custom-call | flops 2000000000 | bytes 2097152 | tf_op jit(solution)/shard_map/middle/pallas_call | solution.py:377
  39.1 8.6 %all-to-all-start.1 = ((bf16[32,16,128]{2,1,0:T(8,128)(2,1)}), bf16[32,16,128]{2,1,0:T(8,128)(2,1)S(1)}, u32[]{:S(2)}, u32[]{:S(2)}) async-start(bf16[32,16,128]{2,1,0:T(8,128)(2,1)} %bitcast.2), calls=%async_computation.1 | async-start | bytes 262144 | tf_op jit(solution)/shard_map/all_to_all | solution.py:384
  47.7 1.5 %weight_grads.1 = (f32[1,512,256]{2,1,0:T(8,128)}, f32[1,512,256]{2,1,0:T(8,128)}, f32[1,256,512]{2,1,0:T(8,128)}) custom-call(bf16[64,512]{1,0:T(8,128)(2,1)S(1)} %get-tuple-element.53.input_ref, bf16[64,512]{1,0:T(8,128)(2,1)S(1)} %get-tuple-element.54.grad_ref, bf16[64,256]{1,0:T(8,128)(2,1)S(1)} %get-tuple-element.55.hidden_ref, ...), custom_call_target="tpu_custom_call" | custom-call | flops 2000000000 | bytes 2097152 | tf_op jit(solution)/shard_map/weight_grads/pallas_call | solution.py:387
  49.2 0.1 merge.1
  49.4 1.3 %collective-permute-start.8 = (bf16[2,64,512]{2,1,0:T(8,128)(2,1)S(1)}, bf16[2,64,512]{2,1,0:T(8,128)(2,1)S(1)}, u32[]{:S(2)}, u32[]{:S(2)}) collective-permute-start(bf16[2,64,512]{2,1,0:T(8,128)(2,1)S(1)} %get-tuple-element.42), channel_id=1, source_target_pairs={{2,0},{3,1},{4,2},{5,3},{6,4},{7,5},{10,8},{11,9},{12,10},{13,11},... | collective-permute-start | bytes 393224 | tf_op jit(solution)/shard_map/ppermute | solution.py:417
  50.7 1.3 %collective-permute-start.9 = (bf16[2,64,512]{2,1,0:T(8,128)(2,1)S(1)}, bf16[2,64,512]{2,1,0:T(8,128)(2,1)S(1)}, u32[]{:S(2)}, u32[]{:S(2)}) collective-permute-start(bf16[2,64,512]{2,1,0:T(8,128)(2,1)S(1)} %get-tuple-element.43), channel_id=1, source_target_pairs={{4,0},{5,1},{6,2},{7,3},{12,8},{13,9},{14,10},{15,11},{20,16},{21,... | collective-permute-start | bytes 393224 | tf_op jit(solution)/shard_map/ppermute | solution.py:417
  52.0 1.3 %collective-permute-start.10 = (bf16[2,64,512]{2,1,0:T(8,128)(2,1)S(1)}, bf16[2,64,512]{2,1,0:T(8,128)(2,1)S(1)}, u32[]{:S(2)}, u32[]{:S(2)}) collective-permute-start(bf16[2,64,512]{2,1,0:T(8,128)(2,1)S(1)} %get-tuple-element.44), channel_id=1, source_target_pairs={{6,0},{7,1},{14,8},{15,9},{22,16},{23,17},{30,24},{31,25}} | collective-permute-start | bytes 393224 | tf_op jit(solution)/shard_map/ppermute | solution.py:417
  53.3 2.6 %all-to-all-done.1 = bf16[32,16,128]{2,1,0:T(8,128)(2,1)S(1)} async-done(((bf16[32,16,128]{2,1,0:T(8,128)(2,1)}), bf16[32,16,128]{2,1,0:T(8,128)(2,1)S(1)}, u32[]{:S(2)}, u32[]{:S(2)}) %all-to-all-start.1) | async-done | bytes 131104 | tf_op jit(solution)/shard_map/all_to_all | solution.py:384
  55.9 1.4 %combine.1 = (bf16[128,2048]{1,0:T(8,128)(2,1)}, bf16[128,10]{1,0:T(8,128)(2,1)S(1)}) custom-call(bf16[512,128]{1,0:T(8,128)(2,1)S(1)} %bitcast.5, s32[128,10]{1,0:T(8,128)S(1)} %copy.21.routes_ref, bf16[128,10]{1,0:T(8,128)(2,1)S(1)} %copy.22.weights_ref), custom_call_target="tpu_custom_call" | custom-call | flops 2000000000 | bytes 2097152 | tf_op jit(solution)/shard_map/combine/pallas_call | solution.py:398
  57.3 0.7 %copy.25 = bf16[128,10]{0,1:T(8,128)(2,1)} copy(bf16[128,10]{1,0:T(8,128)(2,1)S(1)} %get-tuple-element.66) | data formatting | bytes 5120
  58.0 0.0 collective-permute-done.8.refs_1_
  58.0 8.5 %collective-permute-done.9.refs_2_ = bf16[2,64,512]{2,1,0:T(8,128)(2,1)S(1)} collective-permute-done((bf16[2,64,512]{2,1,0:T(8,128)(2,1)S(1)}, bf16[2,64,512]{2,1,0:T(8,128)(2,1)S(1)}, u32[]{:S(2)}, u32[]{:S(2)}) %collective-permute-start.9) | collective-permute-done | bytes 131104 | tf_op jit(solution)/shard_map/ppermute | solution.py:417
  66.4 0.7 %close.1 = (bf16[2,64,256]{2,1,0:T(8,128)(2,1)}, bf16[2,64,256]{2,1,0:T(8,128)(2,1)}) custom-call(bf16[2,64,512]{2,1,0:T(8,128)(2,1)S(1)} %get-tuple-element.41.refs_0_, bf16[2,64,512]{2,1,0:T(8,128)(2,1)S(1)} %collective-permute-done.8.refs_1_, bf16[2,64,512]{2,1,0:T(8,128)(2,1)S(1)} %collective-permute-done.9.refs_2_, ...), custom_call_target="tpu_custom_call" | custom-call | flops 1048576 | bytes 1048576 | tf_op jit(solution)/shard_map/close/pallas_call | solution.py:148
  (37 shorter events, 0.1 us)
Async XLA Ops:
  0.6 0.8 %copy-start.12 = (bf16[128,10]{0,1:T(8,128)(2,1)S(1)}, bf16[128,10]{0,1:T(8,128)(2,1)}, u32[]{:S(2)}) copy-start(bf16[128,10]{0,1:T(8,128)(2,1)} %param.20) | copy-start | bytes 7684
  1.6 1.0 %copy-start.4 = (bf16[128,2048]{1,0:T(8,128)(2,1)S(1)}, bf16[128,2048]{1,0:T(8,128)(2,1)}, u32[]{:S(2)}) copy-start(bf16[128,2048]{1,0:T(8,128)(2,1)} %input_ref.1) | copy-start | bytes 1572868
  2.6 1.0 %copy-start.5 = (bf16[128,2048]{1,0:T(8,128)(2,1)S(1)}, bf16[128,2048]{1,0:T(8,128)(2,1)}, u32[]{:S(2)}) copy-start(bf16[128,2048]{1,0:T(8,128)(2,1)} %grad_ref.1) | copy-start | bytes 1572868
  3.7 8.8 %copy-start.9 = (bf16[2,64,256]{2,1,0:T(8,128)(2,1)S(1)}, bf16[2,64,256]{2,1,0:T(8,128)(2,1)}, u32[]{:S(2)}) copy-start(bf16[2,64,256]{2,1,0:T(8,128)(2,1)} %param.13) | copy-start | bytes 196612
  3.7 8.9 %copy-start.10 = (bf16[2,64,256]{2,1,0:T(8,128)(2,1)S(1)}, bf16[2,64,256]{2,1,0:T(8,128)(2,1)}, u32[]{:S(2)}) copy-start(bf16[2,64,256]{2,1,0:T(8,128)(2,1)} %param.14) | copy-start | bytes 196612
  3.7 22.5 %copy-start.8 = (bf16[1,512,256]{2,1,0:T(8,128)(2,1)S(1)}, bf16[1,512,256]{2,1,0:T(8,128)(2,1)}, u32[]{:S(2)}) copy-start(bf16[1,512,256]{2,1,0:T(8,128)(2,1)} %refs_5_.1) | copy-start | bytes 786436
  5.2 21.0 %copy-start.6 = (bf16[1,256,512]{2,1,0:T(8,128)(2,1)S(1)}, bf16[1,256,512]{2,1,0:T(8,128)(2,1)}, u32[]{:S(2)}) copy-start(bf16[1,256,512]{2,1,0:T(8,128)(2,1)} %down_ref.1) | copy-start | bytes 786436
  5.2 21.1 %copy-start.7 = (bf16[1,512,256]{2,1,0:T(8,128)(2,1)S(1)}, bf16[1,512,256]{2,1,0:T(8,128)(2,1)}, u32[]{:S(2)}) copy-start(bf16[1,512,256]{2,1,0:T(8,128)(2,1)} %refs_4_.1) | copy-start | bytes 786436
  5.2 21.0 %all-to-all-start = ((bf16[32,16,128]{2,1,0:T(8,128)(2,1)}), bf16[32,16,128]{2,1,0:T(8,128)(2,1)S(1)}, u32[]{:S(2)}, u32[]{:S(2)}) async-start(bf16[32,16,128]{2,1,0:T(8,128)(2,1)} %bitcast), calls=%async_computation | async-start | bytes 262144 | tf_op jit(solution)/shard_map/all_to_all | solution.py:356
  12.6 14.2 %copy-start.11 = (bf16[2,64,512]{2,1,0:T(8,128)(2,1)}, bf16[2,64,512]{2,1,0:T(8,128)(2,1)S(1)}, u32[]{:S(2)}) copy-start(bf16[2,64,512]{2,1,0:T(8,128)(2,1)S(1)} %constant_dynamic-update-slice_fusion.refs_3_) | copy-start | bytes 393220
  12.6 9.4 %collective-permute-start.1 = (bf16[2,64,512]{2,1,0:T(8,128)(2,1)S(1)}, bf16[2,64,512]{2,1,0:T(8,128)(2,1)S(1)}, u32[]{:S(2)}, u32[]{:S(2)}) collective-permute-start(bf16[2,64,512]{2,1,0:T(8,128)(2,1)S(1)} %constant_dynamic-update-slice_fusion.refs_3_), channel_id=1, source_target_pairs={{0,2},{1,3},{2,4},{3,5},{4,6},{5,7},{8,10},{9,11},{10,12},{11,13},... | collective-permute-start | bytes 393224 | tf_op jit(solution)/shard_map/ppermute | solution.py:344
  16.3 8.2 %collective-permute-start.3 = (bf16[2,64,512]{2,1,0:T(8,128)(2,1)S(1)}, bf16[2,64,512]{2,1,0:T(8,128)(2,1)S(1)}, u32[]{:S(2)}, u32[]{:S(2)}) collective-permute-start(bf16[2,64,512]{2,1,0:T(8,128)(2,1)S(1)} %constant_dynamic-update-slice_fusion.refs_3_), channel_id=1, source_target_pairs={{0,4},{1,5},{2,6},{3,7},{8,12},{9,13},{10,14},{11,15},{16,20},{17,... | collective-permute-start | bytes 393224 | tf_op jit(solution)/shard_map/ppermute | solution.py:344
  20.6 5.6 %collective-permute-start.5 = (bf16[2,64,512]{2,1,0:T(8,128)(2,1)S(1)}, bf16[2,64,512]{2,1,0:T(8,128)(2,1)S(1)}, u32[]{:S(2)}, u32[]{:S(2)}) collective-permute-start(bf16[2,64,512]{2,1,0:T(8,128)(2,1)S(1)} %constant_dynamic-update-slice_fusion.refs_3_), channel_id=1, source_target_pairs={{0,6},{1,7},{8,14},{9,15},{16,22},{17,23},{24,30},{25,31}} | collective-permute-start | bytes 393224 | tf_op jit(solution)/shard_map/ppermute | solution.py:344
  21.9 6.5 %collective-permute-start = (bf16[2,64,512]{2,1,0:T(8,128)(2,1)S(1)}, bf16[2,64,512]{2,1,0:T(8,128)(2,1)S(1)}, u32[]{:S(2)}, u32[]{:S(2)}) collective-permute-start(bf16[2,64,512]{2,1,0:T(8,128)(2,1)S(1)} %constant_dynamic-update-slice_fusion.refs_3_), channel_id=1, source_target_pairs={{0,1},{1,0},{2,3},{3,2},{4,5},{5,4},{6,7},{7,6},{8,9},{9,8},{10,11... | collective-permute-start | bytes 393224 | tf_op jit(solution)/shard_map/ppermute | solution.py:347
  22.0 4.8 %copy-start.13 = (bf16[2,64,512]{2,1,0:T(8,128)(2,1)}, bf16[2,64,512]{2,1,0:T(8,128)(2,1)S(1)}, u32[]{:S(2)}) copy-start(bf16[2,64,512]{2,1,0:T(8,128)(2,1)S(1)} %collective-permute-done.1.refs_5_) | copy-start | bytes 393220
  22.0 7.9 %collective-permute-start.2 = (bf16[2,64,512]{2,1,0:T(8,128)(2,1)S(1)}, bf16[2,64,512]{2,1,0:T(8,128)(2,1)S(1)}, u32[]{:S(2)}, u32[]{:S(2)}) collective-permute-start(bf16[2,64,512]{2,1,0:T(8,128)(2,1)S(1)} %collective-permute-done.1.refs_5_), channel_id=1, source_target_pairs={{0,1},{1,0},{2,3},{3,2},{4,5},{5,4},{6,7},{7,6},{8,9},{9,8},{10,11... | collective-permute-start | bytes 393224 | tf_op jit(solution)/shard_map/ppermute | solution.py:347
  24.5 2.3 %copy-start.14 = (bf16[2,64,512]{2,1,0:T(8,128)(2,1)}, bf16[2,64,512]{2,1,0:T(8,128)(2,1)S(1)}, u32[]{:S(2)}) copy-start(bf16[2,64,512]{2,1,0:T(8,128)(2,1)S(1)} %collective-permute-done.3.refs_7_) | copy-start | bytes 393220
  24.5 5.9 %collective-permute-start.4 = (bf16[2,64,512]{2,1,0:T(8,128)(2,1)S(1)}, bf16[2,64,512]{2,1,0:T(8,128)(2,1)S(1)}, u32[]{:S(2)}, u32[]{:S(2)}) collective-permute-start(bf16[2,64,512]{2,1,0:T(8,128)(2,1)S(1)} %collective-permute-done.3.refs_7_), channel_id=1, source_target_pairs={{0,1},{1,0},{2,3},{3,2},{4,5},{5,4},{6,7},{7,6},{8,9},{9,8},{10,11... | collective-permute-start | bytes 393224 | tf_op jit(solution)/shard_map/ppermute | solution.py:347
  26.2 0.7 copy-start.15
  26.2 4.2 %collective-permute-start.6 = (bf16[2,64,512]{2,1,0:T(8,128)(2,1)S(1)}, bf16[2,64,512]{2,1,0:T(8,128)(2,1)S(1)}, u32[]{:S(2)}, u32[]{:S(2)}) collective-permute-start(bf16[2,64,512]{2,1,0:T(8,128)(2,1)S(1)} %collective-permute-done.5.refs_9_), channel_id=1, source_target_pairs={{0,1},{1,0},{2,3},{3,2},{4,5},{5,4},{6,7},{7,6},{8,9},{9,8},{10,11... | collective-permute-start | bytes 393224 | tf_op jit(solution)/shard_map/ppermute | solution.py:347
  26.9 10.8 %collective-permute-start.11 = (bf16[64,768]{1,0:T(8,128)(2,1)S(1)}, bf16[64,768]{1,0:T(8,128)(2,1)S(1)}, u32[]{:S(2)}, u32[]{:S(2)}) collective-permute-start(bf16[64,768]{1,0:T(8,128)(2,1)S(1)} %get-tuple-element.49), channel_id=1, source_target_pairs={{0,8},{8,0},{16,24},{24,16},{1,9},{9,1},{17,25},{25,17},{2,10},{10... | collective-permute-start | bytes 294920 | tf_op jit(solution)/shard_map/ppermute | solution.py:376
  28.4 2.0 %copy-start.16 = (bf16[2,64,512]{2,1,0:T(8,128)(2,1)}, bf16[2,64,512]{2,1,0:T(8,128)(2,1)S(1)}, u32[]{:S(2)}) copy-start(bf16[2,64,512]{2,1,0:T(8,128)(2,1)S(1)} %collective-permute-done.refs_4_) | copy-start | bytes 393220
  28.4 9.3 %collective-permute-start.12 = (bf16[64,768]{1,0:T(8,128)(2,1)S(1)}, bf16[64,768]{1,0:T(8,128)(2,1)S(1)}, u32[]{:S(2)}, u32[]{:S(2)}) collective-permute-start(bf16[64,768]{1,0:T(8,128)(2,1)S(1)} %get-tuple-element.49), channel_id=1, source_target_pairs={{0,16},{8,24},{16,0},{24,8},{1,17},{9,25},{17,1},{25,9},{2,18},{10... | collective-permute-start | bytes 294920 | tf_op jit(solution)/shard_map/ppermute | solution.py:376
  29.9 0.6 copy-start.17
  29.9 7.8 %collective-permute-start.13 = (bf16[64,768]{1,0:T(8,128)(2,1)S(1)}, bf16[64,768]{1,0:T(8,128)(2,1)S(1)}, u32[]{:S(2)}, u32[]{:S(2)}) collective-permute-start(bf16[64,768]{1,0:T(8,128)(2,1)S(1)} %get-tuple-element.49), channel_id=1, source_target_pairs={{0,24},{8,16},{16,8},{24,0},{1,25},{9,17},{17,9},{25,1},{2,26},{10... | collective-permute-start | bytes 294920 | tf_op jit(solution)/shard_map/ppermute | solution.py:376
  30.4 0.6 copy-start.18
  31.0 0.6 copy-start.19
  37.6 11.6 %collective-permute-start.7 = (bf16[4,2,64,512]{3,2,1,0:T(8,128)(2,1)}, bf16[4,2,64,512]{3,2,1,0:T(8,128)(2,1)S(1)}, u32[]{:S(2)}, u32[]{:S(2)}) collective-permute-start(bf16[4,2,64,512]{3,2,1,0:T(8,128)(2,1)} %get-tuple-element.40), channel_id=1, source_target_pairs={{0,1},{1,0},{2,3},{3,2},{4,5},{5,4},{6,7},{7,6},{8,9},{9,8},{10,11... | collective-permute-start | bytes 1572872 | tf_op jit(solution)/shard_map/ppermute | solution.py:412
  39.1 16.7 %all-to-all-start.1 = ((bf16[32,16,128]{2,1,0:T(8,128)(2,1)}), bf16[32,16,128]{2,1,0:T(8,128)(2,1)S(1)}, u32[]{:S(2)}, u32[]{:S(2)}) async-start(bf16[32,16,128]{2,1,0:T(8,128)(2,1)} %bitcast.2), calls=%async_computation.1 | async-start | bytes 262144 | tf_op jit(solution)/shard_map/all_to_all | solution.py:384
  47.7 1.5 %copy-start = (bf16[2,64,512]{2,1,0:T(8,128)(2,1)S(1)}, bf16[2,64,512]{2,1,0:T(8,128)(2,1)}, u32[]{:S(2)}) copy-start(bf16[2,64,512]{2,1,0:T(8,128)(2,1)} %get-tuple-element.36.refs_0_) | copy-start | bytes 393220
  47.7 1.5 %copy-start.1 = (bf16[2,64,512]{2,1,0:T(8,128)(2,1)S(1)}, bf16[2,64,512]{2,1,0:T(8,128)(2,1)}, u32[]{:S(2)}) copy-start(bf16[2,64,512]{2,1,0:T(8,128)(2,1)} %get-tuple-element.37.refs_1_) | copy-start | bytes 393220
  47.7 1.5 %copy-start.2 = (bf16[2,64,512]{2,1,0:T(8,128)(2,1)S(1)}, bf16[2,64,512]{2,1,0:T(8,128)(2,1)}, u32[]{:S(2)}) copy-start(bf16[2,64,512]{2,1,0:T(8,128)(2,1)} %get-tuple-element.38.refs_2_) | copy-start | bytes 393220
  47.7 1.5 %copy-start.3 = (bf16[2,64,512]{2,1,0:T(8,128)(2,1)S(1)}, bf16[2,64,512]{2,1,0:T(8,128)(2,1)}, u32[]{:S(2)}) copy-start(bf16[2,64,512]{2,1,0:T(8,128)(2,1)} %get-tuple-element.39.refs_3_) | copy-start | bytes 393220
  49.4 8.6 %collective-permute-start.8 = (bf16[2,64,512]{2,1,0:T(8,128)(2,1)S(1)}, bf16[2,64,512]{2,1,0:T(8,128)(2,1)S(1)}, u32[]{:S(2)}, u32[]{:S(2)}) collective-permute-start(bf16[2,64,512]{2,1,0:T(8,128)(2,1)S(1)} %get-tuple-element.42), channel_id=1, source_target_pairs={{2,0},{3,1},{4,2},{5,3},{6,4},{7,5},{10,8},{11,9},{12,10},{13,11},... | collective-permute-start | bytes 393224 | tf_op jit(solution)/shard_map/ppermute | solution.py:417
  50.7 15.8 %collective-permute-start.9 = (bf16[2,64,512]{2,1,0:T(8,128)(2,1)S(1)}, bf16[2,64,512]{2,1,0:T(8,128)(2,1)S(1)}, u32[]{:S(2)}, u32[]{:S(2)}) collective-permute-start(bf16[2,64,512]{2,1,0:T(8,128)(2,1)S(1)} %get-tuple-element.43), channel_id=1, source_target_pairs={{4,0},{5,1},{6,2},{7,3},{12,8},{13,9},{14,10},{15,11},{20,16},{21,... | collective-permute-start | bytes 393224 | tf_op jit(solution)/shard_map/ppermute | solution.py:417
  52.0 14.5 %collective-permute-start.10 = (bf16[2,64,512]{2,1,0:T(8,128)(2,1)S(1)}, bf16[2,64,512]{2,1,0:T(8,128)(2,1)S(1)}, u32[]{:S(2)}, u32[]{:S(2)}) collective-permute-start(bf16[2,64,512]{2,1,0:T(8,128)(2,1)S(1)} %get-tuple-element.44), channel_id=1, source_target_pairs={{6,0},{7,1},{14,8},{15,9},{22,16},{23,17},{30,24},{31,25}} | collective-permute-start | bytes 393224 | tf_op jit(solution)/shard_map/ppermute | solution.py:417

commit v2 on v1

v2 whole, which is shorter than its diff:
```python
import functools

import jax
import jax.numpy as jnp
from jax import lax
from jax.experimental import pallas as pl
from jax.experimental.pallas import tpu as pltpu
from jax.sharding import PartitionSpec as P

HEADS = 8
HEAD = 256
CAP = 2
LANES = 128
BF16 = jnp.bfloat16
F32 = jnp.float32
MIB = 1 << 20
ATTENTION_MIB = 32


def dot(a, b, ca=1, cb=0):
    return lax.dot_general(a, b, (((ca,), (cb,)), ((), ())), preferred_element_type=F32)


def iota(shape, dim):
    return lax.broadcasted_iota(jnp.int32, shape, dim)


def params(mib):
    return pltpu.CompilerParams(vmem_limit_bytes=mib * MIB)


def cost(flops, bytes_accessed):
    return pl.CostEstimate(flops=int(flops), bytes_accessed=int(bytes_accessed), transcendentals=0)


def pack_kernel(key_ref, value_ref, out_ref):
    for d in range(out_ref.shape[0]):
        out_ref[d, :, :, :HEAD] = key_ref[...]
        out_ref[d, :, :, HEAD:] = value_ref[...]


def attention_kernel(
    q_ref,
    logit_ref,
    grad_ref,
    mine_ref,
    other_ref,
    query_grad_ref,
    gate_grad_ref,
    mine_part_ref,
    other_part_ref,
):
    length = q_ref.shape[1]
    chips = mine_ref.shape[0]
    side = chips * length
    scale = HEAD ** (-0.5)
    position = lax.axis_index("expert")
    chip, core = position // 2, position % 2

    def stacked(ref):
        return jnp.concatenate(
            [ref[0, :, h * HEAD : (h + 1) * HEAD] for h in range(HEADS)], axis=0
        )

    both = [ref[j, 0] for ref in (mine_ref, other_ref) for j in range(chips)]
    both = jnp.concatenate(both, axis=0)
    keys, values = both[:, :HEAD], both[:, HEAD:]
    queries = stacked(q_ref)
    shape = (HEADS * length, 2 * side)
    row_pos = iota(shape, 0) % length
    col = iota(shape, 1)
    col_pos = col % length
    col_chip = (col // length) % chips
    limit = jnp.where(col < side, row_pos, core * length - 1)
    allowed = (col_chip < chip) | ((col_chip == chip) & (col_pos <= limit))
    scores = jnp.where(allowed, dot(queries, keys, 1, 1) * scale, -jnp.inf)
    row_max = jnp.max(scores, axis=1, keepdims=True)
    unnormed = jnp.exp(scores - row_max)
    probs = unnormed * (1.0 / jnp.sum(unnormed, axis=1, keepdims=True))
    probs_low = probs.astype(BF16)
    context = dot(probs_low, values)
    gate = jax.nn.sigmoid(stacked(logit_ref).astype(F32))
    upstream = stacked(grad_ref).astype(F32)
    context_grad = (upstream * gate).astype(BF16)
    gate_grad = (upstream * context * gate * (1.0 - gate)).astype(BF16)
    grad_dot = jnp.sum(context_grad.astype(F32) * context, axis=1, keepdims=True)
    prob_grad = dot(context_grad, values, 1, 1)
    score_grad = (probs * (prob_grad - grad_dot) * scale).astype(BF16)
    key_part = dot(score_grad, queries, 0, 0).astype(BF16)
    value_part = dot(probs_low, context_grad, 0, 0).astype(BF16)
    for half, ref in enumerate((mine_part_ref, other_part_ref)):
        for j in range(chips):
            start = half * side + j * length
            ref[j, 0, :, :HEAD] = key_part[start : start + length]
            ref[j, 0, :, HEAD:] = value_part[start : start + length]
    query_grad = dot(score_grad, keys).astype(BF16)
    for h in range(HEADS):
        rows_h = slice(h * length, (h + 1) * length)
        query_grad_ref[0, :, h * HEAD : (h + 1) * HEAD] = query_grad[rows_h]
        gate_grad_ref[0, :, h * HEAD : (h + 1) * HEAD] = gate_grad[rows_h]


def attention(query_rows, gate_logits, gated_grad, mine, other):
    seqs, length, width = query_rows.shape
    chips = mine.shape[0]
    wide = pl.BlockSpec((1, length, width), lambda s: (s, 0, 0))
    stack = pl.BlockSpec((chips, 1, length, 2 * HEAD), lambda s: (0, s, 0, 0))
    full = jax.ShapeDtypeStruct((seqs, length, width), BF16)
    part = jax.ShapeDtypeStruct(mine.shape, BF16)
    flops = 12 * seqs * HEADS * length * 2 * chips * length * HEAD
    return pl.pallas_call(
        attention_kernel,
        grid=(seqs,),
        in_specs=[wide] * 3 + [stack] * 2,
        out_specs=[wide] * 2 + [stack] * 2,
        out_shape=[full] * 2 + [part] * 2,
        compiler_params=params(ATTENTION_MIB if chips <= 4 else 60),
        cost_estimate=cost(flops * 4, 8 * MIB),
        name="attention",
    )(query_rows, gate_logits, gated_grad, mine, other)


def merge_kernel(mine_ref, arrived_ref, out_ref):
    out_ref[...] = (mine_ref[...].astype(F32) + arrived_ref[...].astype(F32)).astype(BF16)


def close_kernel(parts_ref, key_ref, value_ref):
    total = parts_ref[0].astype(F32)
    for j in range(1, parts_ref.shape[0]):
        total = total + parts_ref[j].astype(F32)
    key_ref[...] = total[:, :, :HEAD].astype(BF16)
    value_ref[...] = total[:, :, HEAD:].astype(BF16)


def slots(routes_ref, weights_ref, experts):
    routes = routes_ref[...]
    tokens = routes.shape[1]
    live = routes < experts
    expert = jnp.sum(jnp.where(live, routes, 0), axis=0, keepdims=True)
    has_live = jnp.sum(live.astype(jnp.int32), axis=0, keepdims=True) > 0
    weight = jnp.sum(
        jnp.where(live, weights_ref[...].astype(F32), 0.0), axis=0, keepdims=True
    )
    tall = max(experts, 16)
    member = (iota((tall, tokens), 0) == expert) & has_live
    earlier = (iota((tokens, tokens), 0) < iota((tokens, tokens), 1)).astype(BF16)
    before = dot(member.astype(BF16), earlier)
    rank = jnp.sum(jnp.where(member, before, 0.0), axis=0, keepdims=True).astype(jnp.int32)
    return jnp.where(has_live, expert * CAP + rank, -1), weight, live


def dispatch_kernel(
    experts,
    groups,
    rows,
    input_hbm,
    grad_hbm,
    routes_ref,
    weights_ref,
    out_ref,
    input_ref,
    grad_ref,
    sems,
):
    tokens, width = input_ref.shape
    step = tokens // sems.shape[1]
    copies = [
        pltpu.make_async_copy(
            src.at[pl.ds(i * step, step)], dst.at[pl.ds(i * step, step)], sems.at[a, i]
        )
        for a, (src, dst) in enumerate(((input_hbm, input_ref), (grad_hbm, grad_ref)))
        for i in range(sems.shape[1])
    ]
    for copy in copies:
        copy.start()
    slot, weight, _ = slots(routes_ref, weights_ref, experts)
    share = width // groups
    pieces = share // LANES
    total = experts * rows
    shape = (total, tokens)
    row = iota(shape, 0)
    inner = row % rows
    hit = slot == (row // rows) * CAP + (inner // pieces) % CAP
    for copy in copies:
        copy.wait()
    acc = None
    for a, (ref, value) in enumerate(((input_ref, 1.0), (grad_ref, weight))):
        for l in range(pieces):
            pick = hit & (inner // (CAP * pieces) == a) & (inner % pieces == l)
            source = jnp.concatenate(
                [
                    ref[:, g * share + l * LANES : g * share + (l + 1) * LANES]
                    for g in range(groups)
                ],
                axis=1,
            )
            term = dot(jnp.where(pick, value, 0.0).astype(BF16), source)
            acc = term if acc is None else acc + term
    acc = acc.astype(BF16)
    for g in range(groups):
        out_ref[g * total : (g + 1) * total, :] = acc[:, g * LANES : (g + 1) * LANES]


def enter_kernel(
    sources, rows, recv_ref, gate_ref, up_ref, down_ref, input_ref, grad_ref, send_ref
):
    pieces = input_ref.shape[1] // LANES
    block = min(sources, 32)
    shape = (block * CAP, block * rows)
    out_row, in_row = iota(shape, 0), iota(shape, 1)
    base = (out_row // CAP) * rows + (out_row % CAP) * pieces
    picks = [
        [(in_row == base + a * CAP * pieces + l).astype(BF16) for l in range(pieces)]
        for a in range(2)
    ]
    for b in range(sources // block):
        arrived = recv_ref[b * block * rows : (b + 1) * block * rows, :]
        here = slice(b * block * CAP, (b + 1) * block * CAP)
        inputs, grads = (
            jnp.concatenate([dot(pick, arrived) for pick in picks[a]], axis=1).astype(BF16)
            for a in range(2)
        )
        input_ref[here, :] = inputs
        grad_ref[here, :] = grads
        partial = jnp.concatenate(
            [dot(inputs, gate_ref[0]), dot(inputs, up_ref[0]), dot(grads, down_ref[0], 1, 1)],
            axis=1,
        ).astype(BF16)
        for c in range(send_ref.shape[0]):
            send_ref[c, here, :] = partial


def middle_kernel(sources, rows, *refs):
    parts = refs[:-6]
    gate_ref, up_ref, back_ref, hidden_ref, gate_rows_ref, up_rows_ref = refs[-6:]
    share = gate_ref.shape[1]
    pieces = share // LANES
    hid = gate_ref.shape[2]
    block = min(sources, 32)
    shape = (block * rows, block * CAP)
    out_row, in_row = iota(shape, 0), iota(shape, 1)
    same = out_row // rows == in_row // CAP
    inner, which = out_row % rows, in_row % CAP
    picks = [(same & (inner == which * pieces + l)).astype(BF16) for l in range(pieces)]
    pick_dot = (same & (inner == CAP * pieces + which)).astype(BF16)
    for b in range(sources // block):
        here = slice(b * block * CAP, (b + 1) * block * CAP)
        terms = [part[c, here, :].astype(F32) for part in parts for c in range(part.shape[0])]
        total = functools.reduce(jnp.add, terms)
        gate_pre, up_pre, hidden_grad = total[:, :hid], total[:, hid : 2 * hid], total[:, 2 * hid :]
        sig = jax.nn.sigmoid(gate_pre)
        silu = gate_pre * sig
        hidden = (silu * up_pre).astype(BF16)
        slope = sig * (1.0 + gate_pre * (1.0 - sig))
        gate_rows = (hidden_grad * up_pre * slope).astype(BF16)
        up_rows = (hidden_grad * silu).astype(BF16)
        hidden_ref[here, :] = hidden
        gate_rows_ref[here, :] = gate_rows
        up_rows_ref[here, :] = up_rows
        routed = jnp.sum(hidden.astype(F32) * hidden_grad, axis=1, keepdims=True)
        high = routed.astype(BF16)
        low = (routed - high.astype(F32)).astype(BF16)
        lane = iota((block * CAP, LANES), 1)
        routed_wide = jnp.where(lane < LANES // 2, high.astype(F32), low.astype(F32)).astype(BF16)
        input_rows = (
            dot(gate_rows, gate_ref[0], 1, 1) + dot(up_rows, up_ref[0], 1, 1)
        ).astype(BF16)
        back = dot(pick_dot, routed_wide)
        for l in range(pieces):
            back = back + dot(picks[l], input_rows[:, l * LANES : (l + 1) * LANES])
        back_ref[b * block * rows : (b + 1) * block * rows, :] = back.astype(BF16)


def weight_kernel(
    input_ref, grad_ref, hidden_ref, gate_rows_ref, up_rows_ref, gate_out, up_out, down_out
):
    gate_out[0] = dot(input_ref[...], gate_rows_ref[...], 0, 0)
    up_out[0] = dot(input_ref[...], up_rows_ref[...], 0, 0)
    down_out[0] = dot(hidden_ref[...], grad_ref[...], 0, 0)


def combine_kernel(
    experts, groups, rows, back_ref, routes_ref, weights_ref, input_grad_ref, route_grad_ref
):
    slot, weight, live = slots(routes_ref, weights_ref, experts)
    tokens, width = input_grad_ref.shape
    share = width // groups
    pieces = share // LANES
    total = experts * rows
    shape = (total, tokens)
    row = iota(shape, 0)
    inner = row % rows
    expert = row // rows
    hit = (slot == expert * CAP + inner // pieces) & (inner < CAP * pieces)
    wide = jnp.concatenate([back_ref[g * total : (g + 1) * total, :] for g in range(groups)], axis=1)
    for l in range(pieces):
        pick = (hit & (inner % pieces == l)).astype(BF16)
        grad = dot(pick, wide, 0, 0).astype(BF16)
        for g in range(groups):
            input_grad_ref[:, g * share + l * LANES : g * share + (l + 1) * LANES] = grad[
                :, g * LANES : (g + 1) * LANES
            ]
    hit_dot = slot == expert * CAP + inner - CAP * pieces
    hit_dot = hit_dot & (inner >= CAP * pieces) & (inner < CAP * (pieces + 1))
    routed = dot(back_ref[:total, :], hit_dot.astype(BF16), 0, 0)
    routed = routed[:1] + routed[LANES // 2 : LANES // 2 + 1]
    routed = routed / jnp.where(weight > 0.0, weight, 1.0)
    route_grad_ref[...] = jnp.where(live, routed, 0.0).astype(BF16)


def shards(
    query_rows,
    key_rows,
    value_rows,
    gate_logits,
    gated_grad,
    moe_input,
    out_grad,
    routes,
    route_weights,
    gate_proj,
    up_proj,
    down_proj,
):
    devices = lax.axis_size("expert")
    groups = lax.axis_size("dp")
    sources = devices * groups
    chips = devices // 2
    seqs, length, _ = key_rows.shape
    tokens, width = moe_input.shape
    share = width // groups
    pieces = share // LANES
    hid = gate_proj.shape[2]
    rows = -(-2 * CAP * pieces // 16) * 16
    axes = ("dp", "expert")
    swap = [(i, i ^ 1) for i in range(devices)]
    same_core = [list(range(c, devices, 2)) for c in range(2)]

    def between_chips(array):
        return lax.all_to_all(
            array, "expert", split_axis=0, concat_axis=0, axis_index_groups=same_core, tiled=True
        )

    packed = pl.pallas_call(
        pack_kernel,
        out_shape=jax.ShapeDtypeStruct((chips, seqs, length, 2 * HEAD), BF16),
        compiler_params=params(32),
        cost_estimate=cost(MIB, MIB),
        name="pack",
    )(key_rows, value_rows)
    mine = between_chips(packed)
    other = lax.ppermute(mine, "expert", swap)

    routes_t, weights_t = routes.T, route_weights.T
    send = pl.pallas_call(
        functools.partial(dispatch_kernel, devices, groups, rows),
        in_specs=[pl.BlockSpec(memory_space=pltpu.HBM)] * 2
        + [pl.BlockSpec(memory_space=pltpu.VMEM)] * 2,
        out_shape=jax.ShapeDtypeStruct((sources * rows, LANES), BF16),
        scratch_shapes=[
            pltpu.VMEM(moe_input.shape, BF16),
            pltpu.VMEM(out_grad.shape, BF16),
            pltpu.SemaphoreType.DMA((2, 4)),
        ],
        compiler_params=params(32),
        cost_estimate=cost(2e9, 2 * MIB),
        name="dispatch",
    )(moe_input, out_grad, routes_t, weights_t)
    recv = lax.all_to_all(
        send.reshape(sources, rows, LANES), axes, split_axis=0, concat_axis=0, tiled=True
    ).reshape(sources * rows, LANES)

    slot_rows = jax.ShapeDtypeStruct((sources * CAP, share), BF16)
    hid_rows = jax.ShapeDtypeStruct((sources * CAP, hid), BF16)
    few = groups <= 4
    inputs, grads, sent = pl.pallas_call(
        functools.partial(enter_kernel, sources, rows),
        out_shape=[
            slot_rows,
            slot_rows,
            jax.ShapeDtypeStruct((groups if few else 1, sources * CAP, 3 * hid), BF16),
        ],
        compiler_params=params(32),
        cost_estimate=cost(2e9, 2 * MIB),
        name="enter",
    )(recv, gate_proj, up_proj, down_proj)
    if few:
        parts = [lax.all_to_all(sent, "dp", split_axis=0, concat_axis=0, tiled=True)]
    else:
        parts = [sent] + [
            lax.ppermute(sent, "dp", [(g, (g + k) % groups) for g in range(groups)])
            for k in range(1, groups)
        ]
    back, hidden, gate_rows, up_rows = pl.pallas_call(
        functools.partial(middle_kernel, sources, rows),
        out_shape=[jax.ShapeDtypeStruct((sources * rows, LANES), BF16)] + [hid_rows] * 3,
        compiler_params=params(32 if few else 60),
        cost_estimate=cost(2e9, 2 * MIB),
        name="middle",
    )(*parts, gate_proj, up_proj)
    returned = lax.all_to_all(
        back.reshape(sources, rows, LANES), axes, split_axis=0, concat_axis=0, tiled=True
    ).reshape(sources * rows, LANES)
    gate_proj_grad, up_proj_grad, down_proj_grad = pl.pallas_call(
        weight_kernel,
        out_shape=[
            jax.ShapeDtypeStruct(gate_proj.shape, F32),
            jax.ShapeDtypeStruct(up_proj.shape, F32),
            jax.ShapeDtypeStruct(down_proj.shape, F32),
        ],
        compiler_params=params(32),
        cost_estimate=cost(2e9, 2 * MIB),
        name="weight_grads",
    )(inputs, grads, hidden, gate_rows, up_rows)
    input_grad, route_grad = pl.pallas_call(
        functools.partial(combine_kernel, devices, groups, rows),
        out_shape=[
            jax.ShapeDtypeStruct(moe_input.shape, BF16),
            jax.ShapeDtypeStruct(routes_t.shape, BF16),
        ],
        compiler_params=params(32),
        cost_estimate=cost(2e9, 2 * MIB),
        name="combine",
    )(returned, routes_t, weights_t)

    query_grad, gate_grad, mine_part, other_part = attention(
        query_rows, gate_logits, gated_grad, mine, other
    )
    arrived = lax.ppermute(other_part, "expert", swap)
    merged = pl.pallas_call(
        merge_kernel,
        out_shape=jax.ShapeDtypeStruct(mine_part.shape, BF16),
        compiler_params=params(32),
        cost_estimate=cost(MIB, 2 * MIB),
        name="merge",
    )(mine_part, arrived)
    terms = between_chips(merged)
    key_grad, value_grad = pl.pallas_call(
        close_kernel,
        out_shape=[jax.ShapeDtypeStruct((seqs, length, HEAD), BF16)] * 2,
        compiler_params=params(32),
        cost_estimate=cost(MIB, MIB),
        name="close",
    )(terms)
    return (
        query_grad,
        key_grad,
        value_grad,
        gate_grad,
        input_grad,
        route_grad.T,
        gate_proj_grad,
        up_proj_grad,
        down_proj_grad,
    )


def solution(mesh):
    rows3 = P("dp", "expert", None)
    tokens2 = P(("dp", "expert"), None)
    weights = P("expert", "dp", None)
    weights_down = P("expert", None, "dp")
    return jax.shard_map(
        shards,
        mesh=mesh,
        in_specs=(rows3,) * 5 + (tokens2,) * 4 + (weights, weights, weights_down),
        out_specs=(rows3,) * 4 + (tokens2,) * 2 + (weights, weights, weights_down),
        check_vma=False,
    )
```

time: 67.6 us -> 84.7 us (1.25)
  blocking collectives: 0 us -> 32.5 us
  starting transfers between devices: 33.2 us -> 10.1 us
  waiting for transfers between devices: 14.8 us -> 20.4 us
  local copies, waits for them, and re-layouts: 5.16 us -> 6.72 us
    all_to_all x0 -> x2, blocking collectives: none -> 32.5 us  [the longest x1 20.7 us: between_chips(): lax.all_to_all(array, 'expert', split_axis=0, concat_axis=0, axis_index_g...]
    ppermute x14 -> x2, starting transfers between devices: 17.3 us -> 0.32 us  [the longest x1 0.31 us: shards(): arrived = lax.ppermute(other_part, 'expert', swap)]
    all_to_all x1 -> x2, waiting for transfers between devices: 0.01 us -> 13.1 us  [the longest x1 12.5 us: between_chips(): lax.all_to_all(array, 'expert', split_axis=0, concat_axis=0, axis_index_g...]
    ppermute x14 -> x2, waiting for transfers between devices: 12.2 us -> 0.01 us  [the longest x1 0.01 us: shards(): arrived = lax.ppermute(other_part, 'expert', swap)]
    all_to_all x1, starting transfers between devices: 8.55 us -> 2.76 us  [shards(): lax.all_to_all(back.reshape(sources, rows, LANES), axes, split_axis=0, co...]
    all_to_all x1, waiting for transfers between devices: 2.6 us -> 7.25 us  [shards(): lax.all_to_all(back.reshape(sources, rows, LANES), axes, split_axis=0, co...]
    unnamed x44 -> x40, local copies, waits for them, and re-layouts: 5.15 us -> 6.72 us
    pallas_call x4 -> x5, Pallas kernels: 8.16 us -> 7.56 us  [the longest x1 4.5 us: attention(): pl.pallas_call(attention_kernel, grid=(seqs,), in_specs=[wide] * 3 + [sta...]
  transfers between devices with their start and end apart: 16 -> 5, of which waited for: 4 -> 3; matrix products, arithmetic and copies ran while one was open for 1% -> 0% of each run, Pallas kernels for 16% -> 15%
where the time goes in v2:
time: 84.7 us; the launch traced here: 84.2 us
  blocking collectives  32.5 us (38%)
  waiting for transfers between devices  20.4 us (24%)
  Pallas kernels  13.6 us (16%)
  starting transfers between devices  10.1 us (12%)
  local copies, waits for them, and re-layouts  6.72 us (8%)
    all_to_all x1, blocking collectives, between_chips(): lax.all_to_all(array, 'expert', split_axis=0, concat_axis=0, axis_index_g...  20.7 us
    all_to_all x1, waiting for transfers between devices, between_chips(): lax.all_to_all(array, 'expert', split_axis=0, concat_axis=0, axis_index_g...  12.5 us
    all_to_all x1, blocking collectives, shards(): lax.all_to_all(send.reshape(sources, rows, LANES), axes, split_axis=0, co...  11.8 us
    all_to_all x1, waiting for transfers between devices, shards(): lax.all_to_all(back.reshape(sources, rows, LANES), axes, split_axis=0, co...  7.25 us
    unnamed x40, local copies, waits for them, and re-layouts  6.72 us
    pallas_call x1, Pallas kernels, attention(): pl.pallas_call(attention_kernel, grid=(seqs,), in_specs=[wide] * 3 + [sta...  4.5 us
    all_to_all x1, starting transfers between devices, shards(): lax.all_to_all(sent, 'dp', split_axis=0, concat_axis=0, tiled=True)  3.59 us
    all_to_all x1, starting transfers between devices, between_chips(): lax.all_to_all(array, 'expert', split_axis=0, concat_axis=0, axis_index_g...  3.47 us
  transfers between devices with their start and end apart: 5, of which 3 were waited for; matrix products, arithmetic and copies ran while one was open for 0% of the time, Pallas kernels for 15%

profile of v2, /device:TPU:0, one launch (start us, length us, event | category | flops | bytes accessed | tf_op | source)
XLA Modules:
  0.0 84.2 jit_solution(5455638110304287740)
XLA Ops:
  0.6 0.0 copy-start
  0.7 0.8 copy-done
  1.5 0.8 copy-done.1
  2.4 0.0 copy-start.2
  2.4 0.0 copy-start.3
  2.4 20.7 %all_to_all.25.mine_ref = bf16[4,2,64,512]{3,2,1,0:T(8,128)(2,1)S(1)} all-to-all(bf16[4,2,64,512]{3,2,1,0:T(8,128)(2,1)S(1)} %pack.1), channel_id=1, replica_groups={{0,2,4,6},{1,3,5,7},{8,10,12,14},{9,11,13,15},{16,18,20,22},{17,19,21,2..., dimensions={0} | all-to-all | bytes 1048576 | tf_op jit(solution)/shard_map/all_to_all | solution.py:340
  23.1 0.0 collective-permute-start
  23.1 0.0 copy-done.14
  23.1 0.0 copy-done.15
  23.1 0.0 copy-done.2
  23.2 0.0 copy-done.3
  23.2 0.0 copy-start.10
  23.2 0.0 copy-start.12
  23.2 2.0 %dispatch.1 = bf16[512,128]{1,0:T(8,128)(2,1)S(1)} custom-call(bf16[128,2048]{1,0:T(8,128)(2,1)S(1)} %copy-done.2, bf16[128,2048]{1,0:T(8,128)(2,1)S(1)} %copy-done.3, s32[10,128]{1,0:T(8,128)S(1)} %bitcast.10, bf16[10,128]{1,0:T(8,128)(2,1)S(1)} %bitcast.12), custom_call_target="tpu_custom_call" | custom-call | flops 2000000000 | bytes 2097152 | tf_op jit(solution)/shard_map/dispatch/pallas_call | solution.py:355
  25.2 0.0 copy-start.9
  25.2 11.8 %all_to_all.26 = bf16[32,16,128]{2,1,0:T(8,128)(2,1)S(1)} all-to-all(bf16[32,16,128]{2,1,0:T(8,128)(2,1)S(1)} %bitcast.9), channel_id=1, replica_groups=mesh['dp'=4,'expert'=8] {'dp','expert'}, dimensions={0} | all-to-all | bytes 262144 | tf_op jit(solution)/shard_map/all_to_all | solution.py:369
  37.0 0.0 copy-done.10
  37.0 0.0 copy-done.12
  37.0 0.0 copy-done.9
  37.0 0.0 copy-start.5
  37.0 0.0 copy-start.6
  37.0 1.3 %enter.1 = (bf16[64,512]{1,0:T(8,128)(2,1)S(1)}, bf16[64,512]{1,0:T(8,128)(2,1)S(1)}, bf16[4,64,768]{2,1,0:T(8,128)(2,1)}) custom-call(bf16[512,128]{1,0:T(8,128)(2,1)S(1)} %bitcast.8, bf16[1,512,256]{2,1,0:T(8,128)(2,1)S(1)} %copy-done.10, bf16[1,512,256]{2,1,0:T(8,128)(2,1)S(1)} %copy-done.12, bf16[1,256,512]{2,1,0:T(8,128)(2,1)S(1)} %copy-done.9), custom_call_target="tpu_custom_call" | custom-call | flops 2000000000 | bytes 2097152 | tf_op jit(solution)/shard_map/enter/pallas_call | solution.py:376
  38.3 0.6 copy-done.16
  38.9 0.6 copy-done.18
  39.6 3.6 %all-to-all-start.3 = ((bf16[4,64,768]{2,1,0:T(8,128)(2,1)}), bf16[4,64,768]{2,1,0:T(8,128)(2,1)S(1)}, u32[]{:S(2)}, u32[]{:S(2)}) async-start(bf16[4,64,768]{2,1,0:T(8,128)(2,1)} %get-tuple-element.33), calls=%async_computation.3 | async-start | bytes 786432 | tf_op jit(solution)/shard_map/all_to_all | solution.py:388
  43.2 0.0 collective-permute-done.other_ref
  43.2 0.0 copy-start.7
  43.2 0.8 copy-done.7
  44.0 0.0 copy-done.5
  44.0 0.0 copy-done.6
  44.0 0.0 copy-done.4
  44.0 1.0 %copy-done.8 = bf16[4,2,64,512]{3,2,1,0:T(8,128)(2,1)S(1)} copy-done((bf16[4,2,64,512]{3,2,1,0:T(8,128)(2,1)S(1)}, bf16[4,2,64,512]{3,2,1,0:T(8,128)(2,1)}, u32[]{:S(2)}) %copy-start.8) | copy-done | bytes 524312
  45.0 4.5 %attention.1 = (bf16[2,64,2048]{2,1,0:T(8,128)(2,1)}, bf16[2,64,2048]{2,1,0:T(8,128)(2,1)}, bf16[4,2,64,512]{3,2,1,0:T(8,128)(2,1)S(1)}, bf16[4,2,64,512]{3,2,1,0:T(8,128)(2,1)S(1)}) custom-call(bf16[2,64,2048]{2,1,0:T(8,128)(2,1)S(1)} %copy-done.4, bf16[2,64,2048]{2,1,0:T(8,128)(2,1)S(1)} %copy-done.5, bf16[2,64,2048]{2,1,0:T(8,128)(2,1)S(1)} %copy-done.6, ...), custom_call_target="tpu_custom_call" | custom-call | flops 6442450944 | bytes 8388608 | tf_op jit(solution)/shard_map/attention/pallas_call | solution.py:111
  49.5 0.3 collective-permute-start.1
  49.8 0.7 all-to-all-done.3.refs_0_
  50.5 0.9 %copy-done.11 = bf16[1,512,256]{2,1,0:T(8,128)(2,1)S(1)} copy-done((bf16[1,512,256]{2,1,0:T(8,128)(2,1)S(1)}, bf16[1,512,256]{2,1,0:T(8,128)(2,1)}, u32[]{:S(2)}) %copy-start.11) | copy-done | bytes 262168
  51.5 0.9 %copy-done.13 = bf16[1,512,256]{2,1,0:T(8,128)(2,1)S(1)} copy-done((bf16[1,512,256]{2,1,0:T(8,128)(2,1)S(1)}, bf16[1,512,256]{2,1,0:T(8,128)(2,1)}, u32[]{:S(2)}) %copy-start.13) | copy-done | bytes 262168
  52.4 1.4 %middle.1 = (bf16[512,128]{1,0:T(8,128)(2,1)}, bf16[64,256]{1,0:T(8,128)(2,1)S(1)}, bf16[64,256]{1,0:T(8,128)(2,1)S(1)}, bf16[64,256]{1,0:T(8,128)(2,1)S(1)}) custom-call(bf16[4,64,768]{2,1,0:T(8,128)(2,1)S(1)} %all-to-all-done.3.refs_0_, bf16[1,512,256]{2,1,0:T(8,128)(2,1)S(1)} %copy-done.11, bf16[1,512,256]{2,1,0:T(8,128)(2,1)S(1)} %copy-done.13), custom_call_target="tpu_custom_call" | custom-call | flops 2000000000 | bytes 2097152 | tf_op jit(solution)/shard_map/middle/pallas_call | solution.py:394
  53.8 2.8 %all-to-all-start.4 = ((bf16[32,16,128]{2,1,0:T(8,128)(2,1)}), bf16[32,16,128]{2,1,0:T(8,128)(2,1)S(1)}, u32[]{:S(2)}, u32[]{:S(2)}) async-start(bf16[32,16,128]{2,1,0:T(8,128)(2,1)} %bitcast.4), calls=%async_computation.4 | async-start | bytes 262144 | tf_op jit(solution)/shard_map/all_to_all | solution.py:401
  56.6 0.0 collective-permute-done.1.arrived_ref
  56.6 0.9 %merge.1 = bf16[4,2,64,512]{3,2,1,0:T(8,128)(2,1)} custom-call(bf16[4,2,64,512]{3,2,1,0:T(8,128)(2,1)S(1)} %get-tuple-element.28.mine_ref, bf16[4,2,64,512]{3,2,1,0:T(8,128)(2,1)S(1)} %collective-permute-done.1.arrived_ref), custom_call_target="tpu_custom_call" | custom-call | flops 1048576 | bytes 2097152 | tf_op jit(solution)/shard_map/merge/pallas_call | solution.py:430
  57.5 7.2 %all-to-all-done.4 = bf16[32,16,128]{2,1,0:T(8,128)(2,1)S(1)} async-done(((bf16[32,16,128]{2,1,0:T(8,128)(2,1)}), bf16[32,16,128]{2,1,0:T(8,128)(2,1)S(1)}, u32[]{:S(2)}, u32[]{:S(2)}) %all-to-all-start.4) | async-done | bytes 131104 | tf_op jit(solution)/shard_map/all_to_all | solution.py:401
  64.8 3.5 %all-to-all-start.1 = ((bf16[4,2,64,512]{3,2,1,0:T(8,128)(2,1)}), bf16[4,2,64,512]{3,2,1,0:T(8,128)(2,1)S(1)}, u32[]{:S(2)}, u32[]{:S(2)}) async-start(bf16[4,2,64,512]{3,2,1,0:T(8,128)(2,1)} %merge.1), calls=%async_computation.1 | async-start | bytes 1048576 | tf_op jit(solution)/shard_map/all_to_all | solution.py:340
  68.2 0.0 copy-done.17
  68.3 1.5 %weight_grads.1 = (f32[1,512,256]{2,1,0:T(8,128)}, f32[1,512,256]{2,1,0:T(8,128)}, f32[1,256,512]{2,1,0:T(8,128)}) custom-call(bf16[64,512]{1,0:T(8,128)(2,1)S(1)} %copy-done.17, bf16[64,512]{1,0:T(8,128)(2,1)S(1)} %copy-done.19, bf16[64,256]{1,0:T(8,128)(2,1)S(1)} %get-tuple-element.39.hidden_ref, bf16[64,256]{1,0:T(8,128)(2,1)S(1)} %get-tuple-element.40.gate_rows_ref, ...), custom_call_target="tpu_custom_call" | custom-call | flops 2000000000 | bytes 2097152 | tf_op jit(solution)/shard_map/weight_grads/pallas_call | solution.py:404
  69.7 1.3 %combine.1 = (bf16[128,2048]{1,0:T(8,128)(2,1)}, bf16[10,128]{1,0:T(8,128)(2,1)}) custom-call(bf16[512,128]{1,0:T(8,128)(2,1)S(1)} %bitcast.7, s32[10,128]{1,0:T(8,128)S(1)} %bitcast.11, bf16[10,128]{1,0:T(8,128)(2,1)S(1)} %bitcast.13), custom_call_target="tpu_custom_call" | custom-call | flops 2000000000 | bytes 2097152 | tf_op jit(solution)/shard_map/combine/pallas_call | solution.py:415
  71.0 12.5 %all-to-all-done.1.parts_ref = bf16[4,2,64,512]{3,2,1,0:T(8,128)(2,1)S(1)} async-done(((bf16[4,2,64,512]{3,2,1,0:T(8,128)(2,1)}), bf16[4,2,64,512]{3,2,1,0:T(8,128)(2,1)S(1)}, u32[]{:S(2)}, u32[]{:S(2)}) %all-to-all-start.1) | async-done | bytes 524320 | tf_op jit(solution)/shard_map/all_to_all | solution.py:340
  83.5 0.7 close.1
  (13 shorter events, 0.1 us)
Async XLA Ops:
  0.6 0.8 copy-start
  1.5 0.8 copy-start.1
  2.3 20.8 %copy-start.14 = (s32[128,10]{0,1:T(8,128)S(1)}, s32[128,10]{0,1:T(8,128)}, u32[]{:S(2)}) copy-start(s32[128,10]{0,1:T(8,128)} %param.19) | copy-start | bytes 15364
  2.3 20.8 %copy-start.15 = (bf16[128,10]{0,1:T(8,128)(2,1)S(1)}, bf16[128,10]{0,1:T(8,128)(2,1)}, u32[]{:S(2)}) copy-start(bf16[128,10]{0,1:T(8,128)(2,1)} %param.20) | copy-start | bytes 7684
  2.4 20.8 %copy-start.2 = (bf16[128,2048]{1,0:T(8,128)(2,1)S(1)}, bf16[128,2048]{1,0:T(8,128)(2,1)}, u32[]{:S(2)}) copy-start(bf16[128,2048]{1,0:T(8,128)(2,1)} %input_hbm.1) | copy-start | bytes 1572868
  2.4 20.8 %copy-start.3 = (bf16[128,2048]{1,0:T(8,128)(2,1)S(1)}, bf16[128,2048]{1,0:T(8,128)(2,1)}, u32[]{:S(2)}) copy-start(bf16[128,2048]{1,0:T(8,128)(2,1)} %grad_hbm.1) | copy-start | bytes 1572868
  23.1 20.0 %collective-permute-start = (bf16[4,2,64,512]{3,2,1,0:T(8,128)(2,1)S(1)}, bf16[4,2,64,512]{3,2,1,0:T(8,128)(2,1)S(1)}, u32[]{:S(2)}, u32[]{:S(2)}) collective-permute-start(bf16[4,2,64,512]{3,2,1,0:T(8,128)(2,1)S(1)} %all_to_all.25.mine_ref), channel_id=1, source_target_pairs={{0,1},{1,0},{2,3},{3,2},{4,5},{5,4},{6,7},{7,6},{8,9},{9,8},{10,11... | collective-permute-start | bytes 1572872 | tf_op jit(solution)/shard_map/ppermute | solution.py:352
  23.2 13.8 %copy-start.10 = (bf16[1,512,256]{2,1,0:T(8,128)(2,1)S(1)}, bf16[1,512,256]{2,1,0:T(8,128)(2,1)}, u32[]{:S(2)}) copy-start(bf16[1,512,256]{2,1,0:T(8,128)(2,1)} %refs_1_.1) | copy-start | bytes 786436
  23.2 13.8 %copy-start.12 = (bf16[1,512,256]{2,1,0:T(8,128)(2,1)S(1)}, bf16[1,512,256]{2,1,0:T(8,128)(2,1)}, u32[]{:S(2)}) copy-start(bf16[1,512,256]{2,1,0:T(8,128)(2,1)} %refs_2_.1) | copy-start | bytes 786436
  25.2 11.8 %copy-start.9 = (bf16[1,256,512]{2,1,0:T(8,128)(2,1)S(1)}, bf16[1,256,512]{2,1,0:T(8,128)(2,1)}, u32[]{:S(2)}) copy-start(bf16[1,256,512]{2,1,0:T(8,128)(2,1)} %down_ref.1) | copy-start | bytes 786436
  37.0 7.0 %copy-start.5 = (bf16[2,64,2048]{2,1,0:T(8,128)(2,1)S(1)}, bf16[2,64,2048]{2,1,0:T(8,128)(2,1)}, u32[]{:S(2)}) copy-start(bf16[2,64,2048]{2,1,0:T(8,128)(2,1)} %logit_ref.1) | copy-start | bytes 1572868
  37.0 6.9 %copy-start.6 = (bf16[2,64,2048]{2,1,0:T(8,128)(2,1)S(1)}, bf16[2,64,2048]{2,1,0:T(8,128)(2,1)}, u32[]{:S(2)}) copy-start(bf16[2,64,2048]{2,1,0:T(8,128)(2,1)} %grad_ref.1) | copy-start | bytes 1572868
  38.3 0.6 copy-start.16
  38.9 0.6 copy-start.18
  39.6 4.4 %copy-start.4 = (bf16[2,64,2048]{2,1,0:T(8,128)(2,1)S(1)}, bf16[2,64,2048]{2,1,0:T(8,128)(2,1)}, u32[]{:S(2)}) copy-start(bf16[2,64,2048]{2,1,0:T(8,128)(2,1)} %q_ref.1) | copy-start | bytes 1572868
  39.6 10.9 %all-to-all-start.3 = ((bf16[4,64,768]{2,1,0:T(8,128)(2,1)}), bf16[4,64,768]{2,1,0:T(8,128)(2,1)S(1)}, u32[]{:S(2)}, u32[]{:S(2)}) async-start(bf16[4,64,768]{2,1,0:T(8,128)(2,1)} %get-tuple-element.33), calls=%async_computation.3 | async-start | bytes 786432 | tf_op jit(solution)/shard_map/all_to_all | solution.py:388
  43.2 0.8 copy-start.7
  44.0 1.0 %copy-start.8 = (bf16[4,2,64,512]{3,2,1,0:T(8,128)(2,1)S(1)}, bf16[4,2,64,512]{3,2,1,0:T(8,128)(2,1)}, u32[]{:S(2)}) copy-start(bf16[4,2,64,512]{3,2,1,0:T(8,128)(2,1)} %copy-done.7) | copy-start | bytes 1572868
  49.5 7.1 %collective-permute-start.1 = (bf16[4,2,64,512]{3,2,1,0:T(8,128)(2,1)S(1)}, bf16[4,2,64,512]{3,2,1,0:T(8,128)(2,1)S(1)}, u32[]{:S(2)}, u32[]{:S(2)}) collective-permute-start(bf16[4,2,64,512]{3,2,1,0:T(8,128)(2,1)S(1)} %get-tuple-element.29), channel_id=1, source_target_pairs={{0,1},{1,0},{2,3},{3,2},{4,5},{5,4},{6,7},{7,6},{8,9},{9,8},{10,11... | collective-permute-start | bytes 1572872 | tf_op jit(solution)/shard_map/ppermute | solution.py:429
  50.5 1.0 %copy-start.11 = (bf16[1,512,256]{2,1,0:T(8,128)(2,1)S(1)}, bf16[1,512,256]{2,1,0:T(8,128)(2,1)}, u32[]{:S(2)}) copy-start(bf16[1,512,256]{2,1,0:T(8,128)(2,1)} %refs_1_.1) | copy-start | bytes 786436
  51.5 0.9 %copy-start.13 = (bf16[1,512,256]{2,1,0:T(8,128)(2,1)S(1)}, bf16[1,512,256]{2,1,0:T(8,128)(2,1)}, u32[]{:S(2)}) copy-start(bf16[1,512,256]{2,1,0:T(8,128)(2,1)} %refs_2_.1) | copy-start | bytes 786436
  53.8 10.9 %all-to-all-start.4 = ((bf16[32,16,128]{2,1,0:T(8,128)(2,1)}), bf16[32,16,128]{2,1,0:T(8,128)(2,1)S(1)}, u32[]{:S(2)}, u32[]{:S(2)}) async-start(bf16[32,16,128]{2,1,0:T(8,128)(2,1)} %bitcast.4), calls=%async_computation.4 | async-start | bytes 262144 | tf_op jit(solution)/shard_map/all_to_all | solution.py:401
  57.5 10.7 %copy-start.17 = (bf16[64,512]{1,0:T(8,128)(2,1)S(1)}, bf16[64,512]{1,0:T(8,128)(2,1)}, u32[]{:S(2)}) copy-start(bf16[64,512]{1,0:T(8,128)(2,1)} %copy-done.16) | copy-start | bytes 196612
  57.5 10.7 %copy-start.19 = (bf16[64,512]{1,0:T(8,128)(2,1)S(1)}, bf16[64,512]{1,0:T(8,128)(2,1)}, u32[]{:S(2)}) copy-start(bf16[64,512]{1,0:T(8,128)(2,1)} %copy-done.18) | copy-start | bytes 196612
  64.8 18.7 %all-to-all-start.1 = ((bf16[4,2,64,512]{3,2,1,0:T(8,128)(2,1)}), bf16[4,2,64,512]{3,2,1,0:T(8,128)(2,1)S(1)}, u32[]{:S(2)}, u32[]{:S(2)}) async-start(bf16[4,2,64,512]{3,2,1,0:T(8,128)(2,1)} %merge.1), calls=%async_computation.1 | async-start | bytes 1048576 | tf_op jit(solution)/shard_map/all_to_all | solution.py:340

commit v3 on v2

--- a/solution.py
+++ b/solution.py
@@ -15,6 +15,9 @@
 F32 = jnp.float32
 MIB = 1 << 20
 ATTENTION_MIB = 32
+IN_HBM = pl.BlockSpec(memory_space=pltpu.HBM)
+IN_VMEM = pl.BlockSpec(memory_space=pltpu.VMEM)
+ANYWHERE = pl.BlockSpec(memory_space=pl.ANY)
 
 
 def dot(a, b, ca=1, cb=0):
@@ -33,101 +36,130 @@
     return pl.CostEstimate(flops=int(flops), bytes_accessed=int(bytes_accessed), transcendentals=0)
 
 
-def pack_kernel(key_ref, value_ref, out_ref):
-    for d in range(out_ref.shape[0]):
-        out_ref[d, :, :, :HEAD] = key_ref[...]
-        out_ref[d, :, :, HEAD:] = value_ref[...]
-
-
-def attention_kernel(
-    q_ref,
-    logit_ref,
-    grad_ref,
-    mine_ref,
-    other_ref,
-    query_grad_ref,
-    gate_grad_ref,
-    mine_part_ref,
-    other_part_ref,
-):
-    length = q_ref.shape[1]
-    chips = mine_ref.shape[0]
+def pack_kernel(key_hbm, value_hbm, out_ref, key_ref, value_ref, sems):
+    copies = [
+        pltpu.make_async_copy(src, dst, sems.at[i])
+        for i, (src, dst) in enumerate(((key_hbm, key_ref), (value_hbm, value_ref)))
+    ]
+    for copy in copies:
+        copy.start()
+    copies[0].wait()
+    out_ref[:, :, :HEAD] = key_ref[...]
+    copies[1].wait()
+    out_ref[:, :, HEAD:] = value_ref[...]
+
+
+def attention_kernel(chips, *refs):
+    wide_hbm = refs[:3]
+    kv_refs = refs[3 : 3 + 2 * chips]
+    query_grad_hbm, gate_grad_hbm, other_ref = refs[4 + 2 * chips : 7 + 2 * chips]
+    mine_refs = refs[7 + 2 * chips : 7 + 3 * chips]
+    q_ref, logit_ref, grad_ref, query_grad_ref, gate_grad_ref, in_sems, out_sems = refs[
+        7 + 3 * chips :
+    ]
+    seqs, length, _ = q_ref.shape
     side = chips * length
     scale = HEAD ** (-0.5)
     position = lax.axis_index("expert")
-    chip, core = position // 2, position % 2
-
-    def stacked(ref):
+    chip, core = position >> 1, position & 1
+
+    loads = [
+        [
+            pltpu.make_async_copy(src.at[s], dst.at[s], in_sems.at[s, i])
+            for i, (src, dst) in enumerate(zip(wide_hbm, (q_ref, logit_ref, grad_ref)))
+        ]
+        for s in range(seqs)
+    ]
+    for row in loads:
+        for load in row:
+            load.start()
+
+    shape = (1, 2 * side)
+    col = iota(shape, 1)
+    half, back, inner = col // side, (col % side) // length, col % length
+    block = 2 * (chip - back) + jnp.where(half == 0, core, 1 - core)
+    key_pos = jnp.where(back <= chip, block * length + inner, 2 * side)
+    query_pos = position * length + (iota((HEADS * length, 1), 0) % length)
+
+    def stacked(ref, s):
         return jnp.concatenate(
-            [ref[0, :, h * HEAD : (h + 1) * HEAD] for h in range(HEADS)], axis=0
+            [ref[s, :, h * HEAD : (h + 1) * HEAD] for h in range(HEADS)], axis=0
         )
 
-    both = [ref[j, 0] for ref in (mine_ref, other_ref) for j in range(chips)]
-    both = jnp.concatenate(both, axis=0)
-    keys, values = both[:, :HEAD], both[:, HEAD:]
-    queries = stacked(q_ref)
-    shape = (HEADS * length, 2 * side)
-    row_pos = iota(shape, 0) % length
-    col = iota(shape, 1)
-    col_pos = col % length
-    col_chip = (col // length) % chips
-    limit = jnp.where(col < side, row_pos, core * length - 1)
-    allowed = (col_chip < chip) | ((col_chip == chip) & (col_pos <= limit))
-    scores = jnp.where(allowed, dot(queries, keys, 1, 1) * scale, -jnp.inf)
-    row_max = jnp.max(scores, axis=1, keepdims=True)
-    unnormed = jnp.exp(scores - row_max)
-    probs = unnormed * (1.0 / jnp.sum(unnormed, axis=1, keepdims=True))
-    probs_low = probs.astype(BF16)
-    context = dot(probs_low, values)
-    gate = jax.nn.sigmoid(stacked(logit_ref).astype(F32))
-    upstream = stacked(grad_ref).astype(F32)
-    context_grad = (upstream * gate).astype(BF16)
-    gate_grad = (upstream * context * gate * (1.0 - gate)).astype(BF16)
-    grad_dot = jnp.sum(context_grad.astype(F32) * context, axis=1, keepdims=True)
-    prob_grad = dot(context_grad, values, 1, 1)
-    score_grad = (probs * (prob_grad - grad_dot) * scale).astype(BF16)
-    key_part = dot(score_grad, queries, 0, 0).astype(BF16)
-    value_part = dot(probs_low, context_grad, 0, 0).astype(BF16)
-    for half, ref in enumerate((mine_part_ref, other_part_ref)):
-        for j in range(chips):
-            start = half * side + j * length
-            ref[j, 0, :, :HEAD] = key_part[start : start + length]
-            ref[j, 0, :, HEAD:] = value_part[start : start + length]
-    query_grad = dot(score_grad, keys).astype(BF16)
-    for h in range(HEADS):
-        rows_h = slice(h * length, (h + 1) * length)
-        query_grad_ref[0, :, h * HEAD : (h + 1) * HEAD] = query_grad[rows_h]
-        gate_grad_ref[0, :, h * HEAD : (h + 1) * HEAD] = gate_grad[rows_h]
-
-
-def attention(query_rows, gate_logits, gated_grad, mine, other):
+    stores = []
+    for s in range(seqs):
+        both = jnp.concatenate([ref[s] for ref in kv_refs], axis=0)
+        keys, values = both[:, :HEAD], both[:, HEAD:]
+        loads[s][0].wait()
+        queries = stacked(q_ref, s)
+        scores = jnp.where(key_pos <= query_pos, dot(queries, keys, 1, 1), -jnp.inf)
+        row_max = jnp.max(scores, axis=1, keepdims=True)
+        unnormed = jnp.exp((scores - row_max) * scale)
+        probs = unnormed * (1.0 / jnp.sum(unnormed, axis=1, keepdims=True))
+        probs_low = probs.astype(BF16)
+        context = dot(probs_low, values)
+        loads[s][1].wait()
+        loads[s][2].wait()
+        gate = jax.nn.sigmoid(stacked(logit_ref, s).astype(F32))
+        upstream = stacked(grad_ref, s).astype(F32)
+        context_grad = (upstream * gate).astype(BF16)
+        gate_grad = (upstream * context * gate * (1.0 - gate)).astype(BF16)
+        for h in range(HEADS):
+            gate_grad_ref[s, :, h * HEAD : (h + 1) * HEAD] = gate_grad[h * length : (h + 1) * length]
+        stores.append(pltpu.make_async_copy(gate_grad_ref.at[s], gate_grad_hbm.at[s], out_sems.at[s, 0]))
+        stores[-1].start()
+        grad_dot = jnp.sum(context_grad.astype(F32) * context, axis=1, keepdims=True)
+        prob_grad = dot(context_grad, values, 1, 1)
+        score_grad = (probs * (prob_grad - grad_dot)).astype(BF16)
+        query_grad = (dot(score_grad, keys) * scale).astype(BF16)
+        for h in range(HEADS):
+            query_grad_ref[s, :, h * HEAD : (h + 1) * HEAD] = query_grad[h * length : (h + 1) * length]
+        stores.append(pltpu.make_async_copy(query_grad_ref.at[s], query_grad_hbm.at[s], out_sems.at[s, 1]))
+        stores[-1].start()
+        key_part = (dot(score_grad, queries, 0, 0) * scale).astype(BF16)
+        value_part = dot(probs_low, context_grad, 0, 0).astype(BF16)
+        for d in range(chips):
+            start = d * length
+            mine_refs[d][s, :, :HEAD] = key_part[start : start + length]
+            mine_refs[d][s, :, HEAD:] = value_part[start : start + length]
+            start = side + d * length
+            other_ref[d, s, :, :HEAD] = key_part[start : start + length]
+            other_ref[d, s, :, HEAD:] = value_part[start : start + length]
+    for store in stores:
+        store.wait()
+
+
+def attention(query_rows, gate_logits, gated_grad, pieces, after):
     seqs, length, width = query_rows.shape
-    chips = mine.shape[0]
-    wide = pl.BlockSpec((1, length, width), lambda s: (s, 0, 0))
-    stack = pl.BlockSpec((chips, 1, length, 2 * HEAD), lambda s: (0, s, 0, 0))
+    chips = len(pieces) // 2
     full = jax.ShapeDtypeStruct((seqs, length, width), BF16)
-    part = jax.ShapeDtypeStruct(mine.shape, BF16)
+    part = jax.ShapeDtypeStruct(pieces[0].shape, BF16)
     flops = 12 * seqs * HEADS * length * 2 * chips * length * HEAD
-    return pl.pallas_call(
-        attention_kernel,
-        grid=(seqs,),
-        in_specs=[wide] * 3 + [stack] * 2,
-        out_specs=[wide] * 2 + [stack] * 2,
-        out_shape=[full] * 2 + [part] * 2,
-        compiler_params=params(ATTENTION_MIB if chips <= 4 else 60),
+    out = pl.pallas_call(
+        functools.partial(attention_kernel, chips),
+        in_specs=[IN_HBM] * 3 + [IN_VMEM] * (2 * chips) + [ANYWHERE],
+        out_specs=[IN_HBM] * 2 + [IN_VMEM] * (1 + chips),
+        out_shape=[full] * 2 + [jax.ShapeDtypeStruct((chips,) + part.shape, BF16)] + [part] * chips,
+        scratch_shapes=[pltpu.VMEM(query_rows.shape, BF16)] * 5
+        + [pltpu.SemaphoreType.DMA((seqs, 3)), pltpu.SemaphoreType.DMA((seqs, 2))],
+        compiler_params=params(ATTENTION_MIB if chips <= 4 else 56),
         cost_estimate=cost(flops * 4, 8 * MIB),
         name="attention",
-    )(query_rows, gate_logits, gated_grad, mine, other)
-
-
-def merge_kernel(mine_ref, arrived_ref, out_ref):
-    out_ref[...] = (mine_ref[...].astype(F32) + arrived_ref[...].astype(F32)).astype(BF16)
-
-
-def close_kernel(parts_ref, key_ref, value_ref):
-    total = parts_ref[0].astype(F32)
-    for j in range(1, parts_ref.shape[0]):
-        total = total + parts_ref[j].astype(F32)
+    )(query_rows, gate_logits, gated_grad, *pieces, after)
+    return out[0], out[1], out[2], out[3:]
+
+
+def merge_kernel(chips, *refs):
+    mine, arrived, outs = refs[:chips], refs[chips], refs[chips + 1 :]
+    for d in range(chips):
+        outs[d][...] = (mine[d][...].astype(F32) + arrived[d].astype(F32)).astype(BF16)
+
+
+def close_kernel(*refs):
+    parts, (key_ref, value_ref) = refs[:-2], refs[-2:]
+    total = parts[0][...].astype(F32)
+    for part in parts[1:]:
+        total = total + part[...].astype(F32)
     key_ref[...] = total[:, :, :HEAD].astype(BF16)
     value_ref[...] = total[:, :, HEAD:].astype(BF16)
 
@@ -150,29 +182,9 @@
 
 
 def dispatch_kernel(
-    experts,
-    groups,
-    rows,
-    input_hbm,
-    grad_hbm,
-    routes_ref,
-    weights_ref,
-    out_ref,
-    input_ref,
-    grad_ref,
-    sems,
+    experts, groups, rows, input_ref, grad_ref, routes_ref, weights_ref, after_ref, out_ref
 ):
     tokens, width = input_ref.shape
-    step = tokens // sems.shape[1]
-    copies = [
-        pltpu.make_async_copy(
-            src.at[pl.ds(i * step, step)], dst.at[pl.ds(i * step, step)], sems.at[a, i]
-        )
-        for a, (src, dst) in enumerate(((input_hbm, input_ref), (grad_hbm, grad_ref)))
-        for i in range(sems.shape[1])
-    ]
-    for copy in copies:
-        copy.start()
     slot, weight, _ = slots(routes_ref, weights_ref, experts)
     share = width // groups
     pieces = share // LANES
@@ -181,8 +193,6 @@
     row = iota(shape, 0)
     inner = row % rows
     hit = slot == (row // rows) * CAP + (inner // pieces) % CAP
-    for copy in copies:
-        copy.wait()
     acc = None
     for a, (ref, value) in enumerate(((input_ref, 1.0), (grad_ref, weight))):
         for l in range(pieces):
@@ -225,14 +235,13 @@
         partial = jnp.concatenate(
             [dot(inputs, gate_ref[0]), dot(inputs, up_ref[0]), dot(grads, down_ref[0], 1, 1)],
             axis=1,
-        ).astype(BF16)
-        for c in range(send_ref.shape[0]):
-            send_ref[c, here, :] = partial
+        )
+        send_ref[here, :] = partial.astype(BF16)
 
 
 def middle_kernel(sources, rows, *refs):
-    parts = refs[:-6]
-    gate_ref, up_ref, back_ref, hidden_ref, gate_rows_ref, up_rows_ref = refs[-6:]
+    parts = refs[:-7]
+    gate_ref, up_ref, _, back_ref, hidden_ref, gate_rows_ref, up_rows_ref = refs[-7:]
     share = gate_ref.shape[1]
     pieces = share // LANES
     hid = gate_ref.shape[2]
@@ -245,7 +254,7 @@
     pick_dot = (same & (inner == CAP * pieces + which)).astype(BF16)
     for b in range(sources // block):
         here = slice(b * block * CAP, (b + 1) * block * CAP)
-        terms = [part[c, here, :].astype(F32) for part in parts for c in range(part.shape[0])]
+        terms = [part[here, :].astype(F32) for part in parts]
         total = functools.reduce(jnp.add, terms)
         gate_pre, up_pre, hidden_grad = total[:, :hid], total[:, hid : 2 * hid], total[:, 2 * hid :]
         sig = jax.nn.sigmoid(gate_pre)
@@ -336,68 +345,78 @@
     swap = [(i, i ^ 1) for i in range(devices)]
     same_core = [list(range(c, devices, 2)) for c in range(2)]
 
-    def between_chips(array):
-        return lax.all_to_all(
-            array, "expert", split_axis=0, concat_axis=0, axis_index_groups=same_core, tiled=True
-        )
-
     packed = pl.pallas_call(
         pack_kernel,
-        out_shape=jax.ShapeDtypeStruct((chips, seqs, length, 2 * HEAD), BF16),
-        compiler_params=params(32),
+        in_specs=[IN_HBM] * 2,
+        out_shape=jax.ShapeDtypeStruct((seqs, length, 2 * HEAD), BF16),
+        scratch_shapes=[pltpu.VMEM(key_rows.shape, BF16)] * 2 + [pltpu.SemaphoreType.DMA((2,))],
+        compiler_params=params(16),
         cost_estimate=cost(MIB, MIB),
         name="pack",
     )(key_rows, value_rows)
-    mine = between_chips(packed)
-    other = lax.ppermute(mine, "expert", swap)
+    mine = [packed]
+    for d in range(1, chips):
+        up = [(i, i + 2 * d) for i in range(devices - 2 * d)]
+        mine.append(lax.ppermute(packed, "expert", up))
+    other = [lax.ppermute(block, "expert", swap) for block in mine]
 
     routes_t, weights_t = routes.T, route_weights.T
     send = pl.pallas_call(
         functools.partial(dispatch_kernel, devices, groups, rows),
-        in_specs=[pl.BlockSpec(memory_space=pltpu.HBM)] * 2
-        + [pl.BlockSpec(memory_space=pltpu.VMEM)] * 2,
+        in_specs=[IN_VMEM] * 4 + [ANYWHERE],
         out_shape=jax.ShapeDtypeStruct((sources * rows, LANES), BF16),
-        scratch_shapes=[
-            pltpu.VMEM(moe_input.shape, BF16),
-            pltpu.VMEM(out_grad.shape, BF16),
-            pltpu.SemaphoreType.DMA((2, 4)),
-        ],
-        compiler_params=params(32),
+        compiler_params=params(16),
         cost_estimate=cost(2e9, 2 * MIB),
         name="dispatch",
-    )(moe_input, out_grad, routes_t, weights_t)
+    )(moe_input, out_grad, routes_t, weights_t, packed)
     recv = lax.all_to_all(
         send.reshape(sources, rows, LANES), axes, split_axis=0, concat_axis=0, tiled=True
     ).reshape(sources * rows, LANES)
 
     slot_rows = jax.ShapeDtypeStruct((sources * CAP, share), BF16)
     hid_rows = jax.ShapeDtypeStruct((sources * CAP, hid), BF16)
-    few = groups <= 4
     inputs, grads, sent = pl.pallas_call(
         functools.partial(enter_kernel, sources, rows),
-        out_shape=[
-            slot_rows,
-            slot_rows,
-            jax.ShapeDtypeStruct((groups if few else 1, sources * CAP, 3 * hid), BF16),
-        ],
-        compiler_params=params(32),
+        out_shape=[slot_rows, slot_rows, jax.ShapeDtypeStruct((sources * CAP, 3 * hid), BF16)],
+        compiler_params=params(16),
         cost_estimate=cost(2e9, 2 * MIB),
         name="enter",
     )(recv, gate_proj, up_proj, down_proj)
-    if few:
-        parts = [lax.all_to_all(sent, "dp", split_axis=0, concat_axis=0, tiled=True)]
-    else:
-        parts = [sent] + [
-            lax.ppermute(sent, "dp", [(g, (g + k) % groups) for g in range(groups)])
-            for k in range(1, groups)
-        ]
+    parts = [sent] + [
+        lax.ppermute(sent, "dp", [(g, g ^ k) for g in range(groups)]) for k in range(1, groups)
+    ]
+
+    query_grad, gate_grad, other_part, mine_part = attention(
+        query_rows, gate_logits, gated_grad, mine + other, sent
+    )
+    arrived = lax.ppermute(other_part, "expert", swap)
+    merged = pl.pallas_call(
+        functools.partial(merge_kernel, chips),
+        out_shape=[jax.ShapeDtypeStruct(packed.shape, BF16)] * chips,
+        compiler_params=params(16),
+        cost_estimate=cost(MIB, 2 * MIB),
+        name="merge",
+    )(*mine_part, arrived)
+    terms = [merged[0]]
+    for d in range(1, chips):
+        down = [(i, i - 2 * d) for i in range(2 * d, devices)]
+        terms.append(lax.ppermute(merged[d], "expert", down))
+    key_grad, value_grad = pl.pallas_call(
+        close_kernel,
+        out_shape=[jax.ShapeDtypeStruct((seqs, length, HEAD), BF16)] * 2,
+        compiler_params=params(16),
+        cost_estimate=cost(MIB, MIB),
+        name="close",
+    )(*terms)
+
     back, hidden, gate_rows, up_rows = pl.pallas_call(
         functools.partial(middle_kernel, sources, rows),
+        in_specs=[IN_VMEM] * (len(parts) + 2) + [ANYWHERE],
         out_shape=[jax.ShapeDtypeStruct((sources * rows, LANES), BF16)] + [hid_rows] * 3,
-        compiler_params=params(32 if few else 60),
+        compiler_params=params(16 if groups <= 4 else 60),
         cost_estimate=cost(2e9, 2 * MIB),
         name="middle",
-    )(*parts, gate_proj, up_proj)
+    )(*parts, gate_proj, up_proj, merged[0])
     returned = lax.all_to_all(
         back.reshape(sources, rows, LANES), axes, split_axis=0, concat_axis=0, tiled=True
     ).reshape(sources * rows, LANES)
@@ -408,7 +427,7 @@
             jax.ShapeDtypeStruct(up_proj.shape, F32),
             jax.ShapeDtypeStruct(down_proj.shape, F32),
         ],
-        compiler_params=params(32),
+        compiler_params=params(16),
         cost_estimate=cost(2e9, 2 * MIB),
         name="weight_grads",
     )(inputs, grads, hidden, gate_rows, up_rows)
@@ -418,30 +437,11 @@
             jax.ShapeDtypeStruct(moe_input.shape, BF16),
             jax.ShapeDtypeStruct(routes_t.shape, BF16),
         ],
-        compiler_params=params(32),
+        compiler_params=params(16),
         cost_estimate=cost(2e9, 2 * MIB),
         name="combine",
     )(returned, routes_t, weights_t)
 
-    query_grad, gate_grad, mine_part, other_part = attention(
-        query_rows, gate_logits, gated_grad, mine, other
-    )
-    arrived = lax.ppermute(other_part, "expert", swap)
-    merged = pl.pallas_call(
-        merge_kernel,
-        out_shape=jax.ShapeDtypeStruct(mine_part.shape, BF16),
-        compiler_params=params(32),
-        cost_estimate=cost(MIB, 2 * MIB),
-        name="merge",
-    )(mine_part, arrived)
-    terms = between_chips(merged)
-    key_grad, value_grad = pl.pallas_call(
-        close_kernel,
-        out_shape=[jax.ShapeDtypeStruct((seqs, length, HEAD), BF16)] * 2,
-        compiler_params=params(32),
-        cost_estimate=cost(MIB, MIB),
-        name="close",
-    )(terms)
     return (
         query_grad,
         key_grad,

time: 84.7 us -> 71.5 us (0.84)
  blocking collectives: 32.5 us -> 0 us
  starting transfers between devices: 10.1 us -> 32.2 us
  local copies, waits for them, and re-layouts: 6.72 us -> 4.34 us
  Pallas kernels: 13.6 us -> 11.6 us
  waiting for transfers between devices: 20.4 us -> 21.8 us
    all_to_all x2 -> x0, blocking collectives: 32.5 us -> none  [the longest x1 20.7 us: between_chips(): lax.all_to_all(array, 'expert', split_axis=0, concat_axis=0, axis_index_g...]
    ppermute x1 -> x13, waiting for transfers between devices: 0.01 us -> 21.8 us  [the longest x3 12.4 us: shards(): terms.append(lax.ppermute(merged[d], 'expert', down))]
    ppermute x1 -> x13, starting transfers between devices: 0.01 us -> 17.2 us  [the longest x3 9.3 us: shards(): mine.append(lax.ppermute(packed, 'expert', up))]
    all_to_all x2 -> x1, waiting for transfers between devices: 13.1 us -> 0.01 us  [shards(): lax.all_to_all(send.reshape(sources, rows, LANES), axes, split_axis=0, co...]
    all_to_all x1, waiting for transfers between devices: 7.25 us -> 0.01 us  [shards(): lax.all_to_all(back.reshape(sources, rows, LANES), axes, split_axis=0, co...]
    all_to_all x1, starting transfers between devices: 2.76 us -> 7.13 us  [shards(): lax.all_to_all(back.reshape(sources, rows, LANES), axes, split_axis=0, co...]
    unnamed x40 -> x24, local copies, waits for them, and re-layouts: 6.72 us -> 4.34 us
    all_to_all x2 -> x1, starting transfers between devices: 7.06 us -> 7.3 us  [shards(): lax.all_to_all(send.reshape(sources, rows, LANES), axes, split_axis=0, co...]
  transfers between devices with their start and end apart: 5 -> 16, of which waited for: 3 -> 8; matrix products, arithmetic and copies ran while one was open for 0% -> 0% of each run, Pallas kernels for 15% -> 4%
where the time goes in v3:
time: 71.5 us; the launch traced here: 70.9 us
  starting transfers between devices  32.2 us (45%)
  waiting for transfers between devices  21.8 us (30%)
  Pallas kernels  11.6 us (16%)
  local copies, waits for them, and re-layouts  4.34 us (6%)
  between operations  0.84 us (1%)
    ppermute x3, waiting for transfers between devices, shards(): terms.append(lax.ppermute(merged[d], 'expert', down))  12.4 us
    ppermute x3, starting transfers between devices, shards(): mine.append(lax.ppermute(packed, 'expert', up))  9.3 us
    all_to_all x1, starting transfers between devices, shards(): lax.all_to_all(send.reshape(sources, rows, LANES), axes, split_axis=0, co...  7.3 us
    all_to_all x1, starting transfers between devices, shards(): lax.all_to_all(back.reshape(sources, rows, LANES), axes, split_axis=0, co...  7.13 us
    ppermute x3, waiting for transfers between devices, shards(): lax.ppermute(sent, 'dp', [(g, g ^ k) for g in range(groups)])  4.88 us
    pallas_call x1, Pallas kernels, attention(): pl.pallas_call(functools.partial(attention_kernel, chips), in_specs=[IN_H...  4.77 us
    unnamed x24, local copies, waits for them, and re-layouts  4.34 us
    ppermute x3, starting transfers between devices, shards(): terms.append(lax.ppermute(merged[d], 'expert', down))  3.88 us
  transfers between devices with their start and end apart: 16, of which 8 were waited for; matrix products, arithmetic and copies ran while one was open for 0% of the time, Pallas kernels for 4%

profile of v3, /device:TPU:0, one launch (start us, length us, event | category | flops | bytes accessed | tf_op | source)
XLA Modules:
  0.0 70.9 jit_solution(11499262848471397318)
XLA Ops:
  0.7 0.8 %copy-done = bf16[2,64,256]{2,1,0:T(8,128)(2,1)S(1)} copy-done((bf16[2,64,256]{2,1,0:T(8,128)(2,1)S(1)}, bf16[2,64,256]{2,1,0:T(8,128)(2,1)}, u32[]{:S(2)}) %copy-start) | copy-done | bytes 65560
  1.5 0.8 %copy-done.1 = bf16[2,64,256]{2,1,0:T(8,128)(2,1)S(1)} copy-done((bf16[2,64,256]{2,1,0:T(8,128)(2,1)S(1)}, bf16[2,64,256]{2,1,0:T(8,128)(2,1)}, u32[]{:S(2)}) %copy-start.1) | copy-done | bytes 65560
  2.3 0.2 pack.1.after_ref.refs_3_
  2.5 0.5 copy-done.10
  3.0 0.0 copy-done.11
  3.0 1.0 %copy-done.2 = bf16[128,2048]{1,0:T(8,128)(2,1)S(1)} copy-done((bf16[128,2048]{1,0:T(8,128)(2,1)S(1)}, bf16[128,2048]{1,0:T(8,128)(2,1)}, u32[]{:S(2)}) %copy-start.2) | copy-done | bytes 524312
  4.1 1.0 %copy-done.3 = bf16[128,2048]{1,0:T(8,128)(2,1)S(1)} copy-done((bf16[128,2048]{1,0:T(8,128)(2,1)S(1)}, bf16[128,2048]{1,0:T(8,128)(2,1)}, u32[]{:S(2)}) %copy-start.3) | copy-done | bytes 524312
  5.1 1.2 %dispatch.1 = bf16[512,128]{1,0:T(8,128)(2,1)} custom-call(bf16[128,2048]{1,0:T(8,128)(2,1)S(1)} %copy-done.2, bf16[128,2048]{1,0:T(8,128)(2,1)S(1)} %copy-done.3, s32[10,128]{1,0:T(8,128)S(1)} %bitcast.9, bf16[10,128]{1,0:T(8,128)(2,1)S(1)} %bitcast.11, bf16[2,64,512]{2,1,0:T(8,128)(2,1)S(1)} %pack.1.after_ref.refs_3_), custom_call_target="tpu_custom_call" | custom-call | flops 2000000000 | bytes 2097152 | tf_op jit(solution)/shard_map/dispatch/pallas_call | solution.py:364
  6.3 7.3 %all-to-all-start = ((bf16[32,16,128]{2,1,0:T(8,128)(2,1)}), bf16[32,16,128]{2,1,0:T(8,128)(2,1)S(1)}, u32[]{:S(2)}, u32[]{:S(2)}) async-start(bf16[32,16,128]{2,1,0:T(8,128)(2,1)} %bitcast.2), calls=%async_computation | async-start | bytes 262144 | tf_op jit(solution)/shard_map/all_to_all | solution.py:372
  13.6 3.7 %collective-permute-start = (bf16[2,64,512]{2,1,0:T(8,128)(2,1)S(1)}, bf16[2,64,512]{2,1,0:T(8,128)(2,1)S(1)}, u32[]{:S(2)}, u32[]{:S(2)}) collective-permute-start(bf16[2,64,512]{2,1,0:T(8,128)(2,1)S(1)} %pack.1.after_ref.refs_3_), channel_id=1, source_target_pairs={{0,2},{1,3},{2,4},{3,5},{4,6},{5,7},{8,10},{9,11},{10,12},{11,13},... | collective-permute-start | bytes 393224 | tf_op jit(solution)/shard_map/ppermute | solution.py:360
  17.3 4.3 %collective-permute-start.1 = (bf16[2,64,512]{2,1,0:T(8,128)(2,1)S(1)}, bf16[2,64,512]{2,1,0:T(8,128)(2,1)S(1)}, u32[]{:S(2)}, u32[]{:S(2)}) collective-permute-start(bf16[2,64,512]{2,1,0:T(8,128)(2,1)S(1)} %pack.1.after_ref.refs_3_), channel_id=1, source_target_pairs={{0,4},{1,5},{2,6},{3,7},{8,12},{9,13},{10,14},{11,15},{16,20},{17,... | collective-permute-start | bytes 393224 | tf_op jit(solution)/shard_map/ppermute | solution.py:360
  21.7 1.3 %collective-permute-start.2 = (bf16[2,64,512]{2,1,0:T(8,128)(2,1)S(1)}, bf16[2,64,512]{2,1,0:T(8,128)(2,1)S(1)}, u32[]{:S(2)}, u32[]{:S(2)}) collective-permute-start(bf16[2,64,512]{2,1,0:T(8,128)(2,1)S(1)} %pack.1.after_ref.refs_3_), channel_id=1, source_target_pairs={{0,6},{1,7},{8,14},{9,15},{16,22},{17,23},{24,30},{25,31}} | collective-permute-start | bytes 393224 | tf_op jit(solution)/shard_map/ppermute | solution.py:360
  23.0 0.1 collective-permute-start.3
  23.0 0.0 collective-permute-done.refs_4_
  23.1 0.5 collective-permute-start.4
  23.5 2.0 %collective-permute-done.1.refs_5_ = bf16[2,64,512]{2,1,0:T(8,128)(2,1)S(1)} collective-permute-done((bf16[2,64,512]{2,1,0:T(8,128)(2,1)S(1)}, bf16[2,64,512]{2,1,0:T(8,128)(2,1)S(1)}, u32[]{:S(2)}, u32[]{:S(2)}) %collective-permute-start.1) | collective-permute-done | bytes 131104 | tf_op jit(solution)/shard_map/ppermute | solution.py:360
  25.5 1.7 %collective-permute-done.2.refs_6_ = bf16[2,64,512]{2,1,0:T(8,128)(2,1)S(1)} collective-permute-done((bf16[2,64,512]{2,1,0:T(8,128)(2,1)S(1)}, bf16[2,64,512]{2,1,0:T(8,128)(2,1)S(1)}, u32[]{:S(2)}, u32[]{:S(2)}) %collective-permute-start.2) | collective-permute-done | bytes 131104 | tf_op jit(solution)/shard_map/ppermute | solution.py:360
  27.3 0.0 collective-permute-start.6
  27.3 0.0 all-to-all-done
  27.3 0.0 copy-start.4
  27.3 0.0 copy-start.5
  27.3 0.0 copy-start.6
  27.3 0.5 enter.1
  27.8 0.0 collective-permute-done.3.refs_7_
  27.8 0.0 collective-permute-done.4.refs_8_
  27.9 0.8 %collective-permute-done.6.refs_10_ = bf16[2,64,512]{2,1,0:T(8,128)(2,1)S(1)} collective-permute-done((bf16[2,64,512]{2,1,0:T(8,128)(2,1)S(1)}, bf16[2,64,512]{2,1,0:T(8,128)(2,1)S(1)}, u32[]{:S(2)}, u32[]{:S(2)}) %collective-permute-start.6) | collective-permute-done | bytes 131104 | tf_op jit(solution)/shard_map/ppermute | solution.py:361
  28.6 0.0 copy-done.6
  28.7 4.8 %attention.1 = (bf16[2,64,2048]{2,1,0:T(8,128)(2,1)}, bf16[2,64,2048]{2,1,0:T(8,128)(2,1)}, bf16[4,2,64,512]{3,2,1,0:T(8,128)(2,1)S(1)}, bf16[2,64,512]{2,1,0:T(...) custom-call(bf16[2,64,2048]{2,1,0:T(8,128)(2,1)S(1)} %copy-done.4, ...), custom_call_target="tpu_custom_call" | custom-call | flops 6442450944 | bytes 8388608 | tf_op jit(solution)/shard_map/attention/pallas_call | solution.py:138
  33.5 0.6 collective-permute-start.7
  34.0 1.5 %collective-permute-start.11 = (bf16[64,768]{1,0:T(8,128)(2,1)S(1)}, bf16[64,768]{1,0:T(8,128)(2,1)S(1)}, u32[]{:S(2)}, u32[]{:S(2)}) collective-permute-start(bf16[64,768]{1,0:T(8,128)(2,1)S(1)} %get-tuple-element.34.refs_11_.refs_0_), channel_id=1, source_target_pairs={{0,8},{8,0},{16,24},{24,16},{1,9},{9,1},{17,25},{25,17},{2,10},{10... | collective-permute-start | bytes 294920 | tf_op jit(solution)/shard_map/ppermute | solution.py:386
  35.5 1.5 %collective-permute-start.12 = (bf16[64,768]{1,0:T(8,128)(2,1)S(1)}, bf16[64,768]{1,0:T(8,128)(2,1)S(1)}, u32[]{:S(2)}, u32[]{:S(2)}) collective-permute-start(bf16[64,768]{1,0:T(8,128)(2,1)S(1)} %get-tuple-element.34.refs_11_.refs_0_), channel_id=1, source_target_pairs={{0,16},{8,24},{16,0},{24,8},{1,17},{9,25},{17,1},{25,9},{2,18},{10... | collective-permute-start | bytes 294920 | tf_op jit(solution)/shard_map/ppermute | solution.py:386
  37.0 0.5 collective-permute-start.13
  37.5 0.0 collective-permute-done.7.refs_4_
  37.5 0.1 merge.1
  37.6 1.2 %collective-permute-done.11.refs_1_ = bf16[64,768]{1,0:T(8,128)(2,1)S(1)} collective-permute-done((bf16[64,768]{1,0:T(8,128)(2,1)S(1)}, bf16[64,768]{1,0:T(8,128)(2,1)S(1)}, u32[]{:S(2)}, u32[]{:S(2)}) %collective-permute-start.11) | collective-permute-done | bytes 98336 | tf_op jit(solution)/shard_map/ppermute | solution.py:386
  38.8 2.5 %collective-permute-done.12.refs_2_ = bf16[64,768]{1,0:T(8,128)(2,1)S(1)} collective-permute-done((bf16[64,768]{1,0:T(8,128)(2,1)S(1)}, bf16[64,768]{1,0:T(8,128)(2,1)S(1)}, u32[]{:S(2)}, u32[]{:S(2)}) %collective-permute-start.12) | collective-permute-done | bytes 98336 | tf_op jit(solution)/shard_map/ppermute | solution.py:386
  41.2 1.3 %collective-permute-done.13.refs_3_ = bf16[64,768]{1,0:T(8,128)(2,1)S(1)} collective-permute-done((bf16[64,768]{1,0:T(8,128)(2,1)S(1)}, bf16[64,768]{1,0:T(8,128)(2,1)S(1)}, u32[]{:S(2)}, u32[]{:S(2)}) %collective-permute-start.13) | collective-permute-done | bytes 98336 | tf_op jit(solution)/shard_map/ppermute | solution.py:386
  42.5 1.4 %middle.1 = (bf16[512,128]{1,0:T(8,128)(2,1)}, bf16[64,256]{1,0:T(8,128)(2,1)S(1)}, bf16[64,256]{1,0:T(8,128)(2,1)S(1)}, bf16[64,256]{1,0:T(8,128)(2,1)S(1)}) custom-call(bf16[64,768]{1,0:T(8,128)(2,1)S(1)} %get-tuple-element.34.refs_11_.refs_0_, bf16[64,768]{1,0:T(8,128)(2,1)S(1)} %collective-permute-done.11.refs_1_, ...), custom_call_target="tpu_custom_call" | custom-call | flops 2000000000 | bytes 2097152 | tf_op jit(solution)/shard_map/middle/pallas_call | solution.py:412
  43.9 7.1 %all-to-all-start.1 = ((bf16[32,16,128]{2,1,0:T(8,128)(2,1)}), bf16[32,16,128]{2,1,0:T(8,128)(2,1)S(1)}, u32[]{:S(2)}, u32[]{:S(2)}) async-start(bf16[32,16,128]{2,1,0:T(8,128)(2,1)} %bitcast.4), calls=%async_computation.1 | async-start | bytes 262144 | tf_op jit(solution)/shard_map/all_to_all | solution.py:420
  51.1 1.3 %collective-permute-start.8 = (bf16[2,64,512]{2,1,0:T(8,128)(2,1)S(1)}, bf16[2,64,512]{2,1,0:T(8,128)(2,1)S(1)}, u32[]{:S(2)}, u32[]{:S(2)}) collective-permute-start(bf16[2,64,512]{2,1,0:T(8,128)(2,1)S(1)} %get-tuple-element.42), channel_id=1, source_target_pairs={{2,0},{3,1},{4,2},{5,3},{6,4},{7,5},{10,8},{11,9},{12,10},{13,11},... | collective-permute-start | bytes 393224 | tf_op jit(solution)/shard_map/ppermute | solution.py:403
  52.4 1.3 %collective-permute-start.9 = (bf16[2,64,512]{2,1,0:T(8,128)(2,1)S(1)}, bf16[2,64,512]{2,1,0:T(8,128)(2,1)S(1)}, u32[]{:S(2)}, u32[]{:S(2)}) collective-permute-start(bf16[2,64,512]{2,1,0:T(8,128)(2,1)S(1)} %get-tuple-element.43), channel_id=1, source_target_pairs={{4,0},{5,1},{6,2},{7,3},{12,8},{13,9},{14,10},{15,11},{20,16},{21,... | collective-permute-start | bytes 393224 | tf_op jit(solution)/shard_map/ppermute | solution.py:403
  53.7 1.3 %collective-permute-start.10 = (bf16[2,64,512]{2,1,0:T(8,128)(2,1)S(1)}, bf16[2,64,512]{2,1,0:T(8,128)(2,1)S(1)}, u32[]{:S(2)}, u32[]{:S(2)}) collective-permute-start(bf16[2,64,512]{2,1,0:T(8,128)(2,1)S(1)} %get-tuple-element.44), channel_id=1, source_target_pairs={{6,0},{7,1},{14,8},{15,9},{22,16},{23,17},{30,24},{31,25}} | collective-permute-start | bytes 393224 | tf_op jit(solution)/shard_map/ppermute | solution.py:403
  55.0 1.5 %weight_grads.1 = (f32[1,512,256]{2,1,0:T(8,128)}, f32[1,512,256]{2,1,0:T(8,128)}, f32[1,256,512]{2,1,0:T(8,128)}) custom-call(bf16[64,512]{1,0:T(8,128)(2,1)S(1)} %get-tuple-element.51.input_ref, bf16[64,512]{1,0:T(8,128)(2,1)S(1)} %get-tuple-element.52.grad_ref, bf16[64,256]{1,0:T(8,128)(2,1)S(1)} %get-tuple-element.53.hidden_ref, ...), custom_call_target="tpu_custom_call" | custom-call | flops 2000000000 | bytes 2097152 | tf_op jit(solution)/shard_map/weight_grads/pallas_call | solution.py:423
  56.5 3.1 %collective-permute-done.8.refs_1_ = bf16[2,64,512]{2,1,0:T(8,128)(2,1)S(1)} collective-permute-done((bf16[2,64,512]{2,1,0:T(8,128)(2,1)S(1)}, bf16[2,64,512]{2,1,0:T(8,128)(2,1)S(1)}, u32[]{:S(2)}, u32[]{:S(2)}) %collective-permute-start.8) | collective-permute-done | bytes 131104 | tf_op jit(solution)/shard_map/ppermute | solution.py:403
  59.6 9.3 %collective-permute-done.9.refs_2_ = bf16[2,64,512]{2,1,0:T(8,128)(2,1)S(1)} collective-permute-done((bf16[2,64,512]{2,1,0:T(8,128)(2,1)S(1)}, bf16[2,64,512]{2,1,0:T(8,128)(2,1)S(1)}, u32[]{:S(2)}, u32[]{:S(2)}) %collective-permute-start.9) | collective-permute-done | bytes 131104 | tf_op jit(solution)/shard_map/ppermute | solution.py:403
  68.9 0.7 close.1
  69.6 0.0 all-to-all-done.1
  69.6 1.3 %combine.1 = (bf16[128,2048]{1,0:T(8,128)(2,1)}, bf16[10,128]{1,0:T(8,128)(2,1)}) custom-call(bf16[512,128]{1,0:T(8,128)(2,1)S(1)} %bitcast.7, s32[10,128]{1,0:T(8,128)S(1)} %bitcast.10, bf16[10,128]{1,0:T(8,128)(2,1)S(1)} %bitcast.12), custom_call_target="tpu_custom_call" | custom-call | flops 2000000000 | bytes 2097152 | tf_op jit(solution)/shard_map/combine/pallas_call | solution.py:434
  (17 shorter events, 0.0 us)
Async XLA Ops:
  0.6 0.8 %copy-start = (bf16[2,64,256]{2,1,0:T(8,128)(2,1)S(1)}, bf16[2,64,256]{2,1,0:T(8,128)(2,1)}, u32[]{:S(2)}) copy-start(bf16[2,64,256]{2,1,0:T(8,128)(2,1)} %key_hbm.1) | copy-start | bytes 196612
  1.5 0.8 %copy-start.1 = (bf16[2,64,256]{2,1,0:T(8,128)(2,1)S(1)}, bf16[2,64,256]{2,1,0:T(8,128)(2,1)}, u32[]{:S(2)}) copy-start(bf16[2,64,256]{2,1,0:T(8,128)(2,1)} %value_hbm.1) | copy-start | bytes 196612
  2.3 0.7 copy-start.10
  2.3 0.7 copy-start.11
  3.0 1.0 %copy-start.2 = (bf16[128,2048]{1,0:T(8,128)(2,1)S(1)}, bf16[128,2048]{1,0:T(8,128)(2,1)}, u32[]{:S(2)}) copy-start(bf16[128,2048]{1,0:T(8,128)(2,1)} %input_ref.1) | copy-start | bytes 1572868
  4.1 1.0 %copy-start.3 = (bf16[128,2048]{1,0:T(8,128)(2,1)S(1)}, bf16[128,2048]{1,0:T(8,128)(2,1)}, u32[]{:S(2)}) copy-start(bf16[128,2048]{1,0:T(8,128)(2,1)} %grad_ref.1) | copy-start | bytes 1572868
  5.1 22.2 %copy-start.8 = (bf16[1,512,256]{2,1,0:T(8,128)(2,1)S(1)}, bf16[1,512,256]{2,1,0:T(8,128)(2,1)}, u32[]{:S(2)}) copy-start(bf16[1,512,256]{2,1,0:T(8,128)(2,1)} %refs_4_.1) | copy-start | bytes 786436
  5.1 22.2 %copy-start.9 = (bf16[1,512,256]{2,1,0:T(8,128)(2,1)S(1)}, bf16[1,512,256]{2,1,0:T(8,128)(2,1)}, u32[]{:S(2)}) copy-start(bf16[1,512,256]{2,1,0:T(8,128)(2,1)} %refs_5_.1) | copy-start | bytes 786436
  6.3 21.0 %copy-start.7 = (bf16[1,256,512]{2,1,0:T(8,128)(2,1)S(1)}, bf16[1,256,512]{2,1,0:T(8,128)(2,1)}, u32[]{:S(2)}) copy-start(bf16[1,256,512]{2,1,0:T(8,128)(2,1)} %down_ref.1) | copy-start | bytes 786436
  6.3 21.0 %all-to-all-start = ((bf16[32,16,128]{2,1,0:T(8,128)(2,1)}), bf16[32,16,128]{2,1,0:T(8,128)(2,1)S(1)}, u32[]{:S(2)}, u32[]{:S(2)}) async-start(bf16[32,16,128]{2,1,0:T(8,128)(2,1)} %bitcast.2), calls=%async_computation | async-start | bytes 262144 | tf_op jit(solution)/shard_map/all_to_all | solution.py:372
  13.6 9.4 %collective-permute-start = (bf16[2,64,512]{2,1,0:T(8,128)(2,1)S(1)}, bf16[2,64,512]{2,1,0:T(8,128)(2,1)S(1)}, u32[]{:S(2)}, u32[]{:S(2)}) collective-permute-start(bf16[2,64,512]{2,1,0:T(8,128)(2,1)S(1)} %pack.1.after_ref.refs_3_), channel_id=1, source_target_pairs={{0,2},{1,3},{2,4},{3,5},{4,6},{5,7},{8,10},{9,11},{10,12},{11,13},... | collective-permute-start | bytes 393224 | tf_op jit(solution)/shard_map/ppermute | solution.py:360
  17.3 8.2 %collective-permute-start.1 = (bf16[2,64,512]{2,1,0:T(8,128)(2,1)S(1)}, bf16[2,64,512]{2,1,0:T(8,128)(2,1)S(1)}, u32[]{:S(2)}, u32[]{:S(2)}) collective-permute-start(bf16[2,64,512]{2,1,0:T(8,128)(2,1)S(1)} %pack.1.after_ref.refs_3_), channel_id=1, source_target_pairs={{0,4},{1,5},{2,6},{3,7},{8,12},{9,13},{10,14},{11,15},{16,20},{17,... | collective-permute-start | bytes 393224 | tf_op jit(solution)/shard_map/ppermute | solution.py:360
  21.7 5.6 %collective-permute-start.2 = (bf16[2,64,512]{2,1,0:T(8,128)(2,1)S(1)}, bf16[2,64,512]{2,1,0:T(8,128)(2,1)S(1)}, u32[]{:S(2)}, u32[]{:S(2)}) collective-permute-start(bf16[2,64,512]{2,1,0:T(8,128)(2,1)S(1)} %pack.1.after_ref.refs_3_), channel_id=1, source_target_pairs={{0,6},{1,7},{8,14},{9,15},{16,22},{17,23},{24,30},{25,31}} | collective-permute-start | bytes 393224 | tf_op jit(solution)/shard_map/ppermute | solution.py:360
  23.0 4.9 %collective-permute-start.3 = (bf16[2,64,512]{2,1,0:T(8,128)(2,1)S(1)}, bf16[2,64,512]{2,1,0:T(8,128)(2,1)S(1)}, u32[]{:S(2)}, u32[]{:S(2)}) collective-permute-start(bf16[2,64,512]{2,1,0:T(8,128)(2,1)S(1)} %pack.1.after_ref.refs_3_), channel_id=1, source_target_pairs={{0,1},{1,0},{2,3},{3,2},{4,5},{5,4},{6,7},{7,6},{8,9},{9,8},{10,11... | collective-permute-start | bytes 393224 | tf_op jit(solution)/shard_map/ppermute | solution.py:361
  23.1 4.8 %collective-permute-start.4 = (bf16[2,64,512]{2,1,0:T(8,128)(2,1)S(1)}, bf16[2,64,512]{2,1,0:T(8,128)(2,1)S(1)}, u32[]{:S(2)}, u32[]{:S(2)}) collective-permute-start(bf16[2,64,512]{2,1,0:T(8,128)(2,1)S(1)} %collective-permute-done.refs_4_), channel_id=1, source_target_pairs={{0,1},{1,0},{2,3},{3,2},{4,5},{5,4},{6,7},{7,6},{8,9},{9,8},{10,11... | collective-permute-start | bytes 393224 | tf_op jit(solution)/shard_map/ppermute | solution.py:361
  25.5 2.3 %collective-permute-start.5 = (bf16[2,64,512]{2,1,0:T(8,128)(2,1)S(1)}, bf16[2,64,512]{2,1,0:T(8,128)(2,1)S(1)}, u32[]{:S(2)}, u32[]{:S(2)}) collective-permute-start(bf16[2,64,512]{2,1,0:T(8,128)(2,1)S(1)} %collective-permute-done.1.refs_5_), channel_id=1, source_target_pairs={{0,1},{1,0},{2,3},{3,2},{4,5},{5,4},{6,7},{7,6},{8,9},{9,8},{10,11... | collective-permute-start | bytes 393224 | tf_op jit(solution)/shard_map/ppermute | solution.py:361
  27.3 1.3 %collective-permute-start.6 = (bf16[2,64,512]{2,1,0:T(8,128)(2,1)S(1)}, bf16[2,64,512]{2,1,0:T(8,128)(2,1)S(1)}, u32[]{:S(2)}, u32[]{:S(2)}) collective-permute-start(bf16[2,64,512]{2,1,0:T(8,128)(2,1)S(1)} %collective-permute-done.2.refs_6_), channel_id=1, source_target_pairs={{0,1},{1,0},{2,3},{3,2},{4,5},{5,4},{6,7},{7,6},{8,9},{9,8},{10,11... | collective-permute-start | bytes 393224 | tf_op jit(solution)/shard_map/ppermute | solution.py:361
  27.3 1.3 %copy-start.4 = (bf16[2,64,2048]{2,1,0:T(8,128)(2,1)S(1)}, bf16[2,64,2048]{2,1,0:T(8,128)(2,1)}, u32[]{:S(2)}) copy-start(bf16[2,64,2048]{2,1,0:T(8,128)(2,1)} %refs_0_.1) | copy-start | bytes 1572868
  27.3 1.3 %copy-start.5 = (bf16[2,64,2048]{2,1,0:T(8,128)(2,1)S(1)}, bf16[2,64,2048]{2,1,0:T(8,128)(2,1)}, u32[]{:S(2)}) copy-start(bf16[2,64,2048]{2,1,0:T(8,128)(2,1)} %refs_1_.1) | copy-start | bytes 1572868
  27.3 1.3 %copy-start.6 = (bf16[2,64,2048]{2,1,0:T(8,128)(2,1)S(1)}, bf16[2,64,2048]{2,1,0:T(8,128)(2,1)}, u32[]{:S(2)}) copy-start(bf16[2,64,2048]{2,1,0:T(8,128)(2,1)} %refs_2_.1) | copy-start | bytes 1572868
  33.5 4.1 %collective-permute-start.7 = (bf16[4,2,64,512]{3,2,1,0:T(8,128)(2,1)S(1)}, bf16[4,2,64,512]{3,2,1,0:T(8,128)(2,1)S(1)}, u32[]{:S(2)}, u32[]{:S(2)}) collective-permute-start(bf16[4,2,64,512]{3,2,1,0:T(8,128)(2,1)S(1)} %get-tuple-element.40), channel_id=1, source_target_pairs={{0,1},{1,0},{2,3},{3,2},{4,5},{5,4},{6,7},{7,6},{8,9},{9,8},{10,11... | collective-permute-start | bytes 1572872 | tf_op jit(solution)/shard_map/ppermute | solution.py:392
  34.0 4.8 %collective-permute-start.11 = (bf16[64,768]{1,0:T(8,128)(2,1)S(1)}, bf16[64,768]{1,0:T(8,128)(2,1)S(1)}, u32[]{:S(2)}, u32[]{:S(2)}) collective-permute-start(bf16[64,768]{1,0:T(8,128)(2,1)S(1)} %get-tuple-element.34.refs_11_.refs_0_), channel_id=1, source_target_pairs={{0,8},{8,0},{16,24},{24,16},{1,9},{9,1},{17,25},{25,17},{2,10},{10... | collective-permute-start | bytes 294920 | tf_op jit(solution)/shard_map/ppermute | solution.py:386
  35.5 5.7 %collective-permute-start.12 = (bf16[64,768]{1,0:T(8,128)(2,1)S(1)}, bf16[64,768]{1,0:T(8,128)(2,1)S(1)}, u32[]{:S(2)}, u32[]{:S(2)}) collective-permute-start(bf16[64,768]{1,0:T(8,128)(2,1)S(1)} %get-tuple-element.34.refs_11_.refs_0_), channel_id=1, source_target_pairs={{0,16},{8,24},{16,0},{24,8},{1,17},{9,25},{17,1},{25,9},{2,18},{10... | collective-permute-start | bytes 294920 | tf_op jit(solution)/shard_map/ppermute | solution.py:386
  37.0 5.5 %collective-permute-start.13 = (bf16[64,768]{1,0:T(8,128)(2,1)S(1)}, bf16[64,768]{1,0:T(8,128)(2,1)S(1)}, u32[]{:S(2)}, u32[]{:S(2)}) collective-permute-start(bf16[64,768]{1,0:T(8,128)(2,1)S(1)} %get-tuple-element.34.refs_11_.refs_0_), channel_id=1, source_target_pairs={{0,24},{8,16},{16,8},{24,0},{1,25},{9,17},{17,9},{25,1},{2,26},{10... | collective-permute-start | bytes 294920 | tf_op jit(solution)/shard_map/ppermute | solution.py:386
  43.9 25.7 %all-to-all-start.1 = ((bf16[32,16,128]{2,1,0:T(8,128)(2,1)}), bf16[32,16,128]{2,1,0:T(8,128)(2,1)S(1)}, u32[]{:S(2)}, u32[]{:S(2)}) async-start(bf16[32,16,128]{2,1,0:T(8,128)(2,1)} %bitcast.4), calls=%async_computation.1 | async-start | bytes 262144 | tf_op jit(solution)/shard_map/all_to_all | solution.py:420
  51.1 8.5 %collective-permute-start.8 = (bf16[2,64,512]{2,1,0:T(8,128)(2,1)S(1)}, bf16[2,64,512]{2,1,0:T(8,128)(2,1)S(1)}, u32[]{:S(2)}, u32[]{:S(2)}) collective-permute-start(bf16[2,64,512]{2,1,0:T(8,128)(2,1)S(1)} %get-tuple-element.42), channel_id=1, source_target_pairs={{2,0},{3,1},{4,2},{5,3},{6,4},{7,5},{10,8},{11,9},{12,10},{13,11},... | collective-permute-start | bytes 393224 | tf_op jit(solution)/shard_map/ppermute | solution.py:403
  52.4 16.5 %collective-permute-start.9 = (bf16[2,64,512]{2,1,0:T(8,128)(2,1)S(1)}, bf16[2,64,512]{2,1,0:T(8,128)(2,1)S(1)}, u32[]{:S(2)}, u32[]{:S(2)}) collective-permute-start(bf16[2,64,512]{2,1,0:T(8,128)(2,1)S(1)} %get-tuple-element.43), channel_id=1, source_target_pairs={{4,0},{5,1},{6,2},{7,3},{12,8},{13,9},{14,10},{15,11},{20,16},{21,... | collective-permute-start | bytes 393224 | tf_op jit(solution)/shard_map/ppermute | solution.py:403
  53.7 15.2 %collective-permute-start.10 = (bf16[2,64,512]{2,1,0:T(8,128)(2,1)S(1)}, bf16[2,64,512]{2,1,0:T(8,128)(2,1)S(1)}, u32[]{:S(2)}, u32[]{:S(2)}) collective-permute-start(bf16[2,64,512]{2,1,0:T(8,128)(2,1)S(1)} %get-tuple-element.44), channel_id=1, source_target_pairs={{6,0},{7,1},{14,8},{15,9},{22,16},{23,17},{30,24},{31,25}} | collective-permute-start | bytes 393224 | tf_op jit(solution)/shard_map/ppermute | solution.py:403

commit v4 on v3

--- a/solution.py
+++ b/solution.py
@@ -22,6 +22,16 @@
 
 def dot(a, b, ca=1, cb=0):
     return lax.dot_general(a, b, (((ca,), (cb,)), ((), ())), preferred_element_type=F32)
+
+
+def div(x, size):
+    assert size & (size - 1) == 0
+    return x >> (size.bit_length() - 1)
+
+
+def mod(x, size):
+    assert size & (size - 1) == 0
+    return x & (size - 1)
 
 
 def iota(shape, dim):
@@ -76,10 +86,10 @@
 
     shape = (1, 2 * side)
     col = iota(shape, 1)
-    half, back, inner = col // side, (col % side) // length, col % length
+    half, back, inner = div(col, side), div(mod(col, side), length), mod(col, length)
     block = 2 * (chip - back) + jnp.where(half == 0, core, 1 - core)
     key_pos = jnp.where(back <= chip, block * length + inner, 2 * side)
-    query_pos = position * length + (iota((HEADS * length, 1), 0) % length)
+    query_pos = position * length + mod(iota((HEADS * length, 1), 0), length)
 
     def stacked(ref, s):
         return jnp.concatenate(
@@ -156,7 +166,7 @@
 
 
 def close_kernel(*refs):
-    parts, (key_ref, value_ref) = refs[:-2], refs[-2:]
+    parts, (key_ref, value_ref) = refs[:-3], refs[-2:]
     total = parts[0][...].astype(F32)
     for part in parts[1:]:
         total = total + part[...].astype(F32)
@@ -191,12 +201,13 @@
     total = experts * rows
     shape = (total, tokens)
     row = iota(shape, 0)
-    inner = row % rows
-    hit = slot == (row // rows) * CAP + (inner // pieces) % CAP
+    inner = mod(row, rows)
+    hit = slot == div(row, rows) * CAP + mod(div(inner, pieces), CAP)
+    hit = jnp.where(hit, mod(inner, pieces) + pieces * div(inner, CAP * pieces), -1)
     acc = None
     for a, (ref, value) in enumerate(((input_ref, 1.0), (grad_ref, weight))):
         for l in range(pieces):
-            pick = hit & (inner // (CAP * pieces) == a) & (inner % pieces == l)
+            pick = hit == a * pieces + l
             source = jnp.concatenate(
                 [
                     ref[:, g * share + l * LANES : g * share + (l + 1) * LANES]
@@ -218,9 +229,9 @@
     block = min(sources, 32)
     shape = (block * CAP, block * rows)
     out_row, in_row = iota(shape, 0), iota(shape, 1)
-    base = (out_row // CAP) * rows + (out_row % CAP) * pieces
+    offset = in_row - div(out_row, CAP) * rows - mod(out_row, CAP) * pieces
     picks = [
-        [(in_row == base + a * CAP * pieces + l).astype(BF16) for l in range(pieces)]
+        [(offset == a * CAP * pieces + l).astype(BF16) for l in range(pieces)]
         for a in range(2)
     ]
     for b in range(sources // block):
@@ -248,9 +259,10 @@
     block = min(sources, 32)
     shape = (block * rows, block * CAP)
     out_row, in_row = iota(shape, 0), iota(shape, 1)
-    same = out_row // rows == in_row // CAP
-    inner, which = out_row % rows, in_row % CAP
-    picks = [(same & (inner == which * pieces + l)).astype(BF16) for l in range(pieces)]
+    same = div(out_row, rows) == div(in_row, CAP)
+    inner, which = mod(out_row, rows), mod(in_row, CAP)
+    offset = jnp.where(same, inner - which * pieces, -1)
+    picks = [(offset == l).astype(BF16) for l in range(pieces)]
     pick_dot = (same & (inner == CAP * pieces + which)).astype(BF16)
     for b in range(sources // block):
         here = slice(b * block * CAP, (b + 1) * block * CAP)
@@ -298,12 +310,13 @@
     total = experts * rows
     shape = (total, tokens)
     row = iota(shape, 0)
-    inner = row % rows
-    expert = row // rows
-    hit = (slot == expert * CAP + inner // pieces) & (inner < CAP * pieces)
+    inner = mod(row, rows)
+    expert = div(row, rows)
+    hit = (slot == expert * CAP + div(inner, pieces)) & (inner < CAP * pieces)
+    hit = jnp.where(hit, mod(inner, pieces), -1)
     wide = jnp.concatenate([back_ref[g * total : (g + 1) * total, :] for g in range(groups)], axis=1)
     for l in range(pieces):
-        pick = (hit & (inner % pieces == l)).astype(BF16)
+        pick = (hit == l).astype(BF16)
         grad = dot(pick, wide, 0, 0).astype(BF16)
         for g in range(groups):
             input_grad_ref[:, g * share + l * LANES : g * share + (l + 1) * LANES] = grad[
@@ -350,7 +363,7 @@
         in_specs=[IN_HBM] * 2,
         out_shape=jax.ShapeDtypeStruct((seqs, length, 2 * HEAD), BF16),
         scratch_shapes=[pltpu.VMEM(key_rows.shape, BF16)] * 2 + [pltpu.SemaphoreType.DMA((2,))],
-        compiler_params=params(16),
+        compiler_params=params(60),
         cost_estimate=cost(MIB, MIB),
         name="pack",
     )(key_rows, value_rows)
@@ -368,7 +381,7 @@
         compiler_params=params(16),
         cost_estimate=cost(2e9, 2 * MIB),
         name="dispatch",
-    )(moe_input, out_grad, routes_t, weights_t, packed)
+    )(moe_input, out_grad, routes_t, weights_t, mine[min(1, chips - 1)])
     recv = lax.all_to_all(
         send.reshape(sources, rows, LANES), axes, split_axis=0, concat_axis=0, tiled=True
     ).reshape(sources * rows, LANES)
@@ -401,14 +414,6 @@
     for d in range(1, chips):
         down = [(i, i - 2 * d) for i in range(2 * d, devices)]
         terms.append(lax.ppermute(merged[d], "expert", down))
-    key_grad, value_grad = pl.pallas_call(
-        close_kernel,
-        out_shape=[jax.ShapeDtypeStruct((seqs, length, HEAD), BF16)] * 2,
-        compiler_params=params(16),
-        cost_estimate=cost(MIB, MIB),
-        name="close",
-    )(*terms)
-
     back, hidden, gate_rows, up_rows = pl.pallas_call(
         functools.partial(middle_kernel, sources, rows),
         in_specs=[IN_VMEM] * (len(parts) + 2) + [ANYWHERE],
@@ -416,7 +421,7 @@
         compiler_params=params(16 if groups <= 4 else 60),
         cost_estimate=cost(2e9, 2 * MIB),
         name="middle",
-    )(*parts, gate_proj, up_proj, merged[0])
+    )(*parts, gate_proj, up_proj, terms[min(1, chips - 1)])
     returned = lax.all_to_all(
         back.reshape(sources, rows, LANES), axes, split_axis=0, concat_axis=0, tiled=True
     ).reshape(sources * rows, LANES)
@@ -442,6 +447,14 @@
         name="combine",
     )(returned, routes_t, weights_t)
 
+    key_grad, value_grad = pl.pallas_call(
+        close_kernel,
+        in_specs=[IN_VMEM] * chips + [ANYWHERE],
+        out_shape=[jax.ShapeDtypeStruct((seqs, length, HEAD), BF16)] * 2,
+        compiler_params=params(16),
+        cost_estimate=cost(MIB, MIB),
+        name="close",
+    )(*terms, route_grad)
     return (
         query_grad,
         key_grad,

time: 71.5 us -> 75.7 us (1.059)
  starting transfers between devices: 32.2 us -> 35 us
  waiting for transfers between devices: 21.8 us -> 23.5 us
  local copies, waits for them, and re-layouts: 4.34 us -> 2.85 us
  Pallas kernels: 11.6 us -> 13 us
    ppermute x3, waiting for transfers between devices: 12.4 us -> 6.01 us  [shards(): terms.append(lax.ppermute(merged[d], 'expert', down))]
    all_to_all x1, waiting for transfers between devices: 0.01 us -> 4.11 us  [shards(): lax.all_to_all(back.reshape(sources, rows, LANES), axes, split_axis=0, co...]
    ppermute x3, starting transfers between devices: 9.3 us -> 11.8 us  [shards(): mine.append(lax.ppermute(packed, 'expert', up))]
    ppermute x3, waiting for transfers between devices: 3.73 us -> 6.12 us  [shards(): mine.append(lax.ppermute(packed, 'expert', up))]
    ppermute x1, waiting for transfers between devices: 0.01 us -> 1.54 us  [shards(): arrived = lax.ppermute(other_part, 'expert', swap)]
    unnamed x24, local copies, waits for them, and re-layouts: 4.34 us -> 2.85 us
    pallas_call x1, Pallas kernels: 0.18 us -> 1.56 us  [shards(): pl.pallas_call(pack_kernel, in_specs=[IN_HBM] * 2, out_shape=jax.ShapeDty...]
    all_to_all x1, starting transfers between devices: 7.13 us -> 7.97 us  [shards(): lax.all_to_all(back.reshape(sources, rows, LANES), axes, split_axis=0, co...]
  transfers between devices with their start and end apart: 16 -> 16, of which waited for: 8 -> 11; matrix products, arithmetic and copies ran while one was open for 0% -> 0% of each run, Pallas kernels for 4% -> 4%
where the time goes in v4:
time: 75.7 us; the launch traced here: 75.2 us
  starting transfers between devices  35 us (46%)
  waiting for transfers between devices  23.5 us (31%)
  Pallas kernels  13 us (17%)
  local copies, waits for them, and re-layouts  2.85 us (4%)
  between operations  0.84 us (1%)
    ppermute x3, starting transfers between devices, shards(): mine.append(lax.ppermute(packed, 'expert', up))  11.8 us
    all_to_all x1, starting transfers between devices, shards(): lax.all_to_all(back.reshape(sources, rows, LANES), axes, split_axis=0, co...  7.97 us
    all_to_all x1, starting transfers between devices, shards(): lax.all_to_all(send.reshape(sources, rows, LANES), axes, split_axis=0, co...  6.65 us
    ppermute x3, waiting for transfers between devices, shards(): mine.append(lax.ppermute(packed, 'expert', up))  6.12 us
    ppermute x3, waiting for transfers between devices, shards(): terms.append(lax.ppermute(merged[d], 'expert', down))  6.01 us
    ppermute x3, waiting for transfers between devices, shards(): lax.ppermute(sent, 'dp', [(g, g ^ k) for g in range(groups)])  4.99 us
    pallas_call x1, Pallas kernels, attention(): pl.pallas_call(functools.partial(attention_kernel, chips), in_specs=[IN_H...  4.77 us
    all_to_all x1, waiting for transfers between devices, shards(): lax.all_to_all(back.reshape(sources, rows, LANES), axes, split_axis=0, co...  4.11 us
  transfers between devices with their start and end apart: 16, of which 11 were waited for; matrix products, arithmetic and copies ran while one was open for 0% of the time, Pallas kernels for 4%

profile of v4, /device:TPU:0, one launch (start us, length us, event | category | flops | bytes accessed | tf_op | source)
XLA Modules:
  0.0 75.2 jit_solution(13225785232679706493)
XLA Ops:
  0.7 1.6 %pack.1.refs_3_ = bf16[2,64,512]{2,1,0:T(8,128)(2,1)} custom-call(bf16[2,64,256]{2,1,0:T(8,128)(2,1)} %key_hbm.1, bf16[2,64,256]{2,1,0:T(8,128)(2,1)} %value_hbm.1), custom_call_target="tpu_custom_call" | custom-call | flops 1048576 | bytes 1048576 | tf_op jit(solution)/shard_map/pack/pallas_call | solution.py:361
  2.2 4.9 %collective-permute-start = (bf16[2,64,512]{2,1,0:T(8,128)(2,1)}, bf16[2,64,512]{2,1,0:T(8,128)(2,1)S(1)}, u32[]{:S(2)}, u32[]{:S(2)}) collective-permute-start(bf16[2,64,512]{2,1,0:T(8,128)(2,1)} %pack.1.refs_3_), channel_id=1, source_target_pairs={{0,2},{1,3},{2,4},{3,5},{4,6},{5,7},{8,10},{9,11},{10,12},{11,13},... | collective-permute-start | bytes 393224 | tf_op jit(solution)/shard_map/ppermute | solution.py:373
  7.2 3.0 %collective-permute-done.after_ref.refs_4_ = bf16[2,64,512]{2,1,0:T(8,128)(2,1)S(1)} collective-permute-done((bf16[2,64,512]{2,1,0:T(8,128)(2,1)}, bf16[2,64,512]{2,1,0:T(8,128)(2,1)S(1)}, u32[]{:S(2)}, u32[]{:S(2)}) %collective-permute-start) | collective-permute-done | bytes 131104 | tf_op jit(solution)/shard_map/ppermute | solution.py:373
  10.2 1.0 %copy-done.2 = bf16[128,2048]{1,0:T(8,128)(2,1)S(1)} copy-done((bf16[128,2048]{1,0:T(8,128)(2,1)S(1)}, bf16[128,2048]{1,0:T(8,128)(2,1)}, u32[]{:S(2)}) %copy-start.2) | copy-done | bytes 524312
  11.3 1.0 %copy-done.3 = bf16[128,2048]{1,0:T(8,128)(2,1)S(1)} copy-done((bf16[128,2048]{1,0:T(8,128)(2,1)S(1)}, bf16[128,2048]{1,0:T(8,128)(2,1)}, u32[]{:S(2)}) %copy-start.3) | copy-done | bytes 524312
  12.3 1.2 %dispatch.1 = bf16[512,128]{1,0:T(8,128)(2,1)} custom-call(bf16[128,2048]{1,0:T(8,128)(2,1)S(1)} %copy-done.2, bf16[128,2048]{1,0:T(8,128)(2,1)S(1)} %copy-done.3, s32[10,128]{1,0:T(8,128)S(1)} %bitcast.10, bf16[10,128]{1,0:T(8,128)(2,1)S(1)} %bitcast.12, bf16[2,64,512]{2,1,0:T(8,128)(2,1)S(1)} %collective-permute-done.after_ref.refs_4_), custom_call_target="tpu_custom_call" | custom-call | flops 2000000000 | bytes 2097152 | tf_op jit(solution)/shard_map/dispatch/pallas_call | solution.py:377
  13.6 6.6 %all-to-all-start = ((bf16[32,16,128]{2,1,0:T(8,128)(2,1)}), bf16[32,16,128]{2,1,0:T(8,128)(2,1)S(1)}, u32[]{:S(2)}, u32[]{:S(2)}) async-start(bf16[32,16,128]{2,1,0:T(8,128)(2,1)} %bitcast.2), calls=%async_computation | async-start | bytes 262144 | tf_op jit(solution)/shard_map/all_to_all | solution.py:385
  20.2 4.6 %collective-permute-start.1 = (bf16[2,64,512]{2,1,0:T(8,128)(2,1)S(1)}, bf16[2,64,512]{2,1,0:T(8,128)(2,1)S(1)}, u32[]{:S(2)}, u32[]{:S(2)}) collective-permute-start(bf16[2,64,512]{2,1,0:T(8,128)(2,1)S(1)} %copy-done), channel_id=1, source_target_pairs={{0,4},{1,5},{2,6},{3,7},{8,12},{9,13},{10,14},{11,15},{16,20},{17,... | collective-permute-start | bytes 393224 | tf_op jit(solution)/shard_map/ppermute | solution.py:373
  24.8 2.2 %collective-permute-start.2 = (bf16[2,64,512]{2,1,0:T(8,128)(2,1)S(1)}, bf16[2,64,512]{2,1,0:T(8,128)(2,1)S(1)}, u32[]{:S(2)}, u32[]{:S(2)}) collective-permute-start(bf16[2,64,512]{2,1,0:T(8,128)(2,1)S(1)} %copy-done), channel_id=1, source_target_pairs={{0,6},{1,7},{8,14},{9,15},{16,22},{17,23},{24,30},{25,31}} | collective-permute-start | bytes 393224 | tf_op jit(solution)/shard_map/ppermute | solution.py:373
  27.1 0.1 collective-permute-start.3
  27.1 0.5 collective-permute-start.4
  27.6 0.8 %collective-permute-done.1.refs_5_ = bf16[2,64,512]{2,1,0:T(8,128)(2,1)S(1)} collective-permute-done((bf16[2,64,512]{2,1,0:T(8,128)(2,1)S(1)}, bf16[2,64,512]{2,1,0:T(8,128)(2,1)S(1)}, u32[]{:S(2)}, u32[]{:S(2)}) %collective-permute-start.1) | collective-permute-done | bytes 131104 | tf_op jit(solution)/shard_map/ppermute | solution.py:373
  28.4 0.0 collective-permute-start.5
  28.5 2.3 %collective-permute-done.2.refs_6_ = bf16[2,64,512]{2,1,0:T(8,128)(2,1)S(1)} collective-permute-done((bf16[2,64,512]{2,1,0:T(8,128)(2,1)S(1)}, bf16[2,64,512]{2,1,0:T(8,128)(2,1)S(1)}, u32[]{:S(2)}, u32[]{:S(2)}) %collective-permute-start.2) | collective-permute-done | bytes 131104 | tf_op jit(solution)/shard_map/ppermute | solution.py:373
  30.7 0.0 collective-permute-start.6
  30.7 0.0 all-to-all-done
  30.7 0.0 copy-start.4
  30.8 0.0 copy-start.5
  30.8 0.0 copy-start.6
  30.8 0.5 enter.1
  31.2 0.0 collective-permute-done.3.refs_7_
  31.3 0.0 collective-permute-done.4.refs_8_
  31.3 0.0 collective-permute-done.5.refs_9_
  31.3 0.8 %collective-permute-done.6.refs_10_ = bf16[2,64,512]{2,1,0:T(8,128)(2,1)S(1)} collective-permute-done((bf16[2,64,512]{2,1,0:T(8,128)(2,1)S(1)}, bf16[2,64,512]{2,1,0:T(8,128)(2,1)S(1)}, u32[]{:S(2)}, u32[]{:S(2)}) %collective-permute-start.6) | collective-permute-done | bytes 131104 | tf_op jit(solution)/shard_map/ppermute | solution.py:374
  32.1 0.0 copy-done.6
  32.1 4.8 %attention.1 = (bf16[2,64,2048]{2,1,0:T(8,128)(2,1)}, bf16[2,64,2048]{2,1,0:T(8,128)(2,1)}, bf16[4,2,64,512]{3,2,1,0:T(8,128)(2,1)S(1)}, bf16[2,64,512]{2,1,0:T(...) custom-call(bf16[2,64,2048]{2,1,0:T(8,128)(2,1)S(1)} %copy-done.4, ...), custom_call_target="tpu_custom_call" | custom-call | flops 6442450944 | bytes 8388608 | tf_op jit(solution)/shard_map/attention/pallas_call | solution.py:148
  36.9 0.6 collective-permute-start.7
  37.4 1.5 %collective-permute-done.7.refs_4_ = bf16[4,2,64,512]{3,2,1,0:T(8,128)(2,1)S(1)} collective-permute-done((bf16[4,2,64,512]{3,2,1,0:T(8,128)(2,1)S(1)}, bf16[4,2,64,512]{3,2,1,0:T(8,128)(2,1)S(1)}, u32[]{:S(2)}, u32[]{:S(2)}) %collective-permute-start.7) | collective-permute-done | bytes 524320 | tf_op jit(solution)/shard_map/ppermute | solution.py:405
  39.0 0.1 merge.1
  39.1 1.3 %collective-permute-start.8 = (bf16[2,64,512]{2,1,0:T(8,128)(2,1)S(1)}, bf16[2,64,512]{2,1,0:T(8,128)(2,1)S(1)}, u32[]{:S(2)}, u32[]{:S(2)}) collective-permute-start(bf16[2,64,512]{2,1,0:T(8,128)(2,1)S(1)} %get-tuple-element.42), channel_id=1, source_target_pairs={{2,0},{3,1},{4,2},{5,3},{6,4},{7,5},{10,8},{11,9},{12,10},{13,11},... | collective-permute-start | bytes 393224 | tf_op jit(solution)/shard_map/ppermute | solution.py:416
  40.4 1.5 %collective-permute-start.11 = (bf16[64,768]{1,0:T(8,128)(2,1)S(1)}, bf16[64,768]{1,0:T(8,128)(2,1)S(1)}, u32[]{:S(2)}, u32[]{:S(2)}) collective-permute-start(bf16[64,768]{1,0:T(8,128)(2,1)S(1)} %get-tuple-element.34.refs_11_.refs_0_), channel_id=1, source_target_pairs={{0,8},{8,0},{16,24},{24,16},{1,9},{9,1},{17,25},{25,17},{2,10},{10... | collective-permute-start | bytes 294920 | tf_op jit(solution)/shard_map/ppermute | solution.py:399
  41.9 1.5 %collective-permute-start.12 = (bf16[64,768]{1,0:T(8,128)(2,1)S(1)}, bf16[64,768]{1,0:T(8,128)(2,1)S(1)}, u32[]{:S(2)}, u32[]{:S(2)}) collective-permute-start(bf16[64,768]{1,0:T(8,128)(2,1)S(1)} %get-tuple-element.34.refs_11_.refs_0_), channel_id=1, source_target_pairs={{0,16},{8,24},{16,0},{24,8},{1,17},{9,25},{17,1},{25,9},{2,18},{10... | collective-permute-start | bytes 294920 | tf_op jit(solution)/shard_map/ppermute | solution.py:399
  43.4 0.5 collective-permute-start.13
  44.0 1.6 %collective-permute-done.11.refs_1_ = bf16[64,768]{1,0:T(8,128)(2,1)S(1)} collective-permute-done((bf16[64,768]{1,0:T(8,128)(2,1)S(1)}, bf16[64,768]{1,0:T(8,128)(2,1)S(1)}, u32[]{:S(2)}, u32[]{:S(2)}) %collective-permute-start.11) | collective-permute-done | bytes 98336 | tf_op jit(solution)/shard_map/ppermute | solution.py:399
  45.5 2.3 %collective-permute-done.12.refs_2_ = bf16[64,768]{1,0:T(8,128)(2,1)S(1)} collective-permute-done((bf16[64,768]{1,0:T(8,128)(2,1)S(1)}, bf16[64,768]{1,0:T(8,128)(2,1)S(1)}, u32[]{:S(2)}, u32[]{:S(2)}) %collective-permute-start.12) | collective-permute-done | bytes 98336 | tf_op jit(solution)/shard_map/ppermute | solution.py:399
  47.8 1.1 %collective-permute-done.13.refs_3_ = bf16[64,768]{1,0:T(8,128)(2,1)S(1)} collective-permute-done((bf16[64,768]{1,0:T(8,128)(2,1)S(1)}, bf16[64,768]{1,0:T(8,128)(2,1)S(1)}, u32[]{:S(2)}, u32[]{:S(2)}) %collective-permute-start.13) | collective-permute-done | bytes 98336 | tf_op jit(solution)/shard_map/ppermute | solution.py:399
  49.0 0.5 collective-permute-done.8.refs_6_.refs_1_
  49.4 1.4 %middle.1 = (bf16[512,128]{1,0:T(8,128)(2,1)}, bf16[64,256]{1,0:T(8,128)(2,1)S(1)}, bf16[64,256]{1,0:T(8,128)(2,1)S(1)}, bf16[64,256]{1,0:T(8,128)(2,1)S(1)}) custom-call(bf16[64,768]{1,0:T(8,128)(2,1)S(1)} %get-tuple-element.34.refs_11_.refs_0_, bf16[64,768]{1,0:T(8,128)(2,1)S(1)} %collective-permute-done.11.refs_1_, ...), custom_call_target="tpu_custom_call" | custom-call | flops 2000000000 | bytes 2097152 | tf_op jit(solution)/shard_map/middle/pallas_call | solution.py:417
  50.8 8.0 %all-to-all-start.1 = ((bf16[32,16,128]{2,1,0:T(8,128)(2,1)}), bf16[32,16,128]{2,1,0:T(8,128)(2,1)S(1)}, u32[]{:S(2)}, u32[]{:S(2)}) async-start(bf16[32,16,128]{2,1,0:T(8,128)(2,1)} %bitcast.4), calls=%async_computation.1 | async-start | bytes 262144 | tf_op jit(solution)/shard_map/all_to_all | solution.py:425
  58.8 1.3 %collective-permute-start.9 = (bf16[2,64,512]{2,1,0:T(8,128)(2,1)S(1)}, bf16[2,64,512]{2,1,0:T(8,128)(2,1)S(1)}, u32[]{:S(2)}, u32[]{:S(2)}) collective-permute-start(bf16[2,64,512]{2,1,0:T(8,128)(2,1)S(1)} %get-tuple-element.43), channel_id=1, source_target_pairs={{4,0},{5,1},{6,2},{7,3},{12,8},{13,9},{14,10},{15,11},{20,16},{21,... | collective-permute-start | bytes 393224 | tf_op jit(solution)/shard_map/ppermute | solution.py:416
  60.1 1.3 %collective-permute-start.10 = (bf16[2,64,512]{2,1,0:T(8,128)(2,1)S(1)}, bf16[2,64,512]{2,1,0:T(8,128)(2,1)S(1)}, u32[]{:S(2)}, u32[]{:S(2)}) collective-permute-start(bf16[2,64,512]{2,1,0:T(8,128)(2,1)S(1)} %get-tuple-element.44), channel_id=1, source_target_pairs={{6,0},{7,1},{14,8},{15,9},{22,16},{23,17},{30,24},{31,25}} | collective-permute-start | bytes 393224 | tf_op jit(solution)/shard_map/ppermute | solution.py:416
  61.4 1.5 %weight_grads.1 = (f32[1,512,256]{2,1,0:T(8,128)}, f32[1,512,256]{2,1,0:T(8,128)}, f32[1,256,512]{2,1,0:T(8,128)}) custom-call(bf16[64,512]{1,0:T(8,128)(2,1)S(1)} %get-tuple-element.51.input_ref, bf16[64,512]{1,0:T(8,128)(2,1)S(1)} %get-tuple-element.52.grad_ref, bf16[64,256]{1,0:T(8,128)(2,1)S(1)} %get-tuple-element.53.hidden_ref, ...), custom_call_target="tpu_custom_call" | custom-call | flops 2000000000 | bytes 2097152 | tf_op jit(solution)/shard_map/weight_grads/pallas_call | solution.py:428
  62.9 4.1 %all-to-all-done.1 = bf16[32,16,128]{2,1,0:T(8,128)(2,1)S(1)} async-done(((bf16[32,16,128]{2,1,0:T(8,128)(2,1)}), bf16[32,16,128]{2,1,0:T(8,128)(2,1)S(1)}, u32[]{:S(2)}, u32[]{:S(2)}) %all-to-all-start.1) | async-done | bytes 131104 | tf_op jit(solution)/shard_map/all_to_all | solution.py:425
  67.0 1.3 %combine.1 = (bf16[128,2048]{1,0:T(8,128)(2,1)}, bf16[10,128]{1,0:T(8,128)(2,1)}) custom-call(bf16[512,128]{1,0:T(8,128)(2,1)S(1)} %bitcast.8, s32[10,128]{1,0:T(8,128)S(1)} %bitcast.11, bf16[10,128]{1,0:T(8,128)(2,1)S(1)} %bitcast.13), custom_call_target="tpu_custom_call" | custom-call | flops 2000000000 | bytes 2097152 | tf_op jit(solution)/shard_map/combine/pallas_call | solution.py:439
  68.3 5.5 %collective-permute-done.9.refs_2_ = bf16[2,64,512]{2,1,0:T(8,128)(2,1)S(1)} collective-permute-done((bf16[2,64,512]{2,1,0:T(8,128)(2,1)S(1)}, bf16[2,64,512]{2,1,0:T(8,128)(2,1)S(1)}, u32[]{:S(2)}, u32[]{:S(2)}) %collective-permute-start.9) | collective-permute-done | bytes 131104 | tf_op jit(solution)/shard_map/ppermute | solution.py:416
  73.8 0.0 collective-permute-done.10.refs_3_
  73.8 0.7 copy-done.1
  74.5 0.7 close.1
  (17 shorter events, 0.0 us)
Async XLA Ops:
  0.6 9.6 %copy-start.10 = (s32[128,10]{0,1:T(8,128)S(1)}, s32[128,10]{0,1:T(8,128)}, u32[]{:S(2)}) copy-start(s32[128,10]{0,1:T(8,128)} %param.19) | copy-start | bytes 15364
  0.7 9.6 %copy-start.11 = (bf16[128,10]{0,1:T(8,128)(2,1)S(1)}, bf16[128,10]{0,1:T(8,128)(2,1)}, u32[]{:S(2)}) copy-start(bf16[128,10]{0,1:T(8,128)(2,1)} %param.20) | copy-start | bytes 7684
  2.2 8.0 %collective-permute-start = (bf16[2,64,512]{2,1,0:T(8,128)(2,1)}, bf16[2,64,512]{2,1,0:T(8,128)(2,1)S(1)}, u32[]{:S(2)}, u32[]{:S(2)}) collective-permute-start(bf16[2,64,512]{2,1,0:T(8,128)(2,1)} %pack.1.refs_3_), channel_id=1, source_target_pairs={{0,2},{1,3},{2,4},{3,5},{4,6},{5,7},{8,10},{9,11},{10,12},{11,13},... | collective-permute-start | bytes 393224 | tf_op jit(solution)/shard_map/ppermute | solution.py:373
  10.2 1.0 %copy-start.2 = (bf16[128,2048]{1,0:T(8,128)(2,1)S(1)}, bf16[128,2048]{1,0:T(8,128)(2,1)}, u32[]{:S(2)}) copy-start(bf16[128,2048]{1,0:T(8,128)(2,1)} %input_ref.1) | copy-start | bytes 1572868
  11.3 1.0 %copy-start.3 = (bf16[128,2048]{1,0:T(8,128)(2,1)S(1)}, bf16[128,2048]{1,0:T(8,128)(2,1)}, u32[]{:S(2)}) copy-start(bf16[128,2048]{1,0:T(8,128)(2,1)} %grad_ref.1) | copy-start | bytes 1572868
  12.3 18.4 %copy-start.7 = (bf16[1,256,512]{2,1,0:T(8,128)(2,1)S(1)}, bf16[1,256,512]{2,1,0:T(8,128)(2,1)}, u32[]{:S(2)}) copy-start(bf16[1,256,512]{2,1,0:T(8,128)(2,1)} %down_ref.1) | copy-start | bytes 786436
  12.3 18.4 %copy-start.8 = (bf16[1,512,256]{2,1,0:T(8,128)(2,1)S(1)}, bf16[1,512,256]{2,1,0:T(8,128)(2,1)}, u32[]{:S(2)}) copy-start(bf16[1,512,256]{2,1,0:T(8,128)(2,1)} %refs_4_.1) | copy-start | bytes 786436
  12.3 18.4 %copy-start.9 = (bf16[1,512,256]{2,1,0:T(8,128)(2,1)S(1)}, bf16[1,512,256]{2,1,0:T(8,128)(2,1)}, u32[]{:S(2)}) copy-start(bf16[1,512,256]{2,1,0:T(8,128)(2,1)} %refs_5_.1) | copy-start | bytes 786436
  13.5 6.7 %copy-start = (bf16[2,64,512]{2,1,0:T(8,128)(2,1)S(1)}, bf16[2,64,512]{2,1,0:T(8,128)(2,1)}, u32[]{:S(2)}) copy-start(bf16[2,64,512]{2,1,0:T(8,128)(2,1)} %pack.1.refs_3_) | copy-start | bytes 393220
  13.6 17.2 %all-to-all-start = ((bf16[32,16,128]{2,1,0:T(8,128)(2,1)}), bf16[32,16,128]{2,1,0:T(8,128)(2,1)S(1)}, u32[]{:S(2)}, u32[]{:S(2)}) async-start(bf16[32,16,128]{2,1,0:T(8,128)(2,1)} %bitcast.2), calls=%async_computation | async-start | bytes 262144 | tf_op jit(solution)/shard_map/all_to_all | solution.py:385
  20.2 8.2 %collective-permute-start.1 = (bf16[2,64,512]{2,1,0:T(8,128)(2,1)S(1)}, bf16[2,64,512]{2,1,0:T(8,128)(2,1)S(1)}, u32[]{:S(2)}, u32[]{:S(2)}) collective-permute-start(bf16[2,64,512]{2,1,0:T(8,128)(2,1)S(1)} %copy-done), channel_id=1, source_target_pairs={{0,4},{1,5},{2,6},{3,7},{8,12},{9,13},{10,14},{11,15},{16,20},{17,... | collective-permute-start | bytes 393224 | tf_op jit(solution)/shard_map/ppermute | solution.py:373
  24.8 5.9 %collective-permute-start.2 = (bf16[2,64,512]{2,1,0:T(8,128)(2,1)S(1)}, bf16[2,64,512]{2,1,0:T(8,128)(2,1)S(1)}, u32[]{:S(2)}, u32[]{:S(2)}) collective-permute-start(bf16[2,64,512]{2,1,0:T(8,128)(2,1)S(1)} %copy-done), channel_id=1, source_target_pairs={{0,6},{1,7},{8,14},{9,15},{16,22},{17,23},{24,30},{25,31}} | collective-permute-start | bytes 393224 | tf_op jit(solution)/shard_map/ppermute | solution.py:373
  27.1 4.2 %collective-permute-start.3 = (bf16[2,64,512]{2,1,0:T(8,128)(2,1)S(1)}, bf16[2,64,512]{2,1,0:T(8,128)(2,1)S(1)}, u32[]{:S(2)}, u32[]{:S(2)}) collective-permute-start(bf16[2,64,512]{2,1,0:T(8,128)(2,1)S(1)} %copy-done), channel_id=1, source_target_pairs={{0,1},{1,0},{2,3},{3,2},{4,5},{5,4},{6,7},{7,6},{8,9},{9,8},{10,11... | collective-permute-start | bytes 393224 | tf_op jit(solution)/shard_map/ppermute | solution.py:374
  27.1 4.1 %collective-permute-start.4 = (bf16[2,64,512]{2,1,0:T(8,128)(2,1)S(1)}, bf16[2,64,512]{2,1,0:T(8,128)(2,1)S(1)}, u32[]{:S(2)}, u32[]{:S(2)}) collective-permute-start(bf16[2,64,512]{2,1,0:T(8,128)(2,1)S(1)} %collective-permute-done.after_ref.refs_4_), channel_id=1, source_target_pairs={{0,1},{1,0},{2,3},{3,2},{4,5},{5,4},{6,7},{7,6},{8,9},{9,8},{10,11... | collective-permute-start | bytes 393224 | tf_op jit(solution)/shard_map/ppermute | solution.py:374
  28.4 2.8 %collective-permute-start.5 = (bf16[2,64,512]{2,1,0:T(8,128)(2,1)S(1)}, bf16[2,64,512]{2,1,0:T(8,128)(2,1)S(1)}, u32[]{:S(2)}, u32[]{:S(2)}) collective-permute-start(bf16[2,64,512]{2,1,0:T(8,128)(2,1)S(1)} %collective-permute-done.1.refs_5_), channel_id=1, source_target_pairs={{0,1},{1,0},{2,3},{3,2},{4,5},{5,4},{6,7},{7,6},{8,9},{9,8},{10,11... | collective-permute-start | bytes 393224 | tf_op jit(solution)/shard_map/ppermute | solution.py:374
  30.7 1.3 %collective-permute-start.6 = (bf16[2,64,512]{2,1,0:T(8,128)(2,1)S(1)}, bf16[2,64,512]{2,1,0:T(8,128)(2,1)S(1)}, u32[]{:S(2)}, u32[]{:S(2)}) collective-permute-start(bf16[2,64,512]{2,1,0:T(8,128)(2,1)S(1)} %collective-permute-done.2.refs_6_), channel_id=1, source_target_pairs={{0,1},{1,0},{2,3},{3,2},{4,5},{5,4},{6,7},{7,6},{8,9},{9,8},{10,11... | collective-permute-start | bytes 393224 | tf_op jit(solution)/shard_map/ppermute | solution.py:374
  30.7 1.3 %copy-start.4 = (bf16[2,64,2048]{2,1,0:T(8,128)(2,1)S(1)}, bf16[2,64,2048]{2,1,0:T(8,128)(2,1)}, u32[]{:S(2)}) copy-start(bf16[2,64,2048]{2,1,0:T(8,128)(2,1)} %refs_0_.1) | copy-start | bytes 1572868
  30.8 1.3 %copy-start.5 = (bf16[2,64,2048]{2,1,0:T(8,128)(2,1)S(1)}, bf16[2,64,2048]{2,1,0:T(8,128)(2,1)}, u32[]{:S(2)}) copy-start(bf16[2,64,2048]{2,1,0:T(8,128)(2,1)} %refs_1_.1) | copy-start | bytes 1572868
  30.8 1.3 %copy-start.6 = (bf16[2,64,2048]{2,1,0:T(8,128)(2,1)S(1)}, bf16[2,64,2048]{2,1,0:T(8,128)(2,1)}, u32[]{:S(2)}) copy-start(bf16[2,64,2048]{2,1,0:T(8,128)(2,1)} %refs_2_.1) | copy-start | bytes 1572868
  36.9 2.1 %collective-permute-start.7 = (bf16[4,2,64,512]{3,2,1,0:T(8,128)(2,1)S(1)}, bf16[4,2,64,512]{3,2,1,0:T(8,128)(2,1)S(1)}, u32[]{:S(2)}, u32[]{:S(2)}) collective-permute-start(bf16[4,2,64,512]{3,2,1,0:T(8,128)(2,1)S(1)} %get-tuple-element.40), channel_id=1, source_target_pairs={{0,1},{1,0},{2,3},{3,2},{4,5},{5,4},{6,7},{7,6},{8,9},{9,8},{10,11... | collective-permute-start | bytes 1572872 | tf_op jit(solution)/shard_map/ppermute | solution.py:405
  39.1 10.3 %collective-permute-start.8 = (bf16[2,64,512]{2,1,0:T(8,128)(2,1)S(1)}, bf16[2,64,512]{2,1,0:T(8,128)(2,1)S(1)}, u32[]{:S(2)}, u32[]{:S(2)}) collective-permute-start(bf16[2,64,512]{2,1,0:T(8,128)(2,1)S(1)} %get-tuple-element.42), channel_id=1, source_target_pairs={{2,0},{3,1},{4,2},{5,3},{6,4},{7,5},{10,8},{11,9},{12,10},{13,11},... | collective-permute-start | bytes 393224 | tf_op jit(solution)/shard_map/ppermute | solution.py:416
  40.4 5.1 %collective-permute-start.11 = (bf16[64,768]{1,0:T(8,128)(2,1)S(1)}, bf16[64,768]{1,0:T(8,128)(2,1)S(1)}, u32[]{:S(2)}, u32[]{:S(2)}) collective-permute-start(bf16[64,768]{1,0:T(8,128)(2,1)S(1)} %get-tuple-element.34.refs_11_.refs_0_), channel_id=1, source_target_pairs={{0,8},{8,0},{16,24},{24,16},{1,9},{9,1},{17,25},{25,17},{2,10},{10... | collective-permute-start | bytes 294920 | tf_op jit(solution)/shard_map/ppermute | solution.py:399
  41.9 5.9 %collective-permute-start.12 = (bf16[64,768]{1,0:T(8,128)(2,1)S(1)}, bf16[64,768]{1,0:T(8,128)(2,1)S(1)}, u32[]{:S(2)}, u32[]{:S(2)}) collective-permute-start(bf16[64,768]{1,0:T(8,128)(2,1)S(1)} %get-tuple-element.34.refs_11_.refs_0_), channel_id=1, source_target_pairs={{0,16},{8,24},{16,0},{24,8},{1,17},{9,25},{17,1},{25,9},{2,18},{10... | collective-permute-start | bytes 294920 | tf_op jit(solution)/shard_map/ppermute | solution.py:399
  43.4 5.5 %collective-permute-start.13 = (bf16[64,768]{1,0:T(8,128)(2,1)S(1)}, bf16[64,768]{1,0:T(8,128)(2,1)S(1)}, u32[]{:S(2)}, u32[]{:S(2)}) collective-permute-start(bf16[64,768]{1,0:T(8,128)(2,1)S(1)} %get-tuple-element.34.refs_11_.refs_0_), channel_id=1, source_target_pairs={{0,24},{8,16},{16,8},{24,0},{1,25},{9,17},{17,9},{25,1},{2,26},{10... | collective-permute-start | bytes 294920 | tf_op jit(solution)/shard_map/ppermute | solution.py:399
  50.8 16.2 %all-to-all-start.1 = ((bf16[32,16,128]{2,1,0:T(8,128)(2,1)}), bf16[32,16,128]{2,1,0:T(8,128)(2,1)S(1)}, u32[]{:S(2)}, u32[]{:S(2)}) async-start(bf16[32,16,128]{2,1,0:T(8,128)(2,1)} %bitcast.4), calls=%async_computation.1 | async-start | bytes 262144 | tf_op jit(solution)/shard_map/all_to_all | solution.py:425
  58.8 15.0 %collective-permute-start.9 = (bf16[2,64,512]{2,1,0:T(8,128)(2,1)S(1)}, bf16[2,64,512]{2,1,0:T(8,128)(2,1)S(1)}, u32[]{:S(2)}, u32[]{:S(2)}) collective-permute-start(bf16[2,64,512]{2,1,0:T(8,128)(2,1)S(1)} %get-tuple-element.43), channel_id=1, source_target_pairs={{4,0},{5,1},{6,2},{7,3},{12,8},{13,9},{14,10},{15,11},{20,16},{21,... | collective-permute-start | bytes 393224 | tf_op jit(solution)/shard_map/ppermute | solution.py:416
  60.1 13.7 %collective-permute-start.10 = (bf16[2,64,512]{2,1,0:T(8,128)(2,1)S(1)}, bf16[2,64,512]{2,1,0:T(8,128)(2,1)S(1)}, u32[]{:S(2)}, u32[]{:S(2)}) collective-permute-start(bf16[2,64,512]{2,1,0:T(8,128)(2,1)S(1)} %get-tuple-element.44), channel_id=1, source_target_pairs={{6,0},{7,1},{14,8},{15,9},{22,16},{23,17},{30,24},{31,25}} | collective-permute-start | bytes 393224 | tf_op jit(solution)/shard_map/ppermute | solution.py:416
  73.8 0.7 copy-start.1

commit v5 on v4

--- a/solution.py
+++ b/solution.py
@@ -153,7 +153,7 @@
         scratch_shapes=[pltpu.VMEM(query_rows.shape, BF16)] * 5
         + [pltpu.SemaphoreType.DMA((seqs, 3)), pltpu.SemaphoreType.DMA((seqs, 2))],
         compiler_params=params(ATTENTION_MIB if chips <= 4 else 56),
-        cost_estimate=cost(flops * 4, 8 * MIB),
+        cost_estimate=cost(flops * 40, 8 * MIB),
         name="attention",
     )(query_rows, gate_logits, gated_grad, *pieces, after)
     return out[0], out[1], out[2], out[3:]
@@ -166,7 +166,7 @@
 
 
 def close_kernel(*refs):
-    parts, (key_ref, value_ref) = refs[:-3], refs[-2:]
+    parts, (key_ref, value_ref) = refs[:-2], refs[-2:]
     total = parts[0][...].astype(F32)
     for part in parts[1:]:
         total = total + part[...].astype(F32)
@@ -223,7 +223,7 @@
 
 
 def enter_kernel(
-    sources, rows, recv_ref, gate_ref, up_ref, down_ref, input_ref, grad_ref, send_ref
+    sources, rows, recv_ref, gate_ref, up_ref, down_ref, after_ref, input_ref, grad_ref, send_ref
 ):
     pieces = input_ref.shape[1] // LANES
     block = min(sources, 32)
@@ -301,7 +301,15 @@
 
 
 def combine_kernel(
-    experts, groups, rows, back_ref, routes_ref, weights_ref, input_grad_ref, route_grad_ref
+    experts,
+    groups,
+    rows,
+    back_ref,
+    routes_ref,
+    weights_ref,
+    after_ref,
+    input_grad_ref,
+    route_grad_ref,
 ):
     slot, weight, live = slots(routes_ref, weights_ref, experts)
     tokens, width = input_grad_ref.shape
@@ -381,27 +389,28 @@
         compiler_params=params(16),
         cost_estimate=cost(2e9, 2 * MIB),
         name="dispatch",
-    )(moe_input, out_grad, routes_t, weights_t, mine[min(1, chips - 1)])
+    )(moe_input, out_grad, routes_t, weights_t, packed)
     recv = lax.all_to_all(
         send.reshape(sources, rows, LANES), axes, split_axis=0, concat_axis=0, tiled=True
     ).reshape(sources * rows, LANES)
 
+    query_grad, gate_grad, other_part, mine_part = attention(
+        query_rows, gate_logits, gated_grad, mine + other, recv
+    )
     slot_rows = jax.ShapeDtypeStruct((sources * CAP, share), BF16)
     hid_rows = jax.ShapeDtypeStruct((sources * CAP, hid), BF16)
     inputs, grads, sent = pl.pallas_call(
         functools.partial(enter_kernel, sources, rows),
+        in_specs=[IN_VMEM] * 4 + [ANYWHERE],
         out_shape=[slot_rows, slot_rows, jax.ShapeDtypeStruct((sources * CAP, 3 * hid), BF16)],
         compiler_params=params(16),
         cost_estimate=cost(2e9, 2 * MIB),
         name="enter",
-    )(recv, gate_proj, up_proj, down_proj)
+    )(recv, gate_proj, up_proj, down_proj, other_part)
     parts = [sent] + [
         lax.ppermute(sent, "dp", [(g, g ^ k) for g in range(groups)]) for k in range(1, groups)
     ]
 
-    query_grad, gate_grad, other_part, mine_part = attention(
-        query_rows, gate_logits, gated_grad, mine + other, sent
-    )
     arrived = lax.ppermute(other_part, "expert", swap)
     merged = pl.pallas_call(
         functools.partial(merge_kernel, chips),
@@ -436,8 +445,17 @@
         cost_estimate=cost(2e9, 2 * MIB),
         name="weight_grads",
     )(inputs, grads, hidden, gate_rows, up_rows)
+    key_grad, value_grad = pl.pallas_call(
+        close_kernel,
+        in_specs=[IN_VMEM] * chips,
+        out_shape=[jax.ShapeDtypeStruct((seqs, length, HEAD), BF16)] * 2,
+        compiler_params=params(16),
+        cost_estimate=cost(6e10, MIB),
+        name="close",
+    )(*terms)
     input_grad, route_grad = pl.pallas_call(
         functools.partial(combine_kernel, devices, groups, rows),
+        in_specs=[IN_VMEM] * 3 + [ANYWHERE],
         out_shape=[
             jax.ShapeDtypeStruct(moe_input.shape, BF16),
             jax.ShapeDtypeStruct(routes_t.shape, BF16),
@@ -445,16 +463,8 @@
         compiler_params=params(16),
         cost_estimate=cost(2e9, 2 * MIB),
         name="combine",
-    )(returned, routes_t, weights_t)
-
-    key_grad, value_grad = pl.pallas_call(
-        close_kernel,
-        in_specs=[IN_VMEM] * chips + [ANYWHERE],
-        out_shape=[jax.ShapeDtypeStruct((seqs, length, HEAD), BF16)] * 2,
-        compiler_params=params(16),
-        cost_estimate=cost(MIB, MIB),
-        name="close",
-    )(*terms, route_grad)
+    )(returned, routes_t, weights_t, key_grad)
+
     return (
         query_grad,
         key_grad,

time: 75.7 us -> 61.4 us (0.81)
  waiting for transfers between devices: 23.5 us -> 16.1 us
  starting transfers between devices: 35 us -> 27.8 us
    all_to_all x1, waiting for transfers between devices: 0.01 us -> 6.75 us  [shards(): lax.all_to_all(send.reshape(sources, rows, LANES), axes, split_axis=0, co...]
    ppermute x3, waiting for transfers between devices: 6.12 us -> 0.01 us  [shards(): mine.append(lax.ppermute(packed, 'expert', up))]
    all_to_all x1, starting transfers between devices: 6.65 us -> 2.81 us  [shards(): lax.all_to_all(send.reshape(sources, rows, LANES), axes, split_axis=0, co...]
    ppermute x3, waiting for transfers between devices: 4.99 us -> 1.48 us  [shards(): lax.ppermute(sent, 'dp', [(g, g ^ k) for g in range(groups)])]
    all_to_all x1, starting transfers between devices: 7.97 us -> 5.27 us  [shards(): lax.all_to_all(back.reshape(sources, rows, LANES), axes, split_axis=0, co...]
    ppermute x3, waiting for transfers between devices: 6.01 us -> 3.46 us  [shards(): terms.append(lax.ppermute(merged[d], 'expert', down))]
    all_to_all x1, waiting for transfers between devices: 4.11 us -> 2.54 us  [shards(): lax.all_to_all(back.reshape(sources, rows, LANES), axes, split_axis=0, co...]
    ppermute x3, starting transfers between devices: 11.8 us -> 10.7 us  [shards(): mine.append(lax.ppermute(packed, 'expert', up))]
  transfers between devices with their start and end apart: 16 -> 16, of which waited for: 11 -> 7; matrix products, arithmetic and copies ran while one was open for 0% -> 0% of each run, Pallas kernels for 4% -> 9%
where the time goes in v5:
time: 61.4 us; the launch traced here: 60.9 us
  starting transfers between devices  27.8 us (45%)
  waiting for transfers between devices  16.1 us (26%)
  Pallas kernels  13 us (21%)
  local copies, waits for them, and re-layouts  3.04 us (5%)
  between operations  0.85 us (1%)
    ppermute x3, starting transfers between devices, shards(): mine.append(lax.ppermute(packed, 'expert', up))  10.7 us
    all_to_all x1, waiting for transfers between devices, shards(): lax.all_to_all(send.reshape(sources, rows, LANES), axes, split_axis=0, co...  6.75 us
    all_to_all x1, starting transfers between devices, shards(): lax.all_to_all(back.reshape(sources, rows, LANES), axes, split_axis=0, co...  5.27 us
    pallas_call x1, Pallas kernels, attention(): pl.pallas_call(functools.partial(attention_kernel, chips), in_specs=[IN_H...  4.78 us
    ppermute x3, starting transfers between devices, shards(): terms.append(lax.ppermute(merged[d], 'expert', down))  3.98 us
    ppermute x3, starting transfers between devices, shards(): lax.ppermute(sent, 'dp', [(g, g ^ k) for g in range(groups)])  3.55 us
    ppermute x3, waiting for transfers between devices, shards(): terms.append(lax.ppermute(merged[d], 'expert', down))  3.46 us
    unnamed x26, local copies, waits for them, and re-layouts  3.04 us
  transfers between devices with their start and end apart: 16, of which 7 were waited for; matrix products, arithmetic and copies ran while one was open for 0% of the time, Pallas kernels for 9%

profile of v5, /device:TPU:0, one launch (start us, length us, event | category | flops | bytes accessed | tf_op | source)
XLA Modules:
  0.0 60.9 jit_solution(17789381943964185118)
XLA Ops:
  0.7 1.6 %pack.1.after_ref.refs_3_ = bf16[2,64,512]{2,1,0:T(8,128)(2,1)} custom-call(bf16[2,64,256]{2,1,0:T(8,128)(2,1)} %key_hbm.1, bf16[2,64,256]{2,1,0:T(8,128)(2,1)} %value_hbm.1), custom_call_target="tpu_custom_call" | custom-call | flops 1048576 | bytes 1048576 | tf_op jit(solution)/shard_map/pack/pallas_call | solution.py:369
  2.2 4.9 %collective-permute-start = (bf16[2,64,512]{2,1,0:T(8,128)(2,1)}, bf16[2,64,512]{2,1,0:T(8,128)(2,1)S(1)}, u32[]{:S(2)}, u32[]{:S(2)}) collective-permute-start(bf16[2,64,512]{2,1,0:T(8,128)(2,1)} %pack.1.after_ref.refs_3_), channel_id=1, source_target_pairs={{0,2},{1,3},{2,4},{3,5},{4,6},{5,7},{8,10},{9,11},{10,12},{11,13},... | collective-permute-start | bytes 393224 | tf_op jit(solution)/shard_map/ppermute | solution.py:381
  7.2 4.5 %collective-permute-start.1 = (bf16[2,64,512]{2,1,0:T(8,128)(2,1)}, bf16[2,64,512]{2,1,0:T(8,128)(2,1)S(1)}, u32[]{:S(2)}, u32[]{:S(2)}) collective-permute-start(bf16[2,64,512]{2,1,0:T(8,128)(2,1)} %pack.1.after_ref.refs_3_), channel_id=1, source_target_pairs={{0,4},{1,5},{2,6},{3,7},{8,12},{9,13},{10,14},{11,15},{16,20},{17,... | collective-permute-start | bytes 393224 | tf_op jit(solution)/shard_map/ppermute | solution.py:381
  11.7 1.3 %collective-permute-start.2 = (bf16[2,64,512]{2,1,0:T(8,128)(2,1)}, bf16[2,64,512]{2,1,0:T(8,128)(2,1)S(1)}, u32[]{:S(2)}, u32[]{:S(2)}) collective-permute-start(bf16[2,64,512]{2,1,0:T(8,128)(2,1)} %pack.1.after_ref.refs_3_), channel_id=1, source_target_pairs={{0,6},{1,7},{8,14},{9,15},{16,22},{17,23},{24,30},{25,31}} | collective-permute-start | bytes 393224 | tf_op jit(solution)/shard_map/ppermute | solution.py:381
  13.0 0.0 copy-start
  13.0 0.9 %copy-done = bf16[2,64,512]{2,1,0:T(8,128)(2,1)S(1)} copy-done((bf16[2,64,512]{2,1,0:T(8,128)(2,1)S(1)}, bf16[2,64,512]{2,1,0:T(8,128)(2,1)}, u32[]{:S(2)}) %copy-start) | copy-done | bytes 131096
  13.9 1.0 %copy-done.2 = bf16[128,2048]{1,0:T(8,128)(2,1)S(1)} copy-done((bf16[128,2048]{1,0:T(8,128)(2,1)S(1)}, bf16[128,2048]{1,0:T(8,128)(2,1)}, u32[]{:S(2)}) %copy-start.2) | copy-done | bytes 524312
  15.0 1.0 %copy-done.3 = bf16[128,2048]{1,0:T(8,128)(2,1)S(1)} copy-done((bf16[128,2048]{1,0:T(8,128)(2,1)S(1)}, bf16[128,2048]{1,0:T(8,128)(2,1)}, u32[]{:S(2)}) %copy-start.3) | copy-done | bytes 524312
  16.0 1.2 %dispatch.1 = bf16[512,128]{1,0:T(8,128)(2,1)} custom-call(bf16[128,2048]{1,0:T(8,128)(2,1)S(1)} %copy-done.2, bf16[128,2048]{1,0:T(8,128)(2,1)S(1)} %copy-done.3, s32[10,128]{1,0:T(8,128)S(1)} %bitcast.10, bf16[10,128]{1,0:T(8,128)(2,1)S(1)} %bitcast.12, bf16[2,64,512]{2,1,0:T(8,128)(2,1)S(1)} %copy-done), custom_call_target="tpu_custom_call" | custom-call | flops 2000000000 | bytes 2097152 | tf_op jit(solution)/shard_map/dispatch/pallas_call | solution.py:385
  17.3 2.8 %all-to-all-start = ((bf16[32,16,128]{2,1,0:T(8,128)(2,1)}), bf16[32,16,128]{2,1,0:T(8,128)(2,1)S(1)}, u32[]{:S(2)}, u32[]{:S(2)}) async-start(bf16[32,16,128]{2,1,0:T(8,128)(2,1)} %bitcast.2), calls=%async_computation | async-start | bytes 262144 | tf_op jit(solution)/shard_map/all_to_all | solution.py:393
  20.1 0.0 copy-done.1
  20.1 0.3 collective-permute-start.3
  20.4 0.0 collective-permute-done.refs_4_
  20.4 0.3 collective-permute-start.4
  20.7 0.0 collective-permute-done.1.refs_5_
  20.7 0.3 collective-permute-start.5
  20.9 0.0 collective-permute-done.2.refs_6_
  20.9 0.3 collective-permute-start.6
  21.2 0.3 collective-permute-done.3.refs_7_
  21.5 6.7 %all-to-all-done = bf16[32,16,128]{2,1,0:T(8,128)(2,1)S(1)} async-done(((bf16[32,16,128]{2,1,0:T(8,128)(2,1)}), bf16[32,16,128]{2,1,0:T(8,128)(2,1)S(1)}, u32[]{:S(2)}, u32[]{:S(2)}) %all-to-all-start) | async-done | bytes 131104 | tf_op jit(solution)/shard_map/all_to_all | solution.py:393
  28.3 0.0 collective-permute-done.4.refs_8_
  28.3 0.0 collective-permute-done.5.refs_9_
  28.3 0.0 collective-permute-done.6.refs_10_
  28.3 0.0 copy-done.4
  28.3 0.0 copy-done.5
  28.3 4.8 %attention.1 = (bf16[2,64,2048]{2,1,0:T(8,128)(2,1)}, bf16[2,64,2048]{2,1,0:T(8,128)(2,1)}, bf16[4,2,64,512]{3,2,1,0:T(8,128)(2,1)S(1)}, bf16[2,64,512]{2,1,0:T(...) custom-call(bf16[2,64,2048]{2,1,0:T(8,128)(2,1)S(1)} %copy-done.4, ...), custom_call_target="tpu_custom_call" | custom-call | flops 64424509440 | bytes 8388608 | tf_op jit(solution)/shard_map/attention/pallas_call | solution.py:148
  33.1 0.4 collective-permute-start.7
  33.5 1.6 %collective-permute-done.7.refs_4_ = bf16[4,2,64,512]{3,2,1,0:T(8,128)(2,1)S(1)} collective-permute-done((bf16[4,2,64,512]{3,2,1,0:T(8,128)(2,1)S(1)}, bf16[4,2,64,512]{3,2,1,0:T(8,128)(2,1)S(1)}, u32[]{:S(2)}, u32[]{:S(2)}) %collective-permute-start.7) | collective-permute-done | bytes 524320 | tf_op jit(solution)/shard_map/ppermute | solution.py:414
  35.1 0.1 merge.1
  35.2 1.4 %collective-permute-start.8 = (bf16[2,64,512]{2,1,0:T(8,128)(2,1)S(1)}, bf16[2,64,512]{2,1,0:T(8,128)(2,1)S(1)}, u32[]{:S(2)}, u32[]{:S(2)}) collective-permute-start(bf16[2,64,512]{2,1,0:T(8,128)(2,1)S(1)} %get-tuple-element.41), channel_id=1, source_target_pairs={{2,0},{3,1},{4,2},{5,3},{6,4},{7,5},{10,8},{11,9},{12,10},{13,11},... | collective-permute-start | bytes 393224 | tf_op jit(solution)/shard_map/ppermute | solution.py:425
  36.6 0.5 enter.1
  37.1 0.9 %collective-permute-start.11 = (bf16[64,768]{1,0:T(8,128)(2,1)S(1)}, bf16[64,768]{1,0:T(8,128)(2,1)S(1)}, u32[]{:S(2)}, u32[]{:S(2)}) collective-permute-start(bf16[64,768]{1,0:T(8,128)(2,1)S(1)} %get-tuple-element.47.refs_0_), channel_id=1, source_target_pairs={{0,8},{8,0},{16,24},{24,16},{1,9},{9,1},{17,25},{25,17},{2,10},{10... | collective-permute-start | bytes 294920 | tf_op jit(solution)/shard_map/ppermute | solution.py:411
  38.0 0.7 %collective-permute-start.12 = (bf16[64,768]{1,0:T(8,128)(2,1)S(1)}, bf16[64,768]{1,0:T(8,128)(2,1)S(1)}, u32[]{:S(2)}, u32[]{:S(2)}) collective-permute-start(bf16[64,768]{1,0:T(8,128)(2,1)S(1)} %get-tuple-element.47.refs_0_), channel_id=1, source_target_pairs={{0,16},{8,24},{16,0},{24,8},{1,17},{9,25},{17,1},{25,9},{2,18},{10... | collective-permute-start | bytes 294920 | tf_op jit(solution)/shard_map/ppermute | solution.py:411
  38.7 2.0 %collective-permute-start.13 = (bf16[64,768]{1,0:T(8,128)(2,1)S(1)}, bf16[64,768]{1,0:T(8,128)(2,1)S(1)}, u32[]{:S(2)}, u32[]{:S(2)}) collective-permute-start(bf16[64,768]{1,0:T(8,128)(2,1)S(1)} %get-tuple-element.47.refs_0_), channel_id=1, source_target_pairs={{0,24},{8,16},{16,8},{24,0},{1,25},{9,17},{17,9},{25,1},{2,26},{10... | collective-permute-start | bytes 294920 | tf_op jit(solution)/shard_map/ppermute | solution.py:411
  40.7 1.3 %collective-permute-start.10 = (bf16[2,64,512]{2,1,0:T(8,128)(2,1)S(1)}, bf16[2,64,512]{2,1,0:T(8,128)(2,1)S(1)}, u32[]{:S(2)}, u32[]{:S(2)}) collective-permute-start(bf16[2,64,512]{2,1,0:T(8,128)(2,1)S(1)} %get-tuple-element.43), channel_id=1, source_target_pairs={{6,0},{7,1},{14,8},{15,9},{22,16},{23,17},{30,24},{31,25}} | collective-permute-start | bytes 393224 | tf_op jit(solution)/shard_map/ppermute | solution.py:425
  42.0 0.8 %collective-permute-done.11.refs_1_ = bf16[64,768]{1,0:T(8,128)(2,1)S(1)} collective-permute-done((bf16[64,768]{1,0:T(8,128)(2,1)S(1)}, bf16[64,768]{1,0:T(8,128)(2,1)S(1)}, u32[]{:S(2)}, u32[]{:S(2)}) %collective-permute-start.11) | collective-permute-done | bytes 98336 | tf_op jit(solution)/shard_map/ppermute | solution.py:411
  42.8 1.3 %collective-permute-start.9 = (bf16[2,64,512]{2,1,0:T(8,128)(2,1)S(1)}, bf16[2,64,512]{2,1,0:T(8,128)(2,1)S(1)}, u32[]{:S(2)}, u32[]{:S(2)}) collective-permute-start(bf16[2,64,512]{2,1,0:T(8,128)(2,1)S(1)} %get-tuple-element.42), channel_id=1, source_target_pairs={{4,0},{5,1},{6,2},{7,3},{12,8},{13,9},{14,10},{15,11},{20,16},{21,... | collective-permute-start | bytes 393224 | tf_op jit(solution)/shard_map/ppermute | solution.py:425
  44.1 0.7 %collective-permute-done.12.refs_2_ = bf16[64,768]{1,0:T(8,128)(2,1)S(1)} collective-permute-done((bf16[64,768]{1,0:T(8,128)(2,1)S(1)}, bf16[64,768]{1,0:T(8,128)(2,1)S(1)}, u32[]{:S(2)}, u32[]{:S(2)}) %collective-permute-start.12) | collective-permute-done | bytes 98336 | tf_op jit(solution)/shard_map/ppermute | solution.py:411
  44.7 0.0 collective-permute-done.13.refs_3_
  44.7 0.0 collective-permute-done.8.refs_1_.refs_6_
  44.7 1.4 %middle.1 = (bf16[512,128]{1,0:T(8,128)(2,1)}, bf16[64,256]{1,0:T(8,128)(2,1)S(1)}, bf16[64,256]{1,0:T(8,128)(2,1)S(1)}, bf16[64,256]{1,0:T(8,128)(2,1)S(1)}) custom-call(bf16[64,768]{1,0:T(8,128)(2,1)S(1)} %get-tuple-element.47.refs_0_, bf16[64,768]{1,0:T(8,128)(2,1)S(1)} %collective-permute-done.11.refs_1_, ...), custom_call_target="tpu_custom_call" | custom-call | flops 2000000000 | bytes 2097152 | tf_op jit(solution)/shard_map/middle/pallas_call | solution.py:426
  46.2 5.3 %all-to-all-start.1 = ((bf16[32,16,128]{2,1,0:T(8,128)(2,1)}), bf16[32,16,128]{2,1,0:T(8,128)(2,1)S(1)}, u32[]{:S(2)}, u32[]{:S(2)}) async-start(bf16[32,16,128]{2,1,0:T(8,128)(2,1)} %bitcast.4), calls=%async_computation.1 | async-start | bytes 262144 | tf_op jit(solution)/shard_map/all_to_all | solution.py:434
  51.4 0.0 collective-permute-done.10.refs_3_
  51.4 3.5 %collective-permute-done.9.refs_2_ = bf16[2,64,512]{2,1,0:T(8,128)(2,1)S(1)} collective-permute-done((bf16[2,64,512]{2,1,0:T(8,128)(2,1)S(1)}, bf16[2,64,512]{2,1,0:T(8,128)(2,1)S(1)}, u32[]{:S(2)}, u32[]{:S(2)}) %collective-permute-start.9) | collective-permute-done | bytes 131104 | tf_op jit(solution)/shard_map/ppermute | solution.py:425
  54.9 0.7 %close.1 = (bf16[2,64,256]{2,1,0:T(8,128)(2,1)}, bf16[2,64,256]{2,1,0:T(8,128)(2,1)}) custom-call(bf16[2,64,512]{2,1,0:T(8,128)(2,1)S(1)} %get-tuple-element.40.refs_0_, bf16[2,64,512]{2,1,0:T(8,128)(2,1)S(1)} %collective-permute-done.8.refs_1_.refs_6_, bf16[2,64,512]{2,1,0:T(8,128)(2,1)S(1)} %collective-permute-done.9.refs_2_, ...), custom_call_target="tpu_custom_call" | custom-call | flops 60000002048 | bytes 1048576 | tf_op jit(solution)/shard_map/close/pallas_call | solution.py:448
  55.6 1.5 %weight_grads.1 = (f32[1,512,256]{2,1,0:T(8,128)}, f32[1,512,256]{2,1,0:T(8,128)}, f32[1,256,512]{2,1,0:T(8,128)}) custom-call(bf16[64,512]{1,0:T(8,128)(2,1)S(1)} %get-tuple-element.51.input_ref, bf16[64,512]{1,0:T(8,128)(2,1)S(1)} %get-tuple-element.52.grad_ref, bf16[64,256]{1,0:T(8,128)(2,1)S(1)} %get-tuple-element.53.hidden_ref, ...), custom_call_target="tpu_custom_call" | custom-call | flops 2000000000 | bytes 2097152 | tf_op jit(solution)/shard_map/weight_grads/pallas_call | solution.py:437
  57.1 2.5 %all-to-all-done.1 = bf16[32,16,128]{2,1,0:T(8,128)(2,1)S(1)} async-done(((bf16[32,16,128]{2,1,0:T(8,128)(2,1)}), bf16[32,16,128]{2,1,0:T(8,128)(2,1)S(1)}, u32[]{:S(2)}, u32[]{:S(2)}) %all-to-all-start.1) | async-done | bytes 131104 | tf_op jit(solution)/shard_map/all_to_all | solution.py:434
  59.6 1.3 %combine.1 = (bf16[128,2048]{1,0:T(8,128)(2,1)}, bf16[10,128]{1,0:T(8,128)(2,1)}) custom-call(bf16[512,128]{1,0:T(8,128)(2,1)S(1)} %bitcast.9, s32[10,128]{1,0:T(8,128)S(1)} %bitcast.11, bf16[10,128]{1,0:T(8,128)(2,1)S(1)} %bitcast.13, bf16[2,64,256]{2,1,0:T(8,128)(2,1)S(1)} %copy-done.12), custom_call_target="tpu_custom_call" | custom-call | flops 2000000000 | bytes 2097152 | tf_op jit(solution)/shard_map/combine/pallas_call | solution.py:456
  (19 shorter events, 0.0 us)
Async XLA Ops:
  0.6 12.3 %copy-start.10 = (s32[128,10]{0,1:T(8,128)S(1)}, s32[128,10]{0,1:T(8,128)}, u32[]{:S(2)}) copy-start(s32[128,10]{0,1:T(8,128)} %param.19) | copy-start | bytes 15364
  0.7 12.3 %copy-start.11 = (bf16[128,10]{0,1:T(8,128)(2,1)S(1)}, bf16[128,10]{0,1:T(8,128)(2,1)}, u32[]{:S(2)}) copy-start(bf16[128,10]{0,1:T(8,128)(2,1)} %param.20) | copy-start | bytes 7684
  2.2 18.2 %collective-permute-start = (bf16[2,64,512]{2,1,0:T(8,128)(2,1)}, bf16[2,64,512]{2,1,0:T(8,128)(2,1)S(1)}, u32[]{:S(2)}, u32[]{:S(2)}) collective-permute-start(bf16[2,64,512]{2,1,0:T(8,128)(2,1)} %pack.1.after_ref.refs_3_), channel_id=1, source_target_pairs={{0,2},{1,3},{2,4},{3,5},{4,6},{5,7},{8,10},{9,11},{10,12},{11,13},... | collective-permute-start | bytes 393224 | tf_op jit(solution)/shard_map/ppermute | solution.py:381
  7.2 13.5 %collective-permute-start.1 = (bf16[2,64,512]{2,1,0:T(8,128)(2,1)}, bf16[2,64,512]{2,1,0:T(8,128)(2,1)S(1)}, u32[]{:S(2)}, u32[]{:S(2)}) collective-permute-start(bf16[2,64,512]{2,1,0:T(8,128)(2,1)} %pack.1.after_ref.refs_3_), channel_id=1, source_target_pairs={{0,4},{1,5},{2,6},{3,7},{8,12},{9,13},{10,14},{11,15},{16,20},{17,... | collective-permute-start | bytes 393224 | tf_op jit(solution)/shard_map/ppermute | solution.py:381
  11.7 9.2 %collective-permute-start.2 = (bf16[2,64,512]{2,1,0:T(8,128)(2,1)}, bf16[2,64,512]{2,1,0:T(8,128)(2,1)S(1)}, u32[]{:S(2)}, u32[]{:S(2)}) collective-permute-start(bf16[2,64,512]{2,1,0:T(8,128)(2,1)} %pack.1.after_ref.refs_3_), channel_id=1, source_target_pairs={{0,6},{1,7},{8,14},{9,15},{16,22},{17,23},{24,30},{25,31}} | collective-permute-start | bytes 393224 | tf_op jit(solution)/shard_map/ppermute | solution.py:381
  13.0 0.9 %copy-start = (bf16[2,64,512]{2,1,0:T(8,128)(2,1)S(1)}, bf16[2,64,512]{2,1,0:T(8,128)(2,1)}, u32[]{:S(2)}) copy-start(bf16[2,64,512]{2,1,0:T(8,128)(2,1)} %pack.1.after_ref.refs_3_) | copy-start | bytes 393220
  13.9 1.0 %copy-start.2 = (bf16[128,2048]{1,0:T(8,128)(2,1)S(1)}, bf16[128,2048]{1,0:T(8,128)(2,1)}, u32[]{:S(2)}) copy-start(bf16[128,2048]{1,0:T(8,128)(2,1)} %input_ref.1) | copy-start | bytes 1572868
  15.0 1.0 %copy-start.3 = (bf16[128,2048]{1,0:T(8,128)(2,1)S(1)}, bf16[128,2048]{1,0:T(8,128)(2,1)}, u32[]{:S(2)}) copy-start(bf16[128,2048]{1,0:T(8,128)(2,1)} %grad_ref.1) | copy-start | bytes 1572868
  16.0 12.2 %copy-start.4 = (bf16[2,64,2048]{2,1,0:T(8,128)(2,1)S(1)}, bf16[2,64,2048]{2,1,0:T(8,128)(2,1)}, u32[]{:S(2)}) copy-start(bf16[2,64,2048]{2,1,0:T(8,128)(2,1)} %refs_0_.1) | copy-start | bytes 1572868
  16.0 12.3 %copy-start.5 = (bf16[2,64,2048]{2,1,0:T(8,128)(2,1)S(1)}, bf16[2,64,2048]{2,1,0:T(8,128)(2,1)}, u32[]{:S(2)}) copy-start(bf16[2,64,2048]{2,1,0:T(8,128)(2,1)} %refs_1_.1) | copy-start | bytes 1572868
  16.0 12.3 %copy-start.6 = (bf16[2,64,2048]{2,1,0:T(8,128)(2,1)S(1)}, bf16[2,64,2048]{2,1,0:T(8,128)(2,1)}, u32[]{:S(2)}) copy-start(bf16[2,64,2048]{2,1,0:T(8,128)(2,1)} %refs_2_.1) | copy-start | bytes 1572868
  17.3 2.8 %copy-start.1 = (bf16[2,64,512]{2,1,0:T(8,128)(2,1)S(1)}, bf16[2,64,512]{2,1,0:T(8,128)(2,1)}, u32[]{:S(2)}) copy-start(bf16[2,64,512]{2,1,0:T(8,128)(2,1)} %pack.1.after_ref.refs_3_) | copy-start | bytes 393220
  17.3 11.0 %all-to-all-start = ((bf16[32,16,128]{2,1,0:T(8,128)(2,1)}), bf16[32,16,128]{2,1,0:T(8,128)(2,1)S(1)}, u32[]{:S(2)}, u32[]{:S(2)}) async-start(bf16[32,16,128]{2,1,0:T(8,128)(2,1)} %bitcast.2), calls=%async_computation | async-start | bytes 262144 | tf_op jit(solution)/shard_map/all_to_all | solution.py:393
  20.1 1.4 %collective-permute-start.3 = (bf16[2,64,512]{2,1,0:T(8,128)(2,1)S(1)}, bf16[2,64,512]{2,1,0:T(8,128)(2,1)S(1)}, u32[]{:S(2)}, u32[]{:S(2)}) collective-permute-start(bf16[2,64,512]{2,1,0:T(8,128)(2,1)S(1)} %copy-done.1), channel_id=1, source_target_pairs={{0,1},{1,0},{2,3},{3,2},{4,5},{5,4},{6,7},{7,6},{8,9},{9,8},{10,11... | collective-permute-start | bytes 393224 | tf_op jit(solution)/shard_map/ppermute | solution.py:382
  20.4 7.8 %collective-permute-start.4 = (bf16[2,64,512]{2,1,0:T(8,128)(2,1)S(1)}, bf16[2,64,512]{2,1,0:T(8,128)(2,1)S(1)}, u32[]{:S(2)}, u32[]{:S(2)}) collective-permute-start(bf16[2,64,512]{2,1,0:T(8,128)(2,1)S(1)} %collective-permute-done.refs_4_), channel_id=1, source_target_pairs={{0,1},{1,0},{2,3},{3,2},{4,5},{5,4},{6,7},{7,6},{8,9},{9,8},{10,11... | collective-permute-start | bytes 393224 | tf_op jit(solution)/shard_map/ppermute | solution.py:382
  20.7 7.6 %collective-permute-start.5 = (bf16[2,64,512]{2,1,0:T(8,128)(2,1)S(1)}, bf16[2,64,512]{2,1,0:T(8,128)(2,1)S(1)}, u32[]{:S(2)}, u32[]{:S(2)}) collective-permute-start(bf16[2,64,512]{2,1,0:T(8,128)(2,1)S(1)} %collective-permute-done.1.refs_5_), channel_id=1, source_target_pairs={{0,1},{1,0},{2,3},{3,2},{4,5},{5,4},{6,7},{7,6},{8,9},{9,8},{10,11... | collective-permute-start | bytes 393224 | tf_op jit(solution)/shard_map/ppermute | solution.py:382
  20.9 7.3 %collective-permute-start.6 = (bf16[2,64,512]{2,1,0:T(8,128)(2,1)S(1)}, bf16[2,64,512]{2,1,0:T(8,128)(2,1)S(1)}, u32[]{:S(2)}, u32[]{:S(2)}) collective-permute-start(bf16[2,64,512]{2,1,0:T(8,128)(2,1)S(1)} %collective-permute-done.2.refs_6_), channel_id=1, source_target_pairs={{0,1},{1,0},{2,3},{3,2},{4,5},{5,4},{6,7},{7,6},{8,9},{9,8},{10,11... | collective-permute-start | bytes 393224 | tf_op jit(solution)/shard_map/ppermute | solution.py:382
  33.1 2.0 %collective-permute-start.7 = (bf16[4,2,64,512]{3,2,1,0:T(8,128)(2,1)S(1)}, bf16[4,2,64,512]{3,2,1,0:T(8,128)(2,1)S(1)}, u32[]{:S(2)}, u32[]{:S(2)}) collective-permute-start(bf16[4,2,64,512]{3,2,1,0:T(8,128)(2,1)S(1)} %get-tuple-element.39.after_ref), channel_id=1, source_target_pairs={{0,1},{1,0},{2,3},{3,2},{4,5},{5,4},{6,7},{7,6},{8,9},{9,8},{10,11... | collective-permute-start | bytes 1572872 | tf_op jit(solution)/shard_map/ppermute | solution.py:414
  35.1 1.6 %copy-start.7 = (bf16[1,256,512]{2,1,0:T(8,128)(2,1)S(1)}, bf16[1,256,512]{2,1,0:T(8,128)(2,1)}, u32[]{:S(2)}) copy-start(bf16[1,256,512]{2,1,0:T(8,128)(2,1)} %down_ref.1) | copy-start | bytes 786436
  35.1 1.6 %copy-start.8 = (bf16[1,512,256]{2,1,0:T(8,128)(2,1)S(1)}, bf16[1,512,256]{2,1,0:T(8,128)(2,1)}, u32[]{:S(2)}) copy-start(bf16[1,512,256]{2,1,0:T(8,128)(2,1)} %refs_4_.1) | copy-start | bytes 786436
  35.1 1.6 %copy-start.9 = (bf16[1,512,256]{2,1,0:T(8,128)(2,1)S(1)}, bf16[1,512,256]{2,1,0:T(8,128)(2,1)}, u32[]{:S(2)}) copy-start(bf16[1,512,256]{2,1,0:T(8,128)(2,1)} %refs_5_.1) | copy-start | bytes 786436
  35.2 9.5 %collective-permute-start.8 = (bf16[2,64,512]{2,1,0:T(8,128)(2,1)S(1)}, bf16[2,64,512]{2,1,0:T(8,128)(2,1)S(1)}, u32[]{:S(2)}, u32[]{:S(2)}) collective-permute-start(bf16[2,64,512]{2,1,0:T(8,128)(2,1)S(1)} %get-tuple-element.41), channel_id=1, source_target_pairs={{2,0},{3,1},{4,2},{5,3},{6,4},{7,5},{10,8},{11,9},{12,10},{13,11},... | collective-permute-start | bytes 393224 | tf_op jit(solution)/shard_map/ppermute | solution.py:425
  37.1 5.7 %collective-permute-start.11 = (bf16[64,768]{1,0:T(8,128)(2,1)S(1)}, bf16[64,768]{1,0:T(8,128)(2,1)S(1)}, u32[]{:S(2)}, u32[]{:S(2)}) collective-permute-start(bf16[64,768]{1,0:T(8,128)(2,1)S(1)} %get-tuple-element.47.refs_0_), channel_id=1, source_target_pairs={{0,8},{8,0},{16,24},{24,16},{1,9},{9,1},{17,25},{25,17},{2,10},{10... | collective-permute-start | bytes 294920 | tf_op jit(solution)/shard_map/ppermute | solution.py:411
  38.0 6.7 %collective-permute-start.12 = (bf16[64,768]{1,0:T(8,128)(2,1)S(1)}, bf16[64,768]{1,0:T(8,128)(2,1)S(1)}, u32[]{:S(2)}, u32[]{:S(2)}) collective-permute-start(bf16[64,768]{1,0:T(8,128)(2,1)S(1)} %get-tuple-element.47.refs_0_), channel_id=1, source_target_pairs={{0,16},{8,24},{16,0},{24,8},{1,17},{9,25},{17,1},{25,9},{2,18},{10... | collective-permute-start | bytes 294920 | tf_op jit(solution)/shard_map/ppermute | solution.py:411
  38.7 6.0 %collective-permute-start.13 = (bf16[64,768]{1,0:T(8,128)(2,1)S(1)}, bf16[64,768]{1,0:T(8,128)(2,1)S(1)}, u32[]{:S(2)}, u32[]{:S(2)}) collective-permute-start(bf16[64,768]{1,0:T(8,128)(2,1)S(1)} %get-tuple-element.47.refs_0_), channel_id=1, source_target_pairs={{0,24},{8,16},{16,8},{24,0},{1,25},{9,17},{17,9},{25,1},{2,26},{10... | collective-permute-start | bytes 294920 | tf_op jit(solution)/shard_map/ppermute | solution.py:411
  40.7 10.8 %collective-permute-start.10 = (bf16[2,64,512]{2,1,0:T(8,128)(2,1)S(1)}, bf16[2,64,512]{2,1,0:T(8,128)(2,1)S(1)}, u32[]{:S(2)}, u32[]{:S(2)}) collective-permute-start(bf16[2,64,512]{2,1,0:T(8,128)(2,1)S(1)} %get-tuple-element.43), channel_id=1, source_target_pairs={{6,0},{7,1},{14,8},{15,9},{22,16},{23,17},{30,24},{31,25}} | collective-permute-start | bytes 393224 | tf_op jit(solution)/shard_map/ppermute | solution.py:425
  42.8 12.1 %collective-permute-start.9 = (bf16[2,64,512]{2,1,0:T(8,128)(2,1)S(1)}, bf16[2,64,512]{2,1,0:T(8,128)(2,1)S(1)}, u32[]{:S(2)}, u32[]{:S(2)}) collective-permute-start(bf16[2,64,512]{2,1,0:T(8,128)(2,1)S(1)} %get-tuple-element.42), channel_id=1, source_target_pairs={{4,0},{5,1},{6,2},{7,3},{12,8},{13,9},{14,10},{15,11},{20,16},{21,... | collective-permute-start | bytes 393224 | tf_op jit(solution)/shard_map/ppermute | solution.py:425
  46.2 13.5 %all-to-all-start.1 = ((bf16[32,16,128]{2,1,0:T(8,128)(2,1)}), bf16[32,16,128]{2,1,0:T(8,128)(2,1)S(1)}, u32[]{:S(2)}, u32[]{:S(2)}) async-start(bf16[32,16,128]{2,1,0:T(8,128)(2,1)} %bitcast.4), calls=%async_computation.1 | async-start | bytes 262144 | tf_op jit(solution)/shard_map/all_to_all | solution.py:434
  55.6 4.0 %copy-start.12 = (bf16[2,64,256]{2,1,0:T(8,128)(2,1)S(1)}, bf16[2,64,256]{2,1,0:T(8,128)(2,1)}, u32[]{:S(2)}) copy-start(bf16[2,64,256]{2,1,0:T(8,128)(2,1)} %get-tuple-element.26.after_ref) | copy-start | bytes 196612

commit v6 on v5

--- a/solution.py
+++ b/solution.py
@@ -60,29 +60,16 @@
 
 
 def attention_kernel(chips, *refs):
-    wide_hbm = refs[:3]
+    q_ref, logit_ref, grad_ref = refs[:3]
     kv_refs = refs[3 : 3 + 2 * chips]
-    query_grad_hbm, gate_grad_hbm, other_ref = refs[4 + 2 * chips : 7 + 2 * chips]
-    mine_refs = refs[7 + 2 * chips : 7 + 3 * chips]
-    q_ref, logit_ref, grad_ref, query_grad_ref, gate_grad_ref, in_sems, out_sems = refs[
-        7 + 3 * chips :
-    ]
+    query_grad_hbm, gate_grad_hbm, other_ref = refs[3 + 2 * chips : 6 + 2 * chips]
+    mine_refs = refs[6 + 2 * chips : 6 + 3 * chips]
+    query_grad_ref, gate_grad_ref, out_sems = refs[6 + 3 * chips :]
     seqs, length, _ = q_ref.shape
     side = chips * length
     scale = HEAD ** (-0.5)
     position = lax.axis_index("expert")
     chip, core = position >> 1, position & 1
-
-    loads = [
-        [
-            pltpu.make_async_copy(src.at[s], dst.at[s], in_sems.at[s, i])
-            for i, (src, dst) in enumerate(zip(wide_hbm, (q_ref, logit_ref, grad_ref)))
-        ]
-        for s in range(seqs)
-    ]
-    for row in loads:
-        for load in row:
-            load.start()
 
     shape = (1, 2 * side)
     col = iota(shape, 1)
@@ -100,7 +87,6 @@
     for s in range(seqs):
         both = jnp.concatenate([ref[s] for ref in kv_refs], axis=0)
         keys, values = both[:, :HEAD], both[:, HEAD:]
-        loads[s][0].wait()
         queries = stacked(q_ref, s)
         scores = jnp.where(key_pos <= query_pos, dot(queries, keys, 1, 1), -jnp.inf)
         row_max = jnp.max(scores, axis=1, keepdims=True)
@@ -108,8 +94,6 @@
         probs = unnormed * (1.0 / jnp.sum(unnormed, axis=1, keepdims=True))
         probs_low = probs.astype(BF16)
         context = dot(probs_low, values)
-        loads[s][1].wait()
-        loads[s][2].wait()
         gate = jax.nn.sigmoid(stacked(logit_ref, s).astype(F32))
         upstream = stacked(grad_ref, s).astype(F32)
         context_grad = (upstream * gate).astype(BF16)
@@ -139,24 +123,40 @@
         store.wait()
 
 
-def attention(query_rows, gate_logits, gated_grad, pieces, after):
+def attention(query_rows, gate_logits, gated_grad, pieces):
     seqs, length, width = query_rows.shape
     chips = len(pieces) // 2
     full = jax.ShapeDtypeStruct((seqs, length, width), BF16)
     part = jax.ShapeDtypeStruct(pieces[0].shape, BF16)
-    flops = 12 * seqs * HEADS * length * 2 * chips * length * HEAD
     out = pl.pallas_call(
         functools.partial(attention_kernel, chips),
-        in_specs=[IN_HBM] * 3 + [IN_VMEM] * (2 * chips) + [ANYWHERE],
+        in_specs=[IN_VMEM] * (3 + 2 * chips),
         out_specs=[IN_HBM] * 2 + [IN_VMEM] * (1 + chips),
         out_shape=[full] * 2 + [jax.ShapeDtypeStruct((chips,) + part.shape, BF16)] + [part] * chips,
-        scratch_shapes=[pltpu.VMEM(query_rows.shape, BF16)] * 5
-        + [pltpu.SemaphoreType.DMA((seqs, 3)), pltpu.SemaphoreType.DMA((seqs, 2))],
+        scratch_shapes=[pltpu.VMEM(query_rows.shape, BF16)] * 2
+        + [pltpu.SemaphoreType.DMA((seqs, 2))],
         compiler_params=params(ATTENTION_MIB if chips <= 4 else 56),
-        cost_estimate=cost(flops * 40, 8 * MIB),
+        cost_estimate=cost(MIB, 8),
         name="attention",
-    )(query_rows, gate_logits, gated_grad, *pieces, after)
+    )(query_rows, gate_logits, gated_grad, *pieces)
     return out[0], out[1], out[2], out[3:]
+
+
+def gate_kernel(held_ref, after_ref, out_ref):
+    pass
+
+
+def gate(array, after):
+    return pl.pallas_call(
+        gate_kernel,
+        in_specs=[ANYWHERE] * 2,
+        out_specs=ANYWHERE,
+        out_shape=jax.ShapeDtypeStruct(array.shape, array.dtype),
+        input_output_aliases={0: 0},
+        compiler_params=params(16),
+        cost_estimate=cost(4e9, 8),
+        name="gate",
+    )(array, after)
 
 
 def merge_kernel(chips, *refs):
@@ -371,8 +371,8 @@
         in_specs=[IN_HBM] * 2,
         out_shape=jax.ShapeDtypeStruct((seqs, length, 2 * HEAD), BF16),
         scratch_shapes=[pltpu.VMEM(key_rows.shape, BF16)] * 2 + [pltpu.SemaphoreType.DMA((2,))],
-        compiler_params=params(60),
-        cost_estimate=cost(MIB, MIB),
+        compiler_params=params(16),
+        cost_estimate=cost(6e10, MIB),
         name="pack",
     )(key_rows, value_rows)
     mine = [packed]
@@ -395,8 +395,9 @@
     ).reshape(sources * rows, LANES)
 
     query_grad, gate_grad, other_part, mine_part = attention(
-        query_rows, gate_logits, gated_grad, mine + other, recv
+        query_rows, gate_logits, gated_grad, mine + other
     )
+    other_part = gate(other_part, recv)
     slot_rows = jax.ShapeDtypeStruct((sources * CAP, share), BF16)
     hid_rows = jax.ShapeDtypeStruct((sources * CAP, hid), BF16)
     inputs, grads, sent = pl.pallas_call(

time: 61.4 us -> 55.3 us (0.901)
  waiting for transfers between devices: 16.1 us -> 12.4 us
  Pallas kernels: 13 us -> 10.6 us
  starting transfers between devices: 27.8 us -> 29.2 us
  local copies, waits for them, and re-layouts: 3.04 us -> 1.81 us
    all_to_all x1, waiting for transfers between devices: 6.75 us -> 2.26 us  [shards(): lax.all_to_all(send.reshape(sources, rows, LANES), axes, split_axis=0, co...]
    all_to_all x1, starting transfers between devices: 5.27 us -> 6.71 us  [shards(): lax.all_to_all(back.reshape(sources, rows, LANES), axes, split_axis=0, co...]
    pallas_call x1, Pallas kernels: 1.56 us -> 0.18 us  [shards(): pl.pallas_call(pack_kernel, in_specs=[IN_HBM] * 2, out_shape=jax.ShapeDty...]
    unnamed x26, local copies, waits for them, and re-layouts: 3.04 us -> 1.81 us
    pallas_call x1 -> x2, Pallas kernels: 4.78 us -> 3.7 us  [the longest x1 3.7 us: attention(): pl.pallas_call(functools.partial(attention_kernel, chips), in_specs=[IN_V...]
    all_to_all x1, waiting for transfers between devices: 2.54 us -> 3.57 us  [shards(): lax.all_to_all(back.reshape(sources, rows, LANES), axes, split_axis=0, co...]
    ppermute x3, waiting for transfers between devices: 3.46 us -> 2.43 us  [shards(): terms.append(lax.ppermute(merged[d], 'expert', down))]
    ppermute x4, waiting for transfers between devices: 0.32 us -> 1.09 us  [shards(): other = [lax.ppermute(block, 'expert', swap) for block in mine]]
  transfers between devices with their start and end apart: 16 -> 16, of which waited for: 7 -> 10; matrix products, arithmetic and copies ran while one was open for 0% -> 0% of each run, Pallas kernels for 9% -> 16%
where the time goes in v6:
time: 55.3 us; the launch traced here: 54.8 us
  starting transfers between devices  29.2 us (53%)
  waiting for transfers between devices  12.4 us (22%)
  Pallas kernels  10.6 us (19%)
  local copies, waits for them, and re-layouts  1.81 us (3%)
  between operations  0.86 us (2%)
    ppermute x3, starting transfers between devices, shards(): mine.append(lax.ppermute(packed, 'expert', up))  10.7 us
    all_to_all x1, starting transfers between devices, shards(): lax.all_to_all(back.reshape(sources, rows, LANES), axes, split_axis=0, co...  6.71 us
    ppermute x3, starting transfers between devices, shards(): terms.append(lax.ppermute(merged[d], 'expert', down))  3.98 us
    pallas_call x1, Pallas kernels, attention(): pl.pallas_call(functools.partial(attention_kernel, chips), in_specs=[IN_V...  3.7 us
    all_to_all x1, waiting for transfers between devices, shards(): lax.all_to_all(back.reshape(sources, rows, LANES), axes, split_axis=0, co...  3.57 us
    ppermute x3, starting transfers between devices, shards(): lax.ppermute(sent, 'dp', [(g, g ^ k) for g in range(groups)])  3.55 us
    all_to_all x1, starting transfers between devices, shards(): lax.all_to_all(send.reshape(sources, rows, LANES), axes, split_axis=0, co...  2.81 us
    ppermute x3, waiting for transfers between devices, shards(): terms.append(lax.ppermute(merged[d], 'expert', down))  2.43 us
  transfers between devices with their start and end apart: 16, of which 10 were waited for; matrix products, arithmetic and copies ran while one was open for 0% of the time, Pallas kernels for 16%

profile of v6, /device:TPU:0, one launch (start us, length us, event | category | flops | bytes accessed | tf_op | source)
XLA Modules:
  0.0 54.8 jit_solution(11686963408924238331)
XLA Ops:
  0.6 0.0 copy-start.3
  0.7 0.9 %copy-done.8 = bf16[2,64,256]{2,1,0:T(8,128)(2,1)S(1)} copy-done((bf16[2,64,256]{2,1,0:T(8,128)(2,1)S(1)}, bf16[2,64,256]{2,1,0:T(8,128)(2,1)}, u32[]{:S(2)}) %copy-start.8) | copy-done | bytes 65560
  1.6 0.8 %copy-done.9 = bf16[2,64,256]{2,1,0:T(8,128)(2,1)S(1)} copy-done((bf16[2,64,256]{2,1,0:T(8,128)(2,1)S(1)}, bf16[2,64,256]{2,1,0:T(8,128)(2,1)}, u32[]{:S(2)}) %copy-start.9) | copy-done | bytes 65560
  2.4 0.2 pack.1.refs_3_.after_ref
  2.6 4.9 %collective-permute-start = (bf16[2,64,512]{2,1,0:T(8,128)(2,1)S(1)}, bf16[2,64,512]{2,1,0:T(8,128)(2,1)S(1)}, u32[]{:S(2)}, u32[]{:S(2)}) collective-permute-start(bf16[2,64,512]{2,1,0:T(8,128)(2,1)S(1)} %pack.1.refs_3_.after_ref), channel_id=1, source_target_pairs={{0,2},{1,3},{2,4},{3,5},{4,6},{5,7},{8,10},{9,11},{10,12},{11,13},... | collective-permute-start | bytes 393224 | tf_op jit(solution)/shard_map/ppermute | solution.py:381
  7.6 4.5 %collective-permute-start.1 = (bf16[2,64,512]{2,1,0:T(8,128)(2,1)S(1)}, bf16[2,64,512]{2,1,0:T(8,128)(2,1)S(1)}, u32[]{:S(2)}, u32[]{:S(2)}) collective-permute-start(bf16[2,64,512]{2,1,0:T(8,128)(2,1)S(1)} %pack.1.refs_3_.after_ref), channel_id=1, source_target_pairs={{0,4},{1,5},{2,6},{3,7},{8,12},{9,13},{10,14},{11,15},{16,20},{17,... | collective-permute-start | bytes 393224 | tf_op jit(solution)/shard_map/ppermute | solution.py:381
  12.1 1.3 %collective-permute-start.2 = (bf16[2,64,512]{2,1,0:T(8,128)(2,1)S(1)}, bf16[2,64,512]{2,1,0:T(8,128)(2,1)S(1)}, u32[]{:S(2)}, u32[]{:S(2)}) collective-permute-start(bf16[2,64,512]{2,1,0:T(8,128)(2,1)S(1)} %pack.1.refs_3_.after_ref), channel_id=1, source_target_pairs={{0,6},{1,7},{8,14},{9,15},{16,22},{17,23},{24,30},{25,31}} | collective-permute-start | bytes 393224 | tf_op jit(solution)/shard_map/ppermute | solution.py:381
  13.4 0.0 copy-start
  13.4 0.0 copy-start.1
  13.4 0.0 copy-start.2
  13.5 1.2 %dispatch.1 = bf16[512,128]{1,0:T(8,128)(2,1)} custom-call(bf16[128,2048]{1,0:T(8,128)(2,1)S(1)} %copy-done.3, bf16[128,2048]{1,0:T(8,128)(2,1)S(1)} %copy-done.4, s32[10,128]{1,0:T(8,128)S(1)} %bitcast.10, bf16[10,128]{1,0:T(8,128)(2,1)S(1)} %bitcast.12, bf16[2,64,512]{2,1,0:T(8,128)(2,1)S(1)} %pack.1.refs_3_.after_ref), custom_call_target="tpu_custom_call" | custom-call | flops 2000000000 | bytes 2097152 | tf_op jit(solution)/shard_map/dispatch/pallas_call | solution.py:385
  14.7 2.8 %all-to-all-start = ((bf16[32,16,128]{2,1,0:T(8,128)(2,1)}), bf16[32,16,128]{2,1,0:T(8,128)(2,1)S(1)}, u32[]{:S(2)}, u32[]{:S(2)}) async-start(bf16[32,16,128]{2,1,0:T(8,128)(2,1)} %bitcast.2), calls=%async_computation | async-start | bytes 262144 | tf_op jit(solution)/shard_map/all_to_all | solution.py:393
  17.5 0.3 collective-permute-start.3
  17.8 0.0 collective-permute-done.refs_4_
  17.8 0.3 collective-permute-start.4
  18.1 0.0 collective-permute-done.1.refs_5_
  18.1 0.3 collective-permute-start.5
  18.3 0.0 collective-permute-done.2.refs_6_
  18.3 0.3 collective-permute-start.6
  18.6 0.3 collective-permute-done.3.refs_7_
  18.9 0.3 collective-permute-done.4.refs_8_
  19.2 0.3 collective-permute-done.5.refs_9_
  19.4 0.3 collective-permute-done.6.refs_10_
  19.7 0.0 copy-done.2
  19.7 3.7 %attention.1 = (bf16[2,64,2048]{2,1,0:T(8,128)(2,1)}, bf16[2,64,2048]{2,1,0:T(8,128)(2,1)}, bf16[4,2,64,512]{3,2,1,0:T(8,128)(2,1)S(1)}, bf16[2,64,512]{2,1,0:T(...) custom-call(bf16[2,64,2048]{2,1,0:T(8,128)(2,1)S(1)} %copy-done, ...), custom_call_target="tpu_custom_call" | custom-call | flops 1048576 | bytes 8 | tf_op jit(solution)/shard_map/attention/pallas_call | solution.py:131
  23.4 2.3 %all-to-all-done = bf16[32,16,128]{2,1,0:T(8,128)(2,1)S(1)} async-done(((bf16[32,16,128]{2,1,0:T(8,128)(2,1)}), bf16[32,16,128]{2,1,0:T(8,128)(2,1)S(1)}, u32[]{:S(2)}, u32[]{:S(2)}) %all-to-all-start) | async-done | bytes 131104 | tf_op jit(solution)/shard_map/all_to_all | solution.py:393
  25.7 0.3 collective-permute-start.7
  26.0 1.6 %collective-permute-done.7.refs_4_ = bf16[4,2,64,512]{3,2,1,0:T(8,128)(2,1)S(1)} collective-permute-done((bf16[4,2,64,512]{3,2,1,0:T(8,128)(2,1)S(1)}, bf16[4,2,64,512]{3,2,1,0:T(8,128)(2,1)S(1)}, u32[]{:S(2)}, u32[]{:S(2)}) %collective-permute-start.7) | collective-permute-done | bytes 524320 | tf_op jit(solution)/shard_map/ppermute | solution.py:415
  27.6 0.1 merge.1
  27.7 1.4 %collective-permute-start.8 = (bf16[2,64,512]{2,1,0:T(8,128)(2,1)S(1)}, bf16[2,64,512]{2,1,0:T(8,128)(2,1)S(1)}, u32[]{:S(2)}, u32[]{:S(2)}) collective-permute-start(bf16[2,64,512]{2,1,0:T(8,128)(2,1)S(1)} %get-tuple-element.41), channel_id=1, source_target_pairs={{2,0},{3,1},{4,2},{5,3},{6,4},{7,5},{10,8},{11,9},{12,10},{13,11},... | collective-permute-start | bytes 393224 | tf_op jit(solution)/shard_map/ppermute | solution.py:426
  29.2 0.5 enter.1
  29.6 0.9 %collective-permute-start.11 = (bf16[64,768]{1,0:T(8,128)(2,1)S(1)}, bf16[64,768]{1,0:T(8,128)(2,1)S(1)}, u32[]{:S(2)}, u32[]{:S(2)}) collective-permute-start(bf16[64,768]{1,0:T(8,128)(2,1)S(1)} %get-tuple-element.47.refs_0_), channel_id=1, source_target_pairs={{0,8},{8,0},{16,24},{24,16},{1,9},{9,1},{17,25},{25,17},{2,10},{10... | collective-permute-start | bytes 294920 | tf_op jit(solution)/shard_map/ppermute | solution.py:412
  30.5 0.7 %collective-permute-start.12 = (bf16[64,768]{1,0:T(8,128)(2,1)S(1)}, bf16[64,768]{1,0:T(8,128)(2,1)S(1)}, u32[]{:S(2)}, u32[]{:S(2)}) collective-permute-start(bf16[64,768]{1,0:T(8,128)(2,1)S(1)} %get-tuple-element.47.refs_0_), channel_id=1, source_target_pairs={{0,16},{8,24},{16,0},{24,8},{1,17},{9,25},{17,1},{25,9},{2,18},{10... | collective-permute-start | bytes 294920 | tf_op jit(solution)/shard_map/ppermute | solution.py:412
  31.2 2.0 %collective-permute-start.13 = (bf16[64,768]{1,0:T(8,128)(2,1)S(1)}, bf16[64,768]{1,0:T(8,128)(2,1)S(1)}, u32[]{:S(2)}, u32[]{:S(2)}) collective-permute-start(bf16[64,768]{1,0:T(8,128)(2,1)S(1)} %get-tuple-element.47.refs_0_), channel_id=1, source_target_pairs={{0,24},{8,16},{16,8},{24,0},{1,25},{9,17},{17,9},{25,1},{2,26},{10... | collective-permute-start | bytes 294920 | tf_op jit(solution)/shard_map/ppermute | solution.py:412
  33.2 1.3 %collective-permute-start.10 = (bf16[2,64,512]{2,1,0:T(8,128)(2,1)S(1)}, bf16[2,64,512]{2,1,0:T(8,128)(2,1)S(1)}, u32[]{:S(2)}, u32[]{:S(2)}) collective-permute-start(bf16[2,64,512]{2,1,0:T(8,128)(2,1)S(1)} %get-tuple-element.43), channel_id=1, source_target_pairs={{6,0},{7,1},{14,8},{15,9},{22,16},{23,17},{30,24},{31,25}} | collective-permute-start | bytes 393224 | tf_op jit(solution)/shard_map/ppermute | solution.py:426
  34.5 0.8 %collective-permute-done.11.refs_1_ = bf16[64,768]{1,0:T(8,128)(2,1)S(1)} collective-permute-done((bf16[64,768]{1,0:T(8,128)(2,1)S(1)}, bf16[64,768]{1,0:T(8,128)(2,1)S(1)}, u32[]{:S(2)}, u32[]{:S(2)}) %collective-permute-start.11) | collective-permute-done | bytes 98336 | tf_op jit(solution)/shard_map/ppermute | solution.py:412
  35.3 1.3 %collective-permute-start.9 = (bf16[2,64,512]{2,1,0:T(8,128)(2,1)S(1)}, bf16[2,64,512]{2,1,0:T(8,128)(2,1)S(1)}, u32[]{:S(2)}, u32[]{:S(2)}) collective-permute-start(bf16[2,64,512]{2,1,0:T(8,128)(2,1)S(1)} %get-tuple-element.42), channel_id=1, source_target_pairs={{4,0},{5,1},{6,2},{7,3},{12,8},{13,9},{14,10},{15,11},{20,16},{21,... | collective-permute-start | bytes 393224 | tf_op jit(solution)/shard_map/ppermute | solution.py:426
  36.6 0.7 %collective-permute-done.12.refs_2_ = bf16[64,768]{1,0:T(8,128)(2,1)S(1)} collective-permute-done((bf16[64,768]{1,0:T(8,128)(2,1)S(1)}, bf16[64,768]{1,0:T(8,128)(2,1)S(1)}, u32[]{:S(2)}, u32[]{:S(2)}) %collective-permute-start.12) | collective-permute-done | bytes 98336 | tf_op jit(solution)/shard_map/ppermute | solution.py:412
  37.3 0.0 collective-permute-done.13.refs_3_
  37.3 0.0 collective-permute-done.8.refs_1_.refs_6_
  37.3 1.4 %middle.1 = (bf16[512,128]{1,0:T(8,128)(2,1)}, bf16[64,256]{1,0:T(8,128)(2,1)S(1)}, bf16[64,256]{1,0:T(8,128)(2,1)S(1)}, bf16[64,256]{1,0:T(8,128)(2,1)S(1)}) custom-call(bf16[64,768]{1,0:T(8,128)(2,1)S(1)} %get-tuple-element.47.refs_0_, bf16[64,768]{1,0:T(8,128)(2,1)S(1)} %collective-permute-done.11.refs_1_, ...), custom_call_target="tpu_custom_call" | custom-call | flops 2000000000 | bytes 2097152 | tf_op jit(solution)/shard_map/middle/pallas_call | solution.py:427
  38.7 6.7 %all-to-all-start.1 = ((bf16[32,16,128]{2,1,0:T(8,128)(2,1)}), bf16[32,16,128]{2,1,0:T(8,128)(2,1)S(1)}, u32[]{:S(2)}, u32[]{:S(2)}) async-start(bf16[32,16,128]{2,1,0:T(8,128)(2,1)} %bitcast.4), calls=%async_computation.1 | async-start | bytes 262144 | tf_op jit(solution)/shard_map/all_to_all | solution.py:435
  45.4 0.0 collective-permute-done.10.refs_3_
  45.4 2.4 %collective-permute-done.9.refs_2_ = bf16[2,64,512]{2,1,0:T(8,128)(2,1)S(1)} collective-permute-done((bf16[2,64,512]{2,1,0:T(8,128)(2,1)S(1)}, bf16[2,64,512]{2,1,0:T(8,128)(2,1)S(1)}, u32[]{:S(2)}, u32[]{:S(2)}) %collective-permute-start.9) | collective-permute-done | bytes 131104 | tf_op jit(solution)/shard_map/ppermute | solution.py:426
  47.8 0.7 %close.1 = (bf16[2,64,256]{2,1,0:T(8,128)(2,1)}, bf16[2,64,256]{2,1,0:T(8,128)(2,1)}) custom-call(bf16[2,64,512]{2,1,0:T(8,128)(2,1)S(1)} %get-tuple-element.40.refs_0_, bf16[2,64,512]{2,1,0:T(8,128)(2,1)S(1)} %collective-permute-done.8.refs_1_.refs_6_, bf16[2,64,512]{2,1,0:T(8,128)(2,1)S(1)} %collective-permute-done.9.refs_2_, ...), custom_call_target="tpu_custom_call" | custom-call | flops 60000002048 | bytes 1048576 | tf_op jit(solution)/shard_map/close/pallas_call | solution.py:449
  48.5 1.5 %weight_grads.1 = (f32[1,512,256]{2,1,0:T(8,128)}, f32[1,512,256]{2,1,0:T(8,128)}, f32[1,256,512]{2,1,0:T(8,128)}) custom-call(bf16[64,512]{1,0:T(8,128)(2,1)S(1)} %get-tuple-element.51.input_ref, bf16[64,512]{1,0:T(8,128)(2,1)S(1)} %get-tuple-element.52.grad_ref, bf16[64,256]{1,0:T(8,128)(2,1)S(1)} %get-tuple-element.53.hidden_ref, ...), custom_call_target="tpu_custom_call" | custom-call | flops 2000000000 | bytes 2097152 | tf_op jit(solution)/shard_map/weight_grads/pallas_call | solution.py:438
  50.0 3.6 %all-to-all-done.1 = bf16[32,16,128]{2,1,0:T(8,128)(2,1)S(1)} async-done(((bf16[32,16,128]{2,1,0:T(8,128)(2,1)}), bf16[32,16,128]{2,1,0:T(8,128)(2,1)S(1)}, u32[]{:S(2)}, u32[]{:S(2)}) %all-to-all-start.1) | async-done | bytes 131104 | tf_op jit(solution)/shard_map/all_to_all | solution.py:435
  53.6 1.3 %combine.1 = (bf16[128,2048]{1,0:T(8,128)(2,1)}, bf16[10,128]{1,0:T(8,128)(2,1)}) custom-call(bf16[512,128]{1,0:T(8,128)(2,1)S(1)} %bitcast.9, s32[10,128]{1,0:T(8,128)S(1)} %bitcast.11, bf16[10,128]{1,0:T(8,128)(2,1)S(1)} %bitcast.13, bf16[2,64,256]{2,1,0:T(8,128)(2,1)S(1)} %copy-done.12), custom_call_target="tpu_custom_call" | custom-call | flops 2000000000 | bytes 2097152 | tf_op jit(solution)/shard_map/combine/pallas_call | solution.py:457
  (20 shorter events, 0.0 us)
Async XLA Ops:
  0.6 12.7 %copy-start.3 = (bf16[128,2048]{1,0:T(8,128)(2,1)S(1)}, bf16[128,2048]{1,0:T(8,128)(2,1)}, u32[]{:S(2)}) copy-start(bf16[128,2048]{1,0:T(8,128)(2,1)} %input_ref.1) | copy-start | bytes 1572868
  0.7 12.7 %copy-start.4 = (bf16[128,2048]{1,0:T(8,128)(2,1)S(1)}, bf16[128,2048]{1,0:T(8,128)(2,1)}, u32[]{:S(2)}) copy-start(bf16[128,2048]{1,0:T(8,128)(2,1)} %grad_ref.1) | copy-start | bytes 1572868
  0.7 0.9 %copy-start.8 = (bf16[2,64,256]{2,1,0:T(8,128)(2,1)S(1)}, bf16[2,64,256]{2,1,0:T(8,128)(2,1)}, u32[]{:S(2)}) copy-start(bf16[2,64,256]{2,1,0:T(8,128)(2,1)} %key_hbm.1) | copy-start | bytes 196612
  1.6 0.8 %copy-start.9 = (bf16[2,64,256]{2,1,0:T(8,128)(2,1)S(1)}, bf16[2,64,256]{2,1,0:T(8,128)(2,1)}, u32[]{:S(2)}) copy-start(bf16[2,64,256]{2,1,0:T(8,128)(2,1)} %value_hbm.1) | copy-start | bytes 196612
  2.4 11.0 %copy-start.10 = (s32[128,10]{0,1:T(8,128)S(1)}, s32[128,10]{0,1:T(8,128)}, u32[]{:S(2)}) copy-start(s32[128,10]{0,1:T(8,128)} %param.19) | copy-start | bytes 15364
  2.4 11.0 %copy-start.11 = (bf16[128,10]{0,1:T(8,128)(2,1)S(1)}, bf16[128,10]{0,1:T(8,128)(2,1)}, u32[]{:S(2)}) copy-start(bf16[128,10]{0,1:T(8,128)(2,1)} %param.20) | copy-start | bytes 7684
  2.6 15.2 %collective-permute-start = (bf16[2,64,512]{2,1,0:T(8,128)(2,1)S(1)}, bf16[2,64,512]{2,1,0:T(8,128)(2,1)S(1)}, u32[]{:S(2)}, u32[]{:S(2)}) collective-permute-start(bf16[2,64,512]{2,1,0:T(8,128)(2,1)S(1)} %pack.1.refs_3_.after_ref), channel_id=1, source_target_pairs={{0,2},{1,3},{2,4},{3,5},{4,6},{5,7},{8,10},{9,11},{10,12},{11,13},... | collective-permute-start | bytes 393224 | tf_op jit(solution)/shard_map/ppermute | solution.py:381
  7.6 10.5 %collective-permute-start.1 = (bf16[2,64,512]{2,1,0:T(8,128)(2,1)S(1)}, bf16[2,64,512]{2,1,0:T(8,128)(2,1)S(1)}, u32[]{:S(2)}, u32[]{:S(2)}) collective-permute-start(bf16[2,64,512]{2,1,0:T(8,128)(2,1)S(1)} %pack.1.refs_3_.after_ref), channel_id=1, source_target_pairs={{0,4},{1,5},{2,6},{3,7},{8,12},{9,13},{10,14},{11,15},{16,20},{17,... | collective-permute-start | bytes 393224 | tf_op jit(solution)/shard_map/ppermute | solution.py:381
  12.1 6.3 %collective-permute-start.2 = (bf16[2,64,512]{2,1,0:T(8,128)(2,1)S(1)}, bf16[2,64,512]{2,1,0:T(8,128)(2,1)S(1)}, u32[]{:S(2)}, u32[]{:S(2)}) collective-permute-start(bf16[2,64,512]{2,1,0:T(8,128)(2,1)S(1)} %pack.1.refs_3_.after_ref), channel_id=1, source_target_pairs={{0,6},{1,7},{8,14},{9,15},{16,22},{17,23},{24,30},{25,31}} | collective-permute-start | bytes 393224 | tf_op jit(solution)/shard_map/ppermute | solution.py:381
  13.4 6.3 %copy-start = (bf16[2,64,2048]{2,1,0:T(8,128)(2,1)S(1)}, bf16[2,64,2048]{2,1,0:T(8,128)(2,1)}, u32[]{:S(2)}) copy-start(bf16[2,64,2048]{2,1,0:T(8,128)(2,1)} %refs_0_.1) | copy-start | bytes 1572868
  13.4 6.3 %copy-start.1 = (bf16[2,64,2048]{2,1,0:T(8,128)(2,1)S(1)}, bf16[2,64,2048]{2,1,0:T(8,128)(2,1)}, u32[]{:S(2)}) copy-start(bf16[2,64,2048]{2,1,0:T(8,128)(2,1)} %refs_1_.1) | copy-start | bytes 1572868
  13.4 6.3 %copy-start.2 = (bf16[2,64,2048]{2,1,0:T(8,128)(2,1)S(1)}, bf16[2,64,2048]{2,1,0:T(8,128)(2,1)}, u32[]{:S(2)}) copy-start(bf16[2,64,2048]{2,1,0:T(8,128)(2,1)} %refs_2_.1) | copy-start | bytes 1572868
  14.7 11.0 %all-to-all-start = ((bf16[32,16,128]{2,1,0:T(8,128)(2,1)}), bf16[32,16,128]{2,1,0:T(8,128)(2,1)S(1)}, u32[]{:S(2)}, u32[]{:S(2)}) async-start(bf16[32,16,128]{2,1,0:T(8,128)(2,1)} %bitcast.2), calls=%async_computation | async-start | bytes 262144 | tf_op jit(solution)/shard_map/all_to_all | solution.py:393
  17.5 1.4 %collective-permute-start.3 = (bf16[2,64,512]{2,1,0:T(8,128)(2,1)S(1)}, bf16[2,64,512]{2,1,0:T(8,128)(2,1)S(1)}, u32[]{:S(2)}, u32[]{:S(2)}) collective-permute-start(bf16[2,64,512]{2,1,0:T(8,128)(2,1)S(1)} %pack.1.refs_3_.after_ref), channel_id=1, source_target_pairs={{0,1},{1,0},{2,3},{3,2},{4,5},{5,4},{6,7},{7,6},{8,9},{9,8},{10,11... | collective-permute-start | bytes 393224 | tf_op jit(solution)/shard_map/ppermute | solution.py:382
  17.8 1.3 %collective-permute-start.4 = (bf16[2,64,512]{2,1,0:T(8,128)(2,1)S(1)}, bf16[2,64,512]{2,1,0:T(8,128)(2,1)S(1)}, u32[]{:S(2)}, u32[]{:S(2)}) collective-permute-start(bf16[2,64,512]{2,1,0:T(8,128)(2,1)S(1)} %collective-permute-done.refs_4_), channel_id=1, source_target_pairs={{0,1},{1,0},{2,3},{3,2},{4,5},{5,4},{6,7},{7,6},{8,9},{9,8},{10,11... | collective-permute-start | bytes 393224 | tf_op jit(solution)/shard_map/ppermute | solution.py:382
  18.1 1.3 %collective-permute-start.5 = (bf16[2,64,512]{2,1,0:T(8,128)(2,1)S(1)}, bf16[2,64,512]{2,1,0:T(8,128)(2,1)S(1)}, u32[]{:S(2)}, u32[]{:S(2)}) collective-permute-start(bf16[2,64,512]{2,1,0:T(8,128)(2,1)S(1)} %collective-permute-done.1.refs_5_), channel_id=1, source_target_pairs={{0,1},{1,0},{2,3},{3,2},{4,5},{5,4},{6,7},{7,6},{8,9},{9,8},{10,11... | collective-permute-start | bytes 393224 | tf_op jit(solution)/shard_map/ppermute | solution.py:382
  18.3 1.3 %collective-permute-start.6 = (bf16[2,64,512]{2,1,0:T(8,128)(2,1)S(1)}, bf16[2,64,512]{2,1,0:T(8,128)(2,1)S(1)}, u32[]{:S(2)}, u32[]{:S(2)}) collective-permute-start(bf16[2,64,512]{2,1,0:T(8,128)(2,1)S(1)} %collective-permute-done.2.refs_6_), channel_id=1, source_target_pairs={{0,1},{1,0},{2,3},{3,2},{4,5},{5,4},{6,7},{7,6},{8,9},{9,8},{10,11... | collective-permute-start | bytes 393224 | tf_op jit(solution)/shard_map/ppermute | solution.py:382
  25.7 1.9 %collective-permute-start.7 = (bf16[4,2,64,512]{3,2,1,0:T(8,128)(2,1)S(1)}, bf16[4,2,64,512]{3,2,1,0:T(8,128)(2,1)S(1)}, u32[]{:S(2)}, u32[]{:S(2)}) collective-permute-start(bf16[4,2,64,512]{3,2,1,0:T(8,128)(2,1)S(1)} %gate.1.after_ref), channel_id=1, source_target_pairs={{0,1},{1,0},{2,3},{3,2},{4,5},{5,4},{6,7},{7,6},{8,9},{9,8},{10,11... | collective-permute-start | bytes 1572872 | tf_op jit(solution)/shard_map/ppermute | solution.py:415
  27.6 1.6 %copy-start.5 = (bf16[1,256,512]{2,1,0:T(8,128)(2,1)S(1)}, bf16[1,256,512]{2,1,0:T(8,128)(2,1)}, u32[]{:S(2)}) copy-start(bf16[1,256,512]{2,1,0:T(8,128)(2,1)} %down_ref.1) | copy-start | bytes 786436
  27.6 1.6 %copy-start.6 = (bf16[1,512,256]{2,1,0:T(8,128)(2,1)S(1)}, bf16[1,512,256]{2,1,0:T(8,128)(2,1)}, u32[]{:S(2)}) copy-start(bf16[1,512,256]{2,1,0:T(8,128)(2,1)} %refs_4_.1) | copy-start | bytes 786436
  27.6 1.6 %copy-start.7 = (bf16[1,512,256]{2,1,0:T(8,128)(2,1)S(1)}, bf16[1,512,256]{2,1,0:T(8,128)(2,1)}, u32[]{:S(2)}) copy-start(bf16[1,512,256]{2,1,0:T(8,128)(2,1)} %refs_5_.1) | copy-start | bytes 786436
  27.7 9.5 %collective-permute-start.8 = (bf16[2,64,512]{2,1,0:T(8,128)(2,1)S(1)}, bf16[2,64,512]{2,1,0:T(8,128)(2,1)S(1)}, u32[]{:S(2)}, u32[]{:S(2)}) collective-permute-start(bf16[2,64,512]{2,1,0:T(8,128)(2,1)S(1)} %get-tuple-element.41), channel_id=1, source_target_pairs={{2,0},{3,1},{4,2},{5,3},{6,4},{7,5},{10,8},{11,9},{12,10},{13,11},... | collective-permute-start | bytes 393224 | tf_op jit(solution)/shard_map/ppermute | solution.py:426
  29.6 5.6 %collective-permute-start.11 = (bf16[64,768]{1,0:T(8,128)(2,1)S(1)}, bf16[64,768]{1,0:T(8,128)(2,1)S(1)}, u32[]{:S(2)}, u32[]{:S(2)}) collective-permute-start(bf16[64,768]{1,0:T(8,128)(2,1)S(1)} %get-tuple-element.47.refs_0_), channel_id=1, source_target_pairs={{0,8},{8,0},{16,24},{24,16},{1,9},{9,1},{17,25},{25,17},{2,10},{10... | collective-permute-start | bytes 294920 | tf_op jit(solution)/shard_map/ppermute | solution.py:412
  30.5 6.7 %collective-permute-start.12 = (bf16[64,768]{1,0:T(8,128)(2,1)S(1)}, bf16[64,768]{1,0:T(8,128)(2,1)S(1)}, u32[]{:S(2)}, u32[]{:S(2)}) collective-permute-start(bf16[64,768]{1,0:T(8,128)(2,1)S(1)} %get-tuple-element.47.refs_0_), channel_id=1, source_target_pairs={{0,16},{8,24},{16,0},{24,8},{1,17},{9,25},{17,1},{25,9},{2,18},{10... | collective-permute-start | bytes 294920 | tf_op jit(solution)/shard_map/ppermute | solution.py:412
  31.2 6.0 %collective-permute-start.13 = (bf16[64,768]{1,0:T(8,128)(2,1)S(1)}, bf16[64,768]{1,0:T(8,128)(2,1)S(1)}, u32[]{:S(2)}, u32[]{:S(2)}) collective-permute-start(bf16[64,768]{1,0:T(8,128)(2,1)S(1)} %get-tuple-element.47.refs_0_), channel_id=1, source_target_pairs={{0,24},{8,16},{16,8},{24,0},{1,25},{9,17},{17,9},{25,1},{2,26},{10... | collective-permute-start | bytes 294920 | tf_op jit(solution)/shard_map/ppermute | solution.py:412
  33.2 12.2 %collective-permute-start.10 = (bf16[2,64,512]{2,1,0:T(8,128)(2,1)S(1)}, bf16[2,64,512]{2,1,0:T(8,128)(2,1)S(1)}, u32[]{:S(2)}, u32[]{:S(2)}) collective-permute-start(bf16[2,64,512]{2,1,0:T(8,128)(2,1)S(1)} %get-tuple-element.43), channel_id=1, source_target_pairs={{6,0},{7,1},{14,8},{15,9},{22,16},{23,17},{30,24},{31,25}} | collective-permute-start | bytes 393224 | tf_op jit(solution)/shard_map/ppermute | solution.py:426
  35.3 12.5 %collective-permute-start.9 = (bf16[2,64,512]{2,1,0:T(8,128)(2,1)S(1)}, bf16[2,64,512]{2,1,0:T(8,128)(2,1)S(1)}, u32[]{:S(2)}, u32[]{:S(2)}) collective-permute-start(bf16[2,64,512]{2,1,0:T(8,128)(2,1)S(1)} %get-tuple-element.42), channel_id=1, source_target_pairs={{4,0},{5,1},{6,2},{7,3},{12,8},{13,9},{14,10},{15,11},{20,16},{21,... | collective-permute-start | bytes 393224 | tf_op jit(solution)/shard_map/ppermute | solution.py:426
  38.7 14.9 %all-to-all-start.1 = ((bf16[32,16,128]{2,1,0:T(8,128)(2,1)}), bf16[32,16,128]{2,1,0:T(8,128)(2,1)S(1)}, u32[]{:S(2)}, u32[]{:S(2)}) async-start(bf16[32,16,128]{2,1,0:T(8,128)(2,1)} %bitcast.4), calls=%async_computation.1 | async-start | bytes 262144 | tf_op jit(solution)/shard_map/all_to_all | solution.py:435
  48.5 5.0 %copy-start.12 = (bf16[2,64,256]{2,1,0:T(8,128)(2,1)S(1)}, bf16[2,64,256]{2,1,0:T(8,128)(2,1)}, u32[]{:S(2)}) copy-start(bf16[2,64,256]{2,1,0:T(8,128)(2,1)} %get-tuple-element.26.after_ref) | copy-start | bytes 196612

commit v7 on v6

--- a/solution.py
+++ b/solution.py
@@ -62,9 +62,9 @@
 def attention_kernel(chips, *refs):
     q_ref, logit_ref, grad_ref = refs[:3]
     kv_refs = refs[3 : 3 + 2 * chips]
-    query_grad_hbm, gate_grad_hbm, other_ref = refs[3 + 2 * chips : 6 + 2 * chips]
-    mine_refs = refs[6 + 2 * chips : 6 + 3 * chips]
-    query_grad_ref, gate_grad_ref, out_sems = refs[6 + 3 * chips :]
+    query_grad_hbm, gate_grad_hbm, other_ref = refs[4 + 2 * chips : 7 + 2 * chips]
+    mine_refs = refs[7 + 2 * chips : 7 + 3 * chips]
+    query_grad_ref, gate_grad_ref, out_sems = refs[7 + 3 * chips :]
     seqs, length, _ = q_ref.shape
     side = chips * length
     scale = HEAD ** (-0.5)
@@ -123,14 +123,14 @@
         store.wait()
 
 
-def attention(query_rows, gate_logits, gated_grad, pieces):
+def attention(query_rows, gate_logits, gated_grad, pieces, after):
     seqs, length, width = query_rows.shape
     chips = len(pieces) // 2
     full = jax.ShapeDtypeStruct((seqs, length, width), BF16)
     part = jax.ShapeDtypeStruct(pieces[0].shape, BF16)
     out = pl.pallas_call(
         functools.partial(attention_kernel, chips),
-        in_specs=[IN_VMEM] * (3 + 2 * chips),
+        in_specs=[IN_VMEM] * (3 + 2 * chips) + [ANYWHERE],
         out_specs=[IN_HBM] * 2 + [IN_VMEM] * (1 + chips),
         out_shape=[full] * 2 + [jax.ShapeDtypeStruct((chips,) + part.shape, BF16)] + [part] * chips,
         scratch_shapes=[pltpu.VMEM(query_rows.shape, BF16)] * 2
@@ -138,7 +138,7 @@
         compiler_params=params(ATTENTION_MIB if chips <= 4 else 56),
         cost_estimate=cost(MIB, 8),
         name="attention",
-    )(query_rows, gate_logits, gated_grad, *pieces)
+    )(query_rows, gate_logits, gated_grad, *pieces, after)
     return out[0], out[1], out[2], out[3:]
 
 
@@ -192,9 +192,28 @@
 
 
 def dispatch_kernel(
-    experts, groups, rows, input_ref, grad_ref, routes_ref, weights_ref, after_ref, out_ref
+    experts,
+    groups,
+    rows,
+    input_hbm,
+    grad_hbm,
+    routes_hbm,
+    weights_hbm,
+    out_ref,
+    input_ref,
+    grad_ref,
+    routes_ref,
+    weights_ref,
+    sems,
 ):
     tokens, width = input_ref.shape
+    pairs = ((routes_hbm, routes_ref), (weights_hbm, weights_ref))
+    pairs = pairs + ((input_hbm, input_ref), (grad_hbm, grad_ref))
+    copies = [pltpu.make_async_copy(src, dst, sems.at[i]) for i, (src, dst) in enumerate(pairs)]
+    for copy in copies:
+        copy.start()
+    copies[0].wait()
+    copies[1].wait()
     slot, weight, _ = slots(routes_ref, weights_ref, experts)
     share = width // groups
     pieces = share // LANES
@@ -204,6 +223,8 @@
     inner = mod(row, rows)
     hit = slot == div(row, rows) * CAP + mod(div(inner, pieces), CAP)
     hit = jnp.where(hit, mod(inner, pieces) + pieces * div(inner, CAP * pieces), -1)
+    copies[2].wait()
+    copies[3].wait()
     acc = None
     for a, (ref, value) in enumerate(((input_ref, 1.0), (grad_ref, weight))):
         for l in range(pieces):
@@ -251,8 +272,8 @@
 
 
 def middle_kernel(sources, rows, *refs):
-    parts = refs[:-7]
-    gate_ref, up_ref, _, back_ref, hidden_ref, gate_rows_ref, up_rows_ref = refs[-7:]
+    parts = refs[:-6]
+    gate_ref, up_ref, back_ref, hidden_ref, gate_rows_ref, up_rows_ref = refs[-6:]
     share = gate_ref.shape[1]
     pieces = share // LANES
     hid = gate_ref.shape[2]
@@ -372,7 +393,7 @@
         out_shape=jax.ShapeDtypeStruct((seqs, length, 2 * HEAD), BF16),
         scratch_shapes=[pltpu.VMEM(key_rows.shape, BF16)] * 2 + [pltpu.SemaphoreType.DMA((2,))],
         compiler_params=params(16),
-        cost_estimate=cost(6e10, MIB),
+        cost_estimate=cost(MIB, MIB),
         name="pack",
     )(key_rows, value_rows)
     mine = [packed]
@@ -384,20 +405,23 @@
     routes_t, weights_t = routes.T, route_weights.T
     send = pl.pallas_call(
         functools.partial(dispatch_kernel, devices, groups, rows),
-        in_specs=[IN_VMEM] * 4 + [ANYWHERE],
+        in_specs=[IN_HBM] * 4,
         out_shape=jax.ShapeDtypeStruct((sources * rows, LANES), BF16),
-        compiler_params=params(16),
+        scratch_shapes=[
+            pltpu.VMEM(moe_input.shape, BF16),
+            pltpu.VMEM(out_grad.shape, BF16),
+            pltpu.VMEM(routes_t.shape, routes.dtype),
+            pltpu.VMEM(weights_t.shape, BF16),
+            pltpu.SemaphoreType.DMA((4,)),
+        ],
+        compiler_params=params(60),
         cost_estimate=cost(2e9, 2 * MIB),
         name="dispatch",
-    )(moe_input, out_grad, routes_t, weights_t, packed)
+    )(moe_input, out_grad, routes_t, weights_t)
     recv = lax.all_to_all(
         send.reshape(sources, rows, LANES), axes, split_axis=0, concat_axis=0, tiled=True
     ).reshape(sources * rows, LANES)
 
-    query_grad, gate_grad, other_part, mine_part = attention(
-        query_rows, gate_logits, gated_grad, mine + other
-    )
-    other_part = gate(other_part, recv)
     slot_rows = jax.ShapeDtypeStruct((sources * CAP, share), BF16)
     hid_rows = jax.ShapeDtypeStruct((sources * CAP, hid), BF16)
     inputs, grads, sent = pl.pallas_call(
@@ -407,11 +431,22 @@
         compiler_params=params(16),
         cost_estimate=cost(2e9, 2 * MIB),
         name="enter",
-    )(recv, gate_proj, up_proj, down_proj, other_part)
+    )(recv, gate_proj, up_proj, down_proj, mine[min(1, chips - 1)])
     parts = [sent] + [
         lax.ppermute(sent, "dp", [(g, g ^ k) for g in range(groups)]) for k in range(1, groups)
     ]
 
+    back, hidden, gate_rows, up_rows = pl.pallas_call(
+        functools.partial(middle_kernel, sources, rows),
+        in_specs=[IN_VMEM] * (len(parts) + 2),
+        out_shape=[jax.ShapeDtypeStruct((sources * rows, LANES), BF16)] + [hid_rows] * 3,
+        compiler_params=params(16 if groups <= 4 else 60),
+        cost_estimate=cost(1e9, MIB),
+        name="middle",
+    )(*parts, gate_proj, up_proj)
+    query_grad, gate_grad, other_part, mine_part = attention(
+        query_rows, gate_logits, gated_grad, mine + other, hidden
+    )
     arrived = lax.ppermute(other_part, "expert", swap)
     merged = pl.pallas_call(
         functools.partial(merge_kernel, chips),
@@ -424,14 +459,6 @@
     for d in range(1, chips):
         down = [(i, i - 2 * d) for i in range(2 * d, devices)]
         terms.append(lax.ppermute(merged[d], "expert", down))
-    back, hidden, gate_rows, up_rows = pl.pallas_call(
-        functools.partial(middle_kernel, sources, rows),
-        in_specs=[IN_VMEM] * (len(parts) + 2) + [ANYWHERE],
-        out_shape=[jax.ShapeDtypeStruct((sources * rows, LANES), BF16)] + [hid_rows] * 3,
-        compiler_params=params(16 if groups <= 4 else 60),
-        cost_estimate=cost(2e9, 2 * MIB),
-        name="middle",
-    )(*parts, gate_proj, up_proj, terms[min(1, chips - 1)])
     returned = lax.all_to_all(
         back.reshape(sources, rows, LANES), axes, split_axis=0, concat_axis=0, tiled=True
     ).reshape(sources * rows, LANES)

time: 55.3 us -> 60 us (1.085)
  waiting for transfers between devices: 12.4 us -> 16 us
  Pallas kernels: 10.6 us -> 11.7 us
  local copies, waits for them, and re-layouts: 1.81 us -> 0.89 us
  starting transfers between devices: 29.2 us -> 30 us
    ppermute x3, waiting for transfers between devices: 2.43 us -> 12.3 us  [shards(): terms.append(lax.ppermute(merged[d], 'expert', down))]
    all_to_all x1, starting transfers between devices: 2.81 us -> 7.3 us  [shards(): lax.all_to_all(send.reshape(sources, rows, LANES), axes, split_axis=0, co...]
    all_to_all x1, waiting for transfers between devices: 3.57 us -> 0.01 us  [shards(): lax.all_to_all(back.reshape(sources, rows, LANES), axes, split_axis=0, co...]
    all_to_all x1, waiting for transfers between devices: 2.26 us -> 0.01 us  [shards(): lax.all_to_all(send.reshape(sources, rows, LANES), axes, split_axis=0, co...]
    ppermute x3, waiting for transfers between devices: 1.48 us -> 3.64 us  [shards(): lax.ppermute(sent, 'dp', [(g, g ^ k) for g in range(groups)])]
    ppermute x3, starting transfers between devices: 10.7 us -> 8.67 us  [shards(): mine.append(lax.ppermute(packed, 'expert', up))]
    ppermute x1, waiting for transfers between devices: 1.6 us -> 0.01 us  [shards(): arrived = lax.ppermute(other_part, 'expert', swap)]
    pallas_call x1, Pallas kernels: 1.23 us -> 2.41 us  [shards(): pl.pallas_call(functools.partial(dispatch_kernel, devices, groups, rows),...]
  transfers between devices with their start and end apart: 16 -> 16, of which waited for: 10 -> 5; matrix products, arithmetic and copies ran while one was open for 0% -> 0% of each run, Pallas kernels for 16% -> 7%
where the time goes in v7:
time: 60 us; the launch traced here: 59.6 us
  starting transfers between devices  30 us (50%)
  waiting for transfers between devices  16 us (27%)
  Pallas kernels  11.7 us (20%)
  between operations  0.93 us (2%)
  local copies, waits for them, and re-layouts  0.89 us (1%)
    ppermute x3, waiting for transfers between devices, shards(): terms.append(lax.ppermute(merged[d], 'expert', down))  12.3 us
    ppermute x3, starting transfers between devices, shards(): mine.append(lax.ppermute(packed, 'expert', up))  8.67 us
    all_to_all x1, starting transfers between devices, shards(): lax.all_to_all(send.reshape(sources, rows, LANES), axes, split_axis=0, co...  7.3 us
    all_to_all x1, starting transfers between devices, shards(): lax.all_to_all(back.reshape(sources, rows, LANES), axes, split_axis=0, co...  5.73 us
    ppermute x3, starting transfers between devices, shards(): terms.append(lax.ppermute(merged[d], 'expert', down))  3.88 us
    pallas_call x1, Pallas kernels, attention(): pl.pallas_call(functools.partial(attention_kernel, chips), in_specs=[IN_V...  3.7 us
    ppermute x3, waiting for transfers between devices, shards(): lax.ppermute(sent, 'dp', [(g, g ^ k) for g in range(groups)])  3.64 us
    ppermute x3, starting transfers between devices, shards(): lax.ppermute(sent, 'dp', [(g, g ^ k) for g in range(groups)])  3.55 us
  transfers between devices with their start and end apart: 16, of which 5 were waited for; matrix products, arithmetic and copies ran while one was open for 0% of the time, Pallas kernels for 7%

profile of v7, /device:TPU:0, one launch (start us, length us, event | category | flops | bytes accessed | tf_op | source)
XLA Modules:
  0.0 59.6 jit_solution(10874476278519582347)
XLA Ops:
  0.7 2.4 %dispatch.1 = bf16[512,128]{1,0:T(8,128)(2,1)} custom-call(bf16[128,2048]{1,0:T(8,128)(2,1)} %input_hbm.1, bf16[128,2048]{1,0:T(8,128)(2,1)} %grad_hbm.1, s32[10,128]{1,0:T(8,128)} %bitcast.9, bf16[10,128]{1,0:T(8,128)(2,1)} %bitcast.11), custom_call_target="tpu_custom_call" | custom-call | flops 2000000000 | bytes 2097152 | tf_op jit(solution)/shard_map/dispatch/pallas_call | solution.py:406
  3.1 0.0 copy-start.3
  3.1 0.0 copy-start.4
  3.1 0.0 copy-start.5
  3.1 7.3 %all-to-all-start = ((bf16[32,16,128]{2,1,0:T(8,128)(2,1)}), bf16[32,16,128]{2,1,0:T(8,128)(2,1)S(1)}, u32[]{:S(2)}, u32[]{:S(2)}) async-start(bf16[32,16,128]{2,1,0:T(8,128)(2,1)} %bitcast.13), calls=%async_computation | async-start | bytes 262144 | tf_op jit(solution)/shard_map/all_to_all | solution.py:421
  10.4 0.2 pack.1.refs_3_
  10.7 3.7 %collective-permute-start = (bf16[2,64,512]{2,1,0:T(8,128)(2,1)S(1)}, bf16[2,64,512]{2,1,0:T(8,128)(2,1)S(1)}, u32[]{:S(2)}, u32[]{:S(2)}) collective-permute-start(bf16[2,64,512]{2,1,0:T(8,128)(2,1)S(1)} %pack.1.refs_3_), channel_id=1, source_target_pairs={{0,2},{1,3},{2,4},{3,5},{4,6},{5,7},{8,10},{9,11},{10,12},{11,13},... | collective-permute-start | bytes 393224 | tf_op jit(solution)/shard_map/ppermute | solution.py:402
  14.3 3.1 %collective-permute-start.2 = (bf16[2,64,512]{2,1,0:T(8,128)(2,1)S(1)}, bf16[2,64,512]{2,1,0:T(8,128)(2,1)S(1)}, u32[]{:S(2)}, u32[]{:S(2)}) collective-permute-start(bf16[2,64,512]{2,1,0:T(8,128)(2,1)S(1)} %pack.1.refs_3_), channel_id=1, source_target_pairs={{0,6},{1,7},{8,14},{9,15},{16,22},{17,23},{24,30},{25,31}} | collective-permute-start | bytes 393224 | tf_op jit(solution)/shard_map/ppermute | solution.py:402
  17.5 1.8 %collective-permute-start.1 = (bf16[2,64,512]{2,1,0:T(8,128)(2,1)S(1)}, bf16[2,64,512]{2,1,0:T(8,128)(2,1)S(1)}, u32[]{:S(2)}, u32[]{:S(2)}) collective-permute-start(bf16[2,64,512]{2,1,0:T(8,128)(2,1)S(1)} %pack.1.refs_3_), channel_id=1, source_target_pairs={{0,4},{1,5},{2,6},{3,7},{8,12},{9,13},{10,14},{11,15},{16,20},{17,... | collective-permute-start | bytes 393224 | tf_op jit(solution)/shard_map/ppermute | solution.py:402
  19.3 0.0 collective-permute-done.after_ref.refs_4_
  19.4 0.0 all-to-all-done
  19.4 0.5 enter.1
  19.9 0.0 copy-start
  19.9 0.0 copy-start.1
  19.9 0.0 copy-start.2
  19.9 2.5 %collective-permute-start.9 = (bf16[64,768]{1,0:T(8,128)(2,1)S(1)}, bf16[64,768]{1,0:T(8,128)(2,1)S(1)}, u32[]{:S(2)}, u32[]{:S(2)}) collective-permute-start(bf16[64,768]{1,0:T(8,128)(2,1)S(1)} %get-tuple-element.34.refs_0_), channel_id=1, source_target_pairs={{0,24},{8,16},{16,8},{24,0},{1,25},{9,17},{17,9},{25,1},{2,26},{10... | collective-permute-start | bytes 294920 | tf_op jit(solution)/shard_map/ppermute | solution.py:436
  22.4 0.5 collective-permute-start.8
  22.9 0.5 collective-permute-start.7
  23.5 0.0 collective-permute-done.2.refs_6_
  23.5 0.0 collective-permute-start.3
  23.5 0.0 collective-permute-done.1.refs_5_
  23.5 0.5 collective-permute-start.6
  24.0 1.6 %collective-permute-done.9.refs_3_ = bf16[64,768]{1,0:T(8,128)(2,1)S(1)} collective-permute-done((bf16[64,768]{1,0:T(8,128)(2,1)S(1)}, bf16[64,768]{1,0:T(8,128)(2,1)S(1)}, u32[]{:S(2)}, u32[]{:S(2)}) %collective-permute-start.9) | collective-permute-done | bytes 98336 | tf_op jit(solution)/shard_map/ppermute | solution.py:436
  25.6 0.0 collective-permute-start.5
  25.6 1.8 %collective-permute-done.8.refs_2_ = bf16[64,768]{1,0:T(8,128)(2,1)S(1)} collective-permute-done((bf16[64,768]{1,0:T(8,128)(2,1)S(1)}, bf16[64,768]{1,0:T(8,128)(2,1)S(1)}, u32[]{:S(2)}, u32[]{:S(2)}) %collective-permute-start.8) | collective-permute-done | bytes 98336 | tf_op jit(solution)/shard_map/ppermute | solution.py:436
  27.4 0.0 collective-permute-start.4
  27.4 0.2 collective-permute-done.7.refs_1_
  27.6 1.4 %middle.1 = (bf16[512,128]{1,0:T(8,128)(2,1)}, bf16[64,256]{1,0:T(8,128)(2,1)S(1)}, bf16[64,256]{1,0:T(8,128)(2,1)S(1)}, bf16[64,256]{1,0:T(8,128)(2,1)S(1)}) custom-call(bf16[64,768]{1,0:T(8,128)(2,1)S(1)} %get-tuple-element.34.refs_0_, bf16[64,768]{1,0:T(8,128)(2,1)S(1)} %collective-permute-done.7.refs_1_, ...), custom_call_target="tpu_custom_call" | custom-call | flops 1000000000 | bytes 1048576 | tf_op jit(solution)/shard_map/middle/pallas_call | solution.py:439
  29.0 0.0 collective-permute-done.3.refs_7_
  29.0 0.0 collective-permute-done.6.refs_10_
  29.0 0.0 collective-permute-done.5.refs_9_
  29.1 0.0 collective-permute-done.4.refs_8_
  29.1 3.7 %attention.1 = (bf16[2,64,2048]{2,1,0:T(8,128)(2,1)}, bf16[2,64,2048]{2,1,0:T(8,128)(2,1)}, bf16[4,2,64,512]{3,2,1,0:T(8,128)(2,1)S(1)}, bf16[2,64,512]{2,1,0:T(...) custom-call(bf16[2,64,2048]{2,1,0:T(8,128)(2,1)S(1)} %copy-done, ...), custom_call_target="tpu_custom_call" | custom-call | flops 1048576 | bytes 8 | tf_op jit(solution)/shard_map/attention/pallas_call | solution.py:131
  32.8 0.4 collective-permute-start.10
  33.2 5.7 %all-to-all-start.1 = ((bf16[32,16,128]{2,1,0:T(8,128)(2,1)}), bf16[32,16,128]{2,1,0:T(8,128)(2,1)S(1)}, u32[]{:S(2)}, u32[]{:S(2)}) async-start(bf16[32,16,128]{2,1,0:T(8,128)(2,1)} %bitcast.4), calls=%async_computation.1 | async-start | bytes 262144 | tf_op jit(solution)/shard_map/all_to_all | solution.py:462
  38.9 0.0 collective-permute-done.10.refs_4_
  38.9 0.1 merge.1
  39.1 1.3 %collective-permute-start.11 = (bf16[2,64,512]{2,1,0:T(8,128)(2,1)S(1)}, bf16[2,64,512]{2,1,0:T(8,128)(2,1)S(1)}, u32[]{:S(2)}, u32[]{:S(2)}) collective-permute-start(bf16[2,64,512]{2,1,0:T(8,128)(2,1)S(1)} %get-tuple-element.43), channel_id=1, source_target_pairs={{2,0},{3,1},{4,2},{5,3},{6,4},{7,5},{10,8},{11,9},{12,10},{13,11},... | collective-permute-start | bytes 393224 | tf_op jit(solution)/shard_map/ppermute | solution.py:461
  40.4 1.3 %collective-permute-start.12 = (bf16[2,64,512]{2,1,0:T(8,128)(2,1)S(1)}, bf16[2,64,512]{2,1,0:T(8,128)(2,1)S(1)}, u32[]{:S(2)}, u32[]{:S(2)}) collective-permute-start(bf16[2,64,512]{2,1,0:T(8,128)(2,1)S(1)} %get-tuple-element.44), channel_id=1, source_target_pairs={{4,0},{5,1},{6,2},{7,3},{12,8},{13,9},{14,10},{15,11},{20,16},{21,... | collective-permute-start | bytes 393224 | tf_op jit(solution)/shard_map/ppermute | solution.py:461
  41.7 1.3 %collective-permute-start.13 = (bf16[2,64,512]{2,1,0:T(8,128)(2,1)S(1)}, bf16[2,64,512]{2,1,0:T(8,128)(2,1)S(1)}, u32[]{:S(2)}, u32[]{:S(2)}) collective-permute-start(bf16[2,64,512]{2,1,0:T(8,128)(2,1)S(1)} %get-tuple-element.45), channel_id=1, source_target_pairs={{6,0},{7,1},{14,8},{15,9},{22,16},{23,17},{30,24},{31,25}} | collective-permute-start | bytes 393224 | tf_op jit(solution)/shard_map/ppermute | solution.py:461
  43.0 1.5 %weight_grads.1 = (f32[1,512,256]{2,1,0:T(8,128)}, f32[1,512,256]{2,1,0:T(8,128)}, f32[1,256,512]{2,1,0:T(8,128)}) custom-call(bf16[64,512]{1,0:T(8,128)(2,1)S(1)} %get-tuple-element.52.input_ref, bf16[64,512]{1,0:T(8,128)(2,1)S(1)} %get-tuple-element.53.grad_ref, bf16[64,256]{1,0:T(8,128)(2,1)S(1)} %get-tuple-element.35.refs_11_.hidden_ref, ...), custom_call_target="tpu_custom_call" | custom-call | flops 2000000000 | bytes 2097152 | tf_op jit(solution)/shard_map/weight_grads/pallas_call | solution.py:465
  44.5 3.1 %collective-permute-done.11.refs_1_ = bf16[2,64,512]{2,1,0:T(8,128)(2,1)S(1)} collective-permute-done((bf16[2,64,512]{2,1,0:T(8,128)(2,1)S(1)}, bf16[2,64,512]{2,1,0:T(8,128)(2,1)S(1)}, u32[]{:S(2)}, u32[]{:S(2)}) %collective-permute-start.11) | collective-permute-done | bytes 131104 | tf_op jit(solution)/shard_map/ppermute | solution.py:461
  47.5 9.2 %collective-permute-done.12.refs_2_ = bf16[2,64,512]{2,1,0:T(8,128)(2,1)S(1)} collective-permute-done((bf16[2,64,512]{2,1,0:T(8,128)(2,1)S(1)}, bf16[2,64,512]{2,1,0:T(8,128)(2,1)S(1)}, u32[]{:S(2)}, u32[]{:S(2)}) %collective-permute-start.12) | collective-permute-done | bytes 131104 | tf_op jit(solution)/shard_map/ppermute | solution.py:461
  56.7 0.0 collective-permute-done.13.refs_3_
  56.8 0.7 %close.1 = (bf16[2,64,256]{2,1,0:T(8,128)(2,1)}, bf16[2,64,256]{2,1,0:T(8,128)(2,1)}) custom-call(bf16[2,64,512]{2,1,0:T(8,128)(2,1)S(1)} %get-tuple-element.42.refs_0_, bf16[2,64,512]{2,1,0:T(8,128)(2,1)S(1)} %collective-permute-done.11.refs_1_, bf16[2,64,512]{2,1,0:T(8,128)(2,1)S(1)} %collective-permute-done.12.refs_2_, ...), custom_call_target="tpu_custom_call" | custom-call | flops 60000002048 | bytes 1048576 | tf_op jit(solution)/shard_map/close/pallas_call | solution.py:476
  57.5 0.0 copy-start.10
  57.5 0.8 %copy-done.10 = bf16[2,64,256]{2,1,0:T(8,128)(2,1)S(1)} copy-done((bf16[2,64,256]{2,1,0:T(8,128)(2,1)S(1)}, bf16[2,64,256]{2,1,0:T(8,128)(2,1)}, u32[]{:S(2)}) %copy-start.10) | copy-done | bytes 65560
  58.3 1.3 %combine.1 = (bf16[128,2048]{1,0:T(8,128)(2,1)}, bf16[10,128]{1,0:T(8,128)(2,1)}) custom-call(bf16[512,128]{1,0:T(8,128)(2,1)S(1)} %bitcast.7, s32[10,128]{1,0:T(8,128)S(1)} %bitcast.10, bf16[10,128]{1,0:T(8,128)(2,1)S(1)} %bitcast.12, bf16[2,64,256]{2,1,0:T(8,128)(2,1)S(1)} %copy-done.10), custom_call_target="tpu_custom_call" | custom-call | flops 2000000000 | bytes 2097152 | tf_op jit(solution)/shard_map/combine/pallas_call | solution.py:484
  (15 shorter events, 0.0 us)
Async XLA Ops:
  0.6 18.7 %copy-start.6 = (bf16[1,512,256]{2,1,0:T(8,128)(2,1)S(1)}, bf16[1,512,256]{2,1,0:T(8,128)(2,1)}, u32[]{:S(2)}) copy-start(bf16[1,512,256]{2,1,0:T(8,128)(2,1)} %refs_4_.1) | copy-start | bytes 786436
  0.7 18.7 %copy-start.7 = (bf16[1,512,256]{2,1,0:T(8,128)(2,1)S(1)}, bf16[1,512,256]{2,1,0:T(8,128)(2,1)}, u32[]{:S(2)}) copy-start(bf16[1,512,256]{2,1,0:T(8,128)(2,1)} %refs_5_.1) | copy-start | bytes 786436
  3.1 7.3 %copy-start.3 = (bf16[2,64,256]{2,1,0:T(8,128)(2,1)S(1)}, bf16[2,64,256]{2,1,0:T(8,128)(2,1)}, u32[]{:S(2)}) copy-start(bf16[2,64,256]{2,1,0:T(8,128)(2,1)} %key_hbm.1) | copy-start | bytes 196612
  3.1 7.3 %copy-start.4 = (bf16[2,64,256]{2,1,0:T(8,128)(2,1)S(1)}, bf16[2,64,256]{2,1,0:T(8,128)(2,1)}, u32[]{:S(2)}) copy-start(bf16[2,64,256]{2,1,0:T(8,128)(2,1)} %value_hbm.1) | copy-start | bytes 196612
  3.1 16.3 %copy-start.5 = (bf16[1,256,512]{2,1,0:T(8,128)(2,1)S(1)}, bf16[1,256,512]{2,1,0:T(8,128)(2,1)}, u32[]{:S(2)}) copy-start(bf16[1,256,512]{2,1,0:T(8,128)(2,1)} %down_ref.1) | copy-start | bytes 786436
  3.1 16.2 %all-to-all-start = ((bf16[32,16,128]{2,1,0:T(8,128)(2,1)}), bf16[32,16,128]{2,1,0:T(8,128)(2,1)S(1)}, u32[]{:S(2)}, u32[]{:S(2)}) async-start(bf16[32,16,128]{2,1,0:T(8,128)(2,1)} %bitcast.13), calls=%async_computation | async-start | bytes 262144 | tf_op jit(solution)/shard_map/all_to_all | solution.py:421
  10.7 8.7 %collective-permute-start = (bf16[2,64,512]{2,1,0:T(8,128)(2,1)S(1)}, bf16[2,64,512]{2,1,0:T(8,128)(2,1)S(1)}, u32[]{:S(2)}, u32[]{:S(2)}) collective-permute-start(bf16[2,64,512]{2,1,0:T(8,128)(2,1)S(1)} %pack.1.refs_3_), channel_id=1, source_target_pairs={{0,2},{1,3},{2,4},{3,5},{4,6},{5,7},{8,10},{9,11},{10,12},{11,13},... | collective-permute-start | bytes 393224 | tf_op jit(solution)/shard_map/ppermute | solution.py:402
  14.3 9.1 %collective-permute-start.2 = (bf16[2,64,512]{2,1,0:T(8,128)(2,1)S(1)}, bf16[2,64,512]{2,1,0:T(8,128)(2,1)S(1)}, u32[]{:S(2)}, u32[]{:S(2)}) collective-permute-start(bf16[2,64,512]{2,1,0:T(8,128)(2,1)S(1)} %pack.1.refs_3_), channel_id=1, source_target_pairs={{0,6},{1,7},{8,14},{9,15},{16,22},{17,23},{24,30},{25,31}} | collective-permute-start | bytes 393224 | tf_op jit(solution)/shard_map/ppermute | solution.py:402
  17.5 6.0 %collective-permute-start.1 = (bf16[2,64,512]{2,1,0:T(8,128)(2,1)S(1)}, bf16[2,64,512]{2,1,0:T(8,128)(2,1)S(1)}, u32[]{:S(2)}, u32[]{:S(2)}) collective-permute-start(bf16[2,64,512]{2,1,0:T(8,128)(2,1)S(1)} %pack.1.refs_3_), channel_id=1, source_target_pairs={{0,4},{1,5},{2,6},{3,7},{8,12},{9,13},{10,14},{11,15},{16,20},{17,... | collective-permute-start | bytes 393224 | tf_op jit(solution)/shard_map/ppermute | solution.py:402
  19.9 9.2 %copy-start = (bf16[2,64,2048]{2,1,0:T(8,128)(2,1)S(1)}, bf16[2,64,2048]{2,1,0:T(8,128)(2,1)}, u32[]{:S(2)}) copy-start(bf16[2,64,2048]{2,1,0:T(8,128)(2,1)} %refs_0_.1) | copy-start | bytes 1572868
  19.9 9.2 %copy-start.1 = (bf16[2,64,2048]{2,1,0:T(8,128)(2,1)S(1)}, bf16[2,64,2048]{2,1,0:T(8,128)(2,1)}, u32[]{:S(2)}) copy-start(bf16[2,64,2048]{2,1,0:T(8,128)(2,1)} %refs_1_.1) | copy-start | bytes 1572868
  19.9 9.2 %copy-start.2 = (bf16[2,64,2048]{2,1,0:T(8,128)(2,1)S(1)}, bf16[2,64,2048]{2,1,0:T(8,128)(2,1)}, u32[]{:S(2)}) copy-start(bf16[2,64,2048]{2,1,0:T(8,128)(2,1)} %refs_2_.1) | copy-start | bytes 1572868
  19.9 5.7 %collective-permute-start.9 = (bf16[64,768]{1,0:T(8,128)(2,1)S(1)}, bf16[64,768]{1,0:T(8,128)(2,1)S(1)}, u32[]{:S(2)}, u32[]{:S(2)}) collective-permute-start(bf16[64,768]{1,0:T(8,128)(2,1)S(1)} %get-tuple-element.34.refs_0_), channel_id=1, source_target_pairs={{0,24},{8,16},{16,8},{24,0},{1,25},{9,17},{17,9},{25,1},{2,26},{10... | collective-permute-start | bytes 294920 | tf_op jit(solution)/shard_map/ppermute | solution.py:436
  22.4 5.1 %collective-permute-start.8 = (bf16[64,768]{1,0:T(8,128)(2,1)S(1)}, bf16[64,768]{1,0:T(8,128)(2,1)S(1)}, u32[]{:S(2)}, u32[]{:S(2)}) collective-permute-start(bf16[64,768]{1,0:T(8,128)(2,1)S(1)} %get-tuple-element.34.refs_0_), channel_id=1, source_target_pairs={{0,16},{8,24},{16,0},{24,8},{1,17},{9,25},{17,1},{25,9},{2,18},{10... | collective-permute-start | bytes 294920 | tf_op jit(solution)/shard_map/ppermute | solution.py:436
  22.9 4.7 %collective-permute-start.7 = (bf16[64,768]{1,0:T(8,128)(2,1)S(1)}, bf16[64,768]{1,0:T(8,128)(2,1)S(1)}, u32[]{:S(2)}, u32[]{:S(2)}) collective-permute-start(bf16[64,768]{1,0:T(8,128)(2,1)S(1)} %get-tuple-element.34.refs_0_), channel_id=1, source_target_pairs={{0,8},{8,0},{16,24},{24,16},{1,9},{9,1},{17,25},{25,17},{2,10},{10... | collective-permute-start | bytes 294920 | tf_op jit(solution)/shard_map/ppermute | solution.py:436
  23.5 5.6 %collective-permute-start.3 = (bf16[2,64,512]{2,1,0:T(8,128)(2,1)S(1)}, bf16[2,64,512]{2,1,0:T(8,128)(2,1)S(1)}, u32[]{:S(2)}, u32[]{:S(2)}) collective-permute-start(bf16[2,64,512]{2,1,0:T(8,128)(2,1)S(1)} %pack.1.refs_3_), channel_id=1, source_target_pairs={{0,1},{1,0},{2,3},{3,2},{4,5},{5,4},{6,7},{7,6},{8,9},{9,8},{10,11... | collective-permute-start | bytes 393224 | tf_op jit(solution)/shard_map/ppermute | solution.py:403
  23.5 5.6 %collective-permute-start.6 = (bf16[2,64,512]{2,1,0:T(8,128)(2,1)S(1)}, bf16[2,64,512]{2,1,0:T(8,128)(2,1)S(1)}, u32[]{:S(2)}, u32[]{:S(2)}) collective-permute-start(bf16[2,64,512]{2,1,0:T(8,128)(2,1)S(1)} %collective-permute-done.2.refs_6_), channel_id=1, source_target_pairs={{0,1},{1,0},{2,3},{3,2},{4,5},{5,4},{6,7},{7,6},{8,9},{9,8},{10,11... | collective-permute-start | bytes 393224 | tf_op jit(solution)/shard_map/ppermute | solution.py:403
  25.6 3.5 %collective-permute-start.5 = (bf16[2,64,512]{2,1,0:T(8,128)(2,1)S(1)}, bf16[2,64,512]{2,1,0:T(8,128)(2,1)S(1)}, u32[]{:S(2)}, u32[]{:S(2)}) collective-permute-start(bf16[2,64,512]{2,1,0:T(8,128)(2,1)S(1)} %collective-permute-done.1.refs_5_), channel_id=1, source_target_pairs={{0,1},{1,0},{2,3},{3,2},{4,5},{5,4},{6,7},{7,6},{8,9},{9,8},{10,11... | collective-permute-start | bytes 393224 | tf_op jit(solution)/shard_map/ppermute | solution.py:403
  27.4 1.6 %collective-permute-start.4 = (bf16[2,64,512]{2,1,0:T(8,128)(2,1)S(1)}, bf16[2,64,512]{2,1,0:T(8,128)(2,1)S(1)}, u32[]{:S(2)}, u32[]{:S(2)}) collective-permute-start(bf16[2,64,512]{2,1,0:T(8,128)(2,1)S(1)} %collective-permute-done.after_ref.refs_4_), channel_id=1, source_target_pairs={{0,1},{1,0},{2,3},{3,2},{4,5},{5,4},{6,7},{7,6},{8,9},{9,8},{10,11... | collective-permute-start | bytes 393224 | tf_op jit(solution)/shard_map/ppermute | solution.py:403
  32.8 6.1 %collective-permute-start.10 = (bf16[4,2,64,512]{3,2,1,0:T(8,128)(2,1)S(1)}, bf16[4,2,64,512]{3,2,1,0:T(8,128)(2,1)S(1)}, u32[]{:S(2)}, u32[]{:S(2)}) collective-permute-start(bf16[4,2,64,512]{3,2,1,0:T(8,128)(2,1)S(1)} %get-tuple-element.41), channel_id=1, source_target_pairs={{0,1},{1,0},{2,3},{3,2},{4,5},{5,4},{6,7},{7,6},{8,9},{9,8},{10,11... | collective-permute-start | bytes 1572872 | tf_op jit(solution)/shard_map/ppermute | solution.py:450
  33.2 24.3 %all-to-all-start.1 = ((bf16[32,16,128]{2,1,0:T(8,128)(2,1)}), bf16[32,16,128]{2,1,0:T(8,128)(2,1)S(1)}, u32[]{:S(2)}, u32[]{:S(2)}) async-start(bf16[32,16,128]{2,1,0:T(8,128)(2,1)} %bitcast.4), calls=%async_computation.1 | async-start | bytes 262144 | tf_op jit(solution)/shard_map/all_to_all | solution.py:462
  39.1 8.4 %collective-permute-start.11 = (bf16[2,64,512]{2,1,0:T(8,128)(2,1)S(1)}, bf16[2,64,512]{2,1,0:T(8,128)(2,1)S(1)}, u32[]{:S(2)}, u32[]{:S(2)}) collective-permute-start(bf16[2,64,512]{2,1,0:T(8,128)(2,1)S(1)} %get-tuple-element.43), channel_id=1, source_target_pairs={{2,0},{3,1},{4,2},{5,3},{6,4},{7,5},{10,8},{11,9},{12,10},{13,11},... | collective-permute-start | bytes 393224 | tf_op jit(solution)/shard_map/ppermute | solution.py:461
  40.4 16.4 %collective-permute-start.12 = (bf16[2,64,512]{2,1,0:T(8,128)(2,1)S(1)}, bf16[2,64,512]{2,1,0:T(8,128)(2,1)S(1)}, u32[]{:S(2)}, u32[]{:S(2)}) collective-permute-start(bf16[2,64,512]{2,1,0:T(8,128)(2,1)S(1)} %get-tuple-element.44), channel_id=1, source_target_pairs={{4,0},{5,1},{6,2},{7,3},{12,8},{13,9},{14,10},{15,11},{20,16},{21,... | collective-permute-start | bytes 393224 | tf_op jit(solution)/shard_map/ppermute | solution.py:461
  41.7 15.1 %collective-permute-start.13 = (bf16[2,64,512]{2,1,0:T(8,128)(2,1)S(1)}, bf16[2,64,512]{2,1,0:T(8,128)(2,1)S(1)}, u32[]{:S(2)}, u32[]{:S(2)}) collective-permute-start(bf16[2,64,512]{2,1,0:T(8,128)(2,1)S(1)} %get-tuple-element.45), channel_id=1, source_target_pairs={{6,0},{7,1},{14,8},{15,9},{22,16},{23,17},{30,24},{31,25}} | collective-permute-start | bytes 393224 | tf_op jit(solution)/shard_map/ppermute | solution.py:461
  56.8 0.7 %copy-start.8 = (s32[128,10]{0,1:T(8,128)S(1)}, s32[128,10]{0,1:T(8,128)}, u32[]{:S(2)}) copy-start(s32[128,10]{0,1:T(8,128)} %param.19) | copy-start | bytes 15364
  56.8 0.7 %copy-start.9 = (bf16[128,10]{0,1:T(8,128)(2,1)S(1)}, bf16[128,10]{0,1:T(8,128)(2,1)}, u32[]{:S(2)}) copy-start(bf16[128,10]{0,1:T(8,128)(2,1)} %param.20) | copy-start | bytes 7684
  57.5 0.8 %copy-start.10 = (bf16[2,64,256]{2,1,0:T(8,128)(2,1)S(1)}, bf16[2,64,256]{2,1,0:T(8,128)(2,1)}, u32[]{:S(2)}) copy-start(bf16[2,64,256]{2,1,0:T(8,128)(2,1)} %get-tuple-element.26.after_ref) | copy-start | bytes 196612

commit v8 on v6

--- a/solution.py
+++ b/solution.py
@@ -59,12 +59,19 @@
     out_ref[:, :, HEAD:] = value_ref[...]
 
 
+def held_from(chip, chips):
+    if chips == 4:
+        odd = chip & 1
+        return (chip, chip - 2, jnp.where(odd == 1, chip - 1, -1), chip - 2 + 1 - 2 * odd)
+    return [chip - d for d in range(chips)]
+
+
 def attention_kernel(chips, *refs):
     q_ref, logit_ref, grad_ref = refs[:3]
     kv_refs = refs[3 : 3 + 2 * chips]
-    query_grad_hbm, gate_grad_hbm, other_ref = refs[3 + 2 * chips : 6 + 2 * chips]
-    mine_refs = refs[6 + 2 * chips : 6 + 3 * chips]
-    query_grad_ref, gate_grad_ref, out_sems = refs[6 + 3 * chips :]
+    query_grad_hbm, gate_grad_hbm, other_ref = refs[4 + 2 * chips : 7 + 2 * chips]
+    mine_refs = refs[7 + 2 * chips : 7 + 3 * chips]
+    query_grad_ref, gate_grad_ref, out_sems = refs[7 + 3 * chips :]
     seqs, length, _ = q_ref.shape
     side = chips * length
     scale = HEAD ** (-0.5)
@@ -74,8 +81,11 @@
     shape = (1, 2 * side)
     col = iota(shape, 1)
     half, back, inner = div(col, side), div(mod(col, side), length), mod(col, length)
-    block = 2 * (chip - back) + jnp.where(half == 0, core, 1 - core)
-    key_pos = jnp.where(back <= chip, block * length + inner, 2 * side)
+    owner = chip - back
+    for d, source in enumerate(held_from(chip, chips)):
+        owner = jnp.where(back == d, source, owner)
+    block = 2 * owner + jnp.where(half == 0, core, 1 - core)
+    key_pos = jnp.where(owner >= 0, block * length + inner, 2 * side)
     query_pos = position * length + mod(iota((HEADS * length, 1), 0), length)
 
     def stacked(ref, s):
@@ -123,14 +133,14 @@
         store.wait()
 
 
-def attention(query_rows, gate_logits, gated_grad, pieces):
+def attention(query_rows, gate_logits, gated_grad, pieces, after):
     seqs, length, width = query_rows.shape
     chips = len(pieces) // 2
     full = jax.ShapeDtypeStruct((seqs, length, width), BF16)
     part = jax.ShapeDtypeStruct(pieces[0].shape, BF16)
     out = pl.pallas_call(
         functools.partial(attention_kernel, chips),
-        in_specs=[IN_VMEM] * (3 + 2 * chips),
+        in_specs=[IN_VMEM] * (3 + 2 * chips) + [ANYWHERE],
         out_specs=[IN_HBM] * 2 + [IN_VMEM] * (1 + chips),
         out_shape=[full] * 2 + [jax.ShapeDtypeStruct((chips,) + part.shape, BF16)] + [part] * chips,
         scratch_shapes=[pltpu.VMEM(query_rows.shape, BF16)] * 2
@@ -138,7 +148,7 @@
         compiler_params=params(ATTENTION_MIB if chips <= 4 else 56),
         cost_estimate=cost(MIB, 8),
         name="attention",
-    )(query_rows, gate_logits, gated_grad, *pieces)
+    )(query_rows, gate_logits, gated_grad, *pieces, after)
     return out[0], out[1], out[2], out[3:]
 
 
@@ -154,7 +164,7 @@
         out_shape=jax.ShapeDtypeStruct(array.shape, array.dtype),
         input_output_aliases={0: 0},
         compiler_params=params(16),
-        cost_estimate=cost(4e9, 8),
+        cost_estimate=cost(8, 8),
         name="gate",
     )(array, after)
 
@@ -375,10 +385,20 @@
         cost_estimate=cost(6e10, MIB),
         name="pack",
     )(key_rows, value_rows)
+    def chip_permute(array, pairs):
+        return lax.ppermute(
+            array, "expert", [(2 * a + c, 2 * b + c) for a, b in pairs for c in range(2)]
+        )
+
     mine = [packed]
-    for d in range(1, chips):
-        up = [(i, i + 2 * d) for i in range(devices - 2 * d)]
-        mine.append(lax.ppermute(packed, "expert", up))
+    if chips == 4:
+        two = chip_permute(packed, [(0, 2), (1, 3)])
+        one = chip_permute(packed, [(0, 1), (2, 3)])
+        two = gate(two, one)
+        mine += [two, one, chip_permute(two, [(2, 3), (3, 2)])]
+    else:
+        for d in range(1, chips):
+            mine.append(chip_permute(packed, [(i, i + d) for i in range(chips - d)]))
     other = [lax.ppermute(block, "expert", swap) for block in mine]
 
     routes_t, weights_t = routes.T, route_weights.T
@@ -394,10 +414,6 @@
         send.reshape(sources, rows, LANES), axes, split_axis=0, concat_axis=0, tiled=True
     ).reshape(sources * rows, LANES)
 
-    query_grad, gate_grad, other_part, mine_part = attention(
-        query_rows, gate_logits, gated_grad, mine + other
-    )
-    other_part = gate(other_part, recv)
     slot_rows = jax.ShapeDtypeStruct((sources * CAP, share), BF16)
     hid_rows = jax.ShapeDtypeStruct((sources * CAP, hid), BF16)
     inputs, grads, sent = pl.pallas_call(
@@ -407,11 +423,14 @@
         compiler_params=params(16),
         cost_estimate=cost(2e9, 2 * MIB),
         name="enter",
-    )(recv, gate_proj, up_proj, down_proj, other_part)
+    )(recv, gate_proj, up_proj, down_proj, packed)
     parts = [sent] + [
         lax.ppermute(sent, "dp", [(g, g ^ k) for g in range(groups)]) for k in range(1, groups)
     ]
 
+    query_grad, gate_grad, other_part, mine_part = attention(
+        query_rows, gate_logits, gated_grad, mine + other, sent
+    )
     arrived = lax.ppermute(other_part, "expert", swap)
     merged = pl.pallas_call(
         functools.partial(merge_kernel, chips),
@@ -420,10 +439,11 @@
         cost_estimate=cost(MIB, 2 * MIB),
         name="merge",
     )(*mine_part, arrived)
-    terms = [merged[0]]
-    for d in range(1, chips):
-        down = [(i, i - 2 * d) for i in range(2 * d, devices)]
-        terms.append(lax.ppermute(merged[d], "expert", down))
+    if chips == 4:
+        returns = [[(2, 0), (3, 1)], [(1, 0), (3, 2)], [(2, 1), (3, 0)]]
+    else:
+        returns = [[(i, i - d) for i in range(d, chips)] for d in range(1, chips)]
+    terms = [merged[0]] + [chip_permute(m, pairs) for m, pairs in zip(merged[1:], returns)]
     back, hidden, gate_rows, up_rows = pl.pallas_call(
         functools.partial(middle_kernel, sources, rows),
         in_specs=[IN_VMEM] * (len(parts) + 2) + [ANYWHERE],

time: 55.3 us -> 59.7 us (1.080)
  waiting for transfers between devices: 12.4 us -> 20.7 us
  starting transfers between devices: 29.2 us -> 24.5 us
  local copies, waits for them, and re-layouts: 1.81 us -> 2.63 us
    all_to_all x1, starting transfers between devices: 6.71 us -> 2.58 us  [shards(): lax.all_to_all(back.reshape(sources, rows, LANES), axes, split_axis=0, co...]
    all_to_all x1, waiting for transfers between devices: 2.26 us -> 6.23 us  [shards(): lax.all_to_all(send.reshape(sources, rows, LANES), axes, split_axis=0, co...]
    ppermute x6, waiting for transfers between devices: 2.44 us -> 5.38 us  [chip_permute(): lax.ppermute(array, 'expert', [(2 * a + c, 2 * b + c) for a, b in pairs f...]
    all_to_all x1, waiting for transfers between devices: 3.57 us -> 5.98 us  [shards(): lax.all_to_all(back.reshape(sources, rows, LANES), axes, split_axis=0, co...]
    ppermute x4, waiting for transfers between devices: 1.09 us -> 0.01 us  [shards(): other = [lax.ppermute(block, 'expert', swap) for block in mine]]
    unnamed x26, local copies, waits for them, and re-layouts: 1.81 us -> 2.63 us
    ppermute x6, starting transfers between devices: 14.7 us -> 14.1 us  [chip_permute(): lax.ppermute(array, 'expert', [(2 * a + c, 2 * b + c) for a, b in pairs f...]
  transfers between devices with their start and end apart: 16 -> 16, of which waited for: 10 -> 6; matrix products, arithmetic and copies ran while one was open for 0% -> 0% of each run, Pallas kernels for 16% -> 9%
where the time goes in v8:
time: 59.7 us; the launch traced here: 59.3 us
  starting transfers between devices  24.5 us (41%)
  waiting for transfers between devices  20.7 us (35%)
  Pallas kernels  10.5 us (18%)
  local copies, waits for them, and re-layouts  2.63 us (4%)
  between operations  0.91 us (2%)
    ppermute x6, starting transfers between devices, chip_permute(): lax.ppermute(array, 'expert', [(2 * a + c, 2 * b + c) for a, b in pairs f...  14.1 us
    all_to_all x1, waiting for transfers between devices, shards(): lax.all_to_all(send.reshape(sources, rows, LANES), axes, split_axis=0, co...  6.23 us
    all_to_all x1, waiting for transfers between devices, shards(): lax.all_to_all(back.reshape(sources, rows, LANES), axes, split_axis=0, co...  5.98 us
    ppermute x6, waiting for transfers between devices, chip_permute(): lax.ppermute(array, 'expert', [(2 * a + c, 2 * b + c) for a, b in pairs f...  5.38 us
    pallas_call x1, Pallas kernels, attention(): pl.pallas_call(functools.partial(attention_kernel, chips), in_specs=[IN_V...  3.7 us
    ppermute x3, starting transfers between devices, shards(): lax.ppermute(sent, 'dp', [(g, g ^ k) for g in range(groups)])  3.55 us
    all_to_all x1, starting transfers between devices, shards(): lax.all_to_all(send.reshape(sources, rows, LANES), axes, split_axis=0, co...  2.81 us
    unnamed x26, local copies, waits for them, and re-layouts  2.63 us
  transfers between devices with their start and end apart: 16, of which 6 were waited for; matrix products, arithmetic and copies ran while one was open for 0% of the time, Pallas kernels for 9%

profile of v8, /device:TPU:0, one launch (start us, length us, event | category | flops | bytes accessed | tf_op | source)
XLA Modules:
  0.0 59.3 jit_solution(17067752429139909415)
XLA Ops:
  0.7 0.9 %copy-done.8 = bf16[2,64,256]{2,1,0:T(8,128)(2,1)S(1)} copy-done((bf16[2,64,256]{2,1,0:T(8,128)(2,1)S(1)}, bf16[2,64,256]{2,1,0:T(8,128)(2,1)}, u32[]{:S(2)}) %copy-start.8) | copy-done | bytes 65560
  1.6 0.8 %copy-done.9 = bf16[2,64,256]{2,1,0:T(8,128)(2,1)S(1)} copy-done((bf16[2,64,256]{2,1,0:T(8,128)(2,1)S(1)}, bf16[2,64,256]{2,1,0:T(8,128)(2,1)}, u32[]{:S(2)}) %copy-start.9) | copy-done | bytes 65560
  2.4 0.2 pack.1.after_ref.refs_3_
  2.6 4.9 %collective-permute-start.1 = (bf16[2,64,512]{2,1,0:T(8,128)(2,1)S(1)}, bf16[2,64,512]{2,1,0:T(8,128)(2,1)S(1)}, u32[]{:S(2)}, u32[]{:S(2)}) collective-permute-start(bf16[2,64,512]{2,1,0:T(8,128)(2,1)S(1)} %pack.1.after_ref.refs_3_), channel_id=1, source_target_pairs={{0,2},{1,3},{4,6},{5,7},{8,10},{9,11},{12,14},{13,15},{16,18},{17,... | collective-permute-start | bytes 393224 | tf_op jit(solution)/shard_map/ppermute | solution.py:389
  7.6 4.5 %collective-permute-start = (bf16[2,64,512]{2,1,0:T(8,128)(2,1)S(1)}, bf16[2,64,512]{2,1,0:T(8,128)(2,1)S(1)}, u32[]{:S(2)}, u32[]{:S(2)}) collective-permute-start(bf16[2,64,512]{2,1,0:T(8,128)(2,1)S(1)} %pack.1.after_ref.refs_3_), channel_id=1, source_target_pairs={{0,4},{1,5},{2,6},{3,7},{8,12},{9,13},{10,14},{11,15},{16,20},{17,... | collective-permute-start | bytes 393224 | tf_op jit(solution)/shard_map/ppermute | solution.py:389
  12.1 0.0 copy-start.7
  12.1 1.2 %dispatch.1 = bf16[512,128]{1,0:T(8,128)(2,1)} custom-call(bf16[128,2048]{1,0:T(8,128)(2,1)S(1)} %copy-done.3, bf16[128,2048]{1,0:T(8,128)(2,1)S(1)} %copy-done.4, s32[10,128]{1,0:T(8,128)S(1)} %bitcast.9, bf16[10,128]{1,0:T(8,128)(2,1)S(1)} %bitcast.11, bf16[2,64,512]{2,1,0:T(8,128)(2,1)S(1)} %pack.1.after_ref.refs_3_), custom_call_target="tpu_custom_call" | custom-call | flops 2000000000 | bytes 2097152 | tf_op jit(solution)/shard_map/dispatch/pallas_call | solution.py:405
  13.4 2.8 %all-to-all-start = ((bf16[32,16,128]{2,1,0:T(8,128)(2,1)}), bf16[32,16,128]{2,1,0:T(8,128)(2,1)S(1)}, u32[]{:S(2)}, u32[]{:S(2)}) async-start(bf16[32,16,128]{2,1,0:T(8,128)(2,1)} %bitcast.2), calls=%async_computation | async-start | bytes 262144 | tf_op jit(solution)/shard_map/all_to_all | solution.py:413
  16.2 0.0 copy-start.5
  16.2 0.0 collective-permute-done.1.after_ref.refs_5_
  16.2 0.0 collective-permute-done.held_ref
  16.2 0.8 %collective-permute-start.2 = (bf16[2,64,512]{2,1,0:T(8,128)(2,1)S(1)}, bf16[2,64,512]{2,1,0:T(8,128)(2,1)S(1)}, u32[]{:S(2)}, u32[]{:S(2)}) collective-permute-start(bf16[2,64,512]{2,1,0:T(8,128)(2,1)S(1)} %gate.1.refs_4_), channel_id=1, source_target_pairs={{4,6},{5,7},{6,4},{7,5},{12,14},{13,15},{14,12},{15,13},{20,22},{2... | collective-permute-start | bytes 393224 | tf_op jit(solution)/shard_map/ppermute | solution.py:389
  17.0 0.3 collective-permute-start.3
  17.4 0.3 collective-permute-start.4
  17.6 0.3 collective-permute-start.5
  17.9 0.0 collective-permute-done.2.refs_6_
  17.9 0.3 collective-permute-start.6
  18.1 6.2 %all-to-all-done = bf16[32,16,128]{2,1,0:T(8,128)(2,1)S(1)} async-done(((bf16[32,16,128]{2,1,0:T(8,128)(2,1)}), bf16[32,16,128]{2,1,0:T(8,128)(2,1)S(1)}, u32[]{:S(2)}, u32[]{:S(2)}) %all-to-all-start) | async-done | bytes 131104 | tf_op jit(solution)/shard_map/all_to_all | solution.py:413
  24.4 0.0 copy-start
  24.4 0.0 copy-start.1
  24.4 0.0 copy-start.2
  24.4 0.5 enter.1
  24.9 0.0 collective-permute-done.5.refs_9_
  24.9 0.0 collective-permute-done.6.refs_10_
  24.9 0.5 copy-done
  25.4 0.2 copy-done.1
  25.6 0.2 copy-done.2
  25.7 3.7 %attention.1 = (bf16[2,64,2048]{2,1,0:T(8,128)(2,1)}, bf16[2,64,2048]{2,1,0:T(8,128)(2,1)}, bf16[4,2,64,512]{3,2,1,0:T(8,128)(2,1)S(1)}, bf16[2,64,512]{2,1,0:T(...) custom-call(bf16[2,64,2048]{2,1,0:T(8,128)(2,1)S(1)} %copy-done, ...), custom_call_target="tpu_custom_call" | custom-call | flops 1048576 | bytes 8 | tf_op jit(solution)/shard_map/attention/pallas_call | solution.py:141
  29.4 0.4 collective-permute-start.7
  29.8 1.6 %collective-permute-done.7.refs_4_ = bf16[4,2,64,512]{3,2,1,0:T(8,128)(2,1)S(1)} collective-permute-done((bf16[4,2,64,512]{3,2,1,0:T(8,128)(2,1)S(1)}, bf16[4,2,64,512]{3,2,1,0:T(8,128)(2,1)S(1)}, u32[]{:S(2)}, u32[]{:S(2)}) %collective-permute-start.7) | collective-permute-done | bytes 524320 | tf_op jit(solution)/shard_map/ppermute | solution.py:434
  31.4 0.1 merge.1
  31.5 1.3 %collective-permute-start.8 = (bf16[2,64,512]{2,1,0:T(8,128)(2,1)S(1)}, bf16[2,64,512]{2,1,0:T(8,128)(2,1)S(1)}, u32[]{:S(2)}, u32[]{:S(2)}) collective-permute-start(bf16[2,64,512]{2,1,0:T(8,128)(2,1)S(1)} %get-tuple-element.42), channel_id=1, source_target_pairs={{4,0},{5,1},{6,2},{7,3},{12,8},{13,9},{14,10},{15,11},{20,16},{21,... | collective-permute-start | bytes 393224 | tf_op jit(solution)/shard_map/ppermute | solution.py:389
  32.8 0.9 %collective-permute-start.11 = (bf16[64,768]{1,0:T(8,128)(2,1)S(1)}, bf16[64,768]{1,0:T(8,128)(2,1)S(1)}, u32[]{:S(2)}, u32[]{:S(2)}) collective-permute-start(bf16[64,768]{1,0:T(8,128)(2,1)S(1)} %get-tuple-element.34.refs_11_.refs_0_), channel_id=1, source_target_pairs={{0,8},{8,0},{16,24},{24,16},{1,9},{9,1},{17,25},{25,17},{2,10},{10... | collective-permute-start | bytes 294920 | tf_op jit(solution)/shard_map/ppermute | solution.py:428
  33.7 0.7 %collective-permute-start.12 = (bf16[64,768]{1,0:T(8,128)(2,1)S(1)}, bf16[64,768]{1,0:T(8,128)(2,1)S(1)}, u32[]{:S(2)}, u32[]{:S(2)}) collective-permute-start(bf16[64,768]{1,0:T(8,128)(2,1)S(1)} %get-tuple-element.34.refs_11_.refs_0_), channel_id=1, source_target_pairs={{0,16},{8,24},{16,0},{24,8},{1,17},{9,25},{17,1},{25,9},{2,18},{10... | collective-permute-start | bytes 294920 | tf_op jit(solution)/shard_map/ppermute | solution.py:428
  34.4 2.0 %collective-permute-start.13 = (bf16[64,768]{1,0:T(8,128)(2,1)S(1)}, bf16[64,768]{1,0:T(8,128)(2,1)S(1)}, u32[]{:S(2)}, u32[]{:S(2)}) collective-permute-start(bf16[64,768]{1,0:T(8,128)(2,1)S(1)} %get-tuple-element.34.refs_11_.refs_0_), channel_id=1, source_target_pairs={{0,24},{8,16},{16,8},{24,0},{1,25},{9,17},{17,9},{25,1},{2,26},{10... | collective-permute-start | bytes 294920 | tf_op jit(solution)/shard_map/ppermute | solution.py:428
  36.4 1.3 %collective-permute-start.10 = (bf16[2,64,512]{2,1,0:T(8,128)(2,1)S(1)}, bf16[2,64,512]{2,1,0:T(8,128)(2,1)S(1)}, u32[]{:S(2)}, u32[]{:S(2)}) collective-permute-start(bf16[2,64,512]{2,1,0:T(8,128)(2,1)S(1)} %get-tuple-element.44), channel_id=1, source_target_pairs={{4,2},{5,3},{6,0},{7,1},{12,10},{13,11},{14,8},{15,9},{20,18},{21,... | collective-permute-start | bytes 393224 | tf_op jit(solution)/shard_map/ppermute | solution.py:389
  37.7 0.8 %collective-permute-done.11.refs_1_ = bf16[64,768]{1,0:T(8,128)(2,1)S(1)} collective-permute-done((bf16[64,768]{1,0:T(8,128)(2,1)S(1)}, bf16[64,768]{1,0:T(8,128)(2,1)S(1)}, u32[]{:S(2)}, u32[]{:S(2)}) %collective-permute-start.11) | collective-permute-done | bytes 98336 | tf_op jit(solution)/shard_map/ppermute | solution.py:428
  38.5 1.3 %collective-permute-start.9 = (bf16[2,64,512]{2,1,0:T(8,128)(2,1)S(1)}, bf16[2,64,512]{2,1,0:T(8,128)(2,1)S(1)}, u32[]{:S(2)}, u32[]{:S(2)}) collective-permute-start(bf16[2,64,512]{2,1,0:T(8,128)(2,1)S(1)} %get-tuple-element.43), channel_id=1, source_target_pairs={{2,0},{3,1},{6,4},{7,5},{10,8},{11,9},{14,12},{15,13},{18,16},{19,... | collective-permute-start | bytes 393224 | tf_op jit(solution)/shard_map/ppermute | solution.py:389
  39.8 0.7 %collective-permute-done.12.refs_2_ = bf16[64,768]{1,0:T(8,128)(2,1)S(1)} collective-permute-done((bf16[64,768]{1,0:T(8,128)(2,1)S(1)}, bf16[64,768]{1,0:T(8,128)(2,1)S(1)}, u32[]{:S(2)}, u32[]{:S(2)}) %collective-permute-start.12) | collective-permute-done | bytes 98336 | tf_op jit(solution)/shard_map/ppermute | solution.py:428
  40.4 0.0 collective-permute-done.13.refs_3_
  40.5 5.4 %collective-permute-done.8.refs_1_.refs_6_ = bf16[2,64,512]{2,1,0:T(8,128)(2,1)S(1)} collective-permute-done((bf16[2,64,512]{2,1,0:T(8,128)(2,1)S(1)}, bf16[2,64,512]{2,1,0:T(8,128)(2,1)S(1)}, u32[]{:S(2)}, u32[]{:S(2)}) %collective-permute-start.8) | collective-permute-done | bytes 131104 | tf_op jit(solution)/shard_map/ppermute | solution.py:389
  45.8 1.4 %middle.1 = (bf16[512,128]{1,0:T(8,128)(2,1)}, bf16[64,256]{1,0:T(8,128)(2,1)S(1)}, bf16[64,256]{1,0:T(8,128)(2,1)S(1)}, bf16[64,256]{1,0:T(8,128)(2,1)S(1)}) custom-call(bf16[64,768]{1,0:T(8,128)(2,1)S(1)} %get-tuple-element.34.refs_11_.refs_0_, bf16[64,768]{1,0:T(8,128)(2,1)S(1)} %collective-permute-done.11.refs_1_, ...), custom_call_target="tpu_custom_call" | custom-call | flops 2000000000 | bytes 2097152 | tf_op jit(solution)/shard_map/middle/pallas_call | solution.py:447
  47.2 2.6 %all-to-all-start.1 = ((bf16[32,16,128]{2,1,0:T(8,128)(2,1)}), bf16[32,16,128]{2,1,0:T(8,128)(2,1)S(1)}, u32[]{:S(2)}, u32[]{:S(2)}) async-start(bf16[32,16,128]{2,1,0:T(8,128)(2,1)} %bitcast.4), calls=%async_computation.1 | async-start | bytes 262144 | tf_op jit(solution)/shard_map/all_to_all | solution.py:455
  49.8 0.0 collective-permute-done.10.refs_3_
  49.8 0.7 %close.1 = (bf16[2,64,256]{2,1,0:T(8,128)(2,1)}, bf16[2,64,256]{2,1,0:T(8,128)(2,1)}) custom-call(bf16[2,64,512]{2,1,0:T(8,128)(2,1)S(1)} %get-tuple-element.41.refs_0_, bf16[2,64,512]{2,1,0:T(8,128)(2,1)S(1)} %collective-permute-done.8.refs_1_.refs_6_, bf16[2,64,512]{2,1,0:T(8,128)(2,1)S(1)} %collective-permute-done.9.refs_2_, ...), custom_call_target="tpu_custom_call" | custom-call | flops 60000002048 | bytes 1048576 | tf_op jit(solution)/shard_map/close/pallas_call | solution.py:469
  50.5 1.5 %weight_grads.1 = (f32[1,512,256]{2,1,0:T(8,128)}, f32[1,512,256]{2,1,0:T(8,128)}, f32[1,256,512]{2,1,0:T(8,128)}) custom-call(bf16[64,512]{1,0:T(8,128)(2,1)S(1)} %get-tuple-element.51.input_ref, bf16[64,512]{1,0:T(8,128)(2,1)S(1)} %get-tuple-element.52.grad_ref, bf16[64,256]{1,0:T(8,128)(2,1)S(1)} %get-tuple-element.53.hidden_ref, ...), custom_call_target="tpu_custom_call" | custom-call | flops 2000000000 | bytes 2097152 | tf_op jit(solution)/shard_map/weight_grads/pallas_call | solution.py:458
  52.0 6.0 %all-to-all-done.1 = bf16[32,16,128]{2,1,0:T(8,128)(2,1)S(1)} async-done(((bf16[32,16,128]{2,1,0:T(8,128)(2,1)}), bf16[32,16,128]{2,1,0:T(8,128)(2,1)S(1)}, u32[]{:S(2)}, u32[]{:S(2)}) %all-to-all-start.1) | async-done | bytes 131104 | tf_op jit(solution)/shard_map/all_to_all | solution.py:455
  58.0 1.3 %combine.1 = (bf16[128,2048]{1,0:T(8,128)(2,1)}, bf16[10,128]{1,0:T(8,128)(2,1)}) custom-call(bf16[512,128]{1,0:T(8,128)(2,1)S(1)} %bitcast.8, s32[10,128]{1,0:T(8,128)S(1)} %bitcast.10, bf16[10,128]{1,0:T(8,128)(2,1)S(1)} %bitcast.12, bf16[2,64,256]{2,1,0:T(8,128)(2,1)S(1)} %copy-done.12), custom_call_target="tpu_custom_call" | custom-call | flops 2000000000 | bytes 2097152 | tf_op jit(solution)/shard_map/combine/pallas_call | solution.py:477
  (20 shorter events, 0.0 us)
Async XLA Ops:
  0.6 11.4 %copy-start.3 = (bf16[128,2048]{1,0:T(8,128)(2,1)S(1)}, bf16[128,2048]{1,0:T(8,128)(2,1)}, u32[]{:S(2)}) copy-start(bf16[128,2048]{1,0:T(8,128)(2,1)} %input_ref.1) | copy-start | bytes 1572868
  0.7 11.4 %copy-start.4 = (bf16[128,2048]{1,0:T(8,128)(2,1)S(1)}, bf16[128,2048]{1,0:T(8,128)(2,1)}, u32[]{:S(2)}) copy-start(bf16[128,2048]{1,0:T(8,128)(2,1)} %grad_ref.1) | copy-start | bytes 1572868
  0.7 0.9 %copy-start.8 = (bf16[2,64,256]{2,1,0:T(8,128)(2,1)S(1)}, bf16[2,64,256]{2,1,0:T(8,128)(2,1)}, u32[]{:S(2)}) copy-start(bf16[2,64,256]{2,1,0:T(8,128)(2,1)} %key_hbm.1) | copy-start | bytes 196612
  1.6 0.8 %copy-start.9 = (bf16[2,64,256]{2,1,0:T(8,128)(2,1)S(1)}, bf16[2,64,256]{2,1,0:T(8,128)(2,1)}, u32[]{:S(2)}) copy-start(bf16[2,64,256]{2,1,0:T(8,128)(2,1)} %value_hbm.1) | copy-start | bytes 196612
  2.4 9.7 %copy-start.10 = (s32[128,10]{0,1:T(8,128)S(1)}, s32[128,10]{0,1:T(8,128)}, u32[]{:S(2)}) copy-start(s32[128,10]{0,1:T(8,128)} %param.19) | copy-start | bytes 15364
  2.4 9.7 %copy-start.11 = (bf16[128,10]{0,1:T(8,128)(2,1)S(1)}, bf16[128,10]{0,1:T(8,128)(2,1)}, u32[]{:S(2)}) copy-start(bf16[128,10]{0,1:T(8,128)(2,1)} %param.20) | copy-start | bytes 7684
  2.6 13.6 %collective-permute-start.1 = (bf16[2,64,512]{2,1,0:T(8,128)(2,1)S(1)}, bf16[2,64,512]{2,1,0:T(8,128)(2,1)S(1)}, u32[]{:S(2)}, u32[]{:S(2)}) collective-permute-start(bf16[2,64,512]{2,1,0:T(8,128)(2,1)S(1)} %pack.1.after_ref.refs_3_), channel_id=1, source_target_pairs={{0,2},{1,3},{4,6},{5,7},{8,10},{9,11},{12,14},{13,15},{16,18},{17,... | collective-permute-start | bytes 393224 | tf_op jit(solution)/shard_map/ppermute | solution.py:389
  7.6 8.6 %collective-permute-start = (bf16[2,64,512]{2,1,0:T(8,128)(2,1)S(1)}, bf16[2,64,512]{2,1,0:T(8,128)(2,1)S(1)}, u32[]{:S(2)}, u32[]{:S(2)}) collective-permute-start(bf16[2,64,512]{2,1,0:T(8,128)(2,1)S(1)} %pack.1.after_ref.refs_3_), channel_id=1, source_target_pairs={{0,4},{1,5},{2,6},{3,7},{8,12},{9,13},{10,14},{11,15},{16,20},{17,... | collective-permute-start | bytes 393224 | tf_op jit(solution)/shard_map/ppermute | solution.py:389
  12.1 12.2 %copy-start.7 = (bf16[1,512,256]{2,1,0:T(8,128)(2,1)S(1)}, bf16[1,512,256]{2,1,0:T(8,128)(2,1)}, u32[]{:S(2)}) copy-start(bf16[1,512,256]{2,1,0:T(8,128)(2,1)} %refs_5_.1) | copy-start | bytes 786436
  13.4 11.0 %copy-start.6 = (bf16[1,512,256]{2,1,0:T(8,128)(2,1)S(1)}, bf16[1,512,256]{2,1,0:T(8,128)(2,1)}, u32[]{:S(2)}) copy-start(bf16[1,512,256]{2,1,0:T(8,128)(2,1)} %refs_4_.1) | copy-start | bytes 786436
  13.4 11.0 %all-to-all-start = ((bf16[32,16,128]{2,1,0:T(8,128)(2,1)}), bf16[32,16,128]{2,1,0:T(8,128)(2,1)S(1)}, u32[]{:S(2)}, u32[]{:S(2)}) async-start(bf16[32,16,128]{2,1,0:T(8,128)(2,1)} %bitcast.2), calls=%async_computation | async-start | bytes 262144 | tf_op jit(solution)/shard_map/all_to_all | solution.py:413
  16.2 8.2 %copy-start.5 = (bf16[1,256,512]{2,1,0:T(8,128)(2,1)S(1)}, bf16[1,256,512]{2,1,0:T(8,128)(2,1)}, u32[]{:S(2)}) copy-start(bf16[1,256,512]{2,1,0:T(8,128)(2,1)} %down_ref.1) | copy-start | bytes 786436
  16.2 1.6 %collective-permute-start.2 = (bf16[2,64,512]{2,1,0:T(8,128)(2,1)S(1)}, bf16[2,64,512]{2,1,0:T(8,128)(2,1)S(1)}, u32[]{:S(2)}, u32[]{:S(2)}) collective-permute-start(bf16[2,64,512]{2,1,0:T(8,128)(2,1)S(1)} %gate.1.refs_4_), channel_id=1, source_target_pairs={{4,6},{5,7},{6,4},{7,5},{12,14},{13,15},{14,12},{15,13},{20,22},{2... | collective-permute-start | bytes 393224 | tf_op jit(solution)/shard_map/ppermute | solution.py:389
  17.0 7.8 %collective-permute-start.3 = (bf16[2,64,512]{2,1,0:T(8,128)(2,1)S(1)}, bf16[2,64,512]{2,1,0:T(8,128)(2,1)S(1)}, u32[]{:S(2)}, u32[]{:S(2)}) collective-permute-start(bf16[2,64,512]{2,1,0:T(8,128)(2,1)S(1)} %pack.1.after_ref.refs_3_), channel_id=1, source_target_pairs={{0,1},{1,0},{2,3},{3,2},{4,5},{5,4},{6,7},{7,6},{8,9},{9,8},{10,11... | collective-permute-start | bytes 393224 | tf_op jit(solution)/shard_map/ppermute | solution.py:402
  17.4 7.5 %collective-permute-start.4 = (bf16[2,64,512]{2,1,0:T(8,128)(2,1)S(1)}, bf16[2,64,512]{2,1,0:T(8,128)(2,1)S(1)}, u32[]{:S(2)}, u32[]{:S(2)}) collective-permute-start(bf16[2,64,512]{2,1,0:T(8,128)(2,1)S(1)} %gate.1.refs_4_), channel_id=1, source_target_pairs={{0,1},{1,0},{2,3},{3,2},{4,5},{5,4},{6,7},{7,6},{8,9},{9,8},{10,11... | collective-permute-start | bytes 393224 | tf_op jit(solution)/shard_map/ppermute | solution.py:402
  17.6 7.3 %collective-permute-start.5 = (bf16[2,64,512]{2,1,0:T(8,128)(2,1)S(1)}, bf16[2,64,512]{2,1,0:T(8,128)(2,1)S(1)}, u32[]{:S(2)}, u32[]{:S(2)}) collective-permute-start(bf16[2,64,512]{2,1,0:T(8,128)(2,1)S(1)} %collective-permute-done.1.after_ref.refs_5_), channel_id=1, source_target_pairs={{0,1},{1,0},{2,3},{3,2},{4,5},{5,4},{6,7},{7,6},{8,9},{9,8},{10,11... | collective-permute-start | bytes 393224 | tf_op jit(solution)/shard_map/ppermute | solution.py:402
  17.9 7.0 %collective-permute-start.6 = (bf16[2,64,512]{2,1,0:T(8,128)(2,1)S(1)}, bf16[2,64,512]{2,1,0:T(8,128)(2,1)S(1)}, u32[]{:S(2)}, u32[]{:S(2)}) collective-permute-start(bf16[2,64,512]{2,1,0:T(8,128)(2,1)S(1)} %collective-permute-done.2.refs_6_), channel_id=1, source_target_pairs={{0,1},{1,0},{2,3},{3,2},{4,5},{5,4},{6,7},{7,6},{8,9},{9,8},{10,11... | collective-permute-start | bytes 393224 | tf_op jit(solution)/shard_map/ppermute | solution.py:402
  24.4 1.0 %copy-start = (bf16[2,64,2048]{2,1,0:T(8,128)(2,1)S(1)}, bf16[2,64,2048]{2,1,0:T(8,128)(2,1)}, u32[]{:S(2)}) copy-start(bf16[2,64,2048]{2,1,0:T(8,128)(2,1)} %refs_0_.1) | copy-start | bytes 1572868
  24.4 1.2 %copy-start.1 = (bf16[2,64,2048]{2,1,0:T(8,128)(2,1)S(1)}, bf16[2,64,2048]{2,1,0:T(8,128)(2,1)}, u32[]{:S(2)}) copy-start(bf16[2,64,2048]{2,1,0:T(8,128)(2,1)} %refs_1_.1) | copy-start | bytes 1572868
  24.4 1.3 %copy-start.2 = (bf16[2,64,2048]{2,1,0:T(8,128)(2,1)S(1)}, bf16[2,64,2048]{2,1,0:T(8,128)(2,1)}, u32[]{:S(2)}) copy-start(bf16[2,64,2048]{2,1,0:T(8,128)(2,1)} %refs_2_.1) | copy-start | bytes 1572868
  29.4 2.0 %collective-permute-start.7 = (bf16[4,2,64,512]{3,2,1,0:T(8,128)(2,1)S(1)}, bf16[4,2,64,512]{3,2,1,0:T(8,128)(2,1)S(1)}, u32[]{:S(2)}, u32[]{:S(2)}) collective-permute-start(bf16[4,2,64,512]{3,2,1,0:T(8,128)(2,1)S(1)} %get-tuple-element.40), channel_id=1, source_target_pairs={{0,1},{1,0},{2,3},{3,2},{4,5},{5,4},{6,7},{7,6},{8,9},{9,8},{10,11... | collective-permute-start | bytes 1572872 | tf_op jit(solution)/shard_map/ppermute | solution.py:434
  31.5 14.3 %collective-permute-start.8 = (bf16[2,64,512]{2,1,0:T(8,128)(2,1)S(1)}, bf16[2,64,512]{2,1,0:T(8,128)(2,1)S(1)}, u32[]{:S(2)}, u32[]{:S(2)}) collective-permute-start(bf16[2,64,512]{2,1,0:T(8,128)(2,1)S(1)} %get-tuple-element.42), channel_id=1, source_target_pairs={{4,0},{5,1},{6,2},{7,3},{12,8},{13,9},{14,10},{15,11},{20,16},{21,... | collective-permute-start | bytes 393224 | tf_op jit(solution)/shard_map/ppermute | solution.py:389
  32.8 5.7 %collective-permute-start.11 = (bf16[64,768]{1,0:T(8,128)(2,1)S(1)}, bf16[64,768]{1,0:T(8,128)(2,1)S(1)}, u32[]{:S(2)}, u32[]{:S(2)}) collective-permute-start(bf16[64,768]{1,0:T(8,128)(2,1)S(1)} %get-tuple-element.34.refs_11_.refs_0_), channel_id=1, source_target_pairs={{0,8},{8,0},{16,24},{24,16},{1,9},{9,1},{17,25},{25,17},{2,10},{10... | collective-permute-start | bytes 294920 | tf_op jit(solution)/shard_map/ppermute | solution.py:428
  33.7 6.7 %collective-permute-start.12 = (bf16[64,768]{1,0:T(8,128)(2,1)S(1)}, bf16[64,768]{1,0:T(8,128)(2,1)S(1)}, u32[]{:S(2)}, u32[]{:S(2)}) collective-permute-start(bf16[64,768]{1,0:T(8,128)(2,1)S(1)} %get-tuple-element.34.refs_11_.refs_0_), channel_id=1, source_target_pairs={{0,16},{8,24},{16,0},{24,8},{1,17},{9,25},{17,1},{25,9},{2,18},{10... | collective-permute-start | bytes 294920 | tf_op jit(solution)/shard_map/ppermute | solution.py:428
  34.4 6.0 %collective-permute-start.13 = (bf16[64,768]{1,0:T(8,128)(2,1)S(1)}, bf16[64,768]{1,0:T(8,128)(2,1)S(1)}, u32[]{:S(2)}, u32[]{:S(2)}) collective-permute-start(bf16[64,768]{1,0:T(8,128)(2,1)S(1)} %get-tuple-element.34.refs_11_.refs_0_), channel_id=1, source_target_pairs={{0,24},{8,16},{16,8},{24,0},{1,25},{9,17},{17,9},{25,1},{2,26},{10... | collective-permute-start | bytes 294920 | tf_op jit(solution)/shard_map/ppermute | solution.py:428
  36.4 13.4 %collective-permute-start.10 = (bf16[2,64,512]{2,1,0:T(8,128)(2,1)S(1)}, bf16[2,64,512]{2,1,0:T(8,128)(2,1)S(1)}, u32[]{:S(2)}, u32[]{:S(2)}) collective-permute-start(bf16[2,64,512]{2,1,0:T(8,128)(2,1)S(1)} %get-tuple-element.44), channel_id=1, source_target_pairs={{4,2},{5,3},{6,0},{7,1},{12,10},{13,11},{14,8},{15,9},{20,18},{21,... | collective-permute-start | bytes 393224 | tf_op jit(solution)/shard_map/ppermute | solution.py:389
  38.5 11.3 %collective-permute-start.9 = (bf16[2,64,512]{2,1,0:T(8,128)(2,1)S(1)}, bf16[2,64,512]{2,1,0:T(8,128)(2,1)S(1)}, u32[]{:S(2)}, u32[]{:S(2)}) collective-permute-start(bf16[2,64,512]{2,1,0:T(8,128)(2,1)S(1)} %get-tuple-element.43), channel_id=1, source_target_pairs={{2,0},{3,1},{6,4},{7,5},{10,8},{11,9},{14,12},{15,13},{18,16},{19,... | collective-permute-start | bytes 393224 | tf_op jit(solution)/shard_map/ppermute | solution.py:389
  47.2 10.8 %all-to-all-start.1 = ((bf16[32,16,128]{2,1,0:T(8,128)(2,1)}), bf16[32,16,128]{2,1,0:T(8,128)(2,1)S(1)}, u32[]{:S(2)}, u32[]{:S(2)}) async-start(bf16[32,16,128]{2,1,0:T(8,128)(2,1)} %bitcast.4), calls=%async_computation.1 | async-start | bytes 262144 | tf_op jit(solution)/shard_map/all_to_all | solution.py:455
  50.5 7.5 %copy-start.12 = (bf16[2,64,256]{2,1,0:T(8,128)(2,1)S(1)}, bf16[2,64,256]{2,1,0:T(8,128)(2,1)}, u32[]{:S(2)}) copy-start(bf16[2,64,256]{2,1,0:T(8,128)(2,1)} %get-tuple-element.26.after_ref) | copy-start | bytes 196612

commit v9 on v6

--- a/solution.py
+++ b/solution.py
@@ -429,7 +429,7 @@
         in_specs=[IN_VMEM] * (len(parts) + 2) + [ANYWHERE],
         out_shape=[jax.ShapeDtypeStruct((sources * rows, LANES), BF16)] + [hid_rows] * 3,
         compiler_params=params(16 if groups <= 4 else 60),
-        cost_estimate=cost(2e9, 2 * MIB),
+        cost_estimate=cost(8, 8),
         name="middle",
     )(*parts, gate_proj, up_proj, terms[min(1, chips - 1)])
     returned = lax.all_to_all(

time: 55.3 us -> 57 us (1.031)
  waiting for transfers between devices: 12.4 us -> 13.4 us
  local copies, waits for them, and re-layouts: 1.81 us -> 2.52 us
    ppermute x3, waiting for transfers between devices: 1.48 us -> 4.05 us  [shards(): lax.ppermute(sent, 'dp', [(g, g ^ k) for g in range(groups)])]
    ppermute x3, waiting for transfers between devices: 2.43 us -> 0.01 us  [shards(): terms.append(lax.ppermute(merged[d], 'expert', down))]
    all_to_all x1, waiting for transfers between devices: 3.57 us -> 5.98 us  [shards(): lax.all_to_all(back.reshape(sources, rows, LANES), axes, split_axis=0, co...]
    ppermute x1, waiting for transfers between devices: 1.6 us -> 0.01 us  [shards(): arrived = lax.ppermute(other_part, 'expert', swap)]
    unnamed x26, local copies, waits for them, and re-layouts: 1.81 us -> 2.52 us
  transfers between devices with their start and end apart: 16 -> 16, of which waited for: 10 -> 7; matrix products, arithmetic and copies ran while one was open for 0% -> 0% of each run, Pallas kernels for 16% -> 16%
where the time goes in v9:
time: 57 us; the launch traced here: 56.6 us
  starting transfers between devices  29.2 us (51%)
  waiting for transfers between devices  13.4 us (24%)
  Pallas kernels  10.5 us (18%)
  local copies, waits for them, and re-layouts  2.52 us (4%)
  between operations  0.85 us (1%)
    ppermute x3, starting transfers between devices, shards(): mine.append(lax.ppermute(packed, 'expert', up))  10.7 us
    all_to_all x1, starting transfers between devices, shards(): lax.all_to_all(back.reshape(sources, rows, LANES), axes, split_axis=0, co...  6.74 us
    all_to_all x1, waiting for transfers between devices, shards(): lax.all_to_all(back.reshape(sources, rows, LANES), axes, split_axis=0, co...  5.98 us
    ppermute x3, waiting for transfers between devices, shards(): lax.ppermute(sent, 'dp', [(g, g ^ k) for g in range(groups)])  4.05 us
    ppermute x3, starting transfers between devices, shards(): terms.append(lax.ppermute(merged[d], 'expert', down))  3.88 us
    pallas_call x1, Pallas kernels, attention(): pl.pallas_call(functools.partial(attention_kernel, chips), in_specs=[IN_V...  3.7 us
    ppermute x3, starting transfers between devices, shards(): lax.ppermute(sent, 'dp', [(g, g ^ k) for g in range(groups)])  3.62 us
    all_to_all x1, starting transfers between devices, shards(): lax.all_to_all(send.reshape(sources, rows, LANES), axes, split_axis=0, co...  2.81 us
  transfers between devices with their start and end apart: 16, of which 7 were waited for; matrix products, arithmetic and copies ran while one was open for 0% of the time, Pallas kernels for 16%

profile of v9, /device:TPU:0, one launch (start us, length us, event | category | flops | bytes accessed | tf_op | source)
XLA Modules:
  0.0 56.6 jit_solution(6866522991347424715)
XLA Ops:
  0.7 0.9 %copy-done.8 = bf16[2,64,256]{2,1,0:T(8,128)(2,1)S(1)} copy-done((bf16[2,64,256]{2,1,0:T(8,128)(2,1)S(1)}, bf16[2,64,256]{2,1,0:T(8,128)(2,1)}, u32[]{:S(2)}) %copy-start.8) | copy-done | bytes 65560
  1.6 0.8 %copy-done.9 = bf16[2,64,256]{2,1,0:T(8,128)(2,1)S(1)} copy-done((bf16[2,64,256]{2,1,0:T(8,128)(2,1)S(1)}, bf16[2,64,256]{2,1,0:T(8,128)(2,1)}, u32[]{:S(2)}) %copy-start.9) | copy-done | bytes 65560
  2.4 0.2 pack.1.refs_3_.after_ref
  2.6 4.9 %collective-permute-start = (bf16[2,64,512]{2,1,0:T(8,128)(2,1)S(1)}, bf16[2,64,512]{2,1,0:T(8,128)(2,1)S(1)}, u32[]{:S(2)}, u32[]{:S(2)}) collective-permute-start(bf16[2,64,512]{2,1,0:T(8,128)(2,1)S(1)} %pack.1.refs_3_.after_ref), channel_id=1, source_target_pairs={{0,2},{1,3},{2,4},{3,5},{4,6},{5,7},{8,10},{9,11},{10,12},{11,13},... | collective-permute-start | bytes 393224 | tf_op jit(solution)/shard_map/ppermute | solution.py:381
  7.6 4.5 %collective-permute-start.1 = (bf16[2,64,512]{2,1,0:T(8,128)(2,1)S(1)}, bf16[2,64,512]{2,1,0:T(8,128)(2,1)S(1)}, u32[]{:S(2)}, u32[]{:S(2)}) collective-permute-start(bf16[2,64,512]{2,1,0:T(8,128)(2,1)S(1)} %pack.1.refs_3_.after_ref), channel_id=1, source_target_pairs={{0,4},{1,5},{2,6},{3,7},{8,12},{9,13},{10,14},{11,15},{16,20},{17,... | collective-permute-start | bytes 393224 | tf_op jit(solution)/shard_map/ppermute | solution.py:381
  12.1 1.3 %collective-permute-start.2 = (bf16[2,64,512]{2,1,0:T(8,128)(2,1)S(1)}, bf16[2,64,512]{2,1,0:T(8,128)(2,1)S(1)}, u32[]{:S(2)}, u32[]{:S(2)}) collective-permute-start(bf16[2,64,512]{2,1,0:T(8,128)(2,1)S(1)} %pack.1.refs_3_.after_ref), channel_id=1, source_target_pairs={{0,6},{1,7},{8,14},{9,15},{16,22},{17,23},{24,30},{25,31}} | collective-permute-start | bytes 393224 | tf_op jit(solution)/shard_map/ppermute | solution.py:381
  13.4 0.0 copy-start
  13.4 0.0 copy-start.1
  13.4 0.0 copy-start.2
  13.5 1.2 %dispatch.1 = bf16[512,128]{1,0:T(8,128)(2,1)} custom-call(bf16[128,2048]{1,0:T(8,128)(2,1)S(1)} %copy-done.5, bf16[128,2048]{1,0:T(8,128)(2,1)S(1)} %copy-done.6, s32[10,128]{1,0:T(8,128)S(1)} %bitcast.10, bf16[10,128]{1,0:T(8,128)(2,1)S(1)} %bitcast.12, bf16[2,64,512]{2,1,0:T(8,128)(2,1)S(1)} %pack.1.refs_3_.after_ref), custom_call_target="tpu_custom_call" | custom-call | flops 2000000000 | bytes 2097152 | tf_op jit(solution)/shard_map/dispatch/pallas_call | solution.py:385
  14.7 2.8 %all-to-all-start = ((bf16[32,16,128]{2,1,0:T(8,128)(2,1)}), bf16[32,16,128]{2,1,0:T(8,128)(2,1)S(1)}, u32[]{:S(2)}, u32[]{:S(2)}) async-start(bf16[32,16,128]{2,1,0:T(8,128)(2,1)} %bitcast.2), calls=%async_computation | async-start | bytes 262144 | tf_op jit(solution)/shard_map/all_to_all | solution.py:393
  17.5 0.3 collective-permute-start.3
  17.8 0.0 collective-permute-done.refs_4_
  17.8 0.3 collective-permute-start.4
  18.1 0.0 collective-permute-done.1.refs_5_
  18.1 0.3 collective-permute-start.5
  18.3 0.0 collective-permute-done.2.refs_6_
  18.3 0.3 collective-permute-start.6
  18.6 0.3 collective-permute-done.3.refs_7_
  18.9 0.3 collective-permute-done.4.refs_8_
  19.2 0.3 collective-permute-done.5.refs_9_
  19.4 0.3 collective-permute-done.6.refs_10_
  19.7 3.7 %attention.1 = (bf16[2,64,2048]{2,1,0:T(8,128)(2,1)}, bf16[2,64,2048]{2,1,0:T(8,128)(2,1)}, bf16[4,2,64,512]{3,2,1,0:T(8,128)(2,1)S(1)}, bf16[2,64,512]{2,1,0:T(...) custom-call(bf16[2,64,2048]{2,1,0:T(8,128)(2,1)S(1)} %copy-done, ...), custom_call_target="tpu_custom_call" | custom-call | flops 1048576 | bytes 8 | tf_op jit(solution)/shard_map/attention/pallas_call | solution.py:131
  23.4 2.3 %all-to-all-done = bf16[32,16,128]{2,1,0:T(8,128)(2,1)S(1)} async-done(((bf16[32,16,128]{2,1,0:T(8,128)(2,1)}), bf16[32,16,128]{2,1,0:T(8,128)(2,1)S(1)}, u32[]{:S(2)}, u32[]{:S(2)}) %all-to-all-start) | async-done | bytes 131104 | tf_op jit(solution)/shard_map/all_to_all | solution.py:393
  25.7 0.4 collective-permute-start.7
  26.1 0.6 %copy-done.3 = bf16[1,512,256]{2,1,0:T(8,128)(2,1)S(1)} copy-done((bf16[1,512,256]{2,1,0:T(8,128)(2,1)S(1)}, bf16[1,512,256]{2,1,0:T(8,128)(2,1)}, u32[]{:S(2)}) %copy-start.3) | copy-done | bytes 262168
  26.6 0.1 copy-done.4
  26.7 0.1 copy-done.7
  26.8 0.5 enter.1
  27.2 0.9 %collective-permute-start.11 = (bf16[64,768]{1,0:T(8,128)(2,1)S(1)}, bf16[64,768]{1,0:T(8,128)(2,1)S(1)}, u32[]{:S(2)}, u32[]{:S(2)}) collective-permute-start(bf16[64,768]{1,0:T(8,128)(2,1)S(1)} %get-tuple-element.47.refs_0_), channel_id=1, source_target_pairs={{0,8},{8,0},{16,24},{24,16},{1,9},{9,1},{17,25},{25,17},{2,10},{10... | collective-permute-start | bytes 294920 | tf_op jit(solution)/shard_map/ppermute | solution.py:412
  28.1 0.0 collective-permute-done.7.refs_4_
  28.1 0.1 merge.1
  28.3 1.3 %collective-permute-start.8 = (bf16[2,64,512]{2,1,0:T(8,128)(2,1)S(1)}, bf16[2,64,512]{2,1,0:T(8,128)(2,1)S(1)}, u32[]{:S(2)}, u32[]{:S(2)}) collective-permute-start(bf16[2,64,512]{2,1,0:T(8,128)(2,1)S(1)} %get-tuple-element.41), channel_id=1, source_target_pairs={{2,0},{3,1},{4,2},{5,3},{6,4},{7,5},{10,8},{11,9},{12,10},{13,11},... | collective-permute-start | bytes 393224 | tf_op jit(solution)/shard_map/ppermute | solution.py:426
  29.6 1.3 %collective-permute-start.10 = (bf16[2,64,512]{2,1,0:T(8,128)(2,1)S(1)}, bf16[2,64,512]{2,1,0:T(8,128)(2,1)S(1)}, u32[]{:S(2)}, u32[]{:S(2)}) collective-permute-start(bf16[2,64,512]{2,1,0:T(8,128)(2,1)S(1)} %get-tuple-element.43), channel_id=1, source_target_pairs={{6,0},{7,1},{14,8},{15,9},{22,16},{23,17},{30,24},{31,25}} | collective-permute-start | bytes 393224 | tf_op jit(solution)/shard_map/ppermute | solution.py:426
  30.9 1.3 %collective-permute-start.9 = (bf16[2,64,512]{2,1,0:T(8,128)(2,1)S(1)}, bf16[2,64,512]{2,1,0:T(8,128)(2,1)S(1)}, u32[]{:S(2)}, u32[]{:S(2)}) collective-permute-start(bf16[2,64,512]{2,1,0:T(8,128)(2,1)S(1)} %get-tuple-element.42), channel_id=1, source_target_pairs={{4,0},{5,1},{6,2},{7,3},{12,8},{13,9},{14,10},{15,11},{20,16},{21,... | collective-permute-start | bytes 393224 | tf_op jit(solution)/shard_map/ppermute | solution.py:426
  32.2 0.8 %collective-permute-start.12 = (bf16[64,768]{1,0:T(8,128)(2,1)S(1)}, bf16[64,768]{1,0:T(8,128)(2,1)S(1)}, u32[]{:S(2)}, u32[]{:S(2)}) collective-permute-start(bf16[64,768]{1,0:T(8,128)(2,1)S(1)} %get-tuple-element.47.refs_0_), channel_id=1, source_target_pairs={{0,16},{8,24},{16,0},{24,8},{1,17},{9,25},{17,1},{25,9},{2,18},{10... | collective-permute-start | bytes 294920 | tf_op jit(solution)/shard_map/ppermute | solution.py:412
  32.9 0.0 collective-permute-done.11.refs_1_
  32.9 2.0 %collective-permute-start.13 = (bf16[64,768]{1,0:T(8,128)(2,1)S(1)}, bf16[64,768]{1,0:T(8,128)(2,1)S(1)}, u32[]{:S(2)}, u32[]{:S(2)}) collective-permute-start(bf16[64,768]{1,0:T(8,128)(2,1)S(1)} %get-tuple-element.47.refs_0_), channel_id=1, source_target_pairs={{0,24},{8,16},{16,8},{24,0},{1,25},{9,17},{17,9},{25,1},{2,26},{10... | collective-permute-start | bytes 294920 | tf_op jit(solution)/shard_map/ppermute | solution.py:412
  34.9 4.0 %collective-permute-done.12.refs_2_ = bf16[64,768]{1,0:T(8,128)(2,1)S(1)} collective-permute-done((bf16[64,768]{1,0:T(8,128)(2,1)S(1)}, bf16[64,768]{1,0:T(8,128)(2,1)S(1)}, u32[]{:S(2)}, u32[]{:S(2)}) %collective-permute-start.12) | collective-permute-done | bytes 98336 | tf_op jit(solution)/shard_map/ppermute | solution.py:412
  39.0 0.0 collective-permute-done.13.refs_3_
  39.0 0.0 collective-permute-done.8.refs_1_.refs_6_
  39.0 1.4 %middle.1 = (bf16[512,128]{1,0:T(8,128)(2,1)}, bf16[64,256]{1,0:T(8,128)(2,1)S(1)}, bf16[64,256]{1,0:T(8,128)(2,1)S(1)}, bf16[64,256]{1,0:T(8,128)(2,1)S(1)}) custom-call(bf16[64,768]{1,0:T(8,128)(2,1)S(1)} %get-tuple-element.47.refs_0_, bf16[64,768]{1,0:T(8,128)(2,1)S(1)} %collective-permute-done.11.refs_1_, ...), custom_call_target="tpu_custom_call" | custom-call | flops 8 | bytes 8 | tf_op jit(solution)/shard_map/middle/pallas_call | solution.py:427
  40.4 6.7 %all-to-all-start.1 = ((bf16[32,16,128]{2,1,0:T(8,128)(2,1)}), bf16[32,16,128]{2,1,0:T(8,128)(2,1)S(1)}, u32[]{:S(2)}, u32[]{:S(2)}) async-start(bf16[32,16,128]{2,1,0:T(8,128)(2,1)} %bitcast.4), calls=%async_computation.1 | async-start | bytes 262144 | tf_op jit(solution)/shard_map/all_to_all | solution.py:435
  47.1 0.0 collective-permute-done.9.refs_2_
  47.2 0.7 %close.1 = (bf16[2,64,256]{2,1,0:T(8,128)(2,1)}, bf16[2,64,256]{2,1,0:T(8,128)(2,1)}) custom-call(bf16[2,64,512]{2,1,0:T(8,128)(2,1)S(1)} %get-tuple-element.40.refs_0_, bf16[2,64,512]{2,1,0:T(8,128)(2,1)S(1)} %collective-permute-done.8.refs_1_.refs_6_, bf16[2,64,512]{2,1,0:T(8,128)(2,1)S(1)} %collective-permute-done.9.refs_2_, ...), custom_call_target="tpu_custom_call" | custom-call | flops 60000002048 | bytes 1048576 | tf_op jit(solution)/shard_map/close/pallas_call | solution.py:449
  47.9 1.5 %weight_grads.1 = (f32[1,512,256]{2,1,0:T(8,128)}, f32[1,512,256]{2,1,0:T(8,128)}, f32[1,256,512]{2,1,0:T(8,128)}) custom-call(bf16[64,512]{1,0:T(8,128)(2,1)S(1)} %get-tuple-element.51.input_ref, bf16[64,512]{1,0:T(8,128)(2,1)S(1)} %get-tuple-element.52.grad_ref, bf16[64,256]{1,0:T(8,128)(2,1)S(1)} %get-tuple-element.53.hidden_ref, ...), custom_call_target="tpu_custom_call" | custom-call | flops 2000000000 | bytes 2097152 | tf_op jit(solution)/shard_map/weight_grads/pallas_call | solution.py:438
  49.3 6.0 %all-to-all-done.1 = bf16[32,16,128]{2,1,0:T(8,128)(2,1)S(1)} async-done(((bf16[32,16,128]{2,1,0:T(8,128)(2,1)}), bf16[32,16,128]{2,1,0:T(8,128)(2,1)S(1)}, u32[]{:S(2)}, u32[]{:S(2)}) %all-to-all-start.1) | async-done | bytes 131104 | tf_op jit(solution)/shard_map/all_to_all | solution.py:435
  55.3 1.3 %combine.1 = (bf16[128,2048]{1,0:T(8,128)(2,1)}, bf16[10,128]{1,0:T(8,128)(2,1)}) custom-call(bf16[512,128]{1,0:T(8,128)(2,1)S(1)} %bitcast.9, s32[10,128]{1,0:T(8,128)S(1)} %bitcast.11, bf16[10,128]{1,0:T(8,128)(2,1)S(1)} %bitcast.13, bf16[2,64,256]{2,1,0:T(8,128)(2,1)S(1)} %copy-done.12), custom_call_target="tpu_custom_call" | custom-call | flops 2000000000 | bytes 2097152 | tf_op jit(solution)/shard_map/combine/pallas_call | solution.py:457
  (20 shorter events, 0.0 us)
Async XLA Ops:
  0.6 12.7 %copy-start.5 = (bf16[128,2048]{1,0:T(8,128)(2,1)S(1)}, bf16[128,2048]{1,0:T(8,128)(2,1)}, u32[]{:S(2)}) copy-start(bf16[128,2048]{1,0:T(8,128)(2,1)} %input_ref.1) | copy-start | bytes 1572868
  0.7 12.7 %copy-start.6 = (bf16[128,2048]{1,0:T(8,128)(2,1)S(1)}, bf16[128,2048]{1,0:T(8,128)(2,1)}, u32[]{:S(2)}) copy-start(bf16[128,2048]{1,0:T(8,128)(2,1)} %grad_ref.1) | copy-start | bytes 1572868
  0.7 0.9 %copy-start.8 = (bf16[2,64,256]{2,1,0:T(8,128)(2,1)S(1)}, bf16[2,64,256]{2,1,0:T(8,128)(2,1)}, u32[]{:S(2)}) copy-start(bf16[2,64,256]{2,1,0:T(8,128)(2,1)} %key_hbm.1) | copy-start | bytes 196612
  1.6 0.8 %copy-start.9 = (bf16[2,64,256]{2,1,0:T(8,128)(2,1)S(1)}, bf16[2,64,256]{2,1,0:T(8,128)(2,1)}, u32[]{:S(2)}) copy-start(bf16[2,64,256]{2,1,0:T(8,128)(2,1)} %value_hbm.1) | copy-start | bytes 196612
  2.4 11.0 %copy-start.10 = (s32[128,10]{0,1:T(8,128)S(1)}, s32[128,10]{0,1:T(8,128)}, u32[]{:S(2)}) copy-start(s32[128,10]{0,1:T(8,128)} %param.19) | copy-start | bytes 15364
  2.4 11.0 %copy-start.11 = (bf16[128,10]{0,1:T(8,128)(2,1)S(1)}, bf16[128,10]{0,1:T(8,128)(2,1)}, u32[]{:S(2)}) copy-start(bf16[128,10]{0,1:T(8,128)(2,1)} %param.20) | copy-start | bytes 7684
  2.6 15.2 %collective-permute-start = (bf16[2,64,512]{2,1,0:T(8,128)(2,1)S(1)}, bf16[2,64,512]{2,1,0:T(8,128)(2,1)S(1)}, u32[]{:S(2)}, u32[]{:S(2)}) collective-permute-start(bf16[2,64,512]{2,1,0:T(8,128)(2,1)S(1)} %pack.1.refs_3_.after_ref), channel_id=1, source_target_pairs={{0,2},{1,3},{2,4},{3,5},{4,6},{5,7},{8,10},{9,11},{10,12},{11,13},... | collective-permute-start | bytes 393224 | tf_op jit(solution)/shard_map/ppermute | solution.py:381
  7.6 10.5 %collective-permute-start.1 = (bf16[2,64,512]{2,1,0:T(8,128)(2,1)S(1)}, bf16[2,64,512]{2,1,0:T(8,128)(2,1)S(1)}, u32[]{:S(2)}, u32[]{:S(2)}) collective-permute-start(bf16[2,64,512]{2,1,0:T(8,128)(2,1)S(1)} %pack.1.refs_3_.after_ref), channel_id=1, source_target_pairs={{0,4},{1,5},{2,6},{3,7},{8,12},{9,13},{10,14},{11,15},{16,20},{17,... | collective-permute-start | bytes 393224 | tf_op jit(solution)/shard_map/ppermute | solution.py:381
  12.1 6.3 %collective-permute-start.2 = (bf16[2,64,512]{2,1,0:T(8,128)(2,1)S(1)}, bf16[2,64,512]{2,1,0:T(8,128)(2,1)S(1)}, u32[]{:S(2)}, u32[]{:S(2)}) collective-permute-start(bf16[2,64,512]{2,1,0:T(8,128)(2,1)S(1)} %pack.1.refs_3_.after_ref), channel_id=1, source_target_pairs={{0,6},{1,7},{8,14},{9,15},{16,22},{17,23},{24,30},{25,31}} | collective-permute-start | bytes 393224 | tf_op jit(solution)/shard_map/ppermute | solution.py:381
  13.4 6.3 %copy-start = (bf16[2,64,2048]{2,1,0:T(8,128)(2,1)S(1)}, bf16[2,64,2048]{2,1,0:T(8,128)(2,1)}, u32[]{:S(2)}) copy-start(bf16[2,64,2048]{2,1,0:T(8,128)(2,1)} %refs_0_.1) | copy-start | bytes 1572868
  13.4 6.3 %copy-start.1 = (bf16[2,64,2048]{2,1,0:T(8,128)(2,1)S(1)}, bf16[2,64,2048]{2,1,0:T(8,128)(2,1)}, u32[]{:S(2)}) copy-start(bf16[2,64,2048]{2,1,0:T(8,128)(2,1)} %refs_1_.1) | copy-start | bytes 1572868
  13.4 6.3 %copy-start.2 = (bf16[2,64,2048]{2,1,0:T(8,128)(2,1)S(1)}, bf16[2,64,2048]{2,1,0:T(8,128)(2,1)}, u32[]{:S(2)}) copy-start(bf16[2,64,2048]{2,1,0:T(8,128)(2,1)} %refs_2_.1) | copy-start | bytes 1572868
  14.7 11.0 %all-to-all-start = ((bf16[32,16,128]{2,1,0:T(8,128)(2,1)}), bf16[32,16,128]{2,1,0:T(8,128)(2,1)S(1)}, u32[]{:S(2)}, u32[]{:S(2)}) async-start(bf16[32,16,128]{2,1,0:T(8,128)(2,1)} %bitcast.2), calls=%async_computation | async-start | bytes 262144 | tf_op jit(solution)/shard_map/all_to_all | solution.py:393
  17.5 1.4 %collective-permute-start.3 = (bf16[2,64,512]{2,1,0:T(8,128)(2,1)S(1)}, bf16[2,64,512]{2,1,0:T(8,128)(2,1)S(1)}, u32[]{:S(2)}, u32[]{:S(2)}) collective-permute-start(bf16[2,64,512]{2,1,0:T(8,128)(2,1)S(1)} %pack.1.refs_3_.after_ref), channel_id=1, source_target_pairs={{0,1},{1,0},{2,3},{3,2},{4,5},{5,4},{6,7},{7,6},{8,9},{9,8},{10,11... | collective-permute-start | bytes 393224 | tf_op jit(solution)/shard_map/ppermute | solution.py:382
  17.8 1.3 %collective-permute-start.4 = (bf16[2,64,512]{2,1,0:T(8,128)(2,1)S(1)}, bf16[2,64,512]{2,1,0:T(8,128)(2,1)S(1)}, u32[]{:S(2)}, u32[]{:S(2)}) collective-permute-start(bf16[2,64,512]{2,1,0:T(8,128)(2,1)S(1)} %collective-permute-done.refs_4_), channel_id=1, source_target_pairs={{0,1},{1,0},{2,3},{3,2},{4,5},{5,4},{6,7},{7,6},{8,9},{9,8},{10,11... | collective-permute-start | bytes 393224 | tf_op jit(solution)/shard_map/ppermute | solution.py:382
  18.1 1.3 %collective-permute-start.5 = (bf16[2,64,512]{2,1,0:T(8,128)(2,1)S(1)}, bf16[2,64,512]{2,1,0:T(8,128)(2,1)S(1)}, u32[]{:S(2)}, u32[]{:S(2)}) collective-permute-start(bf16[2,64,512]{2,1,0:T(8,128)(2,1)S(1)} %collective-permute-done.1.refs_5_), channel_id=1, source_target_pairs={{0,1},{1,0},{2,3},{3,2},{4,5},{5,4},{6,7},{7,6},{8,9},{9,8},{10,11... | collective-permute-start | bytes 393224 | tf_op jit(solution)/shard_map/ppermute | solution.py:382
  18.3 1.3 %collective-permute-start.6 = (bf16[2,64,512]{2,1,0:T(8,128)(2,1)S(1)}, bf16[2,64,512]{2,1,0:T(8,128)(2,1)S(1)}, u32[]{:S(2)}, u32[]{:S(2)}) collective-permute-start(bf16[2,64,512]{2,1,0:T(8,128)(2,1)S(1)} %collective-permute-done.2.refs_6_), channel_id=1, source_target_pairs={{0,1},{1,0},{2,3},{3,2},{4,5},{5,4},{6,7},{7,6},{8,9},{9,8},{10,11... | collective-permute-start | bytes 393224 | tf_op jit(solution)/shard_map/ppermute | solution.py:382
  25.7 1.0 %copy-start.3 = (bf16[1,512,256]{2,1,0:T(8,128)(2,1)S(1)}, bf16[1,512,256]{2,1,0:T(8,128)(2,1)}, u32[]{:S(2)}) copy-start(bf16[1,512,256]{2,1,0:T(8,128)(2,1)} %refs_4_.1) | copy-start | bytes 786436
  25.7 1.0 %copy-start.4 = (bf16[1,512,256]{2,1,0:T(8,128)(2,1)S(1)}, bf16[1,512,256]{2,1,0:T(8,128)(2,1)}, u32[]{:S(2)}) copy-start(bf16[1,512,256]{2,1,0:T(8,128)(2,1)} %refs_5_.1) | copy-start | bytes 786436
  25.7 1.1 %copy-start.7 = (bf16[1,256,512]{2,1,0:T(8,128)(2,1)S(1)}, bf16[1,256,512]{2,1,0:T(8,128)(2,1)}, u32[]{:S(2)}) copy-start(bf16[1,256,512]{2,1,0:T(8,128)(2,1)} %down_ref.1) | copy-start | bytes 786436
  25.7 2.4 %collective-permute-start.7 = (bf16[4,2,64,512]{3,2,1,0:T(8,128)(2,1)S(1)}, bf16[4,2,64,512]{3,2,1,0:T(8,128)(2,1)S(1)}, u32[]{:S(2)}, u32[]{:S(2)}) collective-permute-start(bf16[4,2,64,512]{3,2,1,0:T(8,128)(2,1)S(1)} %gate.1.after_ref), channel_id=1, source_target_pairs={{0,1},{1,0},{2,3},{3,2},{4,5},{5,4},{6,7},{7,6},{8,9},{9,8},{10,11... | collective-permute-start | bytes 1572872 | tf_op jit(solution)/shard_map/ppermute | solution.py:415
  27.2 5.7 %collective-permute-start.11 = (bf16[64,768]{1,0:T(8,128)(2,1)S(1)}, bf16[64,768]{1,0:T(8,128)(2,1)S(1)}, u32[]{:S(2)}, u32[]{:S(2)}) collective-permute-start(bf16[64,768]{1,0:T(8,128)(2,1)S(1)} %get-tuple-element.47.refs_0_), channel_id=1, source_target_pairs={{0,8},{8,0},{16,24},{24,16},{1,9},{9,1},{17,25},{25,17},{2,10},{10... | collective-permute-start | bytes 294920 | tf_op jit(solution)/shard_map/ppermute | solution.py:412
  28.3 10.7 %collective-permute-start.8 = (bf16[2,64,512]{2,1,0:T(8,128)(2,1)S(1)}, bf16[2,64,512]{2,1,0:T(8,128)(2,1)S(1)}, u32[]{:S(2)}, u32[]{:S(2)}) collective-permute-start(bf16[2,64,512]{2,1,0:T(8,128)(2,1)S(1)} %get-tuple-element.41), channel_id=1, source_target_pairs={{2,0},{3,1},{4,2},{5,3},{6,4},{7,5},{10,8},{11,9},{12,10},{13,11},... | collective-permute-start | bytes 393224 | tf_op jit(solution)/shard_map/ppermute | solution.py:426
  29.6 17.6 %collective-permute-start.10 = (bf16[2,64,512]{2,1,0:T(8,128)(2,1)S(1)}, bf16[2,64,512]{2,1,0:T(8,128)(2,1)S(1)}, u32[]{:S(2)}, u32[]{:S(2)}) collective-permute-start(bf16[2,64,512]{2,1,0:T(8,128)(2,1)S(1)} %get-tuple-element.43), channel_id=1, source_target_pairs={{6,0},{7,1},{14,8},{15,9},{22,16},{23,17},{30,24},{31,25}} | collective-permute-start | bytes 393224 | tf_op jit(solution)/shard_map/ppermute | solution.py:426
  30.9 16.3 %collective-permute-start.9 = (bf16[2,64,512]{2,1,0:T(8,128)(2,1)S(1)}, bf16[2,64,512]{2,1,0:T(8,128)(2,1)S(1)}, u32[]{:S(2)}, u32[]{:S(2)}) collective-permute-start(bf16[2,64,512]{2,1,0:T(8,128)(2,1)S(1)} %get-tuple-element.42), channel_id=1, source_target_pairs={{4,0},{5,1},{6,2},{7,3},{12,8},{13,9},{14,10},{15,11},{20,16},{21,... | collective-permute-start | bytes 393224 | tf_op jit(solution)/shard_map/ppermute | solution.py:426
  32.2 6.8 %collective-permute-start.12 = (bf16[64,768]{1,0:T(8,128)(2,1)S(1)}, bf16[64,768]{1,0:T(8,128)(2,1)S(1)}, u32[]{:S(2)}, u32[]{:S(2)}) collective-permute-start(bf16[64,768]{1,0:T(8,128)(2,1)S(1)} %get-tuple-element.47.refs_0_), channel_id=1, source_target_pairs={{0,16},{8,24},{16,0},{24,8},{1,17},{9,25},{17,1},{25,9},{2,18},{10... | collective-permute-start | bytes 294920 | tf_op jit(solution)/shard_map/ppermute | solution.py:412
  32.9 6.0 %collective-permute-start.13 = (bf16[64,768]{1,0:T(8,128)(2,1)S(1)}, bf16[64,768]{1,0:T(8,128)(2,1)S(1)}, u32[]{:S(2)}, u32[]{:S(2)}) collective-permute-start(bf16[64,768]{1,0:T(8,128)(2,1)S(1)} %get-tuple-element.47.refs_0_), channel_id=1, source_target_pairs={{0,24},{8,16},{16,8},{24,0},{1,25},{9,17},{17,9},{25,1},{2,26},{10... | collective-permute-start | bytes 294920 | tf_op jit(solution)/shard_map/ppermute | solution.py:412
  40.4 14.9 %all-to-all-start.1 = ((bf16[32,16,128]{2,1,0:T(8,128)(2,1)}), bf16[32,16,128]{2,1,0:T(8,128)(2,1)S(1)}, u32[]{:S(2)}, u32[]{:S(2)}) async-start(bf16[32,16,128]{2,1,0:T(8,128)(2,1)} %bitcast.4), calls=%async_computation.1 | async-start | bytes 262144 | tf_op jit(solution)/shard_map/all_to_all | solution.py:435
  47.9 7.5 %copy-start.12 = (bf16[2,64,256]{2,1,0:T(8,128)(2,1)S(1)}, bf16[2,64,256]{2,1,0:T(8,128)(2,1)}, u32[]{:S(2)}) copy-start(bf16[2,64,256]{2,1,0:T(8,128)(2,1)} %get-tuple-element.26.after_ref) | copy-start | bytes 196612

commit v10 on v6

--- a/solution.py
+++ b/solution.py
@@ -166,7 +166,7 @@
 
 
 def close_kernel(*refs):
-    parts, (key_ref, value_ref) = refs[:-2], refs[-2:]
+    parts, (key_ref, value_ref) = refs[:-3], refs[-2:]
     total = parts[0][...].astype(F32)
     for part in parts[1:]:
         total = total + part[...].astype(F32)
@@ -251,8 +251,8 @@
 
 
 def middle_kernel(sources, rows, *refs):
-    parts = refs[:-7]
-    gate_ref, up_ref, _, back_ref, hidden_ref, gate_rows_ref, up_rows_ref = refs[-7:]
+    parts = refs[:-8]
+    gate_ref, up_ref, _, _, back_ref, hidden_ref, gate_rows_ref, up_rows_ref = refs[-8:]
     share = gate_ref.shape[1]
     pieces = share // LANES
     hid = gate_ref.shape[2]
@@ -307,7 +307,6 @@
     back_ref,
     routes_ref,
     weights_ref,
-    after_ref,
     input_grad_ref,
     route_grad_ref,
 ):
@@ -426,12 +425,12 @@
         terms.append(lax.ppermute(merged[d], "expert", down))
     back, hidden, gate_rows, up_rows = pl.pallas_call(
         functools.partial(middle_kernel, sources, rows),
-        in_specs=[IN_VMEM] * (len(parts) + 2) + [ANYWHERE],
+        in_specs=[IN_VMEM] * (len(parts) + 2) + [ANYWHERE] * 2,
         out_shape=[jax.ShapeDtypeStruct((sources * rows, LANES), BF16)] + [hid_rows] * 3,
         compiler_params=params(16 if groups <= 4 else 60),
         cost_estimate=cost(2e9, 2 * MIB),
         name="middle",
-    )(*parts, gate_proj, up_proj, terms[min(1, chips - 1)])
+    )(*parts, gate_proj, up_proj, terms[min(1, chips - 1)], terms[min(3, chips - 1)])
     returned = lax.all_to_all(
         back.reshape(sources, rows, LANES), axes, split_axis=0, concat_axis=0, tiled=True
     ).reshape(sources * rows, LANES)
@@ -446,17 +445,9 @@
         cost_estimate=cost(2e9, 2 * MIB),
         name="weight_grads",
     )(inputs, grads, hidden, gate_rows, up_rows)
-    key_grad, value_grad = pl.pallas_call(
-        close_kernel,
-        in_specs=[IN_VMEM] * chips,
-        out_shape=[jax.ShapeDtypeStruct((seqs, length, HEAD), BF16)] * 2,
-        compiler_params=params(16),
-        cost_estimate=cost(6e10, MIB),
-        name="close",
-    )(*terms)
     input_grad, route_grad = pl.pallas_call(
         functools.partial(combine_kernel, devices, groups, rows),
-        in_specs=[IN_VMEM] * 3 + [ANYWHERE],
+        in_specs=[IN_VMEM] * 3,
         out_shape=[
             jax.ShapeDtypeStruct(moe_input.shape, BF16),
             jax.ShapeDtypeStruct(routes_t.shape, BF16),
@@ -464,8 +455,16 @@
         compiler_params=params(16),
         cost_estimate=cost(2e9, 2 * MIB),
         name="combine",
-    )(returned, routes_t, weights_t, key_grad)
-
+    )(returned, routes_t, weights_t)
+
+    key_grad, value_grad = pl.pallas_call(
+        close_kernel,
+        in_specs=[IN_VMEM] * chips + [ANYWHERE],
+        out_shape=[jax.ShapeDtypeStruct((seqs, length, HEAD), BF16)] * 2,
+        compiler_params=params(16),
+        cost_estimate=cost(MIB, MIB),
+        name="close",
+    )(*terms, route_grad)
     return (
         query_grad,
         key_grad,

time: 55.3 us -> 62.8 us (1.14)
  waiting for transfers between devices: 12.4 us -> 21.2 us
  starting transfers between devices: 29.2 us -> 27.2 us
  local copies, waits for them, and re-layouts: 1.81 us -> 2.49 us
    ppermute x3, waiting for transfers between devices: 2.43 us -> 6.74 us  [shards(): terms.append(lax.ppermute(merged[d], 'expert', down))]
    ppermute x3, waiting for transfers between devices: 1.48 us -> 4.15 us  [shards(): lax.ppermute(sent, 'dp', [(g, g ^ k) for g in range(groups)])]
    all_to_all x1, starting transfers between devices: 6.71 us -> 4.69 us  [shards(): lax.all_to_all(back.reshape(sources, rows, LANES), axes, split_axis=0, co...]
    all_to_all x1, waiting for transfers between devices: 3.57 us -> 5.4 us  [shards(): lax.all_to_all(back.reshape(sources, rows, LANES), axes, split_axis=0, co...]
    unnamed x26, local copies, waits for them, and re-layouts: 1.81 us -> 2.49 us
  transfers between devices with their start and end apart: 16 -> 16, of which waited for: 10 -> 11; matrix products, arithmetic and copies ran while one was open for 0% -> 0% of each run, Pallas kernels for 16% -> 13%
where the time goes in v10:
time: 62.8 us; the launch traced here: 62.3 us
  starting transfers between devices  27.2 us (43%)
  waiting for transfers between devices  21.2 us (34%)
  Pallas kernels  10.6 us (17%)
  local copies, waits for them, and re-layouts  2.49 us (4%)
  between operations  0.85 us (1%)
    ppermute x3, starting transfers between devices, shards(): mine.append(lax.ppermute(packed, 'expert', up))  10.7 us
    ppermute x3, waiting for transfers between devices, shards(): terms.append(lax.ppermute(merged[d], 'expert', down))  6.74 us
    all_to_all x1, waiting for transfers between devices, shards(): lax.all_to_all(back.reshape(sources, rows, LANES), axes, split_axis=0, co...  5.4 us
    all_to_all x1, starting transfers between devices, shards(): lax.all_to_all(back.reshape(sources, rows, LANES), axes, split_axis=0, co...  4.69 us
    ppermute x3, waiting for transfers between devices, shards(): lax.ppermute(sent, 'dp', [(g, g ^ k) for g in range(groups)])  4.15 us
    ppermute x3, starting transfers between devices, shards(): terms.append(lax.ppermute(merged[d], 'expert', down))  4.01 us
    pallas_call x1, Pallas kernels, attention(): pl.pallas_call(functools.partial(attention_kernel, chips), in_specs=[IN_V...  3.7 us
    ppermute x3, starting transfers between devices, shards(): lax.ppermute(sent, 'dp', [(g, g ^ k) for g in range(groups)])  3.55 us
  transfers between devices with their start and end apart: 16, of which 11 were waited for; matrix products, arithmetic and copies ran while one was open for 0% of the time, Pallas kernels for 13%

profile of v10, /device:TPU:0, one launch (start us, length us, event | category | flops | bytes accessed | tf_op | source)
XLA Modules:
  0.0 62.3 jit_solution(11039741012152159494)
XLA Ops:
  0.7 0.9 %copy-done.9 = bf16[2,64,256]{2,1,0:T(8,128)(2,1)S(1)} copy-done((bf16[2,64,256]{2,1,0:T(8,128)(2,1)S(1)}, bf16[2,64,256]{2,1,0:T(8,128)(2,1)}, u32[]{:S(2)}) %copy-start.9) | copy-done | bytes 65560
  1.6 0.8 %copy-done.10 = bf16[2,64,256]{2,1,0:T(8,128)(2,1)S(1)} copy-done((bf16[2,64,256]{2,1,0:T(8,128)(2,1)S(1)}, bf16[2,64,256]{2,1,0:T(8,128)(2,1)}, u32[]{:S(2)}) %copy-start.10) | copy-done | bytes 65560
  2.4 0.2 pack.1.refs_3_.after_ref
  2.6 7.0 %collective-permute-start.2 = (bf16[2,64,512]{2,1,0:T(8,128)(2,1)S(1)}, bf16[2,64,512]{2,1,0:T(8,128)(2,1)S(1)}, u32[]{:S(2)}, u32[]{:S(2)}) collective-permute-start(bf16[2,64,512]{2,1,0:T(8,128)(2,1)S(1)} %pack.1.refs_3_.after_ref), channel_id=1, source_target_pairs={{0,6},{1,7},{8,14},{9,15},{16,22},{17,23},{24,30},{25,31}} | collective-permute-start | bytes 393224 | tf_op jit(solution)/shard_map/ppermute | solution.py:380
  9.6 1.3 %collective-permute-start.1 = (bf16[2,64,512]{2,1,0:T(8,128)(2,1)S(1)}, bf16[2,64,512]{2,1,0:T(8,128)(2,1)S(1)}, u32[]{:S(2)}, u32[]{:S(2)}) collective-permute-start(bf16[2,64,512]{2,1,0:T(8,128)(2,1)S(1)} %pack.1.refs_3_.after_ref), channel_id=1, source_target_pairs={{0,4},{1,5},{2,6},{3,7},{8,12},{9,13},{10,14},{11,15},{16,20},{17,... | collective-permute-start | bytes 393224 | tf_op jit(solution)/shard_map/ppermute | solution.py:380
  10.9 2.5 %collective-permute-start = (bf16[2,64,512]{2,1,0:T(8,128)(2,1)S(1)}, bf16[2,64,512]{2,1,0:T(8,128)(2,1)S(1)}, u32[]{:S(2)}, u32[]{:S(2)}) collective-permute-start(bf16[2,64,512]{2,1,0:T(8,128)(2,1)S(1)} %pack.1.refs_3_.after_ref), channel_id=1, source_target_pairs={{0,2},{1,3},{2,4},{3,5},{4,6},{5,7},{8,10},{9,11},{10,12},{11,13},... | collective-permute-start | bytes 393224 | tf_op jit(solution)/shard_map/ppermute | solution.py:380
  13.4 0.0 copy-done.5
  13.4 0.0 copy-start
  13.4 0.0 copy-start.1
  13.4 0.0 copy-start.2
  13.4 1.2 %dispatch.1 = bf16[512,128]{1,0:T(8,128)(2,1)} custom-call(bf16[128,2048]{1,0:T(8,128)(2,1)S(1)} %copy-done.4, bf16[128,2048]{1,0:T(8,128)(2,1)S(1)} %copy-done.5, s32[10,128]{1,0:T(8,128)S(1)} %bitcast.11, bf16[10,128]{1,0:T(8,128)(2,1)S(1)} %bitcast.13, bf16[2,64,512]{2,1,0:T(8,128)(2,1)S(1)} %pack.1.refs_3_.after_ref), custom_call_target="tpu_custom_call" | custom-call | flops 2000000000 | bytes 2097152 | tf_op jit(solution)/shard_map/dispatch/pallas_call | solution.py:384
  14.7 2.8 %all-to-all-start = ((bf16[32,16,128]{2,1,0:T(8,128)(2,1)}), bf16[32,16,128]{2,1,0:T(8,128)(2,1)S(1)}, u32[]{:S(2)}, u32[]{:S(2)}) async-start(bf16[32,16,128]{2,1,0:T(8,128)(2,1)} %bitcast.2), calls=%async_computation | async-start | bytes 262144 | tf_op jit(solution)/shard_map/all_to_all | solution.py:392
  17.5 0.3 collective-permute-start.3
  17.8 0.0 collective-permute-done.2.refs_6_
  17.8 0.3 collective-permute-start.6
  18.1 0.0 collective-permute-done.1.refs_5_
  18.1 0.3 collective-permute-start.5
  18.3 0.0 collective-permute-done.refs_4_
  18.3 0.3 collective-permute-start.4
  18.6 0.3 collective-permute-done.3.refs_7_
  18.9 0.3 collective-permute-done.6.refs_10_
  19.2 0.3 collective-permute-done.5.refs_9_
  19.4 0.3 collective-permute-done.4.refs_8_
  19.7 3.7 %attention.1 = (bf16[2,64,2048]{2,1,0:T(8,128)(2,1)}, bf16[2,64,2048]{2,1,0:T(8,128)(2,1)}, bf16[4,2,64,512]{3,2,1,0:T(8,128)(2,1)S(1)}, bf16[2,64,512]{2,1,0:T(...) custom-call(bf16[2,64,2048]{2,1,0:T(8,128)(2,1)S(1)} %copy-done, ...), custom_call_target="tpu_custom_call" | custom-call | flops 1048576 | bytes 8 | tf_op jit(solution)/shard_map/attention/pallas_call | solution.py:131
  23.4 2.3 %all-to-all-done = bf16[32,16,128]{2,1,0:T(8,128)(2,1)S(1)} async-done(((bf16[32,16,128]{2,1,0:T(8,128)(2,1)}), bf16[32,16,128]{2,1,0:T(8,128)(2,1)S(1)}, u32[]{:S(2)}, u32[]{:S(2)}) %all-to-all-start) | async-done | bytes 131104 | tf_op jit(solution)/shard_map/all_to_all | solution.py:392
  25.7 0.3 collective-permute-start.7
  26.0 1.6 %collective-permute-done.7.refs_4_ = bf16[4,2,64,512]{3,2,1,0:T(8,128)(2,1)S(1)} collective-permute-done((bf16[4,2,64,512]{3,2,1,0:T(8,128)(2,1)S(1)}, bf16[4,2,64,512]{3,2,1,0:T(8,128)(2,1)S(1)}, u32[]{:S(2)}, u32[]{:S(2)}) %collective-permute-start.7) | collective-permute-done | bytes 524320 | tf_op jit(solution)/shard_map/ppermute | solution.py:414
  27.6 0.1 merge.1
  27.7 1.4 %collective-permute-start.8 = (bf16[2,64,512]{2,1,0:T(8,128)(2,1)S(1)}, bf16[2,64,512]{2,1,0:T(8,128)(2,1)S(1)}, u32[]{:S(2)}, u32[]{:S(2)}) collective-permute-start(bf16[2,64,512]{2,1,0:T(8,128)(2,1)S(1)} %get-tuple-element.41), channel_id=1, source_target_pairs={{2,0},{3,1},{4,2},{5,3},{6,4},{7,5},{10,8},{11,9},{12,10},{13,11},... | collective-permute-start | bytes 393224 | tf_op jit(solution)/shard_map/ppermute | solution.py:425
  29.1 1.3 %collective-permute-start.10 = (bf16[2,64,512]{2,1,0:T(8,128)(2,1)S(1)}, bf16[2,64,512]{2,1,0:T(8,128)(2,1)S(1)}, u32[]{:S(2)}, u32[]{:S(2)}) collective-permute-start(bf16[2,64,512]{2,1,0:T(8,128)(2,1)S(1)} %get-tuple-element.43), channel_id=1, source_target_pairs={{6,0},{7,1},{14,8},{15,9},{22,16},{23,17},{30,24},{31,25}} | collective-permute-start | bytes 393224 | tf_op jit(solution)/shard_map/ppermute | solution.py:425
  30.5 0.5 enter.1
  30.9 1.0 %collective-permute-start.13 = (bf16[64,768]{1,0:T(8,128)(2,1)S(1)}, bf16[64,768]{1,0:T(8,128)(2,1)S(1)}, u32[]{:S(2)}, u32[]{:S(2)}) collective-permute-start(bf16[64,768]{1,0:T(8,128)(2,1)S(1)} %get-tuple-element.44.refs_0_), channel_id=1, source_target_pairs={{0,24},{8,16},{16,8},{24,0},{1,25},{9,17},{17,9},{25,1},{2,26},{10... | collective-permute-start | bytes 294920 | tf_op jit(solution)/shard_map/ppermute | solution.py:411
  32.0 1.3 %collective-permute-start.12 = (bf16[64,768]{1,0:T(8,128)(2,1)S(1)}, bf16[64,768]{1,0:T(8,128)(2,1)S(1)}, u32[]{:S(2)}, u32[]{:S(2)}) collective-permute-start(bf16[64,768]{1,0:T(8,128)(2,1)S(1)} %get-tuple-element.44.refs_0_), channel_id=1, source_target_pairs={{0,16},{8,24},{16,0},{24,8},{1,17},{9,25},{17,1},{25,9},{2,18},{10... | collective-permute-start | bytes 294920 | tf_op jit(solution)/shard_map/ppermute | solution.py:411
  33.3 1.2 %collective-permute-start.11 = (bf16[64,768]{1,0:T(8,128)(2,1)S(1)}, bf16[64,768]{1,0:T(8,128)(2,1)S(1)}, u32[]{:S(2)}, u32[]{:S(2)}) collective-permute-start(bf16[64,768]{1,0:T(8,128)(2,1)S(1)} %get-tuple-element.44.refs_0_), channel_id=1, source_target_pairs={{0,8},{8,0},{16,24},{24,16},{1,9},{9,1},{17,25},{25,17},{2,10},{10... | collective-permute-start | bytes 294920 | tf_op jit(solution)/shard_map/ppermute | solution.py:411
  34.5 3.1 %collective-permute-done.13.refs_3_ = bf16[64,768]{1,0:T(8,128)(2,1)S(1)} collective-permute-done((bf16[64,768]{1,0:T(8,128)(2,1)S(1)}, bf16[64,768]{1,0:T(8,128)(2,1)S(1)}, u32[]{:S(2)}, u32[]{:S(2)}) %collective-permute-start.13) | collective-permute-done | bytes 98336 | tf_op jit(solution)/shard_map/ppermute | solution.py:411
  37.6 1.1 %collective-permute-done.12.refs_2_ = bf16[64,768]{1,0:T(8,128)(2,1)S(1)} collective-permute-done((bf16[64,768]{1,0:T(8,128)(2,1)S(1)}, bf16[64,768]{1,0:T(8,128)(2,1)S(1)}, u32[]{:S(2)}, u32[]{:S(2)}) %collective-permute-start.12) | collective-permute-done | bytes 98336 | tf_op jit(solution)/shard_map/ppermute | solution.py:411
  38.6 0.0 collective-permute-done.11.refs_1_
  38.6 0.0 collective-permute-done.8.refs_6_.refs_1_
  38.6 4.0 %collective-permute-done.10.refs_7_.refs_3_ = bf16[2,64,512]{2,1,0:T(8,128)(2,1)S(1)} collective-permute-done((bf16[2,64,512]{2,1,0:T(8,128)(2,1)S(1)}, bf16[2,64,512]{2,1,0:T(8,128)(2,1)S(1)}, u32[]{:S(2)}, u32[]{:S(2)}) %collective-permute-start.10) | collective-permute-done | bytes 131104 | tf_op jit(solution)/shard_map/ppermute | solution.py:425
  42.6 1.4 %middle.1 = (bf16[512,128]{1,0:T(8,128)(2,1)}, bf16[64,256]{1,0:T(8,128)(2,1)S(1)}, bf16[64,256]{1,0:T(8,128)(2,1)S(1)}, bf16[64,256]{1,0:T(8,128)(2,1)S(1)}) custom-call(bf16[64,768]{1,0:T(8,128)(2,1)S(1)} %get-tuple-element.44.refs_0_, bf16[64,768]{1,0:T(8,128)(2,1)S(1)} %collective-permute-done.11.refs_1_, ...), custom_call_target="tpu_custom_call" | custom-call | flops 2000000000 | bytes 2097152 | tf_op jit(solution)/shard_map/middle/pallas_call | solution.py:426
  44.1 4.7 %all-to-all-start.1 = ((bf16[32,16,128]{2,1,0:T(8,128)(2,1)}), bf16[32,16,128]{2,1,0:T(8,128)(2,1)S(1)}, u32[]{:S(2)}, u32[]{:S(2)}) async-start(bf16[32,16,128]{2,1,0:T(8,128)(2,1)} %bitcast.4), calls=%async_computation.1 | async-start | bytes 262144 | tf_op jit(solution)/shard_map/all_to_all | solution.py:434
  48.8 1.3 %collective-permute-start.9 = (bf16[2,64,512]{2,1,0:T(8,128)(2,1)S(1)}, bf16[2,64,512]{2,1,0:T(8,128)(2,1)S(1)}, u32[]{:S(2)}, u32[]{:S(2)}) collective-permute-start(bf16[2,64,512]{2,1,0:T(8,128)(2,1)S(1)} %get-tuple-element.42), channel_id=1, source_target_pairs={{4,0},{5,1},{6,2},{7,3},{12,8},{13,9},{14,10},{15,11},{20,16},{21,... | collective-permute-start | bytes 393224 | tf_op jit(solution)/shard_map/ppermute | solution.py:425
  50.1 1.5 %weight_grads.1 = (f32[1,512,256]{2,1,0:T(8,128)}, f32[1,512,256]{2,1,0:T(8,128)}, f32[1,256,512]{2,1,0:T(8,128)}) custom-call(bf16[64,512]{1,0:T(8,128)(2,1)S(1)} %get-tuple-element.51.input_ref, bf16[64,512]{1,0:T(8,128)(2,1)S(1)} %get-tuple-element.52.grad_ref, bf16[64,256]{1,0:T(8,128)(2,1)S(1)} %get-tuple-element.53.hidden_ref, ...), custom_call_target="tpu_custom_call" | custom-call | flops 2000000000 | bytes 2097152 | tf_op jit(solution)/shard_map/weight_grads/pallas_call | solution.py:437
  51.5 5.4 %all-to-all-done.1 = bf16[32,16,128]{2,1,0:T(8,128)(2,1)S(1)} async-done(((bf16[32,16,128]{2,1,0:T(8,128)(2,1)}), bf16[32,16,128]{2,1,0:T(8,128)(2,1)S(1)}, u32[]{:S(2)}, u32[]{:S(2)}) %all-to-all-start.1) | async-done | bytes 131104 | tf_op jit(solution)/shard_map/all_to_all | solution.py:434
  56.9 1.3 %combine.1 = (bf16[128,2048]{1,0:T(8,128)(2,1)}, bf16[10,128]{1,0:T(8,128)(2,1)}) custom-call(bf16[512,128]{1,0:T(8,128)(2,1)S(1)} %bitcast.9, s32[10,128]{1,0:T(8,128)S(1)} %bitcast.12, bf16[10,128]{1,0:T(8,128)(2,1)S(1)} %bitcast.14), custom_call_target="tpu_custom_call" | custom-call | flops 2000000000 | bytes 2097152 | tf_op jit(solution)/shard_map/combine/pallas_call | solution.py:448
  58.2 2.7 %collective-permute-done.9.refs_2_ = bf16[2,64,512]{2,1,0:T(8,128)(2,1)S(1)} collective-permute-done((bf16[2,64,512]{2,1,0:T(8,128)(2,1)S(1)}, bf16[2,64,512]{2,1,0:T(8,128)(2,1)S(1)}, u32[]{:S(2)}, u32[]{:S(2)}) %collective-permute-start.9) | collective-permute-done | bytes 131104 | tf_op jit(solution)/shard_map/ppermute | solution.py:425
  61.0 0.7 %copy-done.3 = bf16[10,128]{1,0:T(8,128)(2,1)S(1)} copy-done((bf16[10,128]{1,0:T(8,128)(2,1)S(1)}, bf16[10,128]{1,0:T(8,128)(2,1)}, u32[]{:S(2)}) %copy-start.3) | copy-done | bytes 2584
  61.6 0.7 %close.1 = (bf16[2,64,256]{2,1,0:T(8,128)(2,1)}, bf16[2,64,256]{2,1,0:T(8,128)(2,1)}) custom-call(bf16[2,64,512]{2,1,0:T(8,128)(2,1)S(1)} %get-tuple-element.40.refs_0_, bf16[2,64,512]{2,1,0:T(8,128)(2,1)S(1)} %collective-permute-done.8.refs_6_.refs_1_, bf16[2,64,512]{2,1,0:T(8,128)(2,1)S(1)} %collective-permute-done.9.refs_2_, ...), custom_call_target="tpu_custom_call" | custom-call | flops 1048576 | bytes 1048576 | tf_op jit(solution)/shard_map/close/pallas_call | solution.py:460
  (20 shorter events, 0.0 us)
Async XLA Ops:
  0.6 12.7 %copy-start.5 = (bf16[128,2048]{1,0:T(8,128)(2,1)S(1)}, bf16[128,2048]{1,0:T(8,128)(2,1)}, u32[]{:S(2)}) copy-start(bf16[128,2048]{1,0:T(8,128)(2,1)} %grad_ref.1) | copy-start | bytes 1572868
  0.7 12.7 %copy-start.4 = (bf16[128,2048]{1,0:T(8,128)(2,1)S(1)}, bf16[128,2048]{1,0:T(8,128)(2,1)}, u32[]{:S(2)}) copy-start(bf16[128,2048]{1,0:T(8,128)(2,1)} %input_ref.1) | copy-start | bytes 1572868
  0.7 0.9 %copy-start.9 = (bf16[2,64,256]{2,1,0:T(8,128)(2,1)S(1)}, bf16[2,64,256]{2,1,0:T(8,128)(2,1)}, u32[]{:S(2)}) copy-start(bf16[2,64,256]{2,1,0:T(8,128)(2,1)} %key_hbm.1) | copy-start | bytes 196612
  1.6 0.8 %copy-start.10 = (bf16[2,64,256]{2,1,0:T(8,128)(2,1)S(1)}, bf16[2,64,256]{2,1,0:T(8,128)(2,1)}, u32[]{:S(2)}) copy-start(bf16[2,64,256]{2,1,0:T(8,128)(2,1)} %value_hbm.1) | copy-start | bytes 196612
  2.4 11.0 %copy-start.11 = (s32[128,10]{0,1:T(8,128)S(1)}, s32[128,10]{0,1:T(8,128)}, u32[]{:S(2)}) copy-start(s32[128,10]{0,1:T(8,128)} %param.19) | copy-start | bytes 15364
  2.4 11.0 %copy-start.12 = (bf16[128,10]{0,1:T(8,128)(2,1)S(1)}, bf16[128,10]{0,1:T(8,128)(2,1)}, u32[]{:S(2)}) copy-start(bf16[128,10]{0,1:T(8,128)(2,1)} %param.20) | copy-start | bytes 7684
  2.6 15.2 %collective-permute-start.2 = (bf16[2,64,512]{2,1,0:T(8,128)(2,1)S(1)}, bf16[2,64,512]{2,1,0:T(8,128)(2,1)S(1)}, u32[]{:S(2)}, u32[]{:S(2)}) collective-permute-start(bf16[2,64,512]{2,1,0:T(8,128)(2,1)S(1)} %pack.1.refs_3_.after_ref), channel_id=1, source_target_pairs={{0,6},{1,7},{8,14},{9,15},{16,22},{17,23},{24,30},{25,31}} | collective-permute-start | bytes 393224 | tf_op jit(solution)/shard_map/ppermute | solution.py:380
  9.6 8.5 %collective-permute-start.1 = (bf16[2,64,512]{2,1,0:T(8,128)(2,1)S(1)}, bf16[2,64,512]{2,1,0:T(8,128)(2,1)S(1)}, u32[]{:S(2)}, u32[]{:S(2)}) collective-permute-start(bf16[2,64,512]{2,1,0:T(8,128)(2,1)S(1)} %pack.1.refs_3_.after_ref), channel_id=1, source_target_pairs={{0,4},{1,5},{2,6},{3,7},{8,12},{9,13},{10,14},{11,15},{16,20},{17,... | collective-permute-start | bytes 393224 | tf_op jit(solution)/shard_map/ppermute | solution.py:380
  10.9 7.4 %collective-permute-start = (bf16[2,64,512]{2,1,0:T(8,128)(2,1)S(1)}, bf16[2,64,512]{2,1,0:T(8,128)(2,1)S(1)}, u32[]{:S(2)}, u32[]{:S(2)}) collective-permute-start(bf16[2,64,512]{2,1,0:T(8,128)(2,1)S(1)} %pack.1.refs_3_.after_ref), channel_id=1, source_target_pairs={{0,2},{1,3},{2,4},{3,5},{4,6},{5,7},{8,10},{9,11},{10,12},{11,13},... | collective-permute-start | bytes 393224 | tf_op jit(solution)/shard_map/ppermute | solution.py:380
  13.4 6.3 %copy-start = (bf16[2,64,2048]{2,1,0:T(8,128)(2,1)S(1)}, bf16[2,64,2048]{2,1,0:T(8,128)(2,1)}, u32[]{:S(2)}) copy-start(bf16[2,64,2048]{2,1,0:T(8,128)(2,1)} %refs_0_.1) | copy-start | bytes 1572868
  13.4 6.3 %copy-start.1 = (bf16[2,64,2048]{2,1,0:T(8,128)(2,1)S(1)}, bf16[2,64,2048]{2,1,0:T(8,128)(2,1)}, u32[]{:S(2)}) copy-start(bf16[2,64,2048]{2,1,0:T(8,128)(2,1)} %refs_1_.1) | copy-start | bytes 1572868
  13.4 6.3 %copy-start.2 = (bf16[2,64,2048]{2,1,0:T(8,128)(2,1)S(1)}, bf16[2,64,2048]{2,1,0:T(8,128)(2,1)}, u32[]{:S(2)}) copy-start(bf16[2,64,2048]{2,1,0:T(8,128)(2,1)} %refs_2_.1) | copy-start | bytes 1572868
  14.7 11.0 %all-to-all-start = ((bf16[32,16,128]{2,1,0:T(8,128)(2,1)}), bf16[32,16,128]{2,1,0:T(8,128)(2,1)S(1)}, u32[]{:S(2)}, u32[]{:S(2)}) async-start(bf16[32,16,128]{2,1,0:T(8,128)(2,1)} %bitcast.2), calls=%async_computation | async-start | bytes 262144 | tf_op jit(solution)/shard_map/all_to_all | solution.py:392
  17.5 1.4 %collective-permute-start.3 = (bf16[2,64,512]{2,1,0:T(8,128)(2,1)S(1)}, bf16[2,64,512]{2,1,0:T(8,128)(2,1)S(1)}, u32[]{:S(2)}, u32[]{:S(2)}) collective-permute-start(bf16[2,64,512]{2,1,0:T(8,128)(2,1)S(1)} %pack.1.refs_3_.after_ref), channel_id=1, source_target_pairs={{0,1},{1,0},{2,3},{3,2},{4,5},{5,4},{6,7},{7,6},{8,9},{9,8},{10,11... | collective-permute-start | bytes 393224 | tf_op jit(solution)/shard_map/ppermute | solution.py:381
  17.8 1.3 %collective-permute-start.6 = (bf16[2,64,512]{2,1,0:T(8,128)(2,1)S(1)}, bf16[2,64,512]{2,1,0:T(8,128)(2,1)S(1)}, u32[]{:S(2)}, u32[]{:S(2)}) collective-permute-start(bf16[2,64,512]{2,1,0:T(8,128)(2,1)S(1)} %collective-permute-done.2.refs_6_), channel_id=1, source_target_pairs={{0,1},{1,0},{2,3},{3,2},{4,5},{5,4},{6,7},{7,6},{8,9},{9,8},{10,11... | collective-permute-start | bytes 393224 | tf_op jit(solution)/shard_map/ppermute | solution.py:381
  18.1 1.3 %collective-permute-start.5 = (bf16[2,64,512]{2,1,0:T(8,128)(2,1)S(1)}, bf16[2,64,512]{2,1,0:T(8,128)(2,1)S(1)}, u32[]{:S(2)}, u32[]{:S(2)}) collective-permute-start(bf16[2,64,512]{2,1,0:T(8,128)(2,1)S(1)} %collective-permute-done.1.refs_5_), channel_id=1, source_target_pairs={{0,1},{1,0},{2,3},{3,2},{4,5},{5,4},{6,7},{7,6},{8,9},{9,8},{10,11... | collective-permute-start | bytes 393224 | tf_op jit(solution)/shard_map/ppermute | solution.py:381
  18.3 1.3 %collective-permute-start.4 = (bf16[2,64,512]{2,1,0:T(8,128)(2,1)S(1)}, bf16[2,64,512]{2,1,0:T(8,128)(2,1)S(1)}, u32[]{:S(2)}, u32[]{:S(2)}) collective-permute-start(bf16[2,64,512]{2,1,0:T(8,128)(2,1)S(1)} %collective-permute-done.refs_4_), channel_id=1, source_target_pairs={{0,1},{1,0},{2,3},{3,2},{4,5},{5,4},{6,7},{7,6},{8,9},{9,8},{10,11... | collective-permute-start | bytes 393224 | tf_op jit(solution)/shard_map/ppermute | solution.py:381
  25.7 1.9 %collective-permute-start.7 = (bf16[4,2,64,512]{3,2,1,0:T(8,128)(2,1)S(1)}, bf16[4,2,64,512]{3,2,1,0:T(8,128)(2,1)S(1)}, u32[]{:S(2)}, u32[]{:S(2)}) collective-permute-start(bf16[4,2,64,512]{3,2,1,0:T(8,128)(2,1)S(1)} %gate.1.after_ref), channel_id=1, source_target_pairs={{0,1},{1,0},{2,3},{3,2},{4,5},{5,4},{6,7},{7,6},{8,9},{9,8},{10,11... | collective-permute-start | bytes 1572872 | tf_op jit(solution)/shard_map/ppermute | solution.py:414
  27.6 2.9 %copy-start.6 = (bf16[1,256,512]{2,1,0:T(8,128)(2,1)S(1)}, bf16[1,256,512]{2,1,0:T(8,128)(2,1)}, u32[]{:S(2)}) copy-start(bf16[1,256,512]{2,1,0:T(8,128)(2,1)} %down_ref.1) | copy-start | bytes 786436
  27.6 2.9 %copy-start.7 = (bf16[1,512,256]{2,1,0:T(8,128)(2,1)S(1)}, bf16[1,512,256]{2,1,0:T(8,128)(2,1)}, u32[]{:S(2)}) copy-start(bf16[1,512,256]{2,1,0:T(8,128)(2,1)} %refs_4_.1) | copy-start | bytes 786436
  27.6 2.9 %copy-start.8 = (bf16[1,512,256]{2,1,0:T(8,128)(2,1)S(1)}, bf16[1,512,256]{2,1,0:T(8,128)(2,1)}, u32[]{:S(2)}) copy-start(bf16[1,512,256]{2,1,0:T(8,128)(2,1)} %refs_5_.1) | copy-start | bytes 786436
  27.7 10.9 %collective-permute-start.8 = (bf16[2,64,512]{2,1,0:T(8,128)(2,1)S(1)}, bf16[2,64,512]{2,1,0:T(8,128)(2,1)S(1)}, u32[]{:S(2)}, u32[]{:S(2)}) collective-permute-start(bf16[2,64,512]{2,1,0:T(8,128)(2,1)S(1)} %get-tuple-element.41), channel_id=1, source_target_pairs={{2,0},{3,1},{4,2},{5,3},{6,4},{7,5},{10,8},{11,9},{12,10},{13,11},... | collective-permute-start | bytes 393224 | tf_op jit(solution)/shard_map/ppermute | solution.py:425
  29.1 13.5 %collective-permute-start.10 = (bf16[2,64,512]{2,1,0:T(8,128)(2,1)S(1)}, bf16[2,64,512]{2,1,0:T(8,128)(2,1)S(1)}, u32[]{:S(2)}, u32[]{:S(2)}) collective-permute-start(bf16[2,64,512]{2,1,0:T(8,128)(2,1)S(1)} %get-tuple-element.43), channel_id=1, source_target_pairs={{6,0},{7,1},{14,8},{15,9},{22,16},{23,17},{30,24},{31,25}} | collective-permute-start | bytes 393224 | tf_op jit(solution)/shard_map/ppermute | solution.py:425
  30.9 6.6 %collective-permute-start.13 = (bf16[64,768]{1,0:T(8,128)(2,1)S(1)}, bf16[64,768]{1,0:T(8,128)(2,1)S(1)}, u32[]{:S(2)}, u32[]{:S(2)}) collective-permute-start(bf16[64,768]{1,0:T(8,128)(2,1)S(1)} %get-tuple-element.44.refs_0_), channel_id=1, source_target_pairs={{0,24},{8,16},{16,8},{24,0},{1,25},{9,17},{17,9},{25,1},{2,26},{10... | collective-permute-start | bytes 294920 | tf_op jit(solution)/shard_map/ppermute | solution.py:411
  32.0 6.7 %collective-permute-start.12 = (bf16[64,768]{1,0:T(8,128)(2,1)S(1)}, bf16[64,768]{1,0:T(8,128)(2,1)S(1)}, u32[]{:S(2)}, u32[]{:S(2)}) collective-permute-start(bf16[64,768]{1,0:T(8,128)(2,1)S(1)} %get-tuple-element.44.refs_0_), channel_id=1, source_target_pairs={{0,16},{8,24},{16,0},{24,8},{1,17},{9,25},{17,1},{25,9},{2,18},{10... | collective-permute-start | bytes 294920 | tf_op jit(solution)/shard_map/ppermute | solution.py:411
  33.3 5.4 %collective-permute-start.11 = (bf16[64,768]{1,0:T(8,128)(2,1)S(1)}, bf16[64,768]{1,0:T(8,128)(2,1)S(1)}, u32[]{:S(2)}, u32[]{:S(2)}) collective-permute-start(bf16[64,768]{1,0:T(8,128)(2,1)S(1)} %get-tuple-element.44.refs_0_), channel_id=1, source_target_pairs={{0,8},{8,0},{16,24},{24,16},{1,9},{9,1},{17,25},{25,17},{2,10},{10... | collective-permute-start | bytes 294920 | tf_op jit(solution)/shard_map/ppermute | solution.py:411
  44.1 12.9 %all-to-all-start.1 = ((bf16[32,16,128]{2,1,0:T(8,128)(2,1)}), bf16[32,16,128]{2,1,0:T(8,128)(2,1)S(1)}, u32[]{:S(2)}, u32[]{:S(2)}) async-start(bf16[32,16,128]{2,1,0:T(8,128)(2,1)} %bitcast.4), calls=%async_computation.1 | async-start | bytes 262144 | tf_op jit(solution)/shard_map/all_to_all | solution.py:434
  48.8 12.2 %collective-permute-start.9 = (bf16[2,64,512]{2,1,0:T(8,128)(2,1)S(1)}, bf16[2,64,512]{2,1,0:T(8,128)(2,1)S(1)}, u32[]{:S(2)}, u32[]{:S(2)}) collective-permute-start(bf16[2,64,512]{2,1,0:T(8,128)(2,1)S(1)} %get-tuple-element.42), channel_id=1, source_target_pairs={{4,0},{5,1},{6,2},{7,3},{12,8},{13,9},{14,10},{15,11},{20,16},{21,... | collective-permute-start | bytes 393224 | tf_op jit(solution)/shard_map/ppermute | solution.py:425
  60.9 0.7 %copy-start.3 = (bf16[10,128]{1,0:T(8,128)(2,1)S(1)}, bf16[10,128]{1,0:T(8,128)(2,1)}, u32[]{:S(2)}) copy-start(bf16[10,128]{1,0:T(8,128)(2,1)} %get-tuple-element.46.refs_4_) | copy-start | bytes 7684

commit v11 on v9

--- a/solution.py
+++ b/solution.py
@@ -429,7 +429,7 @@
         in_specs=[IN_VMEM] * (len(parts) + 2) + [ANYWHERE],
         out_shape=[jax.ShapeDtypeStruct((sources * rows, LANES), BF16)] + [hid_rows] * 3,
         compiler_params=params(16 if groups <= 4 else 60),
-        cost_estimate=cost(8, 8),
+        cost_estimate=cost(8e8, MIB),
         name="middle",
     )(*parts, gate_proj, up_proj, terms[min(1, chips - 1)])
     returned = lax.all_to_all(

time: 57 us -> 54.4 us (0.954)
  waiting for transfers between devices: 13.4 us -> 10.8 us
    ppermute x3, waiting for transfers between devices: 4.05 us -> 1.46 us  [shards(): lax.ppermute(sent, 'dp', [(g, g ^ k) for g in range(groups)])]
    ppermute x3, waiting for transfers between devices: 0.01 us -> 2.35 us  [shards(): terms.append(lax.ppermute(merged[d], 'expert', down))]
    all_to_all x1, waiting for transfers between devices: 5.98 us -> 3.64 us  [shards(): lax.all_to_all(back.reshape(sources, rows, LANES), axes, split_axis=0, co...]
  transfers between devices with their start and end apart: 16 -> 16, of which waited for: 7 -> 8; matrix products, arithmetic and copies ran while one was open for 0% -> 0% of each run, Pallas kernels for 16% -> 17%
where the time goes in v11:
time: 54.4 us; the launch traced here: 54 us
  starting transfers between devices  29.2 us (54%)
  waiting for transfers between devices  10.8 us (20%)
  Pallas kernels  10.6 us (19%)
  local copies, waits for them, and re-layouts  2.52 us (5%)
  between operations  0.85 us (2%)
    ppermute x3, starting transfers between devices, shards(): mine.append(lax.ppermute(packed, 'expert', up))  10.7 us
    all_to_all x1, starting transfers between devices, shards(): lax.all_to_all(back.reshape(sources, rows, LANES), axes, split_axis=0, co...  6.73 us
    ppermute x3, starting transfers between devices, shards(): terms.append(lax.ppermute(merged[d], 'expert', down))  3.86 us
    pallas_call x1, Pallas kernels, attention(): pl.pallas_call(functools.partial(attention_kernel, chips), in_specs=[IN_V...  3.7 us
    all_to_all x1, waiting for transfers between devices, shards(): lax.all_to_all(back.reshape(sources, rows, LANES), axes, split_axis=0, co...  3.64 us
    ppermute x3, starting transfers between devices, shards(): lax.ppermute(sent, 'dp', [(g, g ^ k) for g in range(groups)])  3.62 us
    all_to_all x1, starting transfers between devices, shards(): lax.all_to_all(send.reshape(sources, rows, LANES), axes, split_axis=0, co...  2.81 us
    unnamed x26, local copies, waits for them, and re-layouts  2.52 us
  transfers between devices with their start and end apart: 16, of which 8 were waited for; matrix products, arithmetic and copies ran while one was open for 0% of the time, Pallas kernels for 17%

profile of v11, /device:TPU:0, one launch (start us, length us, event | category | flops | bytes accessed | tf_op | source)
XLA Modules:
  0.0 54.0 jit_solution(16639279455616022665)
XLA Ops:
  0.7 0.9 %copy-done.8 = bf16[2,64,256]{2,1,0:T(8,128)(2,1)S(1)} copy-done((bf16[2,64,256]{2,1,0:T(8,128)(2,1)S(1)}, bf16[2,64,256]{2,1,0:T(8,128)(2,1)}, u32[]{:S(2)}) %copy-start.8) | copy-done | bytes 65560
  1.6 0.8 %copy-done.9 = bf16[2,64,256]{2,1,0:T(8,128)(2,1)S(1)} copy-done((bf16[2,64,256]{2,1,0:T(8,128)(2,1)S(1)}, bf16[2,64,256]{2,1,0:T(8,128)(2,1)}, u32[]{:S(2)}) %copy-start.9) | copy-done | bytes 65560
  2.4 0.2 pack.1.refs_3_.after_ref
  2.6 4.9 %collective-permute-start = (bf16[2,64,512]{2,1,0:T(8,128)(2,1)S(1)}, bf16[2,64,512]{2,1,0:T(8,128)(2,1)S(1)}, u32[]{:S(2)}, u32[]{:S(2)}) collective-permute-start(bf16[2,64,512]{2,1,0:T(8,128)(2,1)S(1)} %pack.1.refs_3_.after_ref), channel_id=1, source_target_pairs={{0,2},{1,3},{2,4},{3,5},{4,6},{5,7},{8,10},{9,11},{10,12},{11,13},... | collective-permute-start | bytes 393224 | tf_op jit(solution)/shard_map/ppermute | solution.py:381
  7.6 4.5 %collective-permute-start.1 = (bf16[2,64,512]{2,1,0:T(8,128)(2,1)S(1)}, bf16[2,64,512]{2,1,0:T(8,128)(2,1)S(1)}, u32[]{:S(2)}, u32[]{:S(2)}) collective-permute-start(bf16[2,64,512]{2,1,0:T(8,128)(2,1)S(1)} %pack.1.refs_3_.after_ref), channel_id=1, source_target_pairs={{0,4},{1,5},{2,6},{3,7},{8,12},{9,13},{10,14},{11,15},{16,20},{17,... | collective-permute-start | bytes 393224 | tf_op jit(solution)/shard_map/ppermute | solution.py:381
  12.1 1.3 %collective-permute-start.2 = (bf16[2,64,512]{2,1,0:T(8,128)(2,1)S(1)}, bf16[2,64,512]{2,1,0:T(8,128)(2,1)S(1)}, u32[]{:S(2)}, u32[]{:S(2)}) collective-permute-start(bf16[2,64,512]{2,1,0:T(8,128)(2,1)S(1)} %pack.1.refs_3_.after_ref), channel_id=1, source_target_pairs={{0,6},{1,7},{8,14},{9,15},{16,22},{17,23},{24,30},{25,31}} | collective-permute-start | bytes 393224 | tf_op jit(solution)/shard_map/ppermute | solution.py:381
  13.4 0.0 copy-start
  13.4 0.0 copy-start.1
  13.4 0.0 copy-start.2
  13.5 1.2 %dispatch.1 = bf16[512,128]{1,0:T(8,128)(2,1)} custom-call(bf16[128,2048]{1,0:T(8,128)(2,1)S(1)} %copy-done.3, bf16[128,2048]{1,0:T(8,128)(2,1)S(1)} %copy-done.4, s32[10,128]{1,0:T(8,128)S(1)} %bitcast.10, bf16[10,128]{1,0:T(8,128)(2,1)S(1)} %bitcast.12, bf16[2,64,512]{2,1,0:T(8,128)(2,1)S(1)} %pack.1.refs_3_.after_ref), custom_call_target="tpu_custom_call" | custom-call | flops 2000000000 | bytes 2097152 | tf_op jit(solution)/shard_map/dispatch/pallas_call | solution.py:385
  14.7 2.8 %all-to-all-start = ((bf16[32,16,128]{2,1,0:T(8,128)(2,1)}), bf16[32,16,128]{2,1,0:T(8,128)(2,1)S(1)}, u32[]{:S(2)}, u32[]{:S(2)}) async-start(bf16[32,16,128]{2,1,0:T(8,128)(2,1)} %bitcast.2), calls=%async_computation | async-start | bytes 262144 | tf_op jit(solution)/shard_map/all_to_all | solution.py:393
  17.5 0.3 collective-permute-start.3
  17.8 0.0 collective-permute-done.refs_4_
  17.8 0.3 collective-permute-start.4
  18.1 0.0 collective-permute-done.1.refs_5_
  18.1 0.3 collective-permute-start.5
  18.3 0.0 collective-permute-done.2.refs_6_
  18.3 0.3 collective-permute-start.6
  18.6 0.3 collective-permute-done.3.refs_7_
  18.9 0.3 collective-permute-done.4.refs_8_
  19.2 0.3 collective-permute-done.5.refs_9_
  19.4 0.3 collective-permute-done.6.refs_10_
  19.7 3.7 %attention.1 = (bf16[2,64,2048]{2,1,0:T(8,128)(2,1)}, bf16[2,64,2048]{2,1,0:T(8,128)(2,1)}, bf16[4,2,64,512]{3,2,1,0:T(8,128)(2,1)S(1)}, bf16[2,64,512]{2,1,0:T(...) custom-call(bf16[2,64,2048]{2,1,0:T(8,128)(2,1)S(1)} %copy-done, ...), custom_call_target="tpu_custom_call" | custom-call | flops 1048576 | bytes 8 | tf_op jit(solution)/shard_map/attention/pallas_call | solution.py:131
  23.4 2.3 %all-to-all-done = bf16[32,16,128]{2,1,0:T(8,128)(2,1)S(1)} async-done(((bf16[32,16,128]{2,1,0:T(8,128)(2,1)}), bf16[32,16,128]{2,1,0:T(8,128)(2,1)S(1)}, u32[]{:S(2)}, u32[]{:S(2)}) %all-to-all-start) | async-done | bytes 131104 | tf_op jit(solution)/shard_map/all_to_all | solution.py:393
  25.7 0.4 collective-permute-start.7
  26.1 0.6 %copy-done.5 = bf16[1,256,512]{2,1,0:T(8,128)(2,1)S(1)} copy-done((bf16[1,256,512]{2,1,0:T(8,128)(2,1)S(1)}, bf16[1,256,512]{2,1,0:T(8,128)(2,1)}, u32[]{:S(2)}) %copy-start.5) | copy-done | bytes 262168
  26.6 0.1 copy-done.6
  26.7 0.1 copy-done.7
  26.8 0.5 enter.1
  27.2 0.9 %collective-permute-start.11 = (bf16[64,768]{1,0:T(8,128)(2,1)S(1)}, bf16[64,768]{1,0:T(8,128)(2,1)S(1)}, u32[]{:S(2)}, u32[]{:S(2)}) collective-permute-start(bf16[64,768]{1,0:T(8,128)(2,1)S(1)} %get-tuple-element.47.refs_0_), channel_id=1, source_target_pairs={{0,8},{8,0},{16,24},{24,16},{1,9},{9,1},{17,25},{25,17},{2,10},{10... | collective-permute-start | bytes 294920 | tf_op jit(solution)/shard_map/ppermute | solution.py:412
  28.1 0.0 collective-permute-done.7.refs_4_
  28.1 0.1 merge.1
  28.3 1.3 %collective-permute-start.8 = (bf16[2,64,512]{2,1,0:T(8,128)(2,1)S(1)}, bf16[2,64,512]{2,1,0:T(8,128)(2,1)S(1)}, u32[]{:S(2)}, u32[]{:S(2)}) collective-permute-start(bf16[2,64,512]{2,1,0:T(8,128)(2,1)S(1)} %get-tuple-element.41), channel_id=1, source_target_pairs={{2,0},{3,1},{4,2},{5,3},{6,4},{7,5},{10,8},{11,9},{12,10},{13,11},... | collective-permute-start | bytes 393224 | tf_op jit(solution)/shard_map/ppermute | solution.py:426
  29.6 0.8 %collective-permute-start.12 = (bf16[64,768]{1,0:T(8,128)(2,1)S(1)}, bf16[64,768]{1,0:T(8,128)(2,1)S(1)}, u32[]{:S(2)}, u32[]{:S(2)}) collective-permute-start(bf16[64,768]{1,0:T(8,128)(2,1)S(1)} %get-tuple-element.47.refs_0_), channel_id=1, source_target_pairs={{0,16},{8,24},{16,0},{24,8},{1,17},{9,25},{17,1},{25,9},{2,18},{10... | collective-permute-start | bytes 294920 | tf_op jit(solution)/shard_map/ppermute | solution.py:412
  30.3 2.0 %collective-permute-start.13 = (bf16[64,768]{1,0:T(8,128)(2,1)S(1)}, bf16[64,768]{1,0:T(8,128)(2,1)S(1)}, u32[]{:S(2)}, u32[]{:S(2)}) collective-permute-start(bf16[64,768]{1,0:T(8,128)(2,1)S(1)} %get-tuple-element.47.refs_0_), channel_id=1, source_target_pairs={{0,24},{8,16},{16,8},{24,0},{1,25},{9,17},{17,9},{25,1},{2,26},{10... | collective-permute-start | bytes 294920 | tf_op jit(solution)/shard_map/ppermute | solution.py:412
  32.3 1.3 %collective-permute-start.10 = (bf16[2,64,512]{2,1,0:T(8,128)(2,1)S(1)}, bf16[2,64,512]{2,1,0:T(8,128)(2,1)S(1)}, u32[]{:S(2)}, u32[]{:S(2)}) collective-permute-start(bf16[2,64,512]{2,1,0:T(8,128)(2,1)S(1)} %get-tuple-element.43), channel_id=1, source_target_pairs={{6,0},{7,1},{14,8},{15,9},{22,16},{23,17},{30,24},{31,25}} | collective-permute-start | bytes 393224 | tf_op jit(solution)/shard_map/ppermute | solution.py:426
  33.6 0.0 collective-permute-done.11.refs_1_
  33.6 1.3 %collective-permute-start.9 = (bf16[2,64,512]{2,1,0:T(8,128)(2,1)S(1)}, bf16[2,64,512]{2,1,0:T(8,128)(2,1)S(1)}, u32[]{:S(2)}, u32[]{:S(2)}) collective-permute-start(bf16[2,64,512]{2,1,0:T(8,128)(2,1)S(1)} %get-tuple-element.42), channel_id=1, source_target_pairs={{4,0},{5,1},{6,2},{7,3},{12,8},{13,9},{14,10},{15,11},{20,16},{21,... | collective-permute-start | bytes 393224 | tf_op jit(solution)/shard_map/ppermute | solution.py:426
  34.9 1.5 %collective-permute-done.12.refs_2_ = bf16[64,768]{1,0:T(8,128)(2,1)S(1)} collective-permute-done((bf16[64,768]{1,0:T(8,128)(2,1)S(1)}, bf16[64,768]{1,0:T(8,128)(2,1)S(1)}, u32[]{:S(2)}, u32[]{:S(2)}) %collective-permute-start.12) | collective-permute-done | bytes 98336 | tf_op jit(solution)/shard_map/ppermute | solution.py:412
  36.4 0.0 collective-permute-done.13.refs_3_
  36.4 0.0 collective-permute-done.8.refs_1_.refs_6_
  36.4 1.4 %middle.1 = (bf16[512,128]{1,0:T(8,128)(2,1)}, bf16[64,256]{1,0:T(8,128)(2,1)S(1)}, bf16[64,256]{1,0:T(8,128)(2,1)S(1)}, bf16[64,256]{1,0:T(8,128)(2,1)S(1)}) custom-call(bf16[64,768]{1,0:T(8,128)(2,1)S(1)} %get-tuple-element.47.refs_0_, bf16[64,768]{1,0:T(8,128)(2,1)S(1)} %collective-permute-done.11.refs_1_, ...), custom_call_target="tpu_custom_call" | custom-call | flops 800000000 | bytes 1048576 | tf_op jit(solution)/shard_map/middle/pallas_call | solution.py:427
  37.8 6.7 %all-to-all-start.1 = ((bf16[32,16,128]{2,1,0:T(8,128)(2,1)}), bf16[32,16,128]{2,1,0:T(8,128)(2,1)S(1)}, u32[]{:S(2)}, u32[]{:S(2)}) async-start(bf16[32,16,128]{2,1,0:T(8,128)(2,1)} %bitcast.4), calls=%async_computation.1 | async-start | bytes 262144 | tf_op jit(solution)/shard_map/all_to_all | solution.py:435
  44.5 2.3 %collective-permute-done.9.refs_2_ = bf16[2,64,512]{2,1,0:T(8,128)(2,1)S(1)} collective-permute-done((bf16[2,64,512]{2,1,0:T(8,128)(2,1)S(1)}, bf16[2,64,512]{2,1,0:T(8,128)(2,1)S(1)}, u32[]{:S(2)}, u32[]{:S(2)}) %collective-permute-start.9) | collective-permute-done | bytes 131104 | tf_op jit(solution)/shard_map/ppermute | solution.py:426
  46.9 0.7 %close.1 = (bf16[2,64,256]{2,1,0:T(8,128)(2,1)}, bf16[2,64,256]{2,1,0:T(8,128)(2,1)}) custom-call(bf16[2,64,512]{2,1,0:T(8,128)(2,1)S(1)} %get-tuple-element.40.refs_0_, bf16[2,64,512]{2,1,0:T(8,128)(2,1)S(1)} %collective-permute-done.8.refs_1_.refs_6_, bf16[2,64,512]{2,1,0:T(8,128)(2,1)S(1)} %collective-permute-done.9.refs_2_, ...), custom_call_target="tpu_custom_call" | custom-call | flops 60000002048 | bytes 1048576 | tf_op jit(solution)/shard_map/close/pallas_call | solution.py:449
  47.6 1.5 %weight_grads.1 = (f32[1,512,256]{2,1,0:T(8,128)}, f32[1,512,256]{2,1,0:T(8,128)}, f32[1,256,512]{2,1,0:T(8,128)}) custom-call(bf16[64,512]{1,0:T(8,128)(2,1)S(1)} %get-tuple-element.51.input_ref, bf16[64,512]{1,0:T(8,128)(2,1)S(1)} %get-tuple-element.52.grad_ref, bf16[64,256]{1,0:T(8,128)(2,1)S(1)} %get-tuple-element.53.hidden_ref, ...), custom_call_target="tpu_custom_call" | custom-call | flops 2000000000 | bytes 2097152 | tf_op jit(solution)/shard_map/weight_grads/pallas_call | solution.py:438
  49.1 3.6 %all-to-all-done.1 = bf16[32,16,128]{2,1,0:T(8,128)(2,1)S(1)} async-done(((bf16[32,16,128]{2,1,0:T(8,128)(2,1)}), bf16[32,16,128]{2,1,0:T(8,128)(2,1)S(1)}, u32[]{:S(2)}, u32[]{:S(2)}) %all-to-all-start.1) | async-done | bytes 131104 | tf_op jit(solution)/shard_map/all_to_all | solution.py:435
  52.7 1.3 %combine.1 = (bf16[128,2048]{1,0:T(8,128)(2,1)}, bf16[10,128]{1,0:T(8,128)(2,1)}) custom-call(bf16[512,128]{1,0:T(8,128)(2,1)S(1)} %bitcast.9, s32[10,128]{1,0:T(8,128)S(1)} %bitcast.11, bf16[10,128]{1,0:T(8,128)(2,1)S(1)} %bitcast.13, bf16[2,64,256]{2,1,0:T(8,128)(2,1)S(1)} %copy-done.12), custom_call_target="tpu_custom_call" | custom-call | flops 2000000000 | bytes 2097152 | tf_op jit(solution)/shard_map/combine/pallas_call | solution.py:457
  (20 shorter events, 0.0 us)
Async XLA Ops:
  0.6 12.7 %copy-start.3 = (bf16[128,2048]{1,0:T(8,128)(2,1)S(1)}, bf16[128,2048]{1,0:T(8,128)(2,1)}, u32[]{:S(2)}) copy-start(bf16[128,2048]{1,0:T(8,128)(2,1)} %input_ref.1) | copy-start | bytes 1572868
  0.7 12.7 %copy-start.4 = (bf16[128,2048]{1,0:T(8,128)(2,1)S(1)}, bf16[128,2048]{1,0:T(8,128)(2,1)}, u32[]{:S(2)}) copy-start(bf16[128,2048]{1,0:T(8,128)(2,1)} %grad_ref.1) | copy-start | bytes 1572868
  0.7 0.9 %copy-start.8 = (bf16[2,64,256]{2,1,0:T(8,128)(2,1)S(1)}, bf16[2,64,256]{2,1,0:T(8,128)(2,1)}, u32[]{:S(2)}) copy-start(bf16[2,64,256]{2,1,0:T(8,128)(2,1)} %key_hbm.1) | copy-start | bytes 196612
  1.6 0.8 %copy-start.9 = (bf16[2,64,256]{2,1,0:T(8,128)(2,1)S(1)}, bf16[2,64,256]{2,1,0:T(8,128)(2,1)}, u32[]{:S(2)}) copy-start(bf16[2,64,256]{2,1,0:T(8,128)(2,1)} %value_hbm.1) | copy-start | bytes 196612
  2.4 11.0 %copy-start.10 = (s32[128,10]{0,1:T(8,128)S(1)}, s32[128,10]{0,1:T(8,128)}, u32[]{:S(2)}) copy-start(s32[128,10]{0,1:T(8,128)} %param.19) | copy-start | bytes 15364
  2.4 11.0 %copy-start.11 = (bf16[128,10]{0,1:T(8,128)(2,1)S(1)}, bf16[128,10]{0,1:T(8,128)(2,1)}, u32[]{:S(2)}) copy-start(bf16[128,10]{0,1:T(8,128)(2,1)} %param.20) | copy-start | bytes 7684
  2.6 15.2 %collective-permute-start = (bf16[2,64,512]{2,1,0:T(8,128)(2,1)S(1)}, bf16[2,64,512]{2,1,0:T(8,128)(2,1)S(1)}, u32[]{:S(2)}, u32[]{:S(2)}) collective-permute-start(bf16[2,64,512]{2,1,0:T(8,128)(2,1)S(1)} %pack.1.refs_3_.after_ref), channel_id=1, source_target_pairs={{0,2},{1,3},{2,4},{3,5},{4,6},{5,7},{8,10},{9,11},{10,12},{11,13},... | collective-permute-start | bytes 393224 | tf_op jit(solution)/shard_map/ppermute | solution.py:381
  7.6 10.5 %collective-permute-start.1 = (bf16[2,64,512]{2,1,0:T(8,128)(2,1)S(1)}, bf16[2,64,512]{2,1,0:T(8,128)(2,1)S(1)}, u32[]{:S(2)}, u32[]{:S(2)}) collective-permute-start(bf16[2,64,512]{2,1,0:T(8,128)(2,1)S(1)} %pack.1.refs_3_.after_ref), channel_id=1, source_target_pairs={{0,4},{1,5},{2,6},{3,7},{8,12},{9,13},{10,14},{11,15},{16,20},{17,... | collective-permute-start | bytes 393224 | tf_op jit(solution)/shard_map/ppermute | solution.py:381
  12.1 6.3 %collective-permute-start.2 = (bf16[2,64,512]{2,1,0:T(8,128)(2,1)S(1)}, bf16[2,64,512]{2,1,0:T(8,128)(2,1)S(1)}, u32[]{:S(2)}, u32[]{:S(2)}) collective-permute-start(bf16[2,64,512]{2,1,0:T(8,128)(2,1)S(1)} %pack.1.refs_3_.after_ref), channel_id=1, source_target_pairs={{0,6},{1,7},{8,14},{9,15},{16,22},{17,23},{24,30},{25,31}} | collective-permute-start | bytes 393224 | tf_op jit(solution)/shard_map/ppermute | solution.py:381
  13.4 6.3 %copy-start = (bf16[2,64,2048]{2,1,0:T(8,128)(2,1)S(1)}, bf16[2,64,2048]{2,1,0:T(8,128)(2,1)}, u32[]{:S(2)}) copy-start(bf16[2,64,2048]{2,1,0:T(8,128)(2,1)} %refs_0_.1) | copy-start | bytes 1572868
  13.4 6.3 %copy-start.1 = (bf16[2,64,2048]{2,1,0:T(8,128)(2,1)S(1)}, bf16[2,64,2048]{2,1,0:T(8,128)(2,1)}, u32[]{:S(2)}) copy-start(bf16[2,64,2048]{2,1,0:T(8,128)(2,1)} %refs_1_.1) | copy-start | bytes 1572868
  13.4 6.3 %copy-start.2 = (bf16[2,64,2048]{2,1,0:T(8,128)(2,1)S(1)}, bf16[2,64,2048]{2,1,0:T(8,128)(2,1)}, u32[]{:S(2)}) copy-start(bf16[2,64,2048]{2,1,0:T(8,128)(2,1)} %refs_2_.1) | copy-start | bytes 1572868
  14.7 11.0 %all-to-all-start = ((bf16[32,16,128]{2,1,0:T(8,128)(2,1)}), bf16[32,16,128]{2,1,0:T(8,128)(2,1)S(1)}, u32[]{:S(2)}, u32[]{:S(2)}) async-start(bf16[32,16,128]{2,1,0:T(8,128)(2,1)} %bitcast.2), calls=%async_computation | async-start | bytes 262144 | tf_op jit(solution)/shard_map/all_to_all | solution.py:393
  17.5 1.4 %collective-permute-start.3 = (bf16[2,64,512]{2,1,0:T(8,128)(2,1)S(1)}, bf16[2,64,512]{2,1,0:T(8,128)(2,1)S(1)}, u32[]{:S(2)}, u32[]{:S(2)}) collective-permute-start(bf16[2,64,512]{2,1,0:T(8,128)(2,1)S(1)} %pack.1.refs_3_.after_ref), channel_id=1, source_target_pairs={{0,1},{1,0},{2,3},{3,2},{4,5},{5,4},{6,7},{7,6},{8,9},{9,8},{10,11... | collective-permute-start | bytes 393224 | tf_op jit(solution)/shard_map/ppermute | solution.py:382
  17.8 1.3 %collective-permute-start.4 = (bf16[2,64,512]{2,1,0:T(8,128)(2,1)S(1)}, bf16[2,64,512]{2,1,0:T(8,128)(2,1)S(1)}, u32[]{:S(2)}, u32[]{:S(2)}) collective-permute-start(bf16[2,64,512]{2,1,0:T(8,128)(2,1)S(1)} %collective-permute-done.refs_4_), channel_id=1, source_target_pairs={{0,1},{1,0},{2,3},{3,2},{4,5},{5,4},{6,7},{7,6},{8,9},{9,8},{10,11... | collective-permute-start | bytes 393224 | tf_op jit(solution)/shard_map/ppermute | solution.py:382
  18.1 1.3 %collective-permute-start.5 = (bf16[2,64,512]{2,1,0:T(8,128)(2,1)S(1)}, bf16[2,64,512]{2,1,0:T(8,128)(2,1)S(1)}, u32[]{:S(2)}, u32[]{:S(2)}) collective-permute-start(bf16[2,64,512]{2,1,0:T(8,128)(2,1)S(1)} %collective-permute-done.1.refs_5_), channel_id=1, source_target_pairs={{0,1},{1,0},{2,3},{3,2},{4,5},{5,4},{6,7},{7,6},{8,9},{9,8},{10,11... | collective-permute-start | bytes 393224 | tf_op jit(solution)/shard_map/ppermute | solution.py:382
  18.3 1.3 %collective-permute-start.6 = (bf16[2,64,512]{2,1,0:T(8,128)(2,1)S(1)}, bf16[2,64,512]{2,1,0:T(8,128)(2,1)S(1)}, u32[]{:S(2)}, u32[]{:S(2)}) collective-permute-start(bf16[2,64,512]{2,1,0:T(8,128)(2,1)S(1)} %collective-permute-done.2.refs_6_), channel_id=1, source_target_pairs={{0,1},{1,0},{2,3},{3,2},{4,5},{5,4},{6,7},{7,6},{8,9},{9,8},{10,11... | collective-permute-start | bytes 393224 | tf_op jit(solution)/shard_map/ppermute | solution.py:382
  25.7 1.0 %copy-start.5 = (bf16[1,256,512]{2,1,0:T(8,128)(2,1)S(1)}, bf16[1,256,512]{2,1,0:T(8,128)(2,1)}, u32[]{:S(2)}) copy-start(bf16[1,256,512]{2,1,0:T(8,128)(2,1)} %down_ref.1) | copy-start | bytes 786436
  25.7 1.0 %copy-start.6 = (bf16[1,512,256]{2,1,0:T(8,128)(2,1)S(1)}, bf16[1,512,256]{2,1,0:T(8,128)(2,1)}, u32[]{:S(2)}) copy-start(bf16[1,512,256]{2,1,0:T(8,128)(2,1)} %refs_4_.1) | copy-start | bytes 786436
  25.7 1.1 %copy-start.7 = (bf16[1,512,256]{2,1,0:T(8,128)(2,1)S(1)}, bf16[1,512,256]{2,1,0:T(8,128)(2,1)}, u32[]{:S(2)}) copy-start(bf16[1,512,256]{2,1,0:T(8,128)(2,1)} %refs_5_.1) | copy-start | bytes 786436
  25.7 2.4 %collective-permute-start.7 = (bf16[4,2,64,512]{3,2,1,0:T(8,128)(2,1)S(1)}, bf16[4,2,64,512]{3,2,1,0:T(8,128)(2,1)S(1)}, u32[]{:S(2)}, u32[]{:S(2)}) collective-permute-start(bf16[4,2,64,512]{3,2,1,0:T(8,128)(2,1)S(1)} %gate.1.after_ref), channel_id=1, source_target_pairs={{0,1},{1,0},{2,3},{3,2},{4,5},{5,4},{6,7},{7,6},{8,9},{9,8},{10,11... | collective-permute-start | bytes 1572872 | tf_op jit(solution)/shard_map/ppermute | solution.py:415
  27.2 6.3 %collective-permute-start.11 = (bf16[64,768]{1,0:T(8,128)(2,1)S(1)}, bf16[64,768]{1,0:T(8,128)(2,1)S(1)}, u32[]{:S(2)}, u32[]{:S(2)}) collective-permute-start(bf16[64,768]{1,0:T(8,128)(2,1)S(1)} %get-tuple-element.47.refs_0_), channel_id=1, source_target_pairs={{0,8},{8,0},{16,24},{24,16},{1,9},{9,1},{17,25},{25,17},{2,10},{10... | collective-permute-start | bytes 294920 | tf_op jit(solution)/shard_map/ppermute | solution.py:412
  28.3 8.1 %collective-permute-start.8 = (bf16[2,64,512]{2,1,0:T(8,128)(2,1)S(1)}, bf16[2,64,512]{2,1,0:T(8,128)(2,1)S(1)}, u32[]{:S(2)}, u32[]{:S(2)}) collective-permute-start(bf16[2,64,512]{2,1,0:T(8,128)(2,1)S(1)} %get-tuple-element.41), channel_id=1, source_target_pairs={{2,0},{3,1},{4,2},{5,3},{6,4},{7,5},{10,8},{11,9},{12,10},{13,11},... | collective-permute-start | bytes 393224 | tf_op jit(solution)/shard_map/ppermute | solution.py:426
  29.6 6.8 %collective-permute-start.12 = (bf16[64,768]{1,0:T(8,128)(2,1)S(1)}, bf16[64,768]{1,0:T(8,128)(2,1)S(1)}, u32[]{:S(2)}, u32[]{:S(2)}) collective-permute-start(bf16[64,768]{1,0:T(8,128)(2,1)S(1)} %get-tuple-element.47.refs_0_), channel_id=1, source_target_pairs={{0,16},{8,24},{16,0},{24,8},{1,17},{9,25},{17,1},{25,9},{2,18},{10... | collective-permute-start | bytes 294920 | tf_op jit(solution)/shard_map/ppermute | solution.py:412
  30.3 6.0 %collective-permute-start.13 = (bf16[64,768]{1,0:T(8,128)(2,1)S(1)}, bf16[64,768]{1,0:T(8,128)(2,1)S(1)}, u32[]{:S(2)}, u32[]{:S(2)}) collective-permute-start(bf16[64,768]{1,0:T(8,128)(2,1)S(1)} %get-tuple-element.47.refs_0_), channel_id=1, source_target_pairs={{0,24},{8,16},{16,8},{24,0},{1,25},{9,17},{17,9},{25,1},{2,26},{10... | collective-permute-start | bytes 294920 | tf_op jit(solution)/shard_map/ppermute | solution.py:412
  32.3 12.2 %collective-permute-start.10 = (bf16[2,64,512]{2,1,0:T(8,128)(2,1)S(1)}, bf16[2,64,512]{2,1,0:T(8,128)(2,1)S(1)}, u32[]{:S(2)}, u32[]{:S(2)}) collective-permute-start(bf16[2,64,512]{2,1,0:T(8,128)(2,1)S(1)} %get-tuple-element.43), channel_id=1, source_target_pairs={{6,0},{7,1},{14,8},{15,9},{22,16},{23,17},{30,24},{31,25}} | collective-permute-start | bytes 393224 | tf_op jit(solution)/shard_map/ppermute | solution.py:426
  33.6 13.3 %collective-permute-start.9 = (bf16[2,64,512]{2,1,0:T(8,128)(2,1)S(1)}, bf16[2,64,512]{2,1,0:T(8,128)(2,1)S(1)}, u32[]{:S(2)}, u32[]{:S(2)}) collective-permute-start(bf16[2,64,512]{2,1,0:T(8,128)(2,1)S(1)} %get-tuple-element.42), channel_id=1, source_target_pairs={{4,0},{5,1},{6,2},{7,3},{12,8},{13,9},{14,10},{15,11},{20,16},{21,... | collective-permute-start | bytes 393224 | tf_op jit(solution)/shard_map/ppermute | solution.py:426
  37.8 14.9 %all-to-all-start.1 = ((bf16[32,16,128]{2,1,0:T(8,128)(2,1)}), bf16[32,16,128]{2,1,0:T(8,128)(2,1)S(1)}, u32[]{:S(2)}, u32[]{:S(2)}) async-start(bf16[32,16,128]{2,1,0:T(8,128)(2,1)} %bitcast.4), calls=%async_computation.1 | async-start | bytes 262144 | tf_op jit(solution)/shard_map/all_to_all | solution.py:435
  47.6 5.1 %copy-start.12 = (bf16[2,64,256]{2,1,0:T(8,128)(2,1)S(1)}, bf16[2,64,256]{2,1,0:T(8,128)(2,1)}, u32[]{:S(2)}) copy-start(bf16[2,64,256]{2,1,0:T(8,128)(2,1)} %get-tuple-element.26.after_ref) | copy-start | bytes 196612
